TPU v7x, 32 devices: a whole 2x2x4 slice. The times are simulated.
32 devices in a mesh: seq: 16 (over z, y, core), blk: 2 (over x).
Axes of the slice: x: 2, y: 2, z: 4, core: 2. Of those that a mesh axis runs over, the one named last changes fastest.
Arguments:
- hidden: bfloat16 [32, 1024, 768], P('seq', 'blk'), may hold values from -6 to 6
- segments: int32 [32, 1024], P('seq', 'blk'), may hold values from 0 to 1023, as said below
- query_matrix: bfloat16 [768, 768], replicated, may hold values from -0.21875 to 0.21875
- query_bias: bfloat16 [768], replicated, may hold values from -3 to 3
- key_matrix: bfloat16 [768, 768], replicated, may hold values from -0.21875 to 0.21875
- value_matrix: bfloat16 [768, 768], replicated, may hold values from -0.21875 to 0.21875
- value_bias: bfloat16 [768], replicated, may hold values from -3 to 3
- output_matrix: bfloat16 [768, 768], replicated, may hold values from -0.875 to 0.875
- output_bias: bfloat16 [768], replicated, may hold values from -3 to 3
- first_gain: bfloat16 [768], replicated, may hold values from 0.5 to 1.5
- first_shift: bfloat16 [768], replicated, may hold values from -3 to 3
- inner_matrix: bfloat16 [768, 3072], replicated, may hold values from -0.21875 to 0.21875
- inner_bias: bfloat16 [3072], replicated, may hold values from -3 to 3
- outer_matrix: bfloat16 [3072, 768], replicated, may hold values from -0.109375 to 0.109375
- outer_bias: bfloat16 [768], replicated, may hold values from -3 to 3
- second_gain: bfloat16 [768], replicated, may hold values from 0.5 to 1.5
- second_shift: bfloat16 [768], replicated, may hold values from -3 to 3
- cotangent: bfloat16 [32, 1024, 768], P('seq', 'blk'), may hold values from -6 to 6
Outputs:
- layer_out: bfloat16 [32, 1024, 768], P('seq', 'blk')
- hidden_grad: float32 [32, 1024, 768], P('seq', 'blk')
- query_weight_grad: float32 [768, 768], P('seq', 'blk')
- query_bias_grad: float32 [768], replicated
- key_matrix_gradient: float32 [768, 768], P('seq', 'blk')
- value_weight_grad: float32 [768, 768], P('seq', 'blk')
- value_bias_grad: float32 [768], replicated
- output_weight_grad: float32 [768, 768], P('seq', 'blk')
- output_bias_grad: float32 [768], replicated
- first_gain_grad: float32 [768], replicated
- first_shift_grad: float32 [768], replicated
- inner_weight_grad: float32 [768, 3072], P('seq', 'blk')
- inner_bias_grad: float32 [3072], replicated
- outer_weight_grad: float32 [3072, 768], P('seq', 'blk')
- outer_bias_grad: float32 [768], replicated
- second_gain_grad: float32 [768], replicated
- second_shift_grad: float32 [768], replicated
Inputs may be any that keep to these rules, and one draw needn't show every extreme that they name: `segments`: each position's id is the first position of its word-region pair in the sequence, so ids never fall and equal ids mark one pair; the last position starts a pair of its own. Of the 2 sequences on one index of seq, one holds a pair that reaches from the positions of the first index of blk to those of the last.
All inputs are finite; a program needn't handle non-finite values.
Results may differ from a plain program's by a relative error of at most 0.014.
Values may be sent and summed in bfloat16 or wider, within the bound.
No kernel may reach another device: no remote copies, remote signals or barrier semaphores. Data moves between devices by JAX's collectives and lax.ppermute only.
A program may use at most 256 MiB of HBM per device.

v0:
```python
import math

import jax
import jax.numpy as jnp
from jax import lax
from jax.sharding import PartitionSpec as P

HEADS = 12
HEAD = 64


NEGATIVE = -1e30
EPSILON = 1e-12


def layer_norm(values, norm_gain, norm_shift):
    centre = values - jnp.mean(values, axis=-1, keepdims=True)
    spread = jnp.mean(centre * centre, axis=-1, keepdims=True)
    return centre * lax.rsqrt(spread + EPSILON) * norm_gain + norm_shift


def gelu_exact(values):
    return jax.nn.gelu(values, approximate=False)


def linear(operand, matrix):
    return jnp.dot(operand, matrix, preferred_element_type=jnp.float32)


def split_heads(values):
    return values.reshape(values.shape[0], values.shape[1], HEADS, HEAD)


def block_scores(query_block, key_block, score_scale):
    return (
        jnp.einsum("sqhd,skhd->shqk", query_block, key_block, preferred_element_type=jnp.float32)
        * score_scale
    )


def attention_grads(
    query_block, key_block, value_block, dctx_block, same_doc, log_total, row_delta, score_scale
):
    attn_probs = jnp.where(
        same_doc,
        jnp.exp(block_scores(query_block, key_block, score_scale) - log_total[..., None]),
        0.0,
    )
    slopes = jnp.einsum(
        "sqhd,skhd->shqk", dctx_block, value_block, preferred_element_type=jnp.float32
    )
    return (attn_probs, (attn_probs * (slopes - row_delta[..., None])).astype(jnp.bfloat16))


def over_blocks(length, step, initial):
    block_size = math.gcd(length, 512)

    def scan_step(carried, block_index):
        return (step(carried, block_index * block_size, block_size), None)

    result, unused = lax.scan(scan_step, initial, jnp.arange(length // block_size, dtype=jnp.int32))
    return result


def local(
    hidden,
    segments,
    query_matrix,
    query_bias,
    key_matrix,
    value_matrix,
    value_bias,
    output_matrix,
    output_bias,
    first_gain,
    first_shift,
    inner_matrix,
    inner_bias,
    outer_matrix,
    outer_bias,
    second_gain,
    second_shift,
    cotangent,
):
    seq_count, row_count, model_width = hidden.shape
    score_scale = HEAD ** (-0.5)
    single_float = jnp.float32
    bf16 = jnp.bfloat16
    queries = (linear(hidden, query_matrix) + query_bias.astype(single_float)).astype(bf16)
    key_proj = linear(hidden, key_matrix).astype(bf16)
    value_proj = (linear(hidden, value_matrix) + value_bias.astype(single_float)).astype(bf16)
    seg_all = lax.all_gather(segments, "blk", axis=1, tiled=True)
    keys_all, values_all = (
        lax.all_gather(key_proj, "blk", axis=1, tiled=True),
        lax.all_gather(value_proj, "blk", axis=1, tiled=True),
    )
    length = seg_all.shape[1]
    query_heads = split_heads(queries)
    key_heads = split_heads(keys_all)
    value_heads = split_heads(values_all)

    def key_slices(offset, block_size):
        key_segs = lax.dynamic_slice_in_dim(seg_all, offset, block_size, 1)
        same_doc = (segments[:, :, None] == key_segs[:, None, :])[:, None]
        key_block = lax.dynamic_slice_in_dim(key_heads, offset, block_size, 1)
        value_block = lax.dynamic_slice_in_dim(value_heads, offset, block_size, 1)
        return (same_doc, key_block, value_block)

    def stats_step(carried, offset, block_size):
        same_doc, key_block, value_block = key_slices(offset, block_size)
        running_max, running_sum = carried
        scores = jnp.where(same_doc, block_scores(query_heads, key_block, score_scale), NEGATIVE)
        higher = jnp.maximum(running_max, jnp.max(scores, axis=-1))
        weights = jnp.where(same_doc, jnp.exp(scores - higher[..., None]), 0.0)
        return (higher, running_sum * jnp.exp(running_max - higher) + jnp.sum(weights, axis=-1))

    stat_shape = (seq_count, HEADS, row_count)
    running_max, running_sum = over_blocks(
        length,
        stats_step,
        (jnp.full(stat_shape, NEGATIVE, single_float), jnp.zeros(stat_shape, single_float)),
    )
    log_total = running_max + jnp.log(running_sum)

    def context_step(carried, offset, block_size):
        same_doc, key_block, value_block = key_slices(offset, block_size)
        attn_probs = jnp.where(
            same_doc,
            jnp.exp(block_scores(query_heads, key_block, score_scale) - log_total[..., None]),
            0.0,
        )
        return carried + jnp.einsum(
            "shqk,skhd->sqhd",
            attn_probs.astype(bf16),
            value_block,
            preferred_element_type=single_float,
        )

    head_zeros = jnp.zeros((seq_count, row_count, HEADS, HEAD), single_float)
    context = over_blocks(length, context_step, head_zeros)
    context_reduced = context.reshape(seq_count, row_count, model_width).astype(bf16)
    attn_out = linear(context_reduced, output_matrix) + output_bias.astype(single_float)
    first_pre = hidden.astype(single_float) + attn_out
    first_norm, first_back = jax.vjp(
        layer_norm, first_pre, first_gain.astype(single_float), first_shift.astype(single_float)
    )
    first_reduced = first_norm.astype(bf16)
    inner = linear(first_reduced, inner_matrix) + inner_bias.astype(single_float)
    act_full, gelu_back = jax.vjp(gelu_exact, inner)
    activation_reduced = act_full.astype(bf16)
    outer = linear(activation_reduced, outer_matrix) + outer_bias.astype(single_float)
    layer_full, second_back = jax.vjp(
        layer_norm,
        first_norm + outer,
        second_gain.astype(single_float),
        second_shift.astype(single_float),
    )
    layer_out = layer_full.astype(bf16)
    second_pre_grad, second_gain_grad, second_shift_grad = second_back(
        cotangent.astype(single_float)
    )
    outer_gradient_reduced = second_pre_grad.astype(bf16)
    outer_weight_grad = jnp.einsum(
        "gvx,gvm->xm",
        activation_reduced,
        outer_gradient_reduced,
        preferred_element_type=single_float,
    )
    outer_bias_grad = jnp.sum(outer_gradient_reduced.astype(single_float), axis=(0, 1))
    activation_gradient = jnp.einsum(
        "rzo,uo->rzu", outer_gradient_reduced, outer_matrix, preferred_element_type=single_float
    )
    inner_gradient_reduced = gelu_back(activation_gradient)[0].astype(bf16)
    inner_weight_grad = jnp.einsum(
        "ret,reu->tu", first_reduced, inner_gradient_reduced, preferred_element_type=single_float
    )
    inner_bias_grad = jnp.sum(inner_gradient_reduced.astype(single_float), axis=(0, 1))
    first_norm_grad = second_pre_grad + jnp.einsum(
        "aoi,ni->aon", inner_gradient_reduced, inner_matrix, preferred_element_type=single_float
    )
    first_pre_grad, first_gain_grad, first_shift_grad = first_back(first_norm_grad)
    attention_gradient_reduced = first_pre_grad.astype(bf16)
    output_weight_grad = jnp.einsum(
        "tfm,tfc->mc",
        context_reduced,
        attention_gradient_reduced,
        preferred_element_type=single_float,
    )
    output_bias_grad = jnp.sum(attention_gradient_reduced.astype(single_float), axis=(0, 1))
    dctx_low = jnp.einsum(
        "upx,cx->upc",
        attention_gradient_reduced,
        output_matrix,
        preferred_element_type=single_float,
    ).astype(bf16)
    dctx_heads = split_heads(dctx_low)
    row_delta = jnp.transpose(
        jnp.sum(dctx_heads.astype(single_float) * context, axis=-1), (0, 2, 1)
    )

    def query_step(carried, offset, block_size):
        same_doc, key_block, value_block = key_slices(offset, block_size)
        attn_probs, dscores = attention_grads(
            query_heads,
            key_block,
            value_block,
            dctx_heads,
            same_doc,
            log_total,
            row_delta,
            score_scale,
        )
        return carried + score_scale * jnp.einsum(
            "shqk,skhd->sqhd", dscores, key_block, preferred_element_type=single_float
        )

    query_grad = over_blocks(length, query_step, head_zeros)
    query_all, dctx_all = (
        lax.all_gather(queries, "blk", axis=1, tiled=True),
        lax.all_gather(dctx_low, "blk", axis=1, tiled=True),
    )
    lse_all, delta_all = (
        lax.all_gather(log_total, "blk", axis=2, tiled=True),
        lax.all_gather(row_delta, "blk", axis=2, tiled=True),
    )
    query_all_heads = split_heads(query_all)
    dctx_all_heads = split_heads(dctx_all)
    own_keys = split_heads(key_proj)
    own_values = split_heads(value_proj)

    def key_step(carried, offset, block_size):
        query_segs = lax.dynamic_slice_in_dim(seg_all, offset, block_size, 1)
        same_doc = (query_segs[:, :, None] == segments[:, None, :])[:, None]
        query_block = lax.dynamic_slice_in_dim(query_all_heads, offset, block_size, 1)
        dctx_block = lax.dynamic_slice_in_dim(dctx_all_heads, offset, block_size, 1)
        lse_block = lax.dynamic_slice_in_dim(lse_all, offset, block_size, 2)
        delta_block = lax.dynamic_slice_in_dim(delta_all, offset, block_size, 2)
        key_sum, value_sum = carried
        attn_probs, dscores = attention_grads(
            query_block,
            own_keys,
            own_values,
            dctx_block,
            same_doc,
            lse_block,
            delta_block,
            score_scale,
        )
        key_sum = key_sum + score_scale * jnp.einsum(
            "shqk,sqhd->skhd", dscores, query_block, preferred_element_type=single_float
        )
        value_sum = value_sum + jnp.einsum(
            "shqk,sqhd->skhd",
            attn_probs.astype(bf16),
            dctx_block,
            preferred_element_type=single_float,
        )
        return (key_sum, value_sum)

    key_grad, value_grad = over_blocks(length, key_step, (head_zeros, head_zeros))
    query_gradient_reduced = query_grad.reshape(seq_count, row_count, model_width).astype(bf16)
    key_gradient_reduced = key_grad.reshape(seq_count, row_count, model_width).astype(bf16)
    value_gradient_reduced = value_grad.reshape(seq_count, row_count, model_width).astype(bf16)
    query_weight_grad = jnp.einsum(
        "tfm,tfc->mc", hidden, query_gradient_reduced, preferred_element_type=single_float
    )
    query_bias_grad = jnp.sum(query_gradient_reduced.astype(single_float), axis=(0, 1))
    key_matrix_gradient = jnp.einsum(
        "tfm,tfc->mc", hidden, key_gradient_reduced, preferred_element_type=single_float
    )
    value_weight_grad = jnp.einsum(
        "tfm,tfc->mc", hidden, value_gradient_reduced, preferred_element_type=single_float
    )
    value_bias_grad = jnp.sum(value_gradient_reduced.astype(single_float), axis=(0, 1))
    hidden_grad = first_pre_grad + jnp.einsum(
        "upx,cx->upc", query_gradient_reduced, query_matrix, preferred_element_type=single_float
    )
    hidden_grad = hidden_grad + jnp.einsum(
        "upx,cx->upc", key_gradient_reduced, key_matrix, preferred_element_type=single_float
    )
    hidden_grad = hidden_grad + jnp.einsum(
        "upx,cx->upc", value_gradient_reduced, value_matrix, preferred_element_type=single_float
    )
    partial_sums = (
        lax.psum_scatter(query_weight_grad, "seq", scatter_dimension=0, tiled=True),
        lax.psum_scatter(key_matrix_gradient, "seq", scatter_dimension=0, tiled=True),
        lax.psum_scatter(value_weight_grad, "seq", scatter_dimension=0, tiled=True),
        lax.psum_scatter(output_weight_grad, "seq", scatter_dimension=0, tiled=True),
        lax.psum_scatter(inner_weight_grad, "seq", scatter_dimension=0, tiled=True),
        lax.psum_scatter(outer_weight_grad, "seq", scatter_dimension=0, tiled=True),
    )
    matrices = lax.psum_scatter(tuple(partial_sums), "blk", scatter_dimension=1, tiled=True)
    vectors = lax.psum(
        (
            query_bias_grad,
            value_bias_grad,
            output_bias_grad,
            first_gain_grad,
            first_shift_grad,
            inner_bias_grad,
            outer_bias_grad,
            second_gain_grad,
            second_shift_grad,
        ),
        ("seq", "blk"),
    )
    return (
        layer_out,
        hidden_grad,
        matrices[0],
        vectors[0],
        matrices[1],
        matrices[2],
        vectors[1],
        matrices[3],
        vectors[2],
        vectors[3],
        vectors[4],
        matrices[4],
        vectors[5],
        matrices[5],
        vectors[6],
        vectors[7],
        vectors[8],
    )


def solution(mesh):
    return jax.shard_map(
        local,
        mesh=mesh,
        in_specs=(
            P("seq", "blk", None),
            P("seq", "blk"),
            P(),
            P(),
            P(),
            P(),
            P(),
            P(),
            P(),
            P(),
            P(),
            P(),
            P(),
            P(),
            P(),
            P(),
            P(),
            P("seq", "blk", None),
        ),
        out_specs=(
            P("seq", "blk", None),
            P("seq", "blk", None),
            P("seq", "blk"),
            P(),
            P("seq", "blk"),
            P("seq", "blk"),
            P(),
            P("seq", "blk"),
            P(),
            P(),
            P(),
            P("seq", "blk"),
            P(),
            P("seq", "blk"),
            P(),
            P(),
            P(),
        ),
        check_vma=False,
    )
```

profile of v0, /device:TPU:0, one launch (start us, length us, event | category | flops | bytes accessed | tf_op | source)
XLA Modules:
  0.0 972.3 jit_solution(17483320459694805828)
XLA Ops:
  7.3 4.5 convolution_convert_fusion.1
  27.6 5.3 all_gather.22
  34.8 24.9 %all-gather.7.cloned.1.call-done = bf16[2,1024,768]{2,1,0:T(8,128)(2,1)} async-done(((bf16[2,512,768]{2,1,0:T(8,128)(2,1)}), bf16[2,1024,768]{2,1,0:T(8,128)(2,1)}) %all-gather.7.cloned.1.call-update) | async-done | bytes 3145744 | tf_op jit(solution)/shard_map/all_gather | solution.py:94
  59.7 4.7 copy.78
  64.3 50.5 %while.48 = (s32[]{:T(128)}, f32[2,12,512]{2,1,0:T(8,128)S(1)}, f32[2,12,512]{2,1,0:T(8,128)S(1)}, s32[2,512]{1,0:T(2,128)S(1)}, s32[2]{0:T(128)S(1)}, /*index=5...) while((s32[]{:T(128)}, f32[2,12,512]{2,1,0:T(8,128)S(1)}, ...), condition=%wide.region_3.4_spmd.clone, body=%wide.region_0.3_spmd.clone.sunk | while | flops 856223744 | bytes 55705792 | solution.py:61
  66.0 12.3 %fusion.156 = (f32[2,12,512]{2,1,0:T(8,128)S(1)}, f32[2,12,512,512]{3,2,1,0:T(8,128)}) fusion(pred[2,512,512]{1,2,0:T(8,128)(4,1)S(1)} %broadcast_compare_fusion.8, bf16[2,512,12,64]{1,3,2,0:T(8,128)(2,1)S(1)} %get-tuple-element.897, bf16[2,1024,12,64]{1,3,2,0:T(8,128)(2,1)} %get-tuple-element.896, s32[]{:T(128)S(6)} %select_n.89), kind=kOutput, calls=%fused_computation.2.clone.1 | convolution fusion | flops 824168448 | bytes 28884996 | tf_op jit(solution)/shard_map/while/body/eval_jaxpr/sqhd,skhd->shqk/dot_general | solution.py:36
  78.2 11.4 %select_reduce_fusion.2 = f32[2,12,512]{2,1,0:T(8,128)S(1)} fusion(f32[2,12,512,512]{3,2,1,0:T(8,128)} %get-tuple-element.831, f32[2,12,512]{2,1,0:T(8,128)S(1)} %select_maximum_fusion.2, pred[2,512,512]{1,2,0:T(8,128)(4,1)S(1)} %broadcast_compare_fusion.8), kind=kLoop, calls=%fused_computation.1.clone.1 | loop fusion | flops 31444992 | bytes 25788416 | tf_op jit(solution)/shard_map/while/body/eval_jaxpr/reduce_sum | solution.py:115
  91.4 12.0 %fusion.156 = (f32[2,12,512]{2,1,0:T(8,128)S(1)}, f32[2,12,512,512]{3,2,1,0:T(8,128)}) fusion(pred[2,512,512]{1,2,0:T(8,128)(4,1)S(1)} %broadcast_compare_fusion.8, bf16[2,512,12,64]{1,3,2,0:T(8,128)(2,1)S(1)} %get-tuple-element.897, bf16[2,1024,12,64]{1,3,2,0:T(8,128)(2,1)} %get-tuple-element.896, s32[]{:T(128)S(6)} %select_n.89), kind=kOutput, calls=%fused_computation.2.clone.1 | convolution fusion | flops 824168448 | bytes 28884996 | tf_op jit(solution)/shard_map/while/body/eval_jaxpr/sqhd,skhd->shqk/dot_general | solution.py:36
  103.3 11.4 %select_reduce_fusion.2 = f32[2,12,512]{2,1,0:T(8,128)S(1)} fusion(f32[2,12,512,512]{3,2,1,0:T(8,128)} %get-tuple-element.831, f32[2,12,512]{2,1,0:T(8,128)S(1)} %select_maximum_fusion.2, pred[2,512,512]{1,2,0:T(8,128)(4,1)S(1)} %broadcast_compare_fusion.8), kind=kLoop, calls=%fused_computation.1.clone.1 | loop fusion | flops 31444992 | bytes 25788416 | tf_op jit(solution)/shard_map/while/body/eval_jaxpr/reduce_sum | solution.py:115
  114.9 4.8 copy.77
  119.7 24.6 %while.49 = (s32[]{:T(128)}, f32[2,512,12,64]{1,3,2,0:T(8,128)}, s32[2]{0:T(128)S(1)}, bf16[2,1024,12,64]{1,3,2,0:T(8,128)(2,1)}, s32[2,512]{1,0:T(2,128)S(1)}, ...) while((s32[]{:T(128)}, f32[2,512,12,64]{1,3,2,0:T(8,128)}, ...), condition=%wide.region_5.6_spmd.clone, body=%wide.region_4.5_spmd.clone.sunk | while | flops 1637875712 | bytes 12125892 | solution.py:61
  121.4 10.4 %bitcast_add_fusion.8 = f32[2,512,12,64]{1,3,2,0:T(8,128)} fusion(f32[2,512,12,64]{1,3,2,0:T(8,128)} %get-tuple-element.916, f32[2,12,512]{2,1,0:T(8,128)S(1)} %get-tuple-element.936, pred[2,512,512]{1,2,0:T(8,128)(4,1)S(1)} %broadcast_compare_fusion.9, bf16[2,512,12,64]{1,3,2,0:T(8,128)(2,1)S(1)} %get-tuple-element.935, ...), kind=kOutput, calls=%fused_computation.16.clone.1 | convolution fusion | flops 1637351424 | bytes 11585024 | tf_op jit(solution)/shard_map/while/body/eval_jaxpr/shqk,skhd->sqhd/dot_general | solution.py:132
  133.4 10.9 %bitcast_add_fusion.8 = f32[2,512,12,64]{1,3,2,0:T(8,128)} fusion(f32[2,512,12,64]{1,3,2,0:T(8,128)} %get-tuple-element.916, f32[2,12,512]{2,1,0:T(8,128)S(1)} %get-tuple-element.936, pred[2,512,512]{1,2,0:T(8,128)(4,1)S(1)} %broadcast_compare_fusion.9, bf16[2,512,12,64]{1,3,2,0:T(8,128)(2,1)S(1)} %get-tuple-element.935, ...), kind=kOutput, calls=%fused_computation.16.clone.1 | convolution fusion | flops 1637351424 | bytes 11585024 | tf_op jit(solution)/shard_map/while/body/eval_jaxpr/shqk,skhd->sqhd/dot_general | solution.py:132
  150.0 13.5 %fusion.80 = (u8[512,3072]{1,0:T(8,128)(4,1)S(1)}, u8[512,3072]{1,0:T(8,128)(4,1)S(1)}, f32[2,512,3072]{2,1,0:T(8,128)}) fusion(f32[3072]{0:T(1024)S(1)} %convert_element_type.133, bf16[768,3072]{1,0:T(8,128)(2,1)S(1)} %bitcast.202, f32[2,512,768]{2,1,0:T(8,128)S(1)} %get-tuple-element.607, f32[768]{0:T(1024)S(1)} %convert_element_type.131, ...), kind=kOutput, calls=%fused_computation.124 | convolution fusion | flops 4876664832 | bytes 23619584 | tf_op jit(solution)/shard_map/dot_general | solution.py:27
  163.5 31.6 %multiply_convert_fusion.4 = (bf16[2,512,3072]{2,1,0:T(8,128)(2,1)S(1)}, f32[2,512,3072]{2,1,0:T(8,128)}) fusion(f32[2,512,3072]{2,1,0:T(8,128)} %get-tuple-element.608, f32[3072]{0:T(1024)S(1)} %convert_element_type.133, u8[512,3072]{1,0:T(8,128)(4,1)S(1)} %get-tuple-element.489, u8[512,3072]{1,0:T(8,128)(4,1)S(1)} %get-tuple-element.488), kind=kLoop, calls=%fused_computation.76 | loop fusion | flops 223346688 | bytes 34615296 | tf_op jit(solution)/shard_map/convert_element_type | solution.py:150
  195.2 10.0 %fusion.104 = (f32[2,512]{1,0:T(2,128)S(1)}, f32[2,512,768]{2,1,0:T(8,128)S(1)}) fusion(f32[768]{0:T(1024)S(1)} %copy-done.37, bf16[2,512,3072]{2,1,0:T(8,128)(2,1)S(1)} %get-tuple-element.597, bf16[3072,768]{1,0:T(8,128)(2,1)} %param.39, f32[768]{0:T(1024)S(1)} %convert_element_type.131, f32[768]{0:T(1024)S(1)} %convert_element_type.130, ...), kind=kOutput, calls=%fused_computation.159 | convolution fusion | flops 4837342208 | bytes 17323008 | tf_op jit(solution)/shard_map/dot_general | solution.py:27
  213.3 18.7 %convert_reduce_fusion = (f32[3072]{0:T(1024)}, bf16[2,512,3072]{2,1,0:T(8,128)(2,1)}) fusion(f32[2,512,3072]{2,1,0:T(8,128)} %get-tuple-element.598, bf16[2,512,768]{2,1,0:T(8,128)(2,1)} %get-tuple-element.588, bf16[3072,768]{1,0:T(8,128)(2,1)} %param.39, f32[2,512,3072]{2,1,0:T(8,128)} %get-tuple-element.608, f32[3072]{0:T(1024)S(1)} %convert_element_type.133), kind=kOutput, calls=%fused_computation.74 | convolution fusion | flops 4885312512 | bytes 37773312 | tf_op jit(solution)/shard_map/rzo,uo->rzu/dot_general | solution.py:170
  232.0 11.4 %multiply_reduce_fusion = (f32[768]{0:T(1024)}, f32[2,512]{1,0:T(2,128)S(1)}, f32[768]{0:T(1024)}, f32[2,512,768]{2,1,0:T(8,128)S(1)}) fusion(f32[2,512,768]{2,1,0:T(8,128)} %copy-done.5, f32[2,512]{1,0:T(2,128)S(1)} %fusion.98, f32[2,512]{1,0:T(2,128)S(1)} %broadcast_multiply_fusion.1, f32[768]{0:T(1024)S(1)} %convert_element_type.130, ...), kind=kOutput, calls=%fused_computation.108 | convolution fusion | flops 4845204480 | bytes 22061056 | tf_op jit(solution)/shard_map/aoi,ni->aon/dot_general | solution.py:178
  256.6 62.4 %while.50 = (s32[]{:T(128)}, f32[2,512,12,64]{1,3,2,0:T(8,128)}, s32[2]{0:T(128)S(1)}, bf16[2,1024,12,64]{1,3,2,0:T(8,128)(2,1)}, s32[2,512]{1,0:T(2,128)S(1)}, ...) while((s32[]{:T(128)}, f32[2,512,12,64]{1,3,2,0:T(8,128)}, ...), condition=%wide.region_16.17_spmd.clone, body=%wide.region_15.16_spmd.clone.sunk | while | flops 2456551424 | bytes 65652440 | solution.py:61
  258.1 12.8 %fusion.168 = f32[2,12,512,512]{3,2,1,0:T(8,128)} fusion(bf16[2,512,12,64]{1,3,2,0:T(8,128)(2,1)S(1)} %get-tuple-element.1025, bf16[2,1024,12,64]{1,3,2,0:T(8,128)(2,1)} %get-tuple-element.1022, s32[]{:T(128)S(6)} %select_n.93), kind=kOutput, calls=%fused_computation.33.clone.1 | convolution fusion | flops 805306368 | bytes 28311556 | tf_op jit(solution)/shard_map/while/body/eval_jaxpr/sqhd,skhd->shqk/dot_general | solution.py:36
  271.2 17.1 %bitcast_add_fusion.9 = f32[2,512,12,64]{1,3,2,0:T(8,128)} fusion(f32[2,512,12,64]{1,3,2,0:T(8,128)} %get-tuple-element.1005, f32[2,12,512,512]{3,2,1,0:T(8,128)} %fusion.168, f32[2,12,512]{2,1,0:T(8,128)S(1)} %get-tuple-element.1029, f32[2,12,512]{2,1,0:T(8,128)S(1)} %get-tuple-element.1026, pred[2,512,512]{1,2,0:T(8,128)(4,1)S(1)} %broadcast_compare_fusion.10, ...), kind=kOutput, calls=%fused_computation.30.clone.1 | convolution fusion | flops 1650720768 | bytes 36800000 | tf_op jit(solution)/shard_map/while/body/eval_jaxpr/shqk,skhd->sqhd/dot_general | solution.py:213
  289.5 11.7 %fusion.168 = f32[2,12,512,512]{3,2,1,0:T(8,128)} fusion(bf16[2,512,12,64]{1,3,2,0:T(8,128)(2,1)S(1)} %get-tuple-element.1025, bf16[2,1024,12,64]{1,3,2,0:T(8,128)(2,1)} %get-tuple-element.1022, s32[]{:T(128)S(6)} %select_n.93), kind=kOutput, calls=%fused_computation.33.clone.1 | convolution fusion | flops 805306368 | bytes 28311556 | tf_op jit(solution)/shard_map/while/body/eval_jaxpr/sqhd,skhd->shqk/dot_general | solution.py:36
  301.6 17.5 %bitcast_add_fusion.9 = f32[2,512,12,64]{1,3,2,0:T(8,128)} fusion(f32[2,512,12,64]{1,3,2,0:T(8,128)} %get-tuple-element.1005, f32[2,12,512,512]{3,2,1,0:T(8,128)} %fusion.168, f32[2,12,512]{2,1,0:T(8,128)S(1)} %get-tuple-element.1029, f32[2,12,512]{2,1,0:T(8,128)S(1)} %get-tuple-element.1026, pred[2,512,512]{1,2,0:T(8,128)(4,1)S(1)} %broadcast_compare_fusion.10, ...), kind=kOutput, calls=%fused_computation.30.clone.1 | convolution fusion | flops 1650720768 | bytes 36800000 | tf_op jit(solution)/shard_map/while/body/eval_jaxpr/shqk,skhd->sqhd/dot_general | solution.py:213
  326.4 4.9 all_gather.27
  331.3 4.9 all_gather.25
  336.4 4.9 copy.83
  341.2 4.9 copy.85
  346.1 88.4 %while.51 = (s32[]{:T(128)}, f32[2,512,12,64]{1,3,2,0:T(8,128)}, f32[2,512,12,64]{1,3,2,0:T(8,128)}, s32[2]{0:T(128)S(1)}, bf16[2,1024,12,64]{1,3,2,0:T(8,128)(2...) while((s32[]{:T(128)}, f32[2,512,12,64]{1,3,2,0:T(8,128)}, ...), condition=%wide.region_18.19_spmd.clone, body=%wide.region_17.18_spmd.clone.sunk | while | flops 3288596480 | bytes 99452648 | solution.py:61
  347.3 12.0 %fusion.176 = f32[2,12,512,512]{3,2,1,0:T(8,128)} fusion(bf16[2,512,12,64]{1,3,2,0:T(8,128)(2,1)S(1)} %get-tuple-element.980, bf16[2,1024,12,64]{1,3,2,0:T(8,128)(2,1)} %get-tuple-element.977, s32[]{:T(128)S(6)} %select_n.96), kind=kOutput, calls=%fused_computation.54.clone.1 | convolution fusion | flops 805306368 | bytes 28311556 | tf_op jit(solution)/shard_map/while/body/eval_jaxpr/sqhd,skhd->shqk/dot_general | solution.py:36
  359.8 13.4 %bitcast_add_fusion.11 = f32[2,512,12,64]{1,3,2,0:T(8,128)} fusion(f32[2,512,12,64]{1,3,2,0:T(8,128)} %get-tuple-element.959, f32[2,12,512,512]{3,2,1,0:T(8,128)} %fusion.176, f32[2,12,512]{2,1,0:T(8,128)S(1)} %get-tuple-element.865, pred[2,512,512]{2,1,0:T(8,128)(4,1)S(1)} %broadcast_compare_fusion.11, pred[]{:T(512)S(6)} %compare.15, ...), kind=kOutput, calls=%fused_computation.49.clone.1 | convolution fusion | flops 832045056 | bytes 33603588 | tf_op jit(solution)/shard_map/while/body/eval_jaxpr/shqk,sqhd->skhd/dot_general | solution.py:252
  373.1 16.9 %bitcast_add_fusion.10 = f32[2,512,12,64]{1,3,2,0:T(8,128)} fusion(f32[2,512,12,64]{1,3,2,0:T(8,128)} %get-tuple-element.958, f32[2,12,512,512]{3,2,1,0:T(8,128)} %fusion.176, f32[2,12,512]{2,1,0:T(8,128)S(1)} %get-tuple-element.864, f32[2,12,512]{2,1,0:T(8,128)S(1)} %get-tuple-element.865, pred[2,512,512]{2,1,0:T(8,128)(4,1)S(1)} %broadcast_compare_fusion.11, ...), kind=kOutput, calls=%fused_computation.50.clone.1 | convolution fusion | flops 1650720768 | bytes 36800000 | tf_op jit(solution)/shard_map/while/body/eval_jaxpr/shqk,sqhd->skhd/dot_general | solution.py:249
  391.3 11.7 %fusion.176 = f32[2,12,512,512]{3,2,1,0:T(8,128)} fusion(bf16[2,512,12,64]{1,3,2,0:T(8,128)(2,1)S(1)} %get-tuple-element.980, bf16[2,1024,12,64]{1,3,2,0:T(8,128)(2,1)} %get-tuple-element.977, s32[]{:T(128)S(6)} %select_n.96), kind=kOutput, calls=%fused_computation.54.clone.1 | convolution fusion | flops 805306368 | bytes 28311556 | tf_op jit(solution)/shard_map/while/body/eval_jaxpr/sqhd,skhd->shqk/dot_general | solution.py:36
  403.4 13.9 %bitcast_add_fusion.11 = f32[2,512,12,64]{1,3,2,0:T(8,128)} fusion(f32[2,512,12,64]{1,3,2,0:T(8,128)} %get-tuple-element.959, f32[2,12,512,512]{3,2,1,0:T(8,128)} %fusion.176, f32[2,12,512]{2,1,0:T(8,128)S(1)} %get-tuple-element.865, pred[2,512,512]{2,1,0:T(8,128)(4,1)S(1)} %broadcast_compare_fusion.11, pred[]{:T(512)S(6)} %compare.15, ...), kind=kOutput, calls=%fused_computation.49.clone.1 | convolution fusion | flops 832045056 | bytes 33603588 | tf_op jit(solution)/shard_map/while/body/eval_jaxpr/shqk,sqhd->skhd/dot_general | solution.py:252
  417.3 17.2 %bitcast_add_fusion.10 = f32[2,512,12,64]{1,3,2,0:T(8,128)} fusion(f32[2,512,12,64]{1,3,2,0:T(8,128)} %get-tuple-element.958, f32[2,12,512,512]{3,2,1,0:T(8,128)} %fusion.176, f32[2,12,512]{2,1,0:T(8,128)S(1)} %get-tuple-element.864, f32[2,12,512]{2,1,0:T(8,128)S(1)} %get-tuple-element.865, pred[2,512,512]{2,1,0:T(8,128)(4,1)S(1)} %broadcast_compare_fusion.11, ...), kind=kOutput, calls=%fused_computation.50.clone.1 | convolution fusion | flops 1650720768 | bytes 36800000 | tf_op jit(solution)/shard_map/while/body/eval_jaxpr/shqk,sqhd->skhd/dot_general | solution.py:249
  446.4 4.2 convolution_bitcast_fusion.4
  453.8 4.8 convolution_bitcast_fusion.2
  458.6 11.2 %convolution_bitcast_fusion.1 = f32[768,3072]{1,0:T(8,128)} fusion(bf16[2,512,3072]{2,1,0:T(8,128)(2,1)} %get-tuple-element.613, f32[2,512,768]{2,1,0:T(8,128)} %copy-done.5, f32[768]{0:T(1024)S(1)} %copy-done.19, f32[768]{0:T(1024)S(1)} %copy-done.17, f32[2,512]{1,0:T(2,128)S(1)} %copy-done.27, f32[2,512]{1,0:T(2,128)S(1)} %copy-done.23), kind=kOutput, calls=%fused_computation.90 | convolution fusion | flops 4835770368 | bytes 18888704 | tf_op jit(solution)/shard_map/ret,reu->tu/dot_general | solution.py:174
  469.9 10.2 %convolution_bitcast_fusion = f32[3072,768]{1,0:T(8,128)} fusion(bf16[2,512,3072]{2,1,0:T(8,128)(2,1)} %copy-done.8, bf16[2,512,768]{2,1,0:T(8,128)(2,1)} %get-tuple-element.588), kind=kOutput, calls=%fused_computation.89 | convolution fusion | flops 4831838208 | bytes 17301504 | tf_op jit(solution)/shard_map/gvx,gvm->xm/dot_general | solution.py:163
  482.1 24.2 %reduce-scatter.41.cloned.1.call-done = f32[48,768]{1,0:T(8,128)} async-done(((f32[768,768]{1,0:T(8,128)}), f32[48,768]{1,0:T(8,128)}) %reduce-scatter.41.cloned.1.call-update) | async-done | bytes 147472
  508.2 63.8 %reduce-scatter.39.cloned.1.call-done = f32[48,768]{1,0:T(8,128)} async-done(((f32[768,768]{1,0:T(8,128)}), f32[48,768]{1,0:T(8,128)}) %reduce-scatter.39.cloned.1.call-update) | async-done | bytes 147472
  574.0 64.9 %reduce-scatter.25.cloned.1.call-done = f32[48,768]{1,0:T(8,128)} async-done(((f32[768,768]{1,0:T(8,128)}), f32[48,768]{1,0:T(8,128)}) %reduce-scatter.25.cloned.1.call-update) | async-done | bytes 147472 | tf_op jit(solution)/shard_map/reduce_scatter | solution.py:288
  638.9 114.4 %reduce-scatter.29.cloned.1.call-done = f32[48,3072]{1,0:T(8,128)} async-done(((f32[768,3072]{1,0:T(8,128)}), f32[48,3072]{1,0:T(8,128)}) %reduce-scatter.29.cloned.1.call-update) | async-done | bytes 589840 | tf_op jit(solution)/shard_map/reduce_scatter | solution.py:289
  753.4 115.6 %reduce-scatter.33.cloned.1.call-done = f32[192,768]{1,0:T(8,128)} async-done(((f32[3072,768]{1,0:T(8,128)}), f32[192,768]{1,0:T(8,128)}) %reduce-scatter.33.cloned.1.call-update) | async-done | bytes 589840 | tf_op jit(solution)/shard_map/reduce_scatter | solution.py:290
  869.1 4.9 fusion.88
  874.2 42.1 %all-reduce = (f32[768]{0:T(1024)}, f32[768]{0:T(1024)}, f32[768]{0:T(1024)}, f32[768]{0:T(1024)}, f32[768]{0:T(1024)}, /*index=5*/f32[3072]{0:T(1024)}, f32[768]{0:T(1024)}, f32[768]{0:T(1024)}, f32[768]{0:T(1024)}) all-reduce(f32[768]{0:T(1024)S(1)} %reduce_sum.217, ...), channel_id=1, replica_groups=mesh['seq'=16,'blk'=2] {'seq','blk'}, use_global_device_ids=true, to_apply=%region_22.23 | all-reduce | flops 9216 | bytes 73728 | tf_op jit(solution)/shard_map/psum | solution.py:293
  919.9 4.9 add_add_fusion.2
  929.9 17.3 %reduce-scatter.31.cloned.1.call-done = f32[48,1536]{1,0:T(8,128)} async-done(((f32[48,3072]{1,0:T(8,128)}), f32[48,1536]{1,0:T(8,128)}) %reduce-scatter.31.cloned.1.call-update) | async-done | bytes 294928 | tf_op jit(solution)/shard_map/reduce_scatter | solution.py:292
  947.2 18.0 %reduce-scatter.35.cloned.1.call-done = f32[192,384]{1,0:T(8,128)} async-done(((f32[192,768]{1,0:T(8,128)}), f32[192,384]{1,0:T(8,128)}) %reduce-scatter.35.cloned.1.call-update) | async-done | bytes 294928 | tf_op jit(solution)/shard_map/reduce_scatter | solution.py:292
  (241 shorter events, 89.4 us)
Async XLA Ops:
  7.2 139.4 %copy-start = (bf16[768,768]{1,0:T(8,128)(2,1)S(1)}, bf16[768,768]{1,0:T(8,128)(2,1)}, u32[]{:S(2)}) copy-start(bf16[768,768]{1,0:T(8,128)(2,1)} %param.33) | copy-start | bytes 3538948
  7.2 52.4 %all-gather.7.cloned.1.call-start = ((), (), s32[]{:S(2)}) async-start(), calls=%async_computation.13 | async-start | bytes 4718592 | tf_op jit(solution)/shard_map/all_gather | solution.py:94
  11.8 103.1 %all-gather.5.cloned.1.call-start = ((), (), s32[]{:S(2)}) async-start(), calls=%async_computation.12 | async-start | bytes 4718592 | tf_op jit(solution)/shard_map/all_gather | solution.py:95
  15.9 320.4 %all-gather.9.cloned.1.call-start = ((), (), s32[]{:S(2)}) async-start(), calls=%async_computation.14 | async-start | bytes 4718592 | tf_op jit(solution)/shard_map/all_gather | solution.py:219
  20.0 321.2 %all-gather.11.cloned.1.call-start = ((), (), s32[]{:S(2)}) async-start(), calls=%async_computation.15 | async-start | bytes 4718592 | tf_op jit(solution)/shard_map/all_gather | solution.py:220
  22.0 5.6 copy-start.10
  22.0 10.9 %copy-start.42 = (bf16[768]{0:T(1024)(128)(2,1)S(1)}, bf16[768]{0:T(1024)(128)(2,1)}, u32[]{:S(2)}) copy-start(bf16[768]{0:T(1024)(128)(2,1)} %param.34) | copy-start | bytes 4612
  22.0 10.9 %copy-start.43 = (bf16[768]{0:T(1024)(128)(2,1)S(1)}, bf16[768]{0:T(1024)(128)(2,1)}, u32[]{:S(2)}) copy-start(bf16[768]{0:T(1024)(128)(2,1)} %param.35) | copy-start | bytes 4612
  22.0 10.9 %copy-start.36 = (bf16[3072]{0:T(1024)(128)(2,1)S(1)}, bf16[3072]{0:T(1024)(128)(2,1)}, u32[]{:S(2)}) copy-start(bf16[3072]{0:T(1024)(128)(2,1)} %param.38) | copy-start | bytes 18436
  22.0 10.9 %copy-start.44 = (bf16[768]{0:T(1024)(128)(2,1)S(1)}, bf16[768]{0:T(1024)(128)(2,1)}, u32[]{:S(2)}) copy-start(bf16[768]{0:T(1024)(128)(2,1)} %param.36) | copy-start | bytes 4612
  22.0 10.9 %copy-start.45 = (bf16[768]{0:T(1024)(128)(2,1)S(1)}, bf16[768]{0:T(1024)(128)(2,1)}, u32[]{:S(2)}) copy-start(bf16[768]{0:T(1024)(128)(2,1)} %param.40) | copy-start | bytes 4612
  22.0 11.5 %copy-start.46 = (bf16[768]{0:T(1024)(128)(2,1)S(1)}, bf16[768]{0:T(1024)(128)(2,1)}, u32[]{:S(2)}) copy-start(bf16[768]{0:T(1024)(128)(2,1)} %param.41) | copy-start | bytes 4612
  22.1 12.1 %copy-start.47 = (bf16[768]{0:T(1024)(128)(2,1)S(1)}, bf16[768]{0:T(1024)(128)(2,1)}, u32[]{:S(2)}) copy-start(bf16[768]{0:T(1024)(128)(2,1)} %param.42) | copy-start | bytes 4612
  32.9 210.5 %copy-start.16 = (f32[768]{0:T(1024)}, f32[768]{0:T(1024)S(1)}, u32[]{:S(2)}) copy-start(f32[768]{0:T(1024)S(1)} %convert_element_type.130) | copy-start | bytes 9220
  33.0 162.2 %copy-start.18 = (f32[768]{0:T(1024)}, f32[768]{0:T(1024)S(1)}, u32[]{:S(2)}) copy-start(f32[768]{0:T(1024)S(1)} %convert_element_type.131) | copy-start | bytes 9220
  148.3 46.9 %copy-start.5 = (f32[2,512,768]{2,1,0:T(8,128)}, f32[2,512,768]{2,1,0:T(8,128)S(1)}, u32[]{:S(2)}) copy-start(f32[2,512,768]{2,1,0:T(8,128)S(1)} %get-tuple-element.607) | copy-start | bytes 9437188
  148.3 95.1 %copy-start.22 = (f32[2,512]{1,0:T(2,128)}, f32[2,512]{1,0:T(2,128)S(1)}, u32[]{:S(2)}) copy-start(f32[2,512]{1,0:T(2,128)S(1)} %broadcast_multiply_fusion.1) | copy-start | bytes 12292
  150.0 93.4 %copy-start.26 = (f32[2,512]{1,0:T(2,128)}, f32[2,512]{1,0:T(2,128)S(1)}, u32[]{:S(2)}) copy-start(f32[2,512]{1,0:T(2,128)S(1)} %fusion.98) | copy-start | bytes 12292
  163.5 31.7 %copy-start.37 = (f32[768]{0:T(1024)S(1)}, f32[768]{0:T(1024)}, u32[]{:S(2)}) copy-start(f32[768]{0:T(1024)} %convert_element_type.135) | copy-start | bytes 9220
  195.2 10.1 %copy-start.8 = (bf16[2,512,3072]{2,1,0:T(8,128)(2,1)}, bf16[2,512,3072]{2,1,0:T(8,128)(2,1)S(1)}, u32[]{:S(2)}) copy-start(bf16[2,512,3072]{2,1,0:T(8,128)(2,1)S(1)} %get-tuple-element.597) | copy-start | bytes 18874372
  195.2 10.1 %copy-start.7 = (bf16[2,512,768]{2,1,0:T(8,128)(2,1)S(1)}, bf16[2,512,768]{2,1,0:T(8,128)(2,1)}, u32[]{:S(2)}) copy-start(bf16[2,512,768]{2,1,0:T(8,128)(2,1)} %param.43) | copy-start | bytes 4718596
  195.2 10.1 %copy-start.28 = (f32[768]{0:T(1024)S(1)}, f32[768]{0:T(1024)}, u32[]{:S(2)}) copy-start(f32[768]{0:T(1024)} %convert_element_type.136) | copy-start | bytes 9220
  232.0 11.4 %copy-start.6 = (f32[2,512,768]{2,1,0:T(8,128)S(1)}, f32[2,512,768]{2,1,0:T(8,128)}, u32[]{:S(2)}) copy-start(f32[2,512,768]{2,1,0:T(8,128)} %copy-done.5) | copy-start | bytes 9437188
  244.7 6.3 copy-start.24
  256.6 223.6 %reduce-scatter.37.cloned.1.call-start = ((), (), s32[]{:S(2)}) async-start(), calls=%async_computation.25 | async-start | bytes 2506752
  324.4 6.9 copy-start.21
  336.3 170.0 %reduce-scatter.41.cloned.1.call-start = ((), (), s32[]{:S(2)}) async-start(), calls=%async_computation.27 | async-start | bytes 2506752
  442.7 129.3 %reduce-scatter.39.cloned.1.call-start = ((), (), s32[]{:S(2)}) async-start(), calls=%async_computation.26 | async-start | bytes 2506752
  453.7 4.9 copy-start.17
  453.7 4.9 copy-start.19
  453.7 185.2 %reduce-scatter.25.cloned.1.call-start = ((), (), s32[]{:S(2)}) async-start(), calls=%async_computation.19 | async-start | bytes 2506752 | tf_op jit(solution)/shard_map/reduce_scatter | solution.py:288
  458.6 294.8 %reduce-scatter.29.cloned.1.call-start = ((), (), s32[]{:S(2)}) async-start(), calls=%async_computation.21 | async-start | bytes 10027008 | tf_op jit(solution)/shard_map/reduce_scatter | solution.py:289
  469.9 399.1 %reduce-scatter.33.cloned.1.call-start = ((), (), s32[]{:S(2)}) async-start(), calls=%async_computation.23 | async-start | bytes 10027008 | tf_op jit(solution)/shard_map/reduce_scatter | solution.py:290
  480.1 444.8 %reduce-scatter.19.cloned.1.call-start = ((), (), s32[]{:S(2)}) async-start(), calls=%async_computation.16 | async-start | bytes 589824 | tf_op jit(solution)/shard_map/reduce_scatter | solution.py:292
  482.0 444.5 %reduce-scatter.23.cloned.1.call-start = ((), (), s32[]{:S(2)}) async-start(), calls=%async_computation.18 | async-start | bytes 589824 | tf_op jit(solution)/shard_map/reduce_scatter | solution.py:292
  508.2 420.1 %reduce-scatter.21.cloned.1.call-start = ((), (), s32[]{:S(2)}) async-start(), calls=%async_computation.17 | async-start | bytes 589824 | tf_op jit(solution)/shard_map/reduce_scatter | solution.py:292
  573.9 356.0 %reduce-scatter.27.cloned.1.call-start = ((), (), s32[]{:S(2)}) async-start(), calls=%async_computation.20 | async-start | bytes 221184 | tf_op jit(solution)/shard_map/reduce_scatter | solution.py:292
  638.9 308.3 %reduce-scatter.31.cloned.1.call-start = ((), (), s32[]{:S(2)}) async-start(), calls=%async_computation.22 | async-start | bytes 884736 | tf_op jit(solution)/shard_map/reduce_scatter | solution.py:292
  753.4 211.9 %reduce-scatter.35.cloned.1.call-start = ((), (), s32[]{:S(2)}) async-start(), calls=%async_computation.24 | async-start | bytes 884736 | tf_op jit(solution)/shard_map/reduce_scatter | solution.py:292
  869.0 5.0 copy-start.29
  869.0 5.1 copy-start.31
  869.1 5.1 copy-start.32
  869.1 5.1 copy-start.33
  869.1 5.1 copy-start.34
  869.1 5.1 copy-start.35
  869.1 5.1 copy-start.38
  869.1 5.1 copy-start.39
  919.9 45.3 %copy-start.1 = (bf16[768,768]{1,0:T(8,128)(2,1)S(1)}, bf16[768,768]{1,0:T(8,128)(2,1)}, u32[]{:S(2)}) copy-start(bf16[768,768]{1,0:T(8,128)(2,1)} %param.33) | copy-start | bytes 3538948
  (22 other events, 70.5 us)
Sparse Core Ops, SparseCore 0:
  11.9 47.7 all-gather.6
  61.8 44.9 all-gather.4
  108.3 44.9 all-gather.8
  256.7 45.2 all-gather.10
  336.4 63.3 reduce-scatter.36
  442.9 63.3 reduce-scatter.40
  510.0 61.9 reduce-scatter.38
  576.9 61.9 reduce-scatter.24
  643.0 110.3 reduce-scatter.28
  757.9 111.1 reduce-scatter.32
  871.3 13.2 reduce-scatter.18
  886.7 13.2 reduce-scatter.22
  902.3 13.5 reduce-scatter.20
  918.5 10.5 reduce-scatter.26
  931.9 15.2 reduce-scatter.30
  949.9 15.2 reduce-scatter.34
where the time goes:
time: 977 us; the launch traced here: 972 us
  waiting for transfers between devices  443 us (45%)
  matrix products  308 us (32%)
  other arithmetic  82.4 us (8%)
  local copies, waits for them, and re-layouts  59.8 us (6%)
  blocking collectives  57.2 us (6%)
  between operations  15.2 us (2%)
    reduce_scatter x1, waiting for transfers between devices, local(): lax.psum_scatter(outer_weight_grad, 'seq', scatter_dimension=0, tiled=True)  116 us
    reduce_scatter x1, waiting for transfers between devices, local(): lax.psum_scatter(inner_weight_grad, 'seq', scatter_dimension=0, tiled=True)  114 us
    unnamed x19, waiting for transfers between devices  88.3 us
    dot_general x6, matrix products, block_scores(): jnp.einsum('sqhd,skhd->shqk', query_block, key_block, preferred_element_t...  72.4 us
    reduce_scatter x1, waiting for transfers between devices, local(): lax.psum_scatter(output_weight_grad, 'seq', scatter_dimension=0, tiled=True)  64.9 us
    psum x1, blocking collectives, local(): lax.psum((query_bias_grad, value_bias_grad, output_bias_grad, first_gain_...  42.1 us
    dot_general x6, matrix products, linear(): return jnp.dot(operand, matrix, preferred_element_type=jnp.float32)  37.7 us
    reduce_scatter x6, waiting for transfers between devices, local(): lax.psum_scatter(tuple(partial_sums), 'blk', scatter_dimension=1, tiled=T...  35.3 us
  transfers between devices with their start and end apart: 16, of which 8 were waited for; matrix products, arithmetic and copies ran while one was open for 45% of the time, Pallas kernels for 0%

commit v1 on v0

--- a/solution.py
+++ b/solution.py
@@ -1,8 +1,11 @@
+import functools
 import math
 
 import jax
 import jax.numpy as jnp
 from jax import lax
+from jax.experimental import pallas as pl
+from jax.experimental.pallas import tpu as pltpu
 from jax.sharding import PartitionSpec as P
 
 HEADS = 12
@@ -62,7 +65,7 @@
     return result
 
 
-def local(
+def general(
     hidden,
     segments,
     query_matrix,
@@ -325,9 +328,528 @@
     )
 
 
+BF16 = jnp.bfloat16
+F32 = jnp.float32
+NN = ((1,), (0,))
+NT = ((1,), (1,))
+TN = ((0,), (0,))
+GROUP = 256
+PER_GROUP = GROUP // HEAD
+TILE = 256
+VMEM_LIMIT = 60 * 2**20
+
+
+def mm(a, b, dims):
+    return lax.dot_general(a, b, (dims, ((), ())), preferred_element_type=F32)
+
+
+def fixed(shape):
+    return pl.BlockSpec(shape, lambda *_: (0,) * len(shape), pipeline_mode=pl.Buffered(1))
+
+
+def params(dimensions):
+    return pltpu.CompilerParams(
+        vmem_limit_bytes=VMEM_LIMIT, dimension_semantics=("arbitrary",) * dimensions
+    )
+
+
+def cost(flops, moved):
+    return pl.CostEstimate(flops=int(flops), bytes_accessed=int(moved), transcendentals=0)
+
+
+def head_lanes(shape, head):
+    lane = lax.broadcasted_iota(jnp.int32, shape, 1)
+    return (lane >= head * HEAD) & (lane < (head + 1) * HEAD)
+
+
+def attention_forward_kernel(
+    h_ref,
+    wq_ref,
+    wk_ref,
+    wv_ref,
+    bq_ref,
+    bv_ref,
+    segc_ref,
+    segr_ref,
+    q_ref,
+    k_ref,
+    v_ref,
+    ctx_ref,
+    lse_ref,
+    mask_ref,
+    vaug_ref,
+):
+    length = h_ref.shape[0]
+
+    @pl.when(pl.program_id(0) == 0)
+    def _():
+        mask_ref[...] = jnp.where(segc_ref[...] == segr_ref[...], 0.0, NEGATIVE)
+
+    h = h_ref[...]
+    q_ref[...] = (mm(h, wq_ref[...], NN) + bq_ref[...]).astype(BF16)
+    k_ref[...] = mm(h, wk_ref[...], NN).astype(BF16)
+    v = (mm(h, wv_ref[...], NN) + bv_ref[...]).astype(BF16)
+    v_ref[...] = v
+    lane = lax.broadcasted_iota(jnp.int32, v.shape, 1)
+    for head in range(PER_GROUP):
+        other = (lane // 128) != (head // 2)
+        filler = jnp.where(other, 1.0, 0.0).astype(BF16)
+        vaug_ref[head] = jnp.where(head_lanes(v.shape, head), v, filler)
+
+    def block(i, carry):
+        rows = pl.ds(pl.multiple_of(i * TILE, TILE), TILE)
+        qb = q_ref[rows, :] * BF16(HEAD**-0.5)
+        halves = [None, None]
+        stat_lane = lax.broadcasted_iota(jnp.int32, (TILE, 128), 1)
+        stats = jnp.zeros((TILE, 128), F32)
+        for head in range(PER_GROUP):
+            qm = jnp.where(head_lanes(qb.shape, head), qb, BF16(0))
+            s = mm(qm, k_ref[...], NT) + mask_ref[rows, :]
+            top = jnp.max(s, axis=1, keepdims=True)
+            e = jnp.exp(s - top).astype(BF16)
+            o = mm(e, vaug_ref[head], NN)
+            t = head // 2
+            total = o[:, (1 - t) * 128 : (2 - t) * 128]
+            part = o[:, t * 128 : (t + 1) * 128] / total
+            halves[t] = part if halves[t] is None else halves[t] + part
+            stats = jnp.where(stat_lane == head, top + jnp.log(total), stats)
+        ctx_ref[rows, 0:128] = halves[0].astype(BF16)
+        ctx_ref[rows, 128:256] = halves[1].astype(BF16)
+        lse_ref[:, rows] = jnp.transpose(stats)[0:8]
+        return carry
+
+    lax.fori_loop(0, length // TILE, block, 0)
+
+
+def attention_forward(h, wq, wk, wv, bq, bv, segc, segr):
+    length, width = h.shape
+    groups = width // GROUP
+    column = pl.BlockSpec((width, GROUP), lambda g: (0, g))
+    bias = pl.BlockSpec((1, GROUP), lambda g: (0, g))
+    rows = pl.BlockSpec((length, GROUP), lambda g: (0, g))
+    wide = jax.ShapeDtypeStruct((length, width), BF16)
+    return pl.pallas_call(
+        attention_forward_kernel,
+        grid=(groups,),
+        out_shape=(wide, wide, wide, wide, jax.ShapeDtypeStruct((8 * groups, length), F32)),
+        in_specs=[
+            fixed((length, width)),
+            column,
+            column,
+            column,
+            bias,
+            bias,
+            fixed((length, 1)),
+            fixed((1, length)),
+        ],
+        out_specs=(rows, rows, rows, rows, pl.BlockSpec((8, length), lambda g: (g, 0))),
+        scratch_shapes=[
+            pltpu.VMEM((length, length), F32),
+            pltpu.VMEM((PER_GROUP, length, GROUP), BF16),
+        ],
+        compiler_params=params(1),
+        cost_estimate=cost(20e9, 12e6),
+        name="attention_forward",
+    )(h, wq, wk, wv, bq, bv, segc, segr)
+
+
+def gelu_pair(u):
+    z = jnp.abs(u) * 0.7071067811865476
+    t = 1.0 / (1.0 + 0.3275911 * z)
+    bell = jnp.exp(-z * z)
+    poly = t * (
+        0.127414796 + t * (-0.142248368 + t * (0.7107068705 + t * (-0.7265760135 + t * 0.5307027145)))
+    )
+    tail = poly * bell
+    phi = jnp.where(u < 0, tail, 1.0 - tail)
+    return (u * phi, phi + u * bell * 0.3989422804014327)
+
+
+def normed(x):
+    centre = x - jnp.mean(x, axis=1, keepdims=True)
+    scale = lax.rsqrt(jnp.mean(centre * centre, axis=1, keepdims=True) + EPSILON)
+    return (centre * scale, scale)
+
+
+def norm_back(u, n, scale):
+    return scale * (u - jnp.mean(u, axis=1, keepdims=True) - n * jnp.mean(u * n, axis=1, keepdims=True))
+
+
+def row_sum(x):
+    return jnp.sum(x, axis=0, keepdims=True)
+
+
+def token_kernel(
+    h_ref,
+    ctx_ref,
+    cot_ref,
+    wo_ref,
+    wi_ref,
+    wp_ref,
+    bi_ref,
+    vec_ref,
+    out_ref,
+    first_ref,
+    act_ref,
+    og_ref,
+    ig_ref,
+    fp_ref,
+    ag_ref,
+    dctx_ref,
+    sums_ref,
+    isum_ref,
+    slope_ref,
+):
+    @pl.when(pl.program_id(0) == 0)
+    def _():
+        sums_ref[...] = jnp.zeros_like(sums_ref)
+        isum_ref[...] = jnp.zeros_like(isum_ref)
+
+    ff = wi_ref.shape[1]
+    chunk = 512
+    output_bias, gain1, shift1 = vec_ref[0:1, :], vec_ref[1:2, :], vec_ref[2:3, :]
+    outer_bias, gain2, shift2 = vec_ref[3:4, :], vec_ref[4:5, :], vec_ref[5:6, :]
+    n1, r1 = normed(h_ref[...].astype(F32) + mm(ctx_ref[...], wo_ref[...], NN) + output_bias)
+    fn = n1 * gain1 + shift1
+    first = fn.astype(BF16)
+    first_ref[...] = first
+    for c in range(0, ff, chunk):
+        act, slope = gelu_pair(mm(first, wi_ref[:, c : c + chunk], NN) + bi_ref[:, c : c + chunk])
+        act_ref[:, c : c + chunk] = act.astype(BF16)
+        slope_ref[:, c : c + chunk] = slope
+    n2, r2 = normed(fn + mm(act_ref[...], wp_ref[...], NN) + outer_bias)
+    out_ref[...] = (n2 * gain2 + shift2).astype(BF16)
+    e = cot_ref[...].astype(F32)
+    sums_ref[0:1, :] += row_sum(e * n2)
+    sums_ref[1:2, :] += row_sum(e)
+    sp = norm_back(e * gain2, n2, r2)
+    og = sp.astype(BF16)
+    og_ref[...] = og
+    sums_ref[2:3, :] += row_sum(og.astype(F32))
+    for c in range(0, ff, chunk):
+        ig = (mm(og, wp_ref[c : c + chunk, :], NT) * slope_ref[:, c : c + chunk]).astype(BF16)
+        ig_ref[:, c : c + chunk] = ig
+        isum_ref[:, c : c + chunk] += row_sum(ig.astype(F32))
+    d = sp + mm(ig_ref[...], wi_ref[...], NT)
+    sums_ref[3:4, :] += row_sum(d * n1)
+    sums_ref[4:5, :] += row_sum(d)
+    fp = norm_back(d * gain1, n1, r1)
+    fp_ref[...] = fp
+    ag = fp.astype(BF16)
+    ag_ref[...] = ag
+    sums_ref[5:6, :] += row_sum(ag.astype(F32))
+    dctx_ref[...] = mm(ag, wo_ref[...], NT).astype(BF16)
+
+
+def token_pass(h, ctx, cot, wo, wi, wp, bi, vec):
+    length, width = h.shape
+    ff = wi.shape[1]
+    rows = pl.BlockSpec((TILE, width), lambda i: (i, 0))
+    wide_rows = pl.BlockSpec((TILE, ff), lambda i: (i, 0))
+    low = jax.ShapeDtypeStruct((length, width), BF16)
+    low_ff = jax.ShapeDtypeStruct((length, ff), BF16)
+    return pl.pallas_call(
+        token_kernel,
+        grid=(length // TILE,),
+        out_shape=(
+            low,
+            low,
+            low_ff,
+            low,
+            low_ff,
+            jax.ShapeDtypeStruct((length, width), F32),
+            low,
+            low,
+            jax.ShapeDtypeStruct((8, width), F32),
+            jax.ShapeDtypeStruct((1, ff), F32),
+        ),
+        in_specs=[
+            rows,
+            rows,
+            rows,
+            fixed((width, width)),
+            fixed((width, ff)),
+            fixed((ff, width)),
+            fixed((1, ff)),
+            fixed((8, width)),
+        ],
+        out_specs=(
+            rows,
+            rows,
+            wide_rows,
+            rows,
+            wide_rows,
+            rows,
+            rows,
+            rows,
+            pl.BlockSpec((8, width), lambda i: (0, 0)),
+            pl.BlockSpec((1, ff), lambda i: (0, 0)),
+        ),
+        scratch_shapes=[pltpu.VMEM((TILE, ff), F32)],
+        compiler_params=params(1),
+        cost_estimate=cost(21.7e9, 30e6),
+        name="token_pass",
+    )(h, ctx, cot, wo, wi, wp, bi, vec)
+
+
+def product_kernel(a_ref, b_ref, out_ref):
+    out_ref[...] = mm(a_ref[...], b_ref[...], TN).astype(out_ref.dtype)
+
+
+def weight_grad(a, b, rows, columns, kind):
+    length, height = a.shape
+    width = b.shape[1]
+    a_spec = pl.BlockSpec((length, rows), lambda i, j: (0, i))
+    b_spec = pl.BlockSpec((length, columns), lambda i, j: (0, j))
+    return pl.pallas_call(
+        product_kernel,
+        grid=(height // rows, width // columns),
+        out_shape=jax.ShapeDtypeStruct((height, width), kind),
+        in_specs=[a_spec, b_spec],
+        out_specs=pl.BlockSpec((rows, columns), lambda i, j: (i, j)),
+        compiler_params=params(2),
+        cost_estimate=cost(2 * length * height * width, 2 * length * (height + width) + 2 * height * width),
+        name="weight_grad",
+    )(a, b)
+
+
+def attention_backward_kernel(
+    q_ref,
+    k_ref,
+    v_ref,
+    dctx_ref,
+    ctx_ref,
+    lse_ref,
+    segc_ref,
+    segr_ref,
+    dq_ref,
+    dk_ref,
+    dv_ref,
+    sums_ref,
+    delta_ref,
+    total_ref,
+    ds_ref,
+    km_ref,
+):
+    length = q_ref.shape[0]
+    prod = dctx_ref[...].astype(F32) * ctx_ref[...].astype(F32)
+    high = prod.astype(BF16)
+    rest = (prod - high.astype(F32)).astype(BF16)
+    lane = lax.broadcasted_iota(jnp.int32, (8, GROUP), 1)
+    head_of = lax.broadcasted_iota(jnp.int32, (8, GROUP), 0)
+    chooser = jnp.where(lane // HEAD == head_of, 1.0, 0.0).astype(BF16)
+    delta_ref[...] = mm(chooser, high, NT) + mm(chooser, rest, NT)
+    total_ref[...] = jnp.zeros_like(total_ref)
+
+    def block(j, carry):
+        rows = pl.ds(pl.multiple_of(j * TILE, TILE), TILE)
+        kb = k_ref[rows, :]
+        vb = v_ref[rows, :]
+        mask = jnp.where(segc_ref[rows, :] == segr_ref[...], 0.0, NEGATIVE)
+        dk = jnp.zeros((TILE, GROUP), F32)
+        dv = jnp.zeros((TILE, GROUP), F32)
+        for head in range(PER_GROUP):
+            mine = head_lanes((TILE, GROUP), head)
+            km = jnp.where(mine, kb, BF16(0)) * BF16(HEAD**-0.5)
+            vm = jnp.where(mine, vb, BF16(0))
+            s = mm(km, q_ref[...], NT) + mask
+            p = jnp.exp(s - lse_ref[head : head + 1, :])
+            dp = mm(vm, dctx_ref[...], NT)
+            ds = (p * (dp - delta_ref[head : head + 1, :])).astype(BF16)
+            dv = jnp.where(mine, mm(p.astype(BF16), dctx_ref[...], NN), dv)
+            dk = jnp.where(mine, mm(ds, q_ref[...], NN), dk)
+            ds_ref[head * TILE : (head + 1) * TILE, :] = ds
+            km_ref[head * TILE : (head + 1) * TILE, :] = km
+        dkb = (dk * HEAD**-0.5).astype(BF16)
+        dvb = dv.astype(BF16)
+        dk_ref[rows, :] = dkb
+        dv_ref[rows, :] = dvb
+        total_ref[...] += mm(ds_ref[...], km_ref[...], TN)
+        return carry + row_sum(dvb.astype(F32))
+
+    dv_sum = lax.fori_loop(0, length // TILE, block, jnp.zeros((1, GROUP), F32))
+    dq = total_ref[...].astype(BF16)
+    dq_ref[...] = dq
+    sums_ref[...] = jnp.zeros_like(sums_ref)
+    sums_ref[0:1, :] = row_sum(dq.astype(F32))
+    sums_ref[1:2, :] = dv_sum
+
+
+def attention_backward(q, k, v, dctx, ctx, lse, segc, segr):
+    length, width = q.shape
+    groups = width // GROUP
+    rows = pl.BlockSpec((length, GROUP), lambda g: (0, g))
+    wide = jax.ShapeDtypeStruct((length, width), BF16)
+    return pl.pallas_call(
+        attention_backward_kernel,
+        grid=(groups,),
+        out_shape=(wide, wide, wide, jax.ShapeDtypeStruct((8, width), F32)),
+        in_specs=[
+            rows,
+            rows,
+            rows,
+            rows,
+            rows,
+            pl.BlockSpec((8, length), lambda g: (g, 0)),
+            fixed((length, 1)),
+            fixed((1, length)),
+        ],
+        out_specs=(rows, rows, rows, pl.BlockSpec((8, GROUP), lambda g: (0, g))),
+        scratch_shapes=[
+            pltpu.VMEM((8, length), F32),
+            pltpu.VMEM((length, GROUP), F32),
+            pltpu.VMEM((PER_GROUP * TILE, length), BF16),
+            pltpu.VMEM((PER_GROUP * TILE, GROUP), BF16),
+        ],
+        compiler_params=params(1),
+        cost_estimate=cost(40e9, 14e6),
+        name="attention_backward",
+    )(q, k, v, dctx, ctx, lse, segc, segr)
+
+
+def hidden_grad_kernel(fp_ref, dq_ref, dk_ref, dv_ref, wq_ref, wk_ref, wv_ref, out_ref):
+    total = fp_ref[...] + mm(dq_ref[...], wq_ref[...], NT)
+    total = total + mm(dk_ref[...], wk_ref[...], NT)
+    out_ref[...] = (total + mm(dv_ref[...], wv_ref[...], NT)).astype(out_ref.dtype)
+
+
+def hidden_grad_part(fp, dq, dk, dv, wq, wk, wv, part, kind):
+    length, width = dq.shape
+    half = length // 2
+    steps = half // TILE
+    rows = pl.BlockSpec((TILE, width), lambda i: (i + part * steps, 0))
+    return pl.pallas_call(
+        hidden_grad_kernel,
+        grid=(steps,),
+        out_shape=jax.ShapeDtypeStruct((half, width), kind),
+        in_specs=[rows, rows, rows, rows] + [fixed((width, width))] * 3,
+        out_specs=pl.BlockSpec((TILE, width), lambda i: (i, 0)),
+        compiler_params=params(1),
+        cost_estimate=cost(6 * half * width * width, 8e6),
+        name="hidden_grad",
+    )(fp, dq, dk, dv, wq, wk, wv)
+
+
+def fast(
+    hidden,
+    segments,
+    query_matrix,
+    query_bias,
+    key_matrix,
+    value_matrix,
+    value_bias,
+    output_matrix,
+    output_bias,
+    first_gain,
+    first_shift,
+    inner_matrix,
+    inner_bias,
+    outer_matrix,
+    outer_bias,
+    second_gain,
+    second_shift,
+    cotangent,
+):
+    here = lax.axis_index("blk")
+    swap = [(0, 1), (1, 0)]
+
+    def own(x):
+        return lax.dynamic_index_in_dim(x, here, 0, keepdims=False)
+
+    def other(x):
+        return lax.dynamic_index_in_dim(x, 1 - here, 0, keepdims=False)
+
+    def trade(x):
+        return lax.ppermute(x, "blk", swap)
+
+    def whole(x):
+        return jnp.concatenate([own(x), trade(other(x))], axis=0)
+
+    def back(mine, received):
+        first = jnp.where(here == 0, mine, received)
+        second = jnp.where(here == 0, received, mine)
+        return jnp.stack([first, second], axis=0)
+
+    def row(x):
+        return x.astype(F32)[None, :]
+
+    h = whole(hidden)
+    seg = whole(segments)
+    cot = whole(cotangent)
+    length, width = h.shape
+    half = length // 2
+    segc, segr = seg[:, None], seg[None, :]
+    q, k, v, ctx, lse = attention_forward(
+        h, query_matrix, key_matrix, value_matrix, row(query_bias), row(value_bias), segc, segr
+    )
+    empty = jnp.zeros((1, width), F32)
+    vec = jnp.concatenate(
+        [
+            row(output_bias),
+            row(first_gain),
+            row(first_shift),
+            row(outer_bias),
+            row(second_gain),
+            row(second_shift),
+            empty,
+            empty,
+        ],
+        axis=0,
+    )
+    out, first, act, og, ig, fp, ag, dctx, sums, isum = token_pass(
+        h, ctx, cot, output_matrix, inner_matrix, outer_matrix, row(inner_bias), vec
+    )
+    layer_out = back(out[:half], trade(out[half:]))
+    outer_grad = weight_grad(act, og, 512, width, BF16)
+    inner_grad = weight_grad(first, ig, width, 512, BF16)
+    output_grad = weight_grad(ctx, ag, width, width, BF16)
+    dq, dk, dv, sums2 = attention_backward(q, k, v, dctx, ctx, lse, segc, segr)
+    args = (fp, dq, dk, dv, query_matrix, key_matrix, value_matrix)
+    away = hidden_grad_part(*args, 1, BF16)
+    came = trade(away)
+    home = hidden_grad_part(*args, 0, F32)
+    query_grad = weight_grad(h, dq, width, width, BF16)
+    key_grad = weight_grad(h, dk, width, width, BF16)
+    value_grad = weight_grad(h, dv, width, width, BF16)
+    hidden_grad = back(home, came.astype(F32))
+
+    def scatter(x):
+        y = lax.psum_scatter(x, "seq", scatter_dimension=0, tiled=True)
+        return lax.psum_scatter(y, "blk", scatter_dimension=1, tiled=True).astype(F32)
+
+    vectors = lax.psum((sums, isum[0], sums2), ("seq", "blk"))
+    sums, isum, sums2 = vectors
+    return (
+        layer_out,
+        hidden_grad,
+        scatter(query_grad),
+        sums2[0],
+        scatter(key_grad),
+        scatter(value_grad),
+        sums2[1],
+        scatter(output_grad),
+        sums[5],
+        sums[3],
+        sums[4],
+        scatter(inner_grad),
+        isum,
+        scatter(outer_grad),
+        sums[2],
+        sums[0],
+        sums[1],
+    )
+
+
+def choose(sizes, *args):
+    seq_count, row_count, width = args[0].shape
+    whole_here = sizes[1] == 2 and seq_count == 2 and row_count % TILE == 0 and width % GROUP == 0
+    return fast(*args) if whole_here and sizes[0] == 16 else general(*args)
+
+
 def solution(mesh):
+    sizes = (mesh.shape["seq"], mesh.shape["blk"])
     return jax.shard_map(
-        local,
+        functools.partial(choose, sizes),
         mesh=mesh,
         in_specs=(
             P("seq", "blk", None),

time: 977 us -> 654 us (0.67)
  matrix products: 308 us -> 0 us
  Pallas kernels: 0 us -> 171 us
  waiting for transfers between devices: 443 us -> 371 us
  other arithmetic: 82.4 us -> 15 us
  local copies, waits for them, and re-layouts: 59.8 us -> 20.6 us
    dot_general x32 -> x0, matrix products: 308 us -> none  [the longest x6 72.4 us: block_scores(): jnp.einsum('sqhd,skhd->shqk', query_block, key_block, preferred_element_t...]
    pallas_call x0 -> x11, Pallas kernels: none -> 171 us  [the longest x1 46.6 us: token_pass(): pl.pallas_call(token_kernel, grid=(length // TILE,), out_shape=(low, low,...]
    reduce_sum x11 -> x0, other arithmetic: 41.5 us -> none  [the longest x2 22.9 us: stats_step(): jnp.sum(weights, axis=-1)]
    convert_element_type x12 -> x6, other arithmetic: 37.8 us -> 4.97 us  [scatter(): lax.psum_scatter(y, 'blk', scatter_dimension=1, tiled=True).astype(F32)]
    unnamed x19 -> x17, waiting for transfers between devices: 88.3 us -> 56.7 us
    reduce_scatter x9 -> x7, waiting for transfers between devices: 330 us -> 301 us  [the longest x6 288 us: scatter(): y = lax.psum_scatter(x, 'seq', scatter_dimension=0, tiled=True)]
    all_gather x4 -> x0, waiting for transfers between devices: 24.9 us -> none  [the longest x1 24.9 us: local(): lax.all_gather(key_proj, 'blk', axis=1, tiled=True)]
    all_gather x4 -> x0, local copies, waits for them, and re-layouts: 19.2 us -> none  [the longest x1 4.86 us: local(): lax.all_gather(dctx_low, 'blk', axis=1, tiled=True)]
  transfers between devices with their start and end apart: 16 -> 17, of which waited for: 8 -> 13; matrix products, arithmetic and copies ran while one was open for 45% -> 4% of each run, Pallas kernels for 0% -> 12%
where the time goes in v1:
time: 654 us; the launch traced here: 653 us
  waiting for transfers between devices  371 us (57%)
  Pallas kernels  171 us (26%)
  blocking collectives  52.3 us (8%)
  local copies, waits for them, and re-layouts  20.6 us (3%)
  other arithmetic  15 us (2%)
  between operations  14.6 us (2%)
  starting transfers between devices  8.64 us (1%)
    reduce_scatter x6, waiting for transfers between devices, scatter(): y = lax.psum_scatter(x, 'seq', scatter_dimension=0, tiled=True)  288 us
    unnamed x17, waiting for transfers between devices  56.7 us
    psum x1, blocking collectives, fast(): vectors = lax.psum((sums, isum[0], sums2), ('seq', 'blk'))  52.3 us
    pallas_call x1, Pallas kernels, token_pass(): pl.pallas_call(token_kernel, grid=(length // TILE,), out_shape=(low, low,...  46.6 us
    pallas_call x1, Pallas kernels, attention_backward(): pl.pallas_call(attention_backward_kernel, grid=(groups,), out_shape=(wide...  43.6 us
    pallas_call x6, Pallas kernels, weight_grad(): pl.pallas_call(product_kernel, grid=(height // rows, width // columns), o...  37.5 us
    pallas_call x1, Pallas kernels, attention_forward(): pl.pallas_call(attention_forward_kernel, grid=(groups,), out_shape=(wide,...  31.4 us
    unnamed x44, local copies, waits for them, and re-layouts  14.4 us
  transfers between devices with their start and end apart: 17, of which 13 were waited for; matrix products, arithmetic and copies ran while one was open for 4% of the time, Pallas kernels for 12%

profile of v1, /device:TPU:0, one launch (start us, length us, event | category | flops | bytes accessed | tf_op | source)
XLA Modules:
  0.0 653.3 jit_solution(12885746167285019146)
XLA Ops:
  7.3 2.5 dynamic-slice_bitcast_fusion.3
  9.7 2.9 collective-permute-start
  13.0 2.1 collective-permute-start.2
  17.6 13.7 %collective-permute-done.1 = s32[512]{0:T(512)S(1)} collective-permute-done((s32[512]{0:T(512)S(1)}, s32[512]{0:T(512)S(1)}, u32[]{:S(2)}, u32[]{:S(2)}) %collective-permute-start.1) | collective-permute-done | bytes 2080 | tf_op jit(solution)/shard_map/ppermute | solution.py:763
  31.3 1.1 copy.37.segc_ref
  32.4 1.2 pad_maximum_fusion.1.h_ref.a_ref
  33.6 31.4 %attention_forward.1 = (bf16[1024,768]{1,0:T(8,128)(2,1)}, bf16[1024,768]{1,0:T(8,128)(2,1)}, bf16[1024,768]{1,0:T(8,128)(2,1)}, bf16[1024,768]{1,0:T(8,128)(2,1)}, f32[24,1024]{1,0:T(8,128)}) custom-call(bf16[1024,768]{1,0:T(8,128)(2,1)} %pad_maximum_fusion.1.h_ref.a_ref, bf16[768,768]{1,0:T(8,128)(2,1)} %wq_ref.5, bf16[768,768]{1,0:T(8,128)(2,1)} %wk_ref.5, ...), custom_call_target="tpu_custom_call" | custom-call | flops 20000000000 | bytes 12000000 | tf_op jit(solution)/shard_map/attention_forward/pallas_call | solution.py:431
  65.1 2.4 pad_maximum_fusion.2.cot_ref
  67.5 46.6 %token_pass.1 = (bf16[1024,768]{1,0:T(8,128)(2,1)}, bf16[1024,768]{1,0:T(8,128)(2,1)}, bf16[1024,3072]{1,0:T(8,128)(2,1)}, bf16[1024,768]{1,0:T(8,128)(2,1)}, bf...) custom-call(bf16[1024,768]{1,0:T(8,128)(2,1)} %pad_maximum_fusion.1., ...), custom_call_target="tpu_custom_call" | custom-call | flops 21699999744 | bytes 30000000 | tf_op jit(solution)/shard_map/token_pass/pallas_call | solution.py:551
  114.1 43.6 %attention_backward.1 = (bf16[1024,768]{1,0:T(8,128)(2,1)}, bf16[1024,768]{1,0:T(8,128)(2,1)}, bf16[1024,768]{1,0:T(8,128)(2,1)}, f32[8,768]{1,0:T(8,128)}) custom-call(bf16[1024,768]{1,0:T(8,128)(2,1)} %get-tuple-element.39.q_ref, bf16[1024,768]{1,0:T(8,128)(2,1)} %get-tuple-element.40.k_ref, bf16[1024,768]{1,0:T(8,128)(2,1)} %get-tuple-element.41.v_ref, ...), custom_call_target="tpu_custom_call" | custom-call | flops 40000000000 | bytes 14000000 | tf_op jit(solution)/shard_map/attention_backward/pallas_call | solution.py:683
  157.7 4.4 weight_grad.6
  162.2 4.3 weight_grad.7
  166.5 4.3 weight_grad.8
  170.9 4.4 weight_grad.9
  175.4 10.1 %weight_grad.11 = bf16[3072,768]{1,0:T(8,128)(2,1)} custom-call(bf16[1024,3072]{1,0:T(8,128)(2,1)} %get-tuple-element.53.a_ref, bf16[1024,768]{1,0:T(8,128)(2,1)} %get-tuple-element.54.b_ref), custom_call_target="tpu_custom_call" | custom-call | flops 4831838208 | bytes 12582912 | tf_op jit(solution)/shard_map/weight_grad/pallas_call | solution.py:604
  185.5 10.1 %weight_grad.10 = bf16[768,3072]{1,0:T(8,128)(2,1)} custom-call(bf16[1024,768]{1,0:T(8,128)(2,1)} %get-tuple-element.50.a_ref, bf16[1024,3072]{1,0:T(8,128)(2,1)} %get-tuple-element.51.b_ref), custom_call_target="tpu_custom_call" | custom-call | flops 4831838208 | bytes 12582912 | tf_op jit(solution)/shard_map/weight_grad/pallas_call | solution.py:604
  195.7 26.5 %reduce-scatter.23.cloned.1.call-done = bf16[48,768]{1,0:T(8,128)(2,1)} async-done(((bf16[768,768]{1,0:T(8,128)(2,1)}), bf16[48,768]{1,0:T(8,128)(2,1)}) %reduce-scatter.23.cloned.1.call-update) | async-done | bytes 73744 | tf_op jit(solution)/shard_map/reduce_scatter | solution.py:817
  222.2 1.7 copy.39
  224.0 59.0 %reduce-scatter.25.cloned.1.call-done = bf16[48,768]{1,0:T(8,128)(2,1)} async-done(((bf16[768,768]{1,0:T(8,128)(2,1)}), bf16[48,768]{1,0:T(8,128)(2,1)}) %reduce-scatter.25.cloned.1.call-update) | async-done | bytes 73744 | tf_op jit(solution)/shard_map/reduce_scatter | solution.py:817
  282.9 1.7 copy.41
  284.8 1.6 collective-permute-start.3
  286.4 57.4 %reduce-scatter.27.cloned.1.call-done = bf16[48,768]{1,0:T(8,128)(2,1)} async-done(((bf16[768,768]{1,0:T(8,128)(2,1)}), bf16[48,768]{1,0:T(8,128)(2,1)}) %reduce-scatter.27.cloned.1.call-update) | async-done | bytes 73744 | tf_op jit(solution)/shard_map/reduce_scatter | solution.py:817
  343.7 1.7 copy.43
  345.5 59.4 %reduce-scatter.29.cloned.1.call-done = bf16[48,768]{1,0:T(8,128)(2,1)} async-done(((bf16[768,768]{1,0:T(8,128)(2,1)}), bf16[48,768]{1,0:T(8,128)(2,1)}) %reduce-scatter.29.cloned.1.call-update) | async-done | bytes 73744 | tf_op jit(solution)/shard_map/reduce_scatter | solution.py:817
  404.9 1.7 copy.45
  406.7 5.8 hidden_grad.3
  412.5 1.5 collective-permute-start.4
  414.1 52.3 %all-reduce = (f32[8,768]{1,0:T(8,128)S(1)}, f32[8,768]{1,0:T(8,128)S(1)}, f32[3072]{0:T(1024)}) all-reduce(f32[8,768]{1,0:T(8,128)S(1)} %copy-done.4, f32[8,768]{1,0:T(8,128)S(1)} %copy-done.3, f32[3072]{0:T(1024)S(1)} %bitcast.46), channel_id=1, replica_groups=mesh['seq'=16,'blk'=2] {'seq','blk'}, use_global_device_ids=true, to_apply=%region_2.3 | all-reduce | flops 15360 | bytes 122880 | tf_op jit(solution)/shard_map/psum | solution.py:820
  466.3 17.0 %reduce-scatter.35.cloned.1.call-done = bf16[192,768]{1,0:T(8,128)(2,1)} async-done(((bf16[3072,768]{1,0:T(8,128)(2,1)}), bf16[192,768]{1,0:T(8,128)(2,1)}) %reduce-scatter.35.cloned.1.call-update) | async-done | bytes 294928 | tf_op jit(solution)/shard_map/reduce_scatter | solution.py:817
  483.4 1.9 copy.47
  486.0 6.1 hidden_grad.2
  492.1 1.2 select_bitcast_fusion.1
  493.4 68.9 %reduce-scatter.31.cloned.1.call-done = bf16[48,3072]{1,0:T(8,128)(2,1)} async-done(((bf16[768,3072]{1,0:T(8,128)(2,1)}), bf16[48,3072]{1,0:T(8,128)(2,1)}) %reduce-scatter.31.cloned.1.call-update) | async-done | bytes 294928 | tf_op jit(solution)/shard_map/reduce_scatter | solution.py:817
  562.3 1.3 pad_maximum_fusion.3
  564.2 1.4 fusion
  565.7 1.9 pad_maximum_fusion
  567.5 7.5 %reduce-scatter.37.cloned.1.call-done = bf16[384,48]{1,0:T(8,128)(2,1)} async-done(((bf16[768,48]{1,0:T(8,128)(2,1)}), bf16[384,48]{1,0:T(8,128)(2,1)}) %reduce-scatter.37.cloned.1.call-update) | async-done | bytes 36880
  575.1 1.0 copy.40
  576.7 12.1 %reduce-scatter.39.cloned.1.call-done = bf16[384,48]{1,0:T(8,128)(2,1)} async-done(((bf16[768,48]{1,0:T(8,128)(2,1)}), bf16[384,48]{1,0:T(8,128)(2,1)}) %reduce-scatter.39.cloned.1.call-update) | async-done | bytes 36880
  588.8 1.0 copy.42
  590.5 11.6 %reduce-scatter.41.cloned.1.call-done = bf16[384,48]{1,0:T(8,128)(2,1)} async-done(((bf16[768,48]{1,0:T(8,128)(2,1)}), bf16[384,48]{1,0:T(8,128)(2,1)}) %reduce-scatter.41.cloned.1.call-update) | async-done | bytes 36880
  602.1 1.0 copy.44
  603.7 11.4 %reduce-scatter.43.cloned.1.call-done = bf16[384,48]{1,0:T(8,128)(2,1)} async-done(((bf16[768,48]{1,0:T(8,128)(2,1)}), bf16[384,48]{1,0:T(8,128)(2,1)}) %reduce-scatter.43.cloned.1.call-update) | async-done | bytes 36880
  615.1 1.0 copy.46
  616.8 13.8 %reduce-scatter.45.cloned.1.call-done = bf16[384,192]{1,0:T(8,128)(2,1)} async-done(((bf16[768,192]{1,0:T(8,128)(2,1)}), bf16[384,192]{1,0:T(8,128)(2,1)}) %reduce-scatter.45.cloned.1.call-update) | async-done | bytes 147472
  630.6 1.1 copy.48
  632.4 12.4 %reduce-scatter.33.cloned.1.call-done = bf16[48,1536]{1,0:T(8,128)(2,1)} async-done(((bf16[48,3072]{1,0:T(8,128)(2,1)}), bf16[48,1536]{1,0:T(8,128)(2,1)}) %reduce-scatter.33.cloned.1.call-update) | async-done | bytes 147472 | tf_op jit(solution)/shard_map/reduce_scatter | solution.py:818
  644.8 1.6 convert_element_type.35
  (84 shorter events, 8.2 us)
Async XLA Ops:
  7.2 215.0 %reduce-scatter.23.cloned.1.call-start = ((), (), s32[]{:S(2)}) async-start(), calls=%async_computation.12 | async-start | bytes 1253376 | tf_op jit(solution)/shard_map/reduce_scatter | solution.py:817
  7.2 5.4 copy-start.8
  7.2 5.6 copy-start.1
  9.7 22.6 %collective-permute-start = (bf16[512,768]{1,0:T(8,128)(2,1)}, bf16[512,768]{1,0:T(8,128)(2,1)S(1)}, u32[]{:S(2)}, u32[]{:S(2)}) collective-permute-start(bf16[512,768]{1,0:T(8,128)(2,1)} %get-tuple-element.73), channel_id=1, source_target_pairs={{0,1},{1,0},{2,3},{3,2},{4,5},{5,4},{6,7},{7,6},{8,9},{9,8},{10,11... | collective-permute-start | bytes 2359304 | tf_op jit(solution)/shard_map/ppermute | solution.py:763
  12.7 2.4 copy-start.9
  12.7 2.9 copy-start.10
  12.7 3.5 copy-start.11
  12.7 3.5 copy-start.12
  12.7 3.5 copy-start.13
  12.8 3.5 copy-start.14
  12.8 3.5 copy-start.15
  12.8 3.6 copy-start.16
  12.8 3.6 copy-start.7
  12.8 18.5 %collective-permute-start.1 = (s32[512]{0:T(512)S(1)}, s32[512]{0:T(512)S(1)}, u32[]{:S(2)}, u32[]{:S(2)}) collective-permute-start(s32[512]{0:T(512)S(1)} %bitcast.48), channel_id=1, source_target_pairs={{0,1},{1,0},{2,3},{3,2},{4,5},{5,4},{6,7},{7,6},{8,9},{9,8},{10,11... | collective-permute-start | bytes 6152 | tf_op jit(solution)/shard_map/ppermute | solution.py:763
  13.0 52.0 %collective-permute-start.2 = (bf16[512,768]{1,0:T(8,128)(2,1)S(1)}, bf16[512,768]{1,0:T(8,128)(2,1)}, u32[]{:S(2)}, u32[]{:S(2)}) collective-permute-start(bf16[512,768]{1,0:T(8,128)(2,1)S(1)} %get-tuple-element.71), channel_id=1, source_target_pairs={{0,1},{1,0},{2,3},{3,2},{4,5},{5,4},{6,7},{7,6},{8,9},{9,8},{10,11... | collective-permute-start | bytes 2359304 | tf_op jit(solution)/shard_map/ppermute | solution.py:763
  31.3 2.3 copy-start.5
  162.1 120.8 %reduce-scatter.25.cloned.1.call-start = ((), (), s32[]{:S(2)}) async-start(), calls=%async_computation.13 | async-start | bytes 1253376 | tf_op jit(solution)/shard_map/reduce_scatter | solution.py:817
  166.5 177.2 %reduce-scatter.27.cloned.1.call-start = ((), (), s32[]{:S(2)}) async-start(), calls=%async_computation.14 | async-start | bytes 1253376 | tf_op jit(solution)/shard_map/reduce_scatter | solution.py:817
  170.9 234.0 %reduce-scatter.29.cloned.1.call-start = ((), (), s32[]{:S(2)}) async-start(), calls=%async_computation.15 | async-start | bytes 1253376 | tf_op jit(solution)/shard_map/reduce_scatter | solution.py:817
  175.4 308.0 %reduce-scatter.35.cloned.1.call-start = ((), (), s32[]{:S(2)}) async-start(), calls=%async_computation.18 | async-start | bytes 5013504 | tf_op jit(solution)/shard_map/reduce_scatter | solution.py:817
  185.5 376.8 %reduce-scatter.31.cloned.1.call-start = ((), (), s32[]{:S(2)}) async-start(), calls=%async_computation.16 | async-start | bytes 5013504 | tf_op jit(solution)/shard_map/reduce_scatter | solution.py:817
  195.6 89.1 %copy-start.2 = (bf16[1024,768]{1,0:T(8,128)(2,1)S(1)}, bf16[1024,768]{1,0:T(8,128)(2,1)}, u32[]{:S(2)}) copy-start(bf16[1024,768]{1,0:T(8,128)(2,1)} %get-tuple-element.37) | copy-start | bytes 4718596
  195.6 379.5 %reduce-scatter.37.cloned.1.call-start = ((), (), s32[]{:S(2)}) async-start(), calls=%async_computation.19 | async-start | bytes 294912
  223.9 364.9 %reduce-scatter.39.cloned.1.call-start = ((), (), s32[]{:S(2)}) async-start(), calls=%async_computation.20 | async-start | bytes 294912
  284.7 317.4 %reduce-scatter.41.cloned.1.call-start = ((), (), s32[]{:S(2)}) async-start(), calls=%async_computation.21 | async-start | bytes 294912
  284.8 207.3 %collective-permute-start.3 = (bf16[512,768]{1,0:T(8,128)(2,1)S(1)}, bf16[512,768]{1,0:T(8,128)(2,1)}, u32[]{:S(2)}, u32[]{:S(2)}) collective-permute-start(bf16[512,768]{1,0:T(8,128)(2,1)S(1)} %slice.31), channel_id=1, source_target_pairs={{0,1},{1,0},{2,3},{3,2},{4,5},{5,4},{6,7},{7,6},{8,9},{9,8},{10,11... | collective-permute-start | bytes 2359304 | tf_op jit(solution)/shard_map/ppermute | solution.py:763
  345.5 269.7 %reduce-scatter.43.cloned.1.call-start = ((), (), s32[]{:S(2)}) async-start(), calls=%async_computation.22 | async-start | bytes 294912
  406.7 223.9 %reduce-scatter.45.cloned.1.call-start = ((), (), s32[]{:S(2)}) async-start(), calls=%async_computation.23 | async-start | bytes 589824
  406.7 7.3 %copy-start.3 = (f32[8,768]{1,0:T(8,128)S(1)}, f32[8,768]{1,0:T(8,128)}, u32[]{:S(2)}) copy-start(f32[8,768]{1,0:T(8,128)} %get-tuple-element.49) | copy-start | bytes 73732
  406.7 7.3 %copy-start.4 = (f32[8,768]{1,0:T(8,128)S(1)}, f32[8,768]{1,0:T(8,128)}, u32[]{:S(2)}) copy-start(f32[8,768]{1,0:T(8,128)} %get-tuple-element.47) | copy-start | bytes 73732
  406.7 7.3 %copy-start.6 = (f32[1,3072]{1,0:T(1,128)S(1)}, f32[1,3072]{1,0:T(1,128)}, u32[]{:S(2)}) copy-start(f32[1,3072]{1,0:T(1,128)} %get-tuple-element.52) | copy-start | bytes 36868
  412.5 151.0 %collective-permute-start.4 = (bf16[512,768]{1,0:T(8,128)(2,1)}, bf16[512,768]{1,0:T(8,128)(2,1)}, u32[]{:S(2)}, u32[]{:S(2)}) collective-permute-start(bf16[512,768]{1,0:T(8,128)(2,1)} %hidden_grad.3), channel_id=1, source_target_pairs={{0,1},{1,0},{2,3},{3,2},{4,5},{5,4},{6,7},{7,6},{8,9},{9,8},{10,11... | collective-permute-start | bytes 2359304 | tf_op jit(solution)/shard_map/ppermute | solution.py:763
  485.3 159.5 %reduce-scatter.33.cloned.1.call-start = ((), (), s32[]{:S(2)}) async-start(), calls=%async_computation.17 | async-start | bytes 442368 | tf_op jit(solution)/shard_map/reduce_scatter | solution.py:818
  562.3 2.0 copy-start
Sparse Core Ops, SparseCore 0:
  162.2 59.9 reduce-scatter.22
  225.8 57.1 reduce-scatter.24
  286.6 57.1 reduce-scatter.26
  347.8 57.1 reduce-scatter.28
  408.6 74.6 reduce-scatter.34
  487.6 74.5 reduce-scatter.30
  565.0 9.9 reduce-scatter.36
  577.9 10.9 reduce-scatter.38
  591.1 10.9 reduce-scatter.40
  604.1 10.9 reduce-scatter.42
  617.4 13.1 reduce-scatter.44
  632.7 12.0 reduce-scatter.32

commit v2 on v1

--- a/solution.py
+++ b/solution.py
@@ -592,25 +592,125 @@
     )(h, ctx, cot, wo, wi, wp, bi, vec)
 
 
-def product_kernel(a_ref, b_ref, out_ref):
-    out_ref[...] = mm(a_ref[...], b_ref[...], TN).astype(out_ref.dtype)
-
-
-def weight_grad(a, b, rows, columns, kind):
-    length, height = a.shape
-    width = b.shape[1]
-    a_spec = pl.BlockSpec((length, rows), lambda i, j: (0, i))
-    b_spec = pl.BlockSpec((length, columns), lambda i, j: (0, j))
+def put_pairs(res, core_ref, keep_ref, send_ref, place):
+    even = core_ref[0] == 0
+    for at, (low_part, high_part) in place:
+        zero, one = res[low_part], res[high_part]
+        keep_ref[at] = jnp.where(even, zero, one)
+        send_ref[at] = jnp.where(even, one, zero).astype(BF16)
+
+
+def blocks_of(rows, y_first):
+    columns = [slice(0, 384), slice(384, 768)]
+    places = []
+    for z in range(4):
+        for y in range(2):
+            for x in range(2):
+                base = (z * 2 + y) * 2 * rows
+                lead = (y, x) if y_first else (x, y)
+                places.append(
+                    (
+                        lead + (z, 0),
+                        (
+                            (slice(base, base + rows), columns[x]),
+                            (slice(base + rows, base + 2 * rows), columns[x]),
+                        ),
+                    )
+                )
+    return places
+
+
+def outer_grad_kernel(core_ref, act_ref, og_ref, keep_ref, send_ref):
+    res = mm(act_ref[...], og_ref[...], TN)
+    rows = keep_ref.shape[3]
+    places = [(at[:2] + (0,), pair) for at, pair in blocks_of(rows, False)[:4]]
+    put_pairs(res, core_ref, keep_ref, send_ref, places)
+
+
+SCALAR = pl.BlockSpec(memory_space=pltpu.SMEM)
+
+
+def outer_grad_call(core, act, og):
+    length, ff = act.shape
+    width = og.shape[1]
+    shape = (2, 2, 4, ff // 16, width // 2)
+    spec = pl.BlockSpec((2, 2, 1) + shape[3:], lambda z: (0, 0, z, 0, 0))
     return pl.pallas_call(
-        product_kernel,
-        grid=(height // rows, width // columns),
-        out_shape=jax.ShapeDtypeStruct((height, width), kind),
-        in_specs=[a_spec, b_spec],
-        out_specs=pl.BlockSpec((rows, columns), lambda i, j: (i, j)),
-        compiler_params=params(2),
-        cost_estimate=cost(2 * length * height * width, 2 * length * (height + width) + 2 * height * width),
-        name="weight_grad",
-    )(a, b)
+        outer_grad_kernel,
+        grid=(4,),
+        out_shape=(jax.ShapeDtypeStruct(shape, F32), jax.ShapeDtypeStruct(shape, BF16)),
+        in_specs=[
+            SCALAR,
+            pl.BlockSpec((length, ff // 4), lambda z: (0, z)),
+            fixed((length, width)),
+        ],
+        out_specs=(spec, spec),
+        compiler_params=params(1),
+        cost_estimate=cost(8e9, 16e6),
+        name="outer_grad",
+    )(core, act, og)
+
+
+def inner_grad_kernel(core_ref, first_ref, low_ref, high_ref, ctx_ref, ag_ref, keep_ref, send_ref):
+    step = pl.program_id(0)
+    places = blocks_of(keep_ref.shape[4], True)
+
+    @pl.when(step < 4)
+    def _():
+        both = jnp.concatenate([low_ref[...], high_ref[...]], axis=1)
+        put_pairs(mm(first_ref[...], both, TN), core_ref, keep_ref, send_ref, places)
+
+    @pl.when(step == 4)
+    def _():
+        put_pairs(mm(ctx_ref[...], ag_ref[...], TN), core_ref, keep_ref, send_ref, places)
+
+
+def inner_grad_call(core, first, ig, ctx, ag):
+    length, width = first.shape
+    shape = (2, 2, 4, 5, width // 16, width // 2)
+    spec = pl.BlockSpec((2, 2, 4, 1) + shape[4:], lambda s: (0, 0, 0, s, 0, 0))
+    return pl.pallas_call(
+        inner_grad_kernel,
+        grid=(5,),
+        out_shape=(jax.ShapeDtypeStruct(shape, F32), jax.ShapeDtypeStruct(shape, BF16)),
+        in_specs=[
+            SCALAR,
+            fixed((length, width)),
+            pl.BlockSpec((length, width // 2), lambda s: (0, jnp.minimum(s, 3))),
+            pl.BlockSpec((length, width // 2), lambda s: (0, 4 + jnp.minimum(s, 3))),
+            fixed((length, width)),
+            fixed((length, width)),
+        ],
+        out_specs=(spec, spec),
+        compiler_params=params(1),
+        cost_estimate=cost(9e9, 20e6),
+        name="inner_grad",
+    )(core, first, ig, ig, ctx, ag)
+
+
+def projection_grad_kernel(core_ref, h_ref, d_ref, keep_ref, send_ref):
+    res = mm(h_ref[...], d_ref[0], TN)
+    put_pairs(res, core_ref, keep_ref, send_ref, blocks_of(keep_ref.shape[4], True))
+
+
+def projection_grad_call(core, h, dqkv):
+    length, width = h.shape
+    shape = (2, 2, 4, 3, width // 16, width // 2)
+    spec = pl.BlockSpec((2, 2, 4, 1) + shape[4:], lambda s: (0, 0, 0, s, 0, 0))
+    return pl.pallas_call(
+        projection_grad_kernel,
+        grid=(3,),
+        out_shape=(jax.ShapeDtypeStruct(shape, F32), jax.ShapeDtypeStruct(shape, BF16)),
+        in_specs=[
+            SCALAR,
+            fixed((length, width)),
+            pl.BlockSpec((1, length, width), lambda s: (s, 0, 0)),
+        ],
+        out_specs=(spec, spec),
+        compiler_params=params(1),
+        cost_estimate=cost(6e9, 14e6),
+        name="projection_grad",
+    )(core, h, dqkv)
 
 
 def attention_backward_kernel(
@@ -622,16 +722,11 @@
     lse_ref,
     segc_ref,
     segr_ref,
-    dq_ref,
-    dk_ref,
-    dv_ref,
-    sums_ref,
-    delta_ref,
-    total_ref,
-    ds_ref,
-    km_ref,
+    *rest_refs,
 ):
+    grads_ref, sums_ref, delta_ref, total_ref, ds_ref, km_ref = rest_refs[-6:]
     length = q_ref.shape[0]
+
     prod = dctx_ref[...].astype(F32) * ctx_ref[...].astype(F32)
     high = prod.astype(BF16)
     rest = (prod - high.astype(F32)).astype(BF16)
@@ -662,59 +757,67 @@
             km_ref[head * TILE : (head + 1) * TILE, :] = km
         dkb = (dk * HEAD**-0.5).astype(BF16)
         dvb = dv.astype(BF16)
-        dk_ref[rows, :] = dkb
-        dv_ref[rows, :] = dvb
+        grads_ref[1, rows, :] = dkb
+        grads_ref[2, rows, :] = dvb
         total_ref[...] += mm(ds_ref[...], km_ref[...], TN)
         return carry + row_sum(dvb.astype(F32))
 
     dv_sum = lax.fori_loop(0, length // TILE, block, jnp.zeros((1, GROUP), F32))
     dq = total_ref[...].astype(BF16)
-    dq_ref[...] = dq
+    grads_ref[0] = dq
     sums_ref[...] = jnp.zeros_like(sums_ref)
     sums_ref[0:1, :] = row_sum(dq.astype(F32))
     sums_ref[1:2, :] = dv_sum
 
 
-def attention_backward(q, k, v, dctx, ctx, lse, segc, segr):
+ANY = pl.BlockSpec(memory_space=pl.ANY)
+
+
+def attention_backward(g, q, k, v, dctx, ctx, lse, segc, segr, held, after):
     length, width = q.shape
-    groups = width // GROUP
-    rows = pl.BlockSpec((length, GROUP), lambda g: (0, g))
-    wide = jax.ShapeDtypeStruct((length, width), BF16)
+    rows = pl.BlockSpec((length, GROUP), lambda i: (0, g))
+    grads = jax.ShapeDtypeStruct((3, length, width), BF16)
+    sums = jax.ShapeDtypeStruct((8, width), F32)
     return pl.pallas_call(
         attention_backward_kernel,
-        grid=(groups,),
-        out_shape=(wide, wide, wide, jax.ShapeDtypeStruct((8, width), F32)),
+        grid=(1,),
+        out_shape=(grads, sums),
         in_specs=[
             rows,
             rows,
             rows,
             rows,
             rows,
-            pl.BlockSpec((8, length), lambda g: (g, 0)),
+            pl.BlockSpec((8, length), lambda i: (g, 0)),
             fixed((length, 1)),
             fixed((1, length)),
-        ],
-        out_specs=(rows, rows, rows, pl.BlockSpec((8, GROUP), lambda g: (0, g))),
+        ]
+        + [ANY] * (len(held) + len(after)),
+        out_specs=(
+            pl.BlockSpec((3, length, GROUP), lambda i: (0, 0, g)),
+            pl.BlockSpec((8, GROUP), lambda i: (0, g)),
+        ),
         scratch_shapes=[
             pltpu.VMEM((8, length), F32),
             pltpu.VMEM((length, GROUP), F32),
             pltpu.VMEM((PER_GROUP * TILE, length), BF16),
             pltpu.VMEM((PER_GROUP * TILE, GROUP), BF16),
         ],
+        input_output_aliases={8 + i: i for i in range(len(held))},
         compiler_params=params(1),
-        cost_estimate=cost(40e9, 14e6),
+        cost_estimate=cost(12e9, 6e6),
         name="attention_backward",
-    )(q, k, v, dctx, ctx, lse, segc, segr)
-
-
-def hidden_grad_kernel(fp_ref, dq_ref, dk_ref, dv_ref, wq_ref, wk_ref, wv_ref, out_ref):
-    total = fp_ref[...] + mm(dq_ref[...], wq_ref[...], NT)
-    total = total + mm(dk_ref[...], wk_ref[...], NT)
-    out_ref[...] = (total + mm(dv_ref[...], wv_ref[...], NT)).astype(out_ref.dtype)
-
-
-def hidden_grad_part(fp, dq, dk, dv, wq, wk, wv, part, kind):
-    length, width = dq.shape
+    )(q, k, v, dctx, ctx, lse, segc, segr, *held, *after)
+
+
+def hidden_grad_kernel(fp_ref, d_ref, wq_ref, wk_ref, wv_ref, out_ref):
+    total = fp_ref[...] + mm(d_ref[0], wq_ref[...], NT)
+    total = total + mm(d_ref[1], wk_ref[...], NT)
+    out_ref[...] = (total + mm(d_ref[2], wv_ref[...], NT)).astype(out_ref.dtype)
+
+
+def hidden_grad_part(fp, dqkv, wq, wk, wv, part, kind):
+    length, width = fp.shape
     half = length // 2
     steps = half // TILE
     rows = pl.BlockSpec((TILE, width), lambda i: (i + part * steps, 0))
@@ -722,12 +825,13 @@
         hidden_grad_kernel,
         grid=(steps,),
         out_shape=jax.ShapeDtypeStruct((half, width), kind),
-        in_specs=[rows, rows, rows, rows] + [fixed((width, width))] * 3,
+        in_specs=[rows, pl.BlockSpec((3, TILE, width), lambda i: (0, i + part * steps, 0))]
+        + [fixed((width, width))] * 3,
         out_specs=pl.BlockSpec((TILE, width), lambda i: (i, 0)),
         compiler_params=params(1),
         cost_estimate=cost(6 * half * width * width, 8e6),
         name="hidden_grad",
-    )(fp, dq, dk, dv, wq, wk, wv)
+    )(fp, dqkv, wq, wk, wv)
 
 
 def fast(
@@ -800,43 +904,91 @@
         h, ctx, cot, output_matrix, inner_matrix, outer_matrix, row(inner_bias), vec
     )
     layer_out = back(out[:half], trade(out[half:]))
-    outer_grad = weight_grad(act, og, 512, width, BF16)
-    inner_grad = weight_grad(first, ig, width, 512, BF16)
-    output_grad = weight_grad(ctx, ag, width, width, BF16)
-    dq, dk, dv, sums2 = attention_backward(q, k, v, dctx, ctx, lse, segc, segr)
-    args = (fp, dq, dk, dv, query_matrix, key_matrix, value_matrix)
+    place = lax.axis_index("seq")
+    core, y_at, z_at = place % 2, (place // 2) % 2, place // 4
+    core_id = core.astype(jnp.int32)[None]
+
+    def seq_swap(x, bit):
+        return lax.ppermute(x, "seq", [(i, i ^ bit) for i in range(16)])
+
+    def pick(x, at):
+        return lax.dynamic_index_in_dim(x, at, 0, keepdims=False)
+
+    def exchange(keep, came, at, send):
+        away = (pick(keep, 1 - at) + pick(came, 1 - at).astype(F32)).astype(BF16)
+        mine = pick(keep, at) + pick(came, at).astype(F32)
+        return (mine, send(away), away)
+
+    def exchange_x(keep, came):
+        return exchange(keep, came, here, trade)
+
+    def exchange_y(keep, came):
+        return exchange(keep, came, y_at, lambda x: seq_swap(x, 2))
+
+    def exchange_z(keep, came):
+        total = keep + came.astype(F32)
+        low = total.astype(BF16)
+        parts = [seq_swap(pick(low, z_at ^ d), 4 * d) for d in (1, 2, 3)]
+        return (pick(total, z_at), parts, low)
+
+    def finish(state):
+        mine, parts, _ = state
+        return mine + (parts[0].astype(F32) + parts[1].astype(F32) + parts[2].astype(F32))
+
+    outer_keep, outer_send = outer_grad_call(core_id, act, og)
+    outer_came = seq_swap(outer_send, 1)
+    inner_keep, inner_send = inner_grad_call(core_id, first, ig, ctx, ag)
+    inner_came = seq_swap(inner_send, 1)
+    state_a = exchange_x(outer_keep, outer_came)
+    bwd = (q, k, v, dctx, ctx, lse, segc, segr)
+    dqkv, sums2 = attention_backward(0, *bwd, (), (state_a[2], inner_send))
+    state_b = exchange_y(inner_keep, inner_came)
+    dqkv, sums2 = attention_backward(1, *bwd, (dqkv, sums2), (state_b[2],))
+    state_a = exchange_y(*state_a[:2])
+    state_b = exchange_x(*state_b[:2])
+    dqkv, sums2 = attention_backward(2, *bwd, (dqkv, sums2), (state_a[2], state_b[2]))
+    late_keep, late_send = projection_grad_call(core_id, h, dqkv)
+    late_came = seq_swap(late_send, 1)
+    state_a = exchange_z(*state_a[:2])
+    state_b = exchange_z(*state_b[:2])
+    args = (fp, dqkv, query_matrix, key_matrix, value_matrix)
     away = hidden_grad_part(*args, 1, BF16)
     came = trade(away)
+    state_c = exchange_y(late_keep, late_came)
     home = hidden_grad_part(*args, 0, F32)
-    query_grad = weight_grad(h, dq, width, width, BF16)
-    key_grad = weight_grad(h, dk, width, width, BF16)
-    value_grad = weight_grad(h, dv, width, width, BF16)
+    state_c = exchange_x(*state_c[:2])
+    state_c = exchange_z(*state_c[:2])
     hidden_grad = back(home, came.astype(F32))
-
-    def scatter(x):
-        y = lax.psum_scatter(x, "seq", scatter_dimension=0, tiled=True)
-        return lax.psum_scatter(y, "blk", scatter_dimension=1, tiled=True).astype(F32)
-
-    vectors = lax.psum((sums, isum[0], sums2), ("seq", "blk"))
-    sums, isum, sums2 = vectors
+    outer_grad = finish(state_a)
+    inner_all = finish(state_b)
+    late_all = finish(state_c)
+    output_grad = inner_all[4]
+    inner_grad = jnp.transpose(inner_all[:4], (1, 0, 2)).reshape(width // 16, -1)
+
+    vectors = jnp.concatenate([sums[:6], isum.reshape(-1, width), sums2[:2]], axis=0)
+    vectors = vectors + seq_swap(vectors, 1)
+    vectors = vectors + seq_swap(vectors, 2)
+    vectors = vectors + trade(vectors)
+    near, far, across = (seq_swap(vectors, 4 * d) for d in (1, 2, 3))
+    vectors = (vectors + near) + (far + across)
     return (
         layer_out,
         hidden_grad,
-        scatter(query_grad),
-        sums2[0],
-        scatter(key_grad),
-        scatter(value_grad),
-        sums2[1],
-        scatter(output_grad),
-        sums[5],
-        sums[3],
-        sums[4],
-        scatter(inner_grad),
-        isum,
-        scatter(outer_grad),
-        sums[2],
-        sums[0],
-        sums[1],
+        late_all[0],
+        vectors[10],
+        late_all[1],
+        late_all[2],
+        vectors[11],
+        output_grad,
+        vectors[5],
+        vectors[3],
+        vectors[4],
+        inner_grad,
+        vectors[6:10].reshape(-1),
+        outer_grad,
+        vectors[2],
+        vectors[0],
+        vectors[1],
     )
 
 

time: 654 us -> 330 us (0.50)
  waiting for transfers between devices: 371 us -> 70.1 us
  blocking collectives: 52.3 us -> 0 us
  starting transfers between devices: 8.64 us -> 36.2 us
  other arithmetic: 15 us -> 34.6 us
  between operations: 14.6 us -> 1.48 us
    reduce_scatter x7 -> x0, waiting for transfers between devices: 301 us -> none  [the longest x6 288 us: scatter(): y = lax.psum_scatter(x, 'seq', scatter_dimension=0, tiled=True)]
    unnamed x17 -> x0, waiting for transfers between devices: 56.7 us -> none
    psum x1 -> x0, blocking collectives: 52.3 us -> none  [fast(): vectors = lax.psum((sums, isum[0], sums2), ('seq', 'blk'))]
    ppermute x5 -> x9, waiting for transfers between devices: 13.7 us -> 53.1 us  [trade(): return lax.ppermute(x, 'blk', swap)]
    ppermute x0 -> x20, starting transfers between devices: none -> 23.1 us  [seq_swap(): return lax.ppermute(x, 'seq', [(i, i ^ bit) for i in range(16)])]
    ppermute x0 -> x20, waiting for transfers between devices: none -> 16.9 us  [seq_swap(): return lax.ppermute(x, 'seq', [(i, i ^ bit) for i in range(16)])]
    unnamed x44 -> x39, local copies, waits for them, and re-layouts: 14.4 us -> 1.68 us
    add x0 -> x9, other arithmetic: none -> 10.3 us  [the longest x2 9.28 us: exchange(): mine = pick(keep, at) + pick(came, at).astype(F32)]
  transfers between devices with their start and end apart: 17 -> 29, of which waited for: 13 -> 10; matrix products, arithmetic and copies ran while one was open for 4% -> 13% of each run, Pallas kernels for 12% -> 34%
where the time goes in v2:
time: 330 us; the launch traced here: 325 us
  Pallas kernels  169 us (51%)
  waiting for transfers between devices  70.1 us (21%)
  starting transfers between devices  36.2 us (11%)
  other arithmetic  34.6 us (10%)
  local copies, waits for them, and re-layouts  14.1 us (4%)
    ppermute x9, waiting for transfers between devices, trade(): return lax.ppermute(x, 'blk', swap)  53.1 us
    pallas_call x3, Pallas kernels, attention_backward(): pl.pallas_call(attention_backward_kernel, grid=(1,), out_shape=(grads, su...  49.4 us
    pallas_call x1, Pallas kernels, token_pass(): pl.pallas_call(token_kernel, grid=(length // TILE,), out_shape=(low, low,...  46.6 us
    pallas_call x1, Pallas kernels, attention_forward(): pl.pallas_call(attention_forward_kernel, grid=(groups,), out_shape=(wide,...  31.4 us
    ppermute x20, starting transfers between devices, seq_swap(): return lax.ppermute(x, 'seq', [(i, i ^ bit) for i in range(16)])  23.1 us
    ppermute x20, waiting for transfers between devices, seq_swap(): return lax.ppermute(x, 'seq', [(i, i ^ bit) for i in range(16)])  16.9 us
    ppermute x9, starting transfers between devices, trade(): return lax.ppermute(x, 'blk', swap)  13.1 us
    pallas_call x1, Pallas kernels, inner_grad_call(): pl.pallas_call(inner_grad_kernel, grid=(5,), out_shape=(jax.ShapeDtypeStr...  12.1 us
  transfers between devices with their start and end apart: 29, of which 10 were waited for; matrix products, arithmetic and copies ran while one was open for 13% of the time, Pallas kernels for 34%

profile of v2, /device:TPU:0, one launch (start us, length us, event | category | flops | bytes accessed | tf_op | source)
XLA Modules:
  0.0 325.1 jit_solution(7061045543968062786)
XLA Ops:
  0.7 2.5 dynamic-slice_bitcast_fusion.3
  3.2 2.9 collective-permute-start
  6.4 2.1 collective-permute-start.2
  11.0 13.7 %collective-permute-done.1 = s32[512]{0:T(512)S(1)} collective-permute-done((s32[512]{0:T(512)S(1)}, s32[512]{0:T(512)S(1)}, u32[]{:S(2)}, u32[]{:S(2)}) %collective-permute-start.1) | collective-permute-done | bytes 2080 | tf_op jit(solution)/shard_map/ppermute | solution.py:867
  25.9 2.4 pad_maximum_fusion.1.h_ref
  28.2 31.4 %attention_forward.1 = (bf16[1024,768]{1,0:T(8,128)(2,1)}, bf16[1024,768]{1,0:T(8,128)(2,1)}, bf16[1024,768]{1,0:T(8,128)(2,1)}, bf16[1024,768]{1,0:T(8,128)(2,1)}, f32[24,1024]{1,0:T(8,128)}) custom-call(bf16[1024,768]{1,0:T(8,128)(2,1)} %pad_maximum_fusion.1.h_ref, bf16[768,768]{1,0:T(8,128)(2,1)} %wq_ref.5, bf16[768,768]{1,0:T(8,128)(2,1)} %wk_ref.5, ...), custom_call_target="tpu_custom_call" | custom-call | flops 20000000000 | bytes 12000000 | tf_op jit(solution)/shard_map/attention_forward/pallas_call | solution.py:431
  60.9 46.6 %token_pass.1 = (bf16[1024,768]{1,0:T(8,128)(2,1)}, bf16[1024,768]{1,0:T(8,128)(2,1)}, bf16[1024,3072]{1,0:T(8,128)(2,1)}, bf16[1024,768]{1,0:T(8,128)(2,1)}, bf...) custom-call(bf16[1024,768]{1,0:T(8,128)(2,1)} %pad_maximum_fusion.1., ...), custom_call_target="tpu_custom_call" | custom-call | flops 21699999744 | bytes 30000000 | tf_op jit(solution)/shard_map/token_pass/pallas_call | solution.py:551
  107.5 12.1 %inner_grad.1 = (f32[2,2,4,5,48,384]{5,4,3,2,1,0:T(8,128)}, bf16[2,2,4,5,48,384]{5,4,3,2,1,0:T(8,128)(2,1)}) custom-call(s32[1]{0:T(128)} %bitcast.11.core_ref, bf16[1024,768]{1,0:T(8,128)(2,1)} %get-tuple-element.56.first_ref, bf16[1024,3072]{1,0:T(8,128)(2,1)} %get-tuple-element.57.low_ref.high_ref, bf16[1024,3072]{1,0:T(8,128)(2,1)} %get-tuple-element.57.low_ref.high_ref, ...), custom_call_target="tpu_custom_call" | custom-call | flops 8999999488 | bytes 20000000 | tf_op jit(solution)/shard_map/inner_grad/pallas_call | solution.py:672
  119.6 9.9 %outer_grad.1 = (f32[2,2,4,192,384]{4,3,2,1,0:T(8,128)}, bf16[2,2,4,192,384]{4,3,2,1,0:T(8,128)(2,1)}) custom-call(s32[1]{0:T(128)} %bitcast.11.core_ref, bf16[1024,3072]{1,0:T(8,128)(2,1)} %get-tuple-element.52.act_ref, bf16[1024,768]{1,0:T(8,128)(2,1)} %get-tuple-element.53.og_ref), custom_call_target="tpu_custom_call" | custom-call | flops 8000000000 | bytes 16000000 | tf_op jit(solution)/shard_map/outer_grad/pallas_call | solution.py:638
  129.9 2.1 slice.55
  132.1 2.1 collective-permute-start.3
  135.3 16.8 %collective-permute-done.3 = bf16[512,768]{1,0:T(8,128)(2,1)} collective-permute-done((bf16[512,768]{1,0:T(8,128)(2,1)}, bf16[512,768]{1,0:T(8,128)(2,1)}, u32[]{:S(2)}, u32[]{:S(2)}) %collective-permute-start.3) | collective-permute-done | bytes 786464 | tf_op jit(solution)/shard_map/ppermute | solution.py:867
  152.2 2.7 select_bitcast_fusion.1
  154.8 5.6 %convert_add_fusion.1 = (f32[1,2,4,192,384]{4,3,2,1,0:T(8,128)}, bf16[2,4,192,384]{3,2,1,0:T(8,128)(2,1)}) fusion(f32[2,2,4,192,384]{4,3,2,1,0:T(8,128)} %get-tuple-element.54, s32[]{:T(128)S(6)} %select_n.119, bf16[2,2,4,192,384]{4,3,2,1,0:T(8,128)(2,1)} %collective-permute-done.4, s32[]{:T(128)S(6)} %select_n.120), kind=kLoop, calls=%fused_computation.3 | loop fusion | flops 2949120 | bytes 10616840 | tf_op jit(solution)/shard_map/add | solution.py:919
  160.4 1.7 collective-permute-start.6
  162.2 1.6 copy-done.2
  163.7 3.7 %convert_add_fusion = (f32[1,2,4,5,48,384]{5,4,3,2,1,0:T(8,128)S(1)}, bf16[2,4,5,48,384]{4,3,2,1,0:T(8,128)(2,1)}) fusion(f32[2,2,4,5,48,384]{5,4,3,2,1,0:T(8,128)S(1)} %bitcast.114, s32[]{:T(128)S(6)} %select_n.127, bf16[2,2,4,5,48,384]{5,4,3,2,1,0:T(8,128)(2,1)} %copy-done.2, s32[]{:T(128)S(6)} %select_n.126), kind=kLoop, calls=%fused_computation.1 | loop fusion | flops 3686400 | bytes 13271048 | tf_op jit(solution)/shard_map/add | solution.py:919
  167.4 1.5 collective-permute-start.7
  169.0 16.4 %attention_backward.3 = (bf16[3,1024,768]{2,1,0:T(8,128)(2,1)}, f32[8,768]{1,0:T(8,128)}) custom-call(bf16[1024,768]{1,0:T(8,128)(2,1)} %get-tuple-element.47.q_ref, bf16[1024,768]{1,0:T(8,128)(2,1)} %get-tuple-element.48.k_ref, bf16[1024,768]{1,0:T(8,128)(2,1)} %get-tuple-element.49.v_ref, bf16[1024,768]{1,0:T(8,128)(2,1)} %get-tuple-element.50.dctx_ref, ...), custom_call_target="tpu_custom_call" | custom-call | flops 12000000000 | bytes 6000000 | tf_op jit(solution)/shard_map/attention_backward/pallas_call | solution.py:781
  185.4 16.4 %attention_backward.4 = (bf16[3,1024,768]{2,1,0:T(8,128)(2,1)}, f32[8,768]{1,0:T(8,128)}) custom-call(bf16[1024,768]{1,0:T(8,128)(2,1)} %get-tuple-element.47.q_ref, bf16[1024,768]{1,0:T(8,128)(2,1)} %get-tuple-element.48.k_ref, bf16[1024,768]{1,0:T(8,128)(2,1)} %get-tuple-element.49.v_ref, ...), custom_call_target="tpu_custom_call", output_to_operand_aliasing={{0}: (8, {}), {1}: (9, {})} | custom-call | flops 12000000000 | bytes 6000000 | tf_op jit(solution)/shard_map/attention_backward/pallas_call | solution.py:781
  201.7 2.4 fusion.9.rest_refs_2_
  204.6 2.1 fusion.8.rest_refs_3_
  206.7 16.6 %attention_backward.5 = (bf16[3,1024,768]{2,1,0:T(8,128)(2,1)}, f32[8,768]{1,0:T(8,128)}) custom-call(bf16[1024,768]{1,0:T(8,128)(2,1)} %get-tuple-element.47.q_ref, bf16[1024,768]{1,0:T(8,128)(2,1)} %get-tuple-element.48.k_ref, bf16[1024,768]{1,0:T(8,128)(2,1)} %get-tuple-element.49.v_ref, ...), custom_call_target="tpu_custom_call", output_to_operand_aliasing={{0}: (8, {}), {1}: (9, {})} | custom-call | flops 12000000000 | bytes 6000000 | tf_op jit(solution)/shard_map/attention_backward/pallas_call | solution.py:781
  223.3 8.1 %projection_grad.1 = (f32[2,2,4,3,48,384]{5,4,3,2,1,0:T(8,128)}, bf16[2,2,4,3,48,384]{5,4,3,2,1,0:T(8,128)(2,1)}) custom-call(s32[1]{0:T(128)} %bitcast.11.core_ref, bf16[1024,768]{1,0:T(8,128)(2,1)} %pad_maximum_fusion.1.h_ref, bf16[3,1024,768]{2,1,0:T(8,128)(2,1)} %get-tuple-element.65.d_ref), custom_call_target="tpu_custom_call" | custom-call | flops 6000000000 | bytes 14000000 | tf_op jit(solution)/shard_map/projection_grad/pallas_call | solution.py:700
  231.5 2.8 pad_maximum_fusion.3
  234.3 1.3 fusion.12
  237.0 3.7 %collective-permute-start.28 = (bf16[192,384]{1,0:T(8,128)(2,1)S(1)}, bf16[192,384]{1,0:T(8,128)(2,1)S(1)}, u32[]{:S(2)}, u32[]{:S(2)}) collective-permute-start(bf16[192,384]{1,0:T(8,128)(2,1)S(1)} %get-tuple-element.103), channel_id=1, source_target_pairs={{0,24},{2,26},{4,28},{6,30},{8,16},{10,18},{12,20},{14,22},{16,8},... | collective-permute-start | bytes 442376 | tf_op jit(solution)/shard_map/ppermute | solution.py:912
  241.5 1.6 collective-permute-start.16
  243.1 2.6 collective-permute-done.28
  245.7 7.7 %collective-permute-done.27 = bf16[192,384]{1,0:T(8,128)(2,1)S(1)} collective-permute-done((bf16[192,384]{1,0:T(8,128)(2,1)S(1)}, bf16[192,384]{1,0:T(8,128)(2,1)S(1)}, u32[]{:S(2)}, u32[]{:S(2)}) %collective-permute-start.27) | collective-permute-done | bytes 147488 | tf_op jit(solution)/shard_map/ppermute | solution.py:912
  254.7 1.5 collective-permute-start.17
  256.2 5.7 %hidden_grad.2 = f32[512,768]{1,0:T(8,128)} custom-call(f32[1024,768]{1,0:T(8,128)} %get-tuple-element.46.fp_ref, bf16[3,1024,768]{2,1,0:T(8,128)(2,1)} %get-tuple-element.65.d_ref, bf16[768,768]{1,0:T(8,128)(2,1)} %wq_ref.5, bf16[768,768]{1,0:T(8,128)(2,1)} %wk_ref.5, bf16[768,768]{1,0:T(8,128)(2,1)} %wv_ref.5), custom_call_target="tpu_custom_call" | custom-call | flops 1811939328 | bytes 8000000 | tf_op jit(solution)/shard_map/hidden_grad/pallas_call | solution.py:824
  261.9 11.0 %collective-permute-done.17 = f32[12,768]{1,0:T(8,128)S(1)} collective-permute-done((f32[12,768]{1,0:T(8,128)S(1)}, f32[12,768]{1,0:T(8,128)S(1)}, u32[]{:S(2)}, u32[]{:S(2)}) %collective-permute-start.17) | collective-permute-done | bytes 36896 | tf_op jit(solution)/shard_map/ppermute | solution.py:867
  273.1 2.5 collective-permute-start.20
  276.5 5.6 %hidden_grad.3 = bf16[512,768]{1,0:T(8,128)(2,1)} custom-call(f32[1024,768]{1,0:T(8,128)} %get-tuple-element.46.fp_ref, bf16[3,1024,768]{2,1,0:T(8,128)(2,1)} %get-tuple-element.65.d_ref, bf16[768,768]{1,0:T(8,128)(2,1)} %wq_ref.5, bf16[768,768]{1,0:T(8,128)(2,1)} %wk_ref.5, bf16[768,768]{1,0:T(8,128)(2,1)} %wv_ref.5), custom_call_target="tpu_custom_call" | custom-call | flops 1811939328 | bytes 8000000 | tf_op jit(solution)/shard_map/hidden_grad/pallas_call | solution.py:824
  284.0 2.9 fusion.6
  286.8 1.6 collective-permute-start.10
  288.4 1.7 fusion.13
  290.2 2.5 collective-permute-start.24
  292.8 1.9 collective-permute-start.22
  294.7 4.7 %collective-permute-done.8 = bf16[512,768]{1,0:T(8,128)(2,1)} collective-permute-done((bf16[512,768]{1,0:T(8,128)(2,1)}, bf16[512,768]{1,0:T(8,128)(2,1)}, u32[]{:S(2)}, u32[]{:S(2)}) %collective-permute-start.8) | collective-permute-done | bytes 786464 | tf_op jit(solution)/shard_map/ppermute | solution.py:867
  299.4 1.4 fusion
  300.9 1.9 pad_maximum_fusion
  302.7 3.0 collective-permute-done.10
  305.8 1.5 collective-permute-start.11
  307.5 6.8 %collective-permute-done.11 = bf16[4,3,48,384]{3,2,1,0:T(8,128)(2,1)S(1)} collective-permute-done((bf16[4,3,48,384]{3,2,1,0:T(8,128)(2,1)S(1)}, bf16[4,3,48,384]{3,2,1,0:T(8,128)(2,1)S(1)}, u32[]{:S(2)}, u32[]{:S(2)}) %collective-permute-start.11) | collective-permute-done | bytes 442400 | tf_op jit(solution)/shard_map/ppermute | solution.py:867
  314.5 2.5 collective-permute-start.14
  321.2 2.7 collective-permute-done.13
  (113 shorter events, 19.2 us)
Async XLA Ops:
  0.7 5.4 %copy-start.8 = (s32[2,512]{1,0:T(2,128)S(1)}, s32[2,512]{1,0:T(2,128)}, u32[]{:S(2)}) copy-start(s32[2,512]{1,0:T(2,128)} %param.19) | copy-start | bytes 12292
  0.7 5.6 %copy-start.3 = (bf16[2,512,768]{2,1,0:T(8,128)(2,1)S(1)}, bf16[2,512,768]{2,1,0:T(8,128)(2,1)}, u32[]{:S(2)}) copy-start(bf16[2,512,768]{2,1,0:T(8,128)(2,1)} %param.35) | copy-start | bytes 4718596
  3.2 22.7 %collective-permute-start = (bf16[512,768]{1,0:T(8,128)(2,1)}, bf16[512,768]{1,0:T(8,128)(2,1)}, u32[]{:S(2)}, u32[]{:S(2)}) collective-permute-start(bf16[512,768]{1,0:T(8,128)(2,1)} %get-tuple-element.98), channel_id=1, source_target_pairs={{0,1},{1,0},{2,3},{3,2},{4,5},{5,4},{6,7},{7,6},{8,9},{9,8},{10,11... | collective-permute-start | bytes 2359304 | tf_op jit(solution)/shard_map/ppermute | solution.py:867
  6.1 2.4 copy-start.9
  6.1 2.9 copy-start.10
  6.1 3.5 %copy-start.7 = (bf16[3072]{0:T(1024)(128)(2,1)S(1)}, bf16[3072]{0:T(1024)(128)(2,1)}, u32[]{:S(2)}) copy-start(bf16[3072]{0:T(1024)(128)(2,1)} %param.30) | copy-start | bytes 18436
  6.1 4.1 %copy-start.11 = (bf16[768]{0:T(1024)(128)(2,1)S(1)}, bf16[768]{0:T(1024)(128)(2,1)}, u32[]{:S(2)}) copy-start(bf16[768]{0:T(1024)(128)(2,1)} %param.26) | copy-start | bytes 4612
  6.2 4.1 %copy-start.12 = (bf16[768]{0:T(1024)(128)(2,1)S(1)}, bf16[768]{0:T(1024)(128)(2,1)}, u32[]{:S(2)}) copy-start(bf16[768]{0:T(1024)(128)(2,1)} %param.27) | copy-start | bytes 4612
  6.2 4.1 %copy-start.13 = (bf16[768]{0:T(1024)(128)(2,1)S(1)}, bf16[768]{0:T(1024)(128)(2,1)}, u32[]{:S(2)}) copy-start(bf16[768]{0:T(1024)(128)(2,1)} %param.28) | copy-start | bytes 4612
  6.2 4.1 %copy-start.14 = (bf16[768]{0:T(1024)(128)(2,1)S(1)}, bf16[768]{0:T(1024)(128)(2,1)}, u32[]{:S(2)}) copy-start(bf16[768]{0:T(1024)(128)(2,1)} %param.32) | copy-start | bytes 4612
  6.2 4.1 %copy-start.15 = (bf16[768]{0:T(1024)(128)(2,1)S(1)}, bf16[768]{0:T(1024)(128)(2,1)}, u32[]{:S(2)}) copy-start(bf16[768]{0:T(1024)(128)(2,1)} %param.33) | copy-start | bytes 4612
  6.2 4.1 %copy-start.16 = (bf16[768]{0:T(1024)(128)(2,1)S(1)}, bf16[768]{0:T(1024)(128)(2,1)}, u32[]{:S(2)}) copy-start(bf16[768]{0:T(1024)(128)(2,1)} %param.34) | copy-start | bytes 4612
  6.2 18.6 %collective-permute-start.1 = (s32[512]{0:T(512)S(1)}, s32[512]{0:T(512)S(1)}, u32[]{:S(2)}, u32[]{:S(2)}) collective-permute-start(s32[512]{0:T(512)S(1)} %bitcast.125), channel_id=1, source_target_pairs={{0,1},{1,0},{2,3},{3,2},{4,5},{5,4},{6,7},{7,6},{8,9},{9,8},{10,11... | collective-permute-start | bytes 6152 | tf_op jit(solution)/shard_map/ppermute | solution.py:867
  6.4 53.2 %collective-permute-start.2 = (bf16[512,768]{1,0:T(8,128)(2,1)S(1)}, bf16[512,768]{1,0:T(8,128)(2,1)S(1)}, u32[]{:S(2)}, u32[]{:S(2)}) collective-permute-start(bf16[512,768]{1,0:T(8,128)(2,1)S(1)} %get-tuple-element.96), channel_id=1, source_target_pairs={{0,1},{1,0},{2,3},{3,2},{4,5},{5,4},{6,7},{7,6},{8,9},{9,8},{10,11... | collective-permute-start | bytes 2359304 | tf_op jit(solution)/shard_map/ppermute | solution.py:867
  24.8 3.5 %copy-start.5 = (s32[1024]{0:T(1024)}, s32[1024]{0:T(1024)S(1)}, u32[]{:S(2)}) copy-start(s32[1024]{0:T(1024)S(1)} %pad_add_fusion) | copy-start | bytes 12292
  119.6 42.6 %collective-permute-start.5 = (bf16[2,2,4,5,48,384]{5,4,3,2,1,0:T(8,128)(2,1)}, bf16[2,2,4,5,48,384]{5,4,3,2,1,0:T(8,128)(2,1)S(1)}, u32[]{:S(2)}, u32[]{:S(2)}) collective-permute-start(bf16[2,2,4,5,48,384]{5,4,3,2,1,0:T(8,128)(2,1)} %get-tuple-element.59.rest_refs_1_), channel_id=1, source_target_pairs={{0,2},{2,0},{4,6},{6,4},{8,10},{10,8},{12,14},{14,12},{16,18},{18,... | collective-permute-start | bytes 8847368 | tf_op jit(solution)/shard_map/ppermute | solution.py:912
  129.5 5.2 %copy-start.6 = (f32[1,3072]{1,0:T(1,128)S(1)}, f32[1,3072]{1,0:T(1,128)}, u32[]{:S(2)}) copy-start(f32[1,3072]{1,0:T(1,128)} %get-tuple-element.69) | copy-start | bytes 36868
  129.5 25.4 %collective-permute-start.4 = (bf16[2,2,4,192,384]{4,3,2,1,0:T(8,128)(2,1)}, bf16[2,2,4,192,384]{4,3,2,1,0:T(8,128)(2,1)}, u32[]{:S(2)}, u32[]{:S(2)}) collective-permute-start(bf16[2,2,4,192,384]{4,3,2,1,0:T(8,128)(2,1)} %get-tuple-element.55), channel_id=1, source_target_pairs={{0,2},{2,0},{4,6},{6,4},{8,10},{10,8},{12,14},{14,12},{16,18},{18,... | collective-permute-start | bytes 7077896 | tf_op jit(solution)/shard_map/ppermute | solution.py:912
  132.1 20.1 %collective-permute-start.3 = (bf16[512,768]{1,0:T(8,128)(2,1)}, bf16[512,768]{1,0:T(8,128)(2,1)}, u32[]{:S(2)}, u32[]{:S(2)}) collective-permute-start(bf16[512,768]{1,0:T(8,128)(2,1)} %slice.55), channel_id=1, source_target_pairs={{0,1},{1,0},{2,3},{3,2},{4,5},{5,4},{6,7},{7,6},{8,9},{9,8},{10,11... | collective-permute-start | bytes 2359304 | tf_op jit(solution)/shard_map/ppermute | solution.py:867
  154.8 8.9 %slice-start = ((s8[5898240]{0:T(1024)(128)(4,1)}), s8[4194304]{0:T(1024)(128)(4,1)S(1)}, s32[]{:S(2)}) async-start(s8[5898240]{0:T(1024)(128)(4,1)} %bitcast.113), calls=%async_computation | async-start | bytes 8388608
  154.8 8.9 %slice-start.1 = ((s8[5898240]{0:T(1024)(128)(4,1)}), s8[1703936]{0:T(1024)(128)(4,1)S(1)}, s32[]{:S(2)}) async-start(s8[5898240]{0:T(1024)(128)(4,1)} %bitcast.113), calls=%async_computation.1 | async-start | bytes 3407872
  160.4 41.3 %collective-permute-start.6 = (bf16[2,4,192,384]{3,2,1,0:T(8,128)(2,1)}, bf16[2,4,192,384]{3,2,1,0:T(8,128)(2,1)}, u32[]{:S(2)}, u32[]{:S(2)}) collective-permute-start(bf16[2,4,192,384]{3,2,1,0:T(8,128)(2,1)} %get-tuple-element.88.rest_refs_0_), channel_id=1, source_target_pairs={{0,1},{1,0},{2,3},{3,2},{4,5},{5,4},{6,7},{7,6},{8,9},{9,8},{10,11... | collective-permute-start | bytes 3538952 | tf_op jit(solution)/shard_map/ppermute | solution.py:867
  162.2 1.6 copy-start.2
  167.4 37.2 %collective-permute-start.7 = (bf16[2,4,5,48,384]{4,3,2,1,0:T(8,128)(2,1)}, bf16[2,4,5,48,384]{4,3,2,1,0:T(8,128)(2,1)}, u32[]{:S(2)}, u32[]{:S(2)}) collective-permute-start(bf16[2,4,5,48,384]{4,3,2,1,0:T(8,128)(2,1)} %get-tuple-element.86.rest_refs_2_), channel_id=1, source_target_pairs={{0,4},{2,6},{4,0},{6,2},{8,12},{10,14},{12,8},{14,10},{16,20},{18,... | collective-permute-start | bytes 4423688 | tf_op jit(solution)/shard_map/ppermute | solution.py:912
  204.1 30.2 %collective-permute-start.25 = (bf16[4,192,384]{2,1,0:T(8,128)(2,1)}, bf16[4,192,384]{2,1,0:T(8,128)(2,1)S(1)}, u32[]{:S(2)}, u32[]{:S(2)}) collective-permute-start(bf16[4,192,384]{2,1,0:T(8,128)(2,1)} %fusion.9.rest_refs_2_), channel_id=1, source_target_pairs={{0,4},{2,6},{4,0},{6,2},{8,12},{10,14},{12,8},{14,10},{16,20},{18,... | collective-permute-start | bytes 1769480 | tf_op jit(solution)/shard_map/ppermute | solution.py:912
  231.4 52.5 %collective-permute-start.9 = (bf16[2,2,4,3,48,384]{5,4,3,2,1,0:T(8,128)(2,1)}, bf16[2,2,4,3,48,384]{5,4,3,2,1,0:T(8,128)(2,1)}, u32[]{:S(2)}, u32[]{:S(2)}) collective-permute-start(bf16[2,2,4,3,48,384]{5,4,3,2,1,0:T(8,128)(2,1)} %get-tuple-element.67), channel_id=1, source_target_pairs={{0,2},{2,0},{4,6},{6,4},{8,10},{10,8},{12,14},{14,12},{16,18},{18,... | collective-permute-start | bytes 5308424 | tf_op jit(solution)/shard_map/ppermute | solution.py:912
  231.4 2.8 copy-start
  234.3 2.1 copy-start.4
  236.4 5.1 %collective-permute-start.15 = (f32[12,768]{1,0:T(8,128)S(1)}, f32[12,768]{1,0:T(8,128)S(1)}, u32[]{:S(2)}, u32[]{:S(2)}) collective-permute-start(f32[12,768]{1,0:T(8,128)S(1)} %pad_maximum_fusion.4), channel_id=1, source_target_pairs={{0,2},{2,0},{4,6},{6,4},{8,10},{10,8},{12,14},{14,12},{16,18},{18,... | collective-permute-start | bytes 110600 | tf_op jit(solution)/shard_map/ppermute | solution.py:912
  237.0 8.7 %collective-permute-start.28 = (bf16[192,384]{1,0:T(8,128)(2,1)S(1)}, bf16[192,384]{1,0:T(8,128)(2,1)S(1)}, u32[]{:S(2)}, u32[]{:S(2)}) collective-permute-start(bf16[192,384]{1,0:T(8,128)(2,1)S(1)} %get-tuple-element.103), channel_id=1, source_target_pairs={{0,24},{2,26},{4,28},{6,30},{8,16},{10,18},{12,20},{14,22},{16,8},... | collective-permute-start | bytes 442376 | tf_op jit(solution)/shard_map/ppermute | solution.py:912
  240.7 12.7 %collective-permute-start.27 = (bf16[192,384]{1,0:T(8,128)(2,1)S(1)}, bf16[192,384]{1,0:T(8,128)(2,1)S(1)}, u32[]{:S(2)}, u32[]{:S(2)}) collective-permute-start(bf16[192,384]{1,0:T(8,128)(2,1)S(1)} %get-tuple-element.104), channel_id=1, source_target_pairs={{0,16},{2,18},{4,20},{6,22},{8,24},{10,26},{12,28},{14,30},{16,0},... | collective-permute-start | bytes 442376 | tf_op jit(solution)/shard_map/ppermute | solution.py:912
  240.7 12.7 %collective-permute-start.26 = (bf16[192,384]{1,0:T(8,128)(2,1)S(1)}, bf16[192,384]{1,0:T(8,128)(2,1)S(1)}, u32[]{:S(2)}, u32[]{:S(2)}) collective-permute-start(bf16[192,384]{1,0:T(8,128)(2,1)S(1)} %get-tuple-element.102), channel_id=1, source_target_pairs={{0,8},{2,10},{4,12},{6,14},{8,0},{10,2},{12,4},{14,6},{16,24},{18,... | collective-permute-start | bytes 442376 | tf_op jit(solution)/shard_map/ppermute | solution.py:912
  241.5 13.2 %collective-permute-start.16 = (f32[12,768]{1,0:T(8,128)S(1)}, f32[12,768]{1,0:T(8,128)S(1)}, u32[]{:S(2)}, u32[]{:S(2)}) collective-permute-start(f32[12,768]{1,0:T(8,128)S(1)} %fusion.11), channel_id=1, source_target_pairs={{0,4},{2,6},{4,0},{6,2},{8,12},{10,14},{12,8},{14,10},{16,20},{18,... | collective-permute-start | bytes 110600 | tf_op jit(solution)/shard_map/ppermute | solution.py:912
  254.1 34.3 %collective-permute-start.21 = (bf16[4,5,48,384]{3,2,1,0:T(8,128)(2,1)}, bf16[4,5,48,384]{3,2,1,0:T(8,128)(2,1)}, u32[]{:S(2)}, u32[]{:S(2)}) collective-permute-start(bf16[4,5,48,384]{3,2,1,0:T(8,128)(2,1)} %fusion.8.rest_refs_3_), channel_id=1, source_target_pairs={{0,1},{1,0},{2,3},{3,2},{4,5},{5,4},{6,7},{7,6},{8,9},{9,8},{10,11... | collective-permute-start | bytes 2211848 | tf_op jit(solution)/shard_map/ppermute | solution.py:867
  254.7 18.3 %collective-permute-start.17 = (f32[12,768]{1,0:T(8,128)S(1)}, f32[12,768]{1,0:T(8,128)S(1)}, u32[]{:S(2)}, u32[]{:S(2)}) collective-permute-start(f32[12,768]{1,0:T(8,128)S(1)} %add.223), channel_id=1, source_target_pairs={{0,1},{1,0},{2,3},{3,2},{4,5},{5,4},{6,7},{7,6},{8,9},{9,8},{10,11... | collective-permute-start | bytes 110600 | tf_op jit(solution)/shard_map/ppermute | solution.py:867
  273.0 9.2 %collective-permute-start.19 = (f32[12,768]{1,0:T(8,128)S(1)}, f32[12,768]{1,0:T(8,128)S(1)}, u32[]{:S(2)}, u32[]{:S(2)}) collective-permute-start(f32[12,768]{1,0:T(8,128)S(1)} %add.224), channel_id=1, source_target_pairs={{0,16},{2,18},{4,20},{6,22},{8,24},{10,26},{12,28},{14,30},{16,0},... | collective-permute-start | bytes 110600 | tf_op jit(solution)/shard_map/ppermute | solution.py:912
  273.1 9.6 %collective-permute-start.20 = (f32[12,768]{1,0:T(8,128)S(1)}, f32[12,768]{1,0:T(8,128)S(1)}, u32[]{:S(2)}, u32[]{:S(2)}) collective-permute-start(f32[12,768]{1,0:T(8,128)S(1)} %add.224), channel_id=1, source_target_pairs={{0,24},{2,26},{4,28},{6,30},{8,16},{10,18},{12,20},{14,22},{16,8},... | collective-permute-start | bytes 110600 | tf_op jit(solution)/shard_map/ppermute | solution.py:912
  275.6 7.1 %collective-permute-start.18 = (f32[12,768]{1,0:T(8,128)S(1)}, f32[12,768]{1,0:T(8,128)S(1)}, u32[]{:S(2)}, u32[]{:S(2)}) collective-permute-start(f32[12,768]{1,0:T(8,128)S(1)} %add.224), channel_id=1, source_target_pairs={{0,8},{2,10},{4,12},{6,14},{8,0},{10,2},{12,4},{14,6},{16,24},{18,... | collective-permute-start | bytes 110600 | tf_op jit(solution)/shard_map/ppermute | solution.py:912
  282.1 17.3 %collective-permute-start.8 = (bf16[512,768]{1,0:T(8,128)(2,1)}, bf16[512,768]{1,0:T(8,128)(2,1)}, u32[]{:S(2)}, u32[]{:S(2)}) collective-permute-start(bf16[512,768]{1,0:T(8,128)(2,1)} %hidden_grad.3), channel_id=1, source_target_pairs={{0,1},{1,0},{2,3},{3,2},{4,5},{5,4},{6,7},{7,6},{8,9},{9,8},{10,11... | collective-permute-start | bytes 2359304 | tf_op jit(solution)/shard_map/ppermute | solution.py:867
  286.8 18.9 %collective-permute-start.10 = (bf16[2,4,3,48,384]{4,3,2,1,0:T(8,128)(2,1)S(1)}, bf16[2,4,3,48,384]{4,3,2,1,0:T(8,128)(2,1)S(1)}, u32[]{:S(2)}, u32[]{:S(2)}) collective-permute-start(bf16[2,4,3,48,384]{4,3,2,1,0:T(8,128)(2,1)S(1)} %get-tuple-element.89), channel_id=1, source_target_pairs={{0,4},{2,6},{4,0},{6,2},{8,12},{10,14},{12,8},{14,10},{16,20},{18,... | collective-permute-start | bytes 2654216 | tf_op jit(solution)/shard_map/ppermute | solution.py:912
  288.4 11.0 %copy-start.1 = (f32[512,768]{1,0:T(8,128)S(1)}, f32[512,768]{1,0:T(8,128)}, u32[]{:S(2)}) copy-start(f32[512,768]{1,0:T(8,128)} %hidden_grad.2) | copy-start | bytes 4718596
  290.2 17.1 %collective-permute-start.24 = (bf16[5,48,384]{2,1,0:T(8,128)(2,1)S(1)}, bf16[5,48,384]{2,1,0:T(8,128)(2,1)S(1)}, u32[]{:S(2)}, u32[]{:S(2)}) collective-permute-start(bf16[5,48,384]{2,1,0:T(8,128)(2,1)S(1)} %get-tuple-element.100), channel_id=1, source_target_pairs={{0,24},{2,26},{4,28},{6,30},{8,16},{10,18},{12,20},{14,22},{16,8},... | collective-permute-start | bytes 552968 | tf_op jit(solution)/shard_map/ppermute | solution.py:912
  292.8 14.6 %collective-permute-start.23 = (bf16[5,48,384]{2,1,0:T(8,128)(2,1)S(1)}, bf16[5,48,384]{2,1,0:T(8,128)(2,1)S(1)}, u32[]{:S(2)}, u32[]{:S(2)}) collective-permute-start(bf16[5,48,384]{2,1,0:T(8,128)(2,1)S(1)} %get-tuple-element.101), channel_id=1, source_target_pairs={{0,16},{2,18},{4,20},{6,22},{8,24},{10,26},{12,28},{14,30},{16,0},... | collective-permute-start | bytes 552968 | tf_op jit(solution)/shard_map/ppermute | solution.py:912
  292.8 14.5 %collective-permute-start.22 = (bf16[5,48,384]{2,1,0:T(8,128)(2,1)S(1)}, bf16[5,48,384]{2,1,0:T(8,128)(2,1)S(1)}, u32[]{:S(2)}, u32[]{:S(2)}) collective-permute-start(bf16[5,48,384]{2,1,0:T(8,128)(2,1)S(1)} %get-tuple-element.99), channel_id=1, source_target_pairs={{0,8},{2,10},{4,12},{6,14},{8,0},{10,2},{12,4},{14,6},{16,24},{18,... | collective-permute-start | bytes 552968 | tf_op jit(solution)/shard_map/ppermute | solution.py:912
  305.8 8.5 %collective-permute-start.11 = (bf16[4,3,48,384]{3,2,1,0:T(8,128)(2,1)S(1)}, bf16[4,3,48,384]{3,2,1,0:T(8,128)(2,1)S(1)}, u32[]{:S(2)}, u32[]{:S(2)}) collective-permute-start(bf16[4,3,48,384]{3,2,1,0:T(8,128)(2,1)S(1)} %fusion.10), channel_id=1, source_target_pairs={{0,1},{1,0},{2,3},{3,2},{4,5},{5,4},{6,7},{7,6},{8,9},{9,8},{10,11... | collective-permute-start | bytes 1327112 | tf_op jit(solution)/shard_map/ppermute | solution.py:867
  314.5 6.7 %collective-permute-start.14 = (bf16[3,48,384]{2,1,0:T(8,128)(2,1)S(1)}, bf16[3,48,384]{2,1,0:T(8,128)(2,1)S(1)}, u32[]{:S(2)}, u32[]{:S(2)}) collective-permute-start(bf16[3,48,384]{2,1,0:T(8,128)(2,1)S(1)} %get-tuple-element.106), channel_id=1, source_target_pairs={{0,24},{2,26},{4,28},{6,30},{8,16},{10,18},{12,20},{14,22},{16,8},... | collective-permute-start | bytes 331784 | tf_op jit(solution)/shard_map/ppermute | solution.py:912
  317.0 6.9 %collective-permute-start.13 = (bf16[3,48,384]{2,1,0:T(8,128)(2,1)S(1)}, bf16[3,48,384]{2,1,0:T(8,128)(2,1)S(1)}, u32[]{:S(2)}, u32[]{:S(2)}) collective-permute-start(bf16[3,48,384]{2,1,0:T(8,128)(2,1)S(1)} %get-tuple-element.107), channel_id=1, source_target_pairs={{0,16},{2,18},{4,20},{6,22},{8,24},{10,26},{12,28},{14,30},{16,0},... | collective-permute-start | bytes 331784 | tf_op jit(solution)/shard_map/ppermute | solution.py:912
  317.6 6.3 %collective-permute-start.12 = (bf16[3,48,384]{2,1,0:T(8,128)(2,1)S(1)}, bf16[3,48,384]{2,1,0:T(8,128)(2,1)S(1)}, u32[]{:S(2)}, u32[]{:S(2)}) collective-permute-start(bf16[3,48,384]{2,1,0:T(8,128)(2,1)S(1)} %get-tuple-element.105), channel_id=1, source_target_pairs={{0,8},{2,10},{4,12},{6,14},{8,0},{10,2},{12,4},{14,6},{16,24},{18,... | collective-permute-start | bytes 331784 | tf_op jit(solution)/shard_map/ppermute | solution.py:912

commit v3 on v0

--- a/solution.py
+++ b/solution.py
@@ -1,8 +1,11 @@
+import functools
 import math
 
 import jax
 import jax.numpy as jnp
 from jax import lax
+from jax.experimental import pallas as pl
+from jax.experimental.pallas import tpu as pltpu
 from jax.sharding import PartitionSpec as P
 
 HEADS = 12
@@ -62,7 +65,7 @@
     return result
 
 
-def local(
+def general(
     hidden,
     segments,
     query_matrix,
@@ -325,9 +328,965 @@
     )
 
 
+BF16 = jnp.bfloat16
+F32 = jnp.float32
+NN = ((1,), (0,))
+NT = ((1,), (1,))
+TN = ((0,), (0,))
+UNIT = 128
+GROUP = 256
+PER_GROUP = GROUP // HEAD
+TILE = 256
+TOKENS = 512
+VMEM_LIMIT = 60 * 2**20
+SCALAR = pl.BlockSpec(memory_space=pltpu.SMEM)
+ANY = pl.BlockSpec(memory_space=pl.ANY)
+
+
+def mm(a, b, dims):
+    return lax.dot_general(a, b, (dims, ((), ())), preferred_element_type=F32)
+
+
+def fixed(shape):
+    return pl.BlockSpec(shape, lambda *_: (0,) * len(shape), pipeline_mode=pl.Buffered(1))
+
+
+def run(
+    kernel,
+    name,
+    grid,
+    operands,
+    in_specs,
+    out_shape,
+    out_specs,
+    scratch=(),
+    scalars=0,
+    held=None,
+    passes=(),
+    after=(),
+    micros=1,
+):
+    held = held or {}
+    out_shape, out_specs = list(out_shape), list(out_specs)
+    n_in, n_out, n_held, n_pass = len(operands), len(out_shape), len(held), len(passes)
+    aliases = {n_in + i: at for i, at in enumerate(held)}
+    aliases |= {n_in + n_held + i: n_out + i for i in range(n_pass)}
+
+    def body(*refs):
+        outs = n_in + n_held + n_pass + len(after)
+        kernel(*refs[:n_in], *refs[outs : outs + n_out], *refs[outs + n_out + n_pass :])
+
+    result = pl.pallas_call(
+        body,
+        grid_spec=pltpu.PrefetchScalarGridSpec(
+            num_scalar_prefetch=scalars,
+            grid=grid,
+            in_specs=list(in_specs) + [ANY] * (n_held + n_pass + len(after)),
+            out_specs=out_specs + [ANY] * n_pass,
+            scratch_shapes=list(scratch),
+        ),
+        out_shape=out_shape + [jax.ShapeDtypeStruct(x.shape, x.dtype) for x in passes],
+        input_output_aliases=aliases,
+        compiler_params=pltpu.CompilerParams(
+            vmem_limit_bytes=VMEM_LIMIT, dimension_semantics=("arbitrary",) * len(grid)
+        ),
+        cost_estimate=pl.CostEstimate(
+            flops=int(micros * 1e7), bytes_accessed=0, transcendentals=0
+        ),
+        name=name,
+    )(*operands, *held.values(), *passes, *after)
+    return result
+
+
+def head_lanes(shape, head):
+    lane = lax.broadcasted_iota(jnp.int32, shape, 1)
+    return (lane >= head * HEAD) & (lane < (head + 1) * HEAD)
+
+
+def lanes(*parts):
+    return jnp.concatenate(parts, axis=1)
+
+
+def column_of(row):
+    return jnp.transpose(jnp.broadcast_to(row.astype(F32), (UNIT, row.shape[1])))[:, 0:1]
+
+
+def same_pair(row, column, rows):
+    return jnp.where(column[rows] == row, 0.0, NEGATIVE)
+
+
+def attention_forward_kernel(
+    here_ref,
+    own_ref,
+    far_ref,
+    wq0_ref,
+    wq1_ref,
+    wk0_ref,
+    wk1_ref,
+    wv0_ref,
+    wv1_ref,
+    bq0_ref,
+    bq1_ref,
+    bv0_ref,
+    bv1_ref,
+    seg_ref,
+    q_ref,
+    k_ref,
+    v_ref,
+    ctx_ref,
+    lse_ref,
+    h_ref,
+    mask_ref,
+    vaug_ref,
+):
+    half = far_ref.shape[0]
+    length = 2 * half
+
+    @pl.when(pl.program_id(0) == 0)
+    def _():
+        segr = seg_ref[...].astype(F32)
+        mask_ref[...] = jnp.where(column_of(segr) == segr, 0.0, NEGATIVE)
+        h_ref[0:half, :] = own_ref[0]
+        h_ref[half:, :] = far_ref[...]
+
+    h = h_ref[...]
+    bias_q = lanes(bq0_ref[...], bq1_ref[...])
+    bias_v = lanes(bv0_ref[...], bv1_ref[...])
+    q_ref[...] = (mm(h, lanes(wq0_ref[...], wq1_ref[...]), NN) + bias_q).astype(BF16)
+    k_ref[...] = mm(h, lanes(wk0_ref[...], wk1_ref[...]), NN).astype(BF16)
+    v = (mm(h, lanes(wv0_ref[...], wv1_ref[...]), NN) + bias_v).astype(BF16)
+    v_ref[...] = v
+    lane = lax.broadcasted_iota(jnp.int32, v.shape, 1)
+    for head in range(PER_GROUP):
+        other = (lane // UNIT) != (head // 2)
+        filler = jnp.where(other, 1.0, 0.0).astype(BF16)
+        vaug_ref[head] = jnp.where(head_lanes(v.shape, head), v, filler)
+
+    def block(i, carry):
+        rows = pl.ds(pl.multiple_of(i * TILE, TILE), TILE)
+        qb = q_ref[rows, :] * BF16(HEAD**-0.5)
+        halves = [None, None]
+        stat_lane = lax.broadcasted_iota(jnp.int32, (TILE, UNIT), 1)
+        stats = jnp.zeros((TILE, UNIT), F32)
+        for head in range(PER_GROUP):
+            qm = jnp.where(head_lanes(qb.shape, head), qb, BF16(0))
+            s = mm(qm, k_ref[...], NT) + mask_ref[rows, :]
+            top = jnp.max(s, axis=1, keepdims=True)
+            e = jnp.exp(s - top).astype(BF16)
+            o = mm(e, vaug_ref[head], NN)
+            t = head // 2
+            total = o[:, (1 - t) * UNIT : (2 - t) * UNIT]
+            part = o[:, t * UNIT : (t + 1) * UNIT] / total
+            halves[t] = part if halves[t] is None else halves[t] + part
+            stats = jnp.where(stat_lane == head, top + jnp.log(total), stats)
+        ctx_ref[0, rows, :] = halves[0].astype(BF16)
+        ctx_ref[1, rows, :] = halves[1].astype(BF16)
+        lse_ref[:, rows] = jnp.transpose(stats)[0:8]
+        return carry
+
+    lax.fori_loop(0, length // TILE, block, 0, unroll=True)
+
+
+def attention_forward(here, hidden, far, wq, wk, wv, bq, bv, seg):
+    half, width = far.shape
+    length = 2 * half
+    groups = width // GROUP
+    left = pl.BlockSpec((width, UNIT), lambda g, h: (0, g))
+    right = pl.BlockSpec((width, UNIT), lambda g, h: (0, groups + g))
+    bias_left = pl.BlockSpec((1, UNIT), lambda g, h: (0, g))
+    bias_right = pl.BlockSpec((1, UNIT), lambda g, h: (0, groups + g))
+    rows = pl.BlockSpec((length, GROUP), lambda g, h: (0, g))
+    wide = jax.ShapeDtypeStruct((length, width), BF16)
+    own = pl.BlockSpec((1, half, width), lambda g, h: (h[0], 0, 0), pipeline_mode=pl.Buffered(1))
+    return run(
+        attention_forward_kernel,
+        "attention_forward",
+        (groups,),
+        (here, hidden, far, wq, wq, wk, wk, wv, wv, bq, bq, bv, bv, seg),
+        [own, fixed((half, width))]
+        + [left, right] * 3
+        + [bias_left, bias_right] * 2
+        + [fixed((1, length))],
+        (
+            wide,
+            wide,
+            wide,
+            jax.ShapeDtypeStruct((2, length, width // 2), BF16),
+            jax.ShapeDtypeStruct((8 * groups, length), F32),
+            wide,
+        ),
+        (
+            rows,
+            rows,
+            rows,
+            pl.BlockSpec((2, length, UNIT), lambda g, h: (0, 0, g)),
+            pl.BlockSpec((8, length), lambda g, h: (g, 0)),
+            pl.BlockSpec((length, width), lambda g, h: (0, 0)),
+        ),
+        [pltpu.VMEM((length, length), F32), pltpu.VMEM((PER_GROUP, length, GROUP), BF16)],
+        scalars=1,
+        micros=16,
+    )
+
+
+def gelu_pair(u):
+    phi = 0.5 + 0.5 * lax.erf(u * 0.7071067811865476)
+    bell = jnp.exp2(u * u * -0.7213475204444817)
+    return (u * phi, phi + u * bell * 0.3989422804014327)
+
+
+def normed(x):
+    centre = x - jnp.mean(x, axis=1, keepdims=True)
+    scale = lax.rsqrt(jnp.mean(centre * centre, axis=1, keepdims=True) + EPSILON)
+    return (centre * scale, scale)
+
+
+def norm_back(u, n, scale):
+    return scale * (u - jnp.mean(u, axis=1, keepdims=True) - n * jnp.mean(u * n, axis=1, keepdims=True))
+
+
+def row_sum(x):
+    return jnp.sum(x, axis=0, keepdims=True)
+
+
+def token_kernel(
+    here_ref,
+    h_ref,
+    ctx_ref,
+    cot_own_ref,
+    cot_far_ref,
+    wo_ref,
+    wi_ref,
+    wp_ref,
+    bi_ref,
+    vec_ref,
+    out_ref,
+    far_ref,
+    first_ref,
+    act_ref,
+    og_ref,
+    ig_ref,
+    fp_ref,
+    ag_ref,
+    dctx_ref,
+    sums_ref,
+    isum_ref,
+    slope_ref,
+):
+    step = pl.program_id(0)
+    steps = pl.num_programs(0)
+
+    @pl.when(step == 0)
+    def _():
+        sums_ref[...] = jnp.zeros_like(sums_ref)
+        isum_ref[...] = jnp.zeros_like(isum_ref)
+
+    ff = wi_ref.shape[1]
+    chunk = 512
+    output_bias, gain1, shift1 = vec_ref[0:1, :], vec_ref[1:2, :], vec_ref[2:3, :]
+    outer_bias, gain2, shift2 = vec_ref[3:4, :], vec_ref[4:5, :], vec_ref[5:6, :]
+    middle = wo_ref.shape[0] // 2
+    near = step < steps // 2
+
+    def part(rows):
+        ctx = lanes(ctx_ref[0, rows, :], ctx_ref[1, rows, :])
+        x = h_ref[rows, :].astype(F32) + mm(ctx, wo_ref[...], NN) + output_bias
+        yield
+        n1, r1 = normed(x)
+        fn = n1 * gain1 + shift1
+        first = fn.astype(BF16)
+        first_ref[rows, :] = first
+        yield
+        for c in range(0, ff, chunk):
+            act, slope = gelu_pair(mm(first, wi_ref[:, c : c + chunk], NN) + bi_ref[:, c : c + chunk])
+            act_ref[rows, c : c + chunk] = act.astype(BF16)
+            slope_ref[rows, c : c + chunk] = slope
+            yield
+        x = fn + mm(act_ref[rows, :], wp_ref[...], NN) + outer_bias
+        yield
+        n2, r2 = normed(x)
+        out = (n2 * gain2 + shift2).astype(BF16)
+
+        @pl.when(near)
+        def _():
+            out_ref[0, rows, :] = out
+
+        @pl.when(jnp.logical_not(near))
+        def _():
+            far_ref[rows, :] = out
+
+        e = jnp.where(near, cot_own_ref[0, rows, :], cot_far_ref[rows, :]).astype(F32)
+        sums_ref[0:1, :] += row_sum(e * n2)
+        sums_ref[1:2, :] += row_sum(e)
+        sp = norm_back(e * gain2, n2, r2)
+        og = sp.astype(BF16)
+        og_ref[rows, :] = og
+        sums_ref[2:3, :] += row_sum(og.astype(F32))
+        yield
+        for c in range(0, ff, chunk):
+            ig = (mm(og, wp_ref[c : c + chunk, :], NT) * slope_ref[rows, c : c + chunk]).astype(BF16)
+            ig_ref[rows, c : c + chunk] = ig
+            isum_ref[:, c : c + chunk] += row_sum(ig.astype(F32))
+            yield
+        d = sp + mm(ig_ref[rows, :], wi_ref[...], NT)
+        yield
+        sums_ref[3:4, :] += row_sum(d * n1)
+        sums_ref[4:5, :] += row_sum(d)
+        fp = norm_back(d * gain1, n1, r1)
+        fp_ref[rows, :] = fp
+        ag = fp.astype(BF16)
+        ag_ref[rows, :] = ag
+        sums_ref[5:6, :] += row_sum(ag.astype(F32))
+        yield
+        dctx = mm(ag, wo_ref[...], NT).astype(BF16)
+        dctx_ref[0, rows, :] = dctx[:, :middle]
+        dctx_ref[1, rows, :] = dctx[:, middle:]
+
+    size = h_ref.shape[0]
+    parts = [part(slice(r, r + TILE)) for r in range(0, size, TILE)]
+    live, waiting = [], list(parts)
+    while waiting or live:
+        if waiting:
+            live.append(waiting.pop(0))
+        live = [p for p in live if next(p, 0) is None]
+
+
+def token_pass(here, h, ctx, cot, cot_far, wo, wi, wp, bi, vec):
+    length, width = h.shape
+    half = length // 2
+    ff = wi.shape[1]
+    steps = length // TOKENS
+    near = steps // 2
+    rows = pl.BlockSpec((TOKENS, width), lambda i, b: (i, 0))
+    split_rows = pl.BlockSpec((2, TOKENS, width // 2), lambda i, b: (0, i, 0))
+    wide_rows = pl.BlockSpec((TOKENS, ff), lambda i, b: (i, 0))
+    own_rows = pl.BlockSpec((1, TOKENS, width), lambda i, b: (b[0], jnp.minimum(i, near - 1), 0))
+    far_rows = pl.BlockSpec((TOKENS, width), lambda i, b: (jnp.maximum(i - near, 0), 0))
+    low = jax.ShapeDtypeStruct((length, width), BF16)
+    low_ff = jax.ShapeDtypeStruct((length, ff), BF16)
+    return run(
+        token_kernel,
+        "token_pass",
+        (steps,),
+        (here, h, ctx, cot, cot_far, wo, wi, wp, bi, vec),
+        [
+            rows,
+            split_rows,
+            own_rows,
+            far_rows,
+            fixed((width, width)),
+            fixed((width, ff)),
+            fixed((ff, width)),
+            fixed((1, ff)),
+            fixed((8, width)),
+        ],
+        (
+            jax.ShapeDtypeStruct((2, half, width), BF16),
+            jax.ShapeDtypeStruct((half, width), BF16),
+            low,
+            low_ff,
+            low,
+            low_ff,
+            jax.ShapeDtypeStruct((length, width), F32),
+            low,
+            jax.ShapeDtypeStruct((2, length, width // 2), BF16),
+            jax.ShapeDtypeStruct((8, width), F32),
+            jax.ShapeDtypeStruct((1, ff), F32),
+        ),
+        (
+            own_rows,
+            far_rows,
+            rows,
+            wide_rows,
+            rows,
+            wide_rows,
+            rows,
+            rows,
+            split_rows,
+            pl.BlockSpec((8, width), lambda i, b: (0, 0)),
+            pl.BlockSpec((1, ff), lambda i, b: (0, 0)),
+        ),
+        [pltpu.VMEM((TOKENS, ff), F32)],
+        scalars=1,
+        micros=23,
+    )
+
+
+def put_pairs(res, core_ref, keep_ref, send_ref, columns, rows, count):
+    even = core_ref[0] == 0
+    for z in range(count):
+        for y in range(2):
+            base = (z * 2 + y) * 2 * rows
+            for x in range(2):
+                zero = lanes(*[res[base : base + rows, c] for c in columns[x]])
+                one = lanes(*[res[base + rows : base + 2 * rows, c] for c in columns[x]])
+                keep_ref[y, x, z, 0] = jnp.where(even, zero, one).astype(BF16)
+                send_ref[y, x, z, 0] = jnp.where(even, one, zero).astype(BF16)
+
+
+HALVES = ((slice(0, 384),), (slice(384, 768),))
+VECTOR_ROWS = 32
+BIAS_ROWS = 16
+
+
+def outer_grad_kernel(core_ref, act_ref, og_ref, sums_ref, isum_ref, keep_ref, send_ref, rows_ref):
+    res = mm(act_ref[...], og_ref[...], TN)
+    middle = res.shape[1] // 2
+    rows = res.shape[0] // 4
+    even = core_ref[0] == 0
+    rows_ref[...] = jnp.zeros_like(rows_ref)
+    at = 0
+    for r in range(6):
+        for x in range(2):
+            rows_ref[at : at + 1, :] = sums_ref[r : r + 1, x * middle : (x + 1) * middle]
+            at += 1
+    for r in range(isum_ref.shape[1] // middle):
+        rows_ref[at : at + 1, :] = isum_ref[:, r * middle : (r + 1) * middle]
+        at += 1
+    extra = rows_ref[...].astype(BF16)
+    for y in range(2):
+        for x in range(2):
+            columns = slice(x * middle, (x + 1) * middle)
+            zero = res[2 * y * rows : (2 * y + 1) * rows, columns]
+            one = res[(2 * y + 1) * rows : (2 * y + 2) * rows, columns]
+            keep_ref[x, y, 0, 0:rows, :] = jnp.where(even, zero, one).astype(BF16)
+            send_ref[x, y, 0, 0:rows, :] = jnp.where(even, one, zero).astype(BF16)
+            keep_ref[x, y, 0, rows:, :] = extra
+            send_ref[x, y, 0, rows:, :] = extra
+
+
+def pair_out(shape, block, index):
+    kind = jax.ShapeDtypeStruct(shape, BF16)
+    spec = pl.BlockSpec(block, index)
+    return ((kind, kind), (spec, spec))
+
+
+def outer_grad_call(core, act, og, sums, isum):
+    length, ff = act.shape
+    width = og.shape[1]
+    shape = (2, 2, 4, ff // 16 + VECTOR_ROWS, width // 2)
+    kinds, specs = pair_out(shape, (2, 2, 1) + shape[3:], lambda z: (0, 0, z, 0, 0))
+    return run(
+        outer_grad_kernel,
+        "outer_grad",
+        (4,),
+        (core, act, og, sums, isum),
+        [
+            SCALAR,
+            pl.BlockSpec((length, ff // 4), lambda z: (0, z)),
+            fixed((length, width)),
+            fixed(sums.shape),
+            fixed(isum.shape),
+        ],
+        kinds,
+        specs,
+        [pltpu.VMEM((VECTOR_ROWS, width // 2), F32)],
+        micros=4.5,
+    )
+
+
+def inner_grad_kernel(
+    core_ref, first_ref, low_ref, high_ref, ctx_ref, ag_ref, keep_ref, send_ref
+):
+    step = pl.program_id(0)
+    rows = keep_ref.shape[4]
+
+    @pl.when(step < 4)
+    def _():
+        res = mm(first_ref[...], lanes(low_ref[...], high_ref[...]), TN)
+        put_pairs(res, core_ref, keep_ref, send_ref, HALVES, rows, 4)
+
+    @pl.when(step == 4)
+    def _():
+        res = mm(lanes(ctx_ref[0], ctx_ref[1]), ag_ref[...], TN)
+        put_pairs(res, core_ref, keep_ref, send_ref, HALVES, rows, 4)
+
+
+def inner_grad_call(core, first, ig, ctx, ag, passes):
+    length, width = first.shape
+    shape = (2, 2, 4, 5, width // 16, width // 2)
+    kinds, specs = pair_out(shape, shape[:3] + (1,) + shape[4:], lambda s: (0, 0, 0, s, 0, 0))
+    return run(
+        inner_grad_kernel,
+        "inner_grad",
+        (5,),
+        (core, first, ig, ig, ctx, ag),
+        [
+            SCALAR,
+            fixed((length, width)),
+            pl.BlockSpec((length, width // 2), lambda s: (0, jnp.minimum(s, 3))),
+            pl.BlockSpec((length, width // 2), lambda s: (0, 4 + jnp.minimum(s, 3))),
+            fixed((2, length, width // 2)),
+            fixed((length, width)),
+        ],
+        kinds,
+        specs,
+        passes=passes,
+        micros=6,
+    )
+
+
+def projection_grad_kernel(with_sums, core_ref, h_ref, d_ref, sums_ref, keep_ref, send_ref):
+    step = pl.program_id(0)
+    res = mm(h_ref[...], d_ref[0], TN)
+    rows = res.shape[0] // 16
+    units = res.shape[1] // UNIT
+    columns = [[slice(u * UNIT, (u + 1) * UNIT) for u in range(x, units, 2)] for x in range(2)]
+    even = core_ref[0] == 0
+    for s in range(3):
+
+        @pl.when(step == s)
+        def _(s=s):
+            place = slice(s * rows, (s + 1) * rows)
+            for z in range(4):
+                for y in range(2):
+                    base = (z * 2 + y) * 2 * rows
+                    for x in range(2):
+                        zero = lanes(*[res[base : base + rows, c] for c in columns[x]])
+                        one = lanes(*[res[base + rows : base + 2 * rows, c] for c in columns[x]])
+                        keep_ref[y, x, z, place, :] = jnp.where(even, zero, one).astype(BF16)
+                        send_ref[y, x, z, place, :] = jnp.where(even, one, zero).astype(BF16)
+
+    @pl.when(step == 0)
+    def _():
+        extra = jnp.zeros((BIAS_ROWS, keep_ref.shape[4]), F32)
+        if with_sums:
+            at = lax.broadcasted_iota(jnp.int32, extra.shape, 0)
+            count = sums_ref.shape[1] // UNIT
+            for r in range(2):
+                for u in range(count):
+                    part = sums_ref[r : r + 1, u * UNIT : (u + 1) * UNIT]
+                    extra = jnp.where(at == r * count + u, part, extra)
+        for z in range(4):
+            for y in range(2):
+                for x in range(2):
+                    keep_ref[y, x, z, 3 * rows :, :] = extra.astype(BF16)
+                    send_ref[y, x, z, 3 * rows :, :] = extra.astype(BF16)
+
+
+def projection_grad_call(core, h, dqkv, sums, at, span, with_sums, passes, after):
+    length, width = h.shape
+    shape = (2, 2, 4, 3 * width // 16 + BIAS_ROWS, span // 2)
+    kinds, specs = pair_out(shape, shape, lambda s: (0, 0, 0, 0, 0))
+    return run(
+        functools.partial(projection_grad_kernel, with_sums),
+        "projection_grad",
+        (3,),
+        (core, h, dqkv, sums),
+        [
+            SCALAR,
+            fixed((length, width)),
+            pl.BlockSpec((1, length, span), lambda s: (s, 0, at)),
+            fixed(sums.shape),
+        ],
+        kinds,
+        specs,
+        passes=passes,
+        after=after,
+        micros=2.5,
+    )
+
+
+def attention_backward_kernel(
+    q_ref,
+    k_ref,
+    v_ref,
+    dctx_pair_ref,
+    ctx_pair_ref,
+    lse_ref,
+    seg_ref,
+    grads_ref,
+    sums_ref,
+    delta_ref,
+    total_ref,
+    kt_ref,
+    dctx_ref,
+    segc_ref,
+):
+    length = q_ref.shape[0]
+    dctx_ref[...] = lanes(dctx_pair_ref[0], dctx_pair_ref[1])
+    ctx = lanes(ctx_pair_ref[0], ctx_pair_ref[1])
+    segr = seg_ref[...].astype(F32)
+    segc_ref[...] = column_of(segr)
+    prod = dctx_ref[...].astype(F32) * ctx.astype(F32)
+    high = prod.astype(BF16)
+    rest = (prod - high.astype(F32)).astype(BF16)
+    lane = lax.broadcasted_iota(jnp.int32, (8, GROUP), 1)
+    head_of = lax.broadcasted_iota(jnp.int32, (8, GROUP), 0)
+    chooser = jnp.where(lane // HEAD == head_of, 1.0, 0.0).astype(BF16)
+    delta_ref[...] = mm(chooser, high, NT) + mm(chooser, rest, NT)
+    total_ref[...] = jnp.zeros_like(total_ref)
+    kt_ref[...] = jnp.transpose(k_ref[...])
+
+    def block(j, carry):
+        rows = pl.ds(pl.multiple_of(j * TILE, TILE), TILE)
+        kb = k_ref[rows, :]
+        vb = v_ref[rows, :]
+        mask = jnp.where(segc_ref[rows, :] == segr, 0.0, NEGATIVE)
+        dk = jnp.zeros((TILE, GROUP), F32)
+        dv = jnp.zeros((TILE, GROUP), F32)
+        for head in range(PER_GROUP):
+            mine = head_lanes((TILE, GROUP), head)
+            km = jnp.where(mine, kb, BF16(0)) * BF16(HEAD**-0.5)
+            vm = jnp.where(mine, vb, BF16(0))
+            s = mm(km, q_ref[...], NT) + mask
+            p = jnp.exp(s - lse_ref[head : head + 1, :])
+            dp = mm(vm, dctx_ref[...], NT)
+            ds = (p * (dp - delta_ref[head : head + 1, :])).astype(BF16)
+            dv = jnp.where(mine, mm(p.astype(BF16), dctx_ref[...], NN), dv)
+            dk = jnp.where(mine, mm(ds, q_ref[...], NN), dk)
+            columns = slice(head * HEAD, (head + 1) * HEAD)
+            total_ref[columns, :] += mm(kt_ref[columns, rows], ds, NN)
+        dkb = (dk * HEAD**-0.5).astype(BF16)
+        dvb = dv.astype(BF16)
+        grads_ref[1, rows, :] = dkb
+        grads_ref[2, rows, :] = dvb
+        return carry + row_sum(dvb.astype(F32))
+
+    dv_sum = lax.fori_loop(0, length // TILE, block, jnp.zeros((1, GROUP), F32), unroll=True)
+    dq = jnp.transpose(total_ref[...] * HEAD**-0.5).astype(BF16)
+    grads_ref[0] = dq
+    sums_ref[...] = jnp.zeros_like(sums_ref)
+    sums_ref[0:1, :] = row_sum(dq.astype(F32))
+    sums_ref[1:2, :] = dv_sum
+
+
+def attention_backward(g, q, k, v, dctx, ctx, lse, seg, held, passes, after):
+    length, width = q.shape
+    rows = pl.BlockSpec((length, GROUP), lambda i: (0, g))
+    pair_rows = pl.BlockSpec((2, length, UNIT), lambda i: (0, 0, g))
+    return run(
+        attention_backward_kernel,
+        "attention_backward",
+        (1,),
+        (q, k, v, dctx, ctx, lse, seg),
+        [
+            rows,
+            rows,
+            rows,
+            pair_rows,
+            pair_rows,
+            pl.BlockSpec((8, length), lambda i: (g, 0)),
+            fixed((1, length)),
+        ],
+        (jax.ShapeDtypeStruct((3, length, width), BF16), jax.ShapeDtypeStruct((8, width), F32)),
+        (
+            pl.BlockSpec((3, length, GROUP), lambda i: (0, 0, g)),
+            pl.BlockSpec((8, GROUP), lambda i: (0, g)),
+        ),
+        [
+            pltpu.VMEM((8, length), F32),
+            pltpu.VMEM((GROUP, length), F32),
+            pltpu.VMEM((GROUP, length), BF16),
+            pltpu.VMEM((length, GROUP), BF16),
+            pltpu.VMEM((length, 1), F32),
+        ],
+        held=dict(enumerate(held)),
+        passes=passes,
+        after=after,
+        micros=8,
+    )
+
+
+def hidden_total(fp_ref, d_ref, wq_ref, wk_ref, wv_ref):
+    total = fp_ref[...]
+    for at, w_ref in enumerate((wq_ref, wk_ref, wv_ref)):
+        units = d_ref.shape[2] // UNIT
+        order = list(range(0, units, 2)) + list(range(1, units, 2))
+        d = lanes(*[d_ref[at, :, u * UNIT : (u + 1) * UNIT] for u in order])
+        total = total + mm(d, w_ref[...], NT)
+    return total
+
+
+def hidden_away_kernel(fp_ref, d_ref, wq_ref, wk_ref, wv_ref, out_ref):
+    out_ref[...] = hidden_total(fp_ref, d_ref, wq_ref, wk_ref, wv_ref).astype(BF16)
+
+
+def hidden_home_kernel(
+    here_ref, fp_ref, d_ref, wq_ref, wk_ref, wv_ref, came_ref, out_ref, layer_ref
+):
+    out_ref[0] = hidden_total(fp_ref, d_ref, wq_ref, wk_ref, wv_ref)
+    layer_ref[0] = came_ref[...]
+
+
+def hidden_away(fp, dqkv, wq, wk, wv, passes, after):
+    length, width = fp.shape
+    half = length // 2
+    steps = half // TILE
+    return run(
+        hidden_away_kernel,
+        "hidden_away",
+        (steps,),
+        (fp, dqkv, wq, wk, wv),
+        [
+            pl.BlockSpec((TILE, width), lambda i: (i + steps, 0)),
+            pl.BlockSpec((3, TILE, width), lambda i: (0, i + steps, 0)),
+        ]
+        + [fixed((width, width))] * 3,
+        (jax.ShapeDtypeStruct((half, width), BF16),),
+        (pl.BlockSpec((TILE, width), lambda i: (i, 0)),),
+        passes=passes,
+        after=after,
+        micros=3,
+    )
+
+
+def hidden_home(here, fp, dqkv, wq, wk, wv, came, layer, passes, after):
+    length, width = fp.shape
+    half = length // 2
+    steps = half // TILE
+    return run(
+        hidden_home_kernel,
+        "hidden_home",
+        (steps,),
+        (here, fp, dqkv, wq, wk, wv, came),
+        [
+            pl.BlockSpec((TILE, width), lambda i, b: (i, 0)),
+            pl.BlockSpec((3, TILE, width), lambda i, b: (0, i, 0)),
+        ]
+        + [fixed((width, width))] * 3
+        + [pl.BlockSpec((TILE, width), lambda i, b: (i, 0))],
+        (
+            jax.ShapeDtypeStruct((2, half, width), F32),
+            jax.ShapeDtypeStruct((2, half, width), BF16),
+        ),
+        (
+            pl.BlockSpec((1, TILE, width), lambda i, b: (b[0], i, 0)),
+            pl.BlockSpec((1, TILE, width), lambda i, b: (1 - b[0], i, 0)),
+        ),
+        scalars=1,
+        held={1: layer},
+        passes=passes,
+        after=after,
+        micros=3,
+    )
+
+
+def place_kernel(here_ref, came_ref, out_ref):
+    out_ref[0] = came_ref[...].astype(F32)
+
+
+def place_far(here, came, grad, passes):
+    half, width = came.shape
+    return run(
+        place_kernel,
+        "place_far",
+        (2,),
+        (here, came),
+        [pl.BlockSpec((half // 2, width), lambda i, b: (i, 0))],
+        (jax.ShapeDtypeStruct((2, half, width), F32),),
+        (pl.BlockSpec((1, half // 2, width), lambda i, b: (1 - b[0], i, 0)),),
+        scalars=1,
+        held={0: grad},
+        passes=passes,
+        micros=1,
+    )
+
+
+def fast(
+    hidden,
+    segments,
+    query_matrix,
+    query_bias,
+    key_matrix,
+    value_matrix,
+    value_bias,
+    output_matrix,
+    output_bias,
+    first_gain,
+    first_shift,
+    inner_matrix,
+    inner_bias,
+    outer_matrix,
+    outer_bias,
+    second_gain,
+    second_shift,
+    cotangent,
+):
+    here = lax.axis_index("blk")
+    place = lax.axis_index("seq")
+    core, y_at, z_at = place % 2, (place // 2) % 2, place // 4
+    here_id = here.astype(jnp.int32)[None]
+    core_id = core.astype(jnp.int32)[None]
+    half, width = hidden.shape[1:]
+
+    def pick(x, *at):
+        start = at + (0,) * (x.ndim - len(at))
+        size = (1,) * len(at) + x.shape[len(at) :]
+        return lax.dynamic_slice(x, start, size).reshape(x.shape[len(at) :])
+
+    def trade(x):
+        return lax.ppermute(x, "blk", [(0, 1), (1, 0)])
+
+    def seq_swap(x, bit):
+        return lax.ppermute(x, "seq", [(i, i ^ bit) for i in range(16)])
+
+    def row(x):
+        return x.astype(F32)[None, :]
+
+    def rounded(x):
+        return lax.reduce_precision(x, 8, 7)
+
+    def sum_0(state, *at):
+        return rounded(pick(state[0], *at).astype(F32) + pick(state[1], *at).astype(F32))
+
+    def sum_1(state, mine, *at):
+        return rounded(sum_0(state, mine, *at) + pick(state[2], *at).astype(F32))
+
+    def sum_2(state, mine, then, *at):
+        return rounded(sum_1(state, mine, then, *at) + pick(state[3], *at).astype(F32))
+
+    def send_z(parts):
+        return [seq_swap(x, 4 * d) for d, x in zip((1, 2, 3), parts)]
+
+    def add_z(total, parts):
+        return (total + parts[0].astype(F32)) + (parts[1].astype(F32) + parts[2].astype(F32))
+
+    seg = jnp.concatenate([pick(segments, here), trade(pick(segments, 1 - here))])[None, :]
+    far = trade(pick(hidden, 1 - here))
+    cot_far = trade(pick(cotangent, 1 - here + jnp.minimum(seg[0, -1], 0)))
+    q, k, v, ctx, lse, h = attention_forward(
+        here_id,
+        hidden,
+        far,
+        query_matrix,
+        key_matrix,
+        value_matrix,
+        row(query_bias),
+        row(value_bias),
+        seg,
+    )
+    empty = jnp.zeros((2, width), F32)
+    vec = jnp.concatenate(
+        [
+            row(output_bias),
+            row(first_gain),
+            row(first_shift),
+            row(outer_bias),
+            row(second_gain),
+            row(second_shift),
+            empty,
+        ],
+        axis=0,
+    )
+    out, out_far, first, act, og, ig, fp, ag, dctx, sums, isum = token_pass(
+        here_id, h, ctx, cotangent, cot_far, output_matrix, inner_matrix, outer_matrix, row(inner_bias), vec
+    )
+    out_came = trade(out_far)
+    x_mine, x_away, y_mine, y_away = here, 1 - here, y_at, 1 - y_at
+    a_keep, a_send = outer_grad_call(core_id, act, og, sums, isum)
+    a0 = seq_swap(a_send, 1)
+    b_keep, b_send, a_keep = inner_grad_call(core_id, first, ig, ctx, ag, (a_keep,))
+    b0 = seq_swap(b_send, 1)
+    a = (a_keep, a0)
+    a_away = sum_0(a, x_away).astype(BF16)
+    a1 = trade(a_away)
+    b = (b_keep, b0)
+    b_away = sum_0(b, y_away).astype(BF16)
+    b1 = seq_swap(b_away, 2)
+    bwd = (q, k, v, dctx, ctx, lse, seg)
+    held = attention_backward(0, *bwd, (), (), (a_away, b_away))
+    *held, a_keep, b_keep = attention_backward(1, *bwd, held, (a_keep, b_keep), ())
+    a = (a_keep, a0, a1)
+    a_away = sum_1(a, x_mine, y_away).astype(BF16)
+    a2 = seq_swap(a_away, 2)
+    c_keep, c_send, b_keep = projection_grad_call(
+        core_id, h, held[0], sums, 0, 2 * GROUP, False, (b_keep,), (a_away,)
+    )
+    c0 = seq_swap(c_send, 1)
+    b = (b_keep, b0, b1)
+    b_away = sum_1(b, y_mine, x_away).astype(BF16)
+    b2 = trade(b_away)
+    dqkv, sums2, a_keep, b_keep, c_keep = attention_backward(
+        2, *bwd, held, (a_keep, b_keep, c_keep), (c_send, b_away)
+    )
+    c = (c_keep, c0)
+    c_away = sum_0(c, y_away).astype(BF16)
+    c1 = seq_swap(c_away, 2)
+    d_keep, d_send, a_keep, b_keep, out_came = projection_grad_call(
+        core_id, h, dqkv, sums2, 2, GROUP, True, (a_keep, b_keep, out_came), (c_away,)
+    )
+    d0 = seq_swap(d_send, 1)
+    a = (a_keep, a0, a1, a2)
+    b = (b_keep, b0, b1, b2)
+
+    def both(z):
+        a_part = sum_2(a, x_mine, y_mine, z)
+        b_part = sum_2(b, y_mine, x_mine, z)
+        return jnp.concatenate([a_part, b_part.reshape(-1, width // 2)], axis=0)
+
+    parts = [both(z_at ^ e).astype(BF16) for e in (1, 2, 3)]
+    ab3 = send_z(parts)
+    args = (fp, dqkv, query_matrix, key_matrix, value_matrix)
+    far_grad, c_keep, d_keep = hidden_away(*args, (c_keep, d_keep), (parts[0],))
+    came = trade(far_grad)
+    d = (d_keep, d0)
+    d_away = sum_0(d, y_away).astype(BF16)
+    d1 = seq_swap(d_away, 2)
+    hidden_grad, layer_out, a_keep, b_keep, c_keep, d_keep = hidden_home(
+        here_id, *args, out_came, out, (a_keep, b_keep, c_keep, d_keep), (d_away,)
+    )
+    c = (c_keep, c0, c1)
+    d = (d_keep, d0, d1)
+
+    def late_1(*at):
+        return lanes_of(sum_1(c, y_mine, *at), sum_1(d, y_mine, *at))
+
+    def lanes_of(*parts):
+        return jnp.concatenate(parts, axis=-1)
+
+    e2 = trade(late_1(x_away).astype(BF16))
+
+    def late_2(z):
+        return rounded(late_1(x_mine, z) + pick(e2, z).astype(F32))
+
+    e3 = send_z([late_2(z_at ^ e).astype(BF16) for e in (1, 2, 3)])
+    hidden_grad, a_keep, b_keep = place_far(here_id, came, hidden_grad, (a_keep, b_keep))
+    a = (a_keep, a0, a1, a2)
+    b = (b_keep, b0, b1, b2)
+    early = add_z(both(z_at), ab3)
+    late = add_z(late_2(z_at), e3)
+    rows = width // 16
+    outer_rows = 4 * rows
+    outer_grad = early[:outer_rows]
+    vectors = early[outer_rows : outer_rows + VECTOR_ROWS].reshape(-1, width)
+    inner_all = early[outer_rows + VECTOR_ROWS :].reshape(5, rows, width // 2)
+    output_grad = inner_all[4]
+    inner_grad = jnp.transpose(inner_all[:4], (1, 0, 2)).reshape(rows, -1)
+    units = width // UNIT
+    biases = late[3 * rows :, 2 * UNIT :][: 2 * units].reshape(2, units // 2, 2, UNIT)
+    biases = jnp.transpose(biases, (0, 2, 1, 3)).reshape(2, width)
+    return (
+        layer_out,
+        hidden_grad,
+        late[:rows],
+        biases[0],
+        late[rows : 2 * rows],
+        late[2 * rows : 3 * rows],
+        biases[1],
+        output_grad,
+        vectors[5],
+        vectors[3],
+        vectors[4],
+        inner_grad,
+        vectors[6:10].reshape(-1),
+        outer_grad,
+        vectors[2],
+        vectors[0],
+        vectors[1],
+    )
+
+
+def choose(sizes, *args):
+    seq_count, row_count, width = args[0].shape
+    whole_here = sizes[1] == 2 and seq_count == 2 and row_count % TILE == 0 and width == 3 * GROUP
+    return fast(*args) if whole_here and sizes[0] == 16 else general(*args)
+
+
 def solution(mesh):
+    sizes = (mesh.shape["seq"], mesh.shape["blk"])
     return jax.shard_map(
-        local,
+        functools.partial(choose, sizes),
         mesh=mesh,
         in_specs=(
             P("seq", "blk", None),

time: 977 us -> 290 us (0.30)
  waiting for transfers between devices: 443 us -> 40.5 us
  matrix products: 308 us -> 0 us
  Pallas kernels: 0 us -> 167 us
  blocking collectives: 57.2 us -> 0 us
  other arithmetic: 82.4 us -> 30.2 us
  local copies, waits for them, and re-layouts: 59.8 us -> 24 us
  starting transfers between devices: 0.91 us -> 24.1 us
  between operations: 15.2 us -> 1.99 us
    reduce_scatter x9 -> x0, waiting for transfers between devices: 330 us -> none  [the longest x1 116 us: local(): lax.psum_scatter(outer_weight_grad, 'seq', scatter_dimension=0, tiled=True)]
    dot_general x32 -> x0, matrix products: 308 us -> none  [the longest x6 72.4 us: block_scores(): jnp.einsum('sqhd,skhd->shqk', query_block, key_block, preferred_element_t...]
    pallas_call x0 -> x12, Pallas kernels: none -> 167 us  [run(): pl.pallas_call(body, grid_spec=pltpu.PrefetchScalarGridSpec(num_scalar_pr...]
    unnamed x19 -> x0, waiting for transfers between devices: 88.3 us -> none
    psum x1 -> x0, blocking collectives: 42.1 us -> none  [local(): lax.psum((query_bias_grad, value_bias_grad, output_bias_grad, first_gain_...]
    reduce_sum x11 -> x0, other arithmetic: 41.5 us -> none  [the longest x2 22.9 us: stats_step(): jnp.sum(weights, axis=-1)]
    ppermute x0 -> x22, waiting for transfers between devices: none -> 40.5 us  [the longest x8 33.5 us: trade(): return lax.ppermute(x, 'blk', [(0, 1), (1, 0)])]
    all_gather x4 -> x0, waiting for transfers between devices: 24.9 us -> none  [the longest x1 24.9 us: local(): lax.all_gather(key_proj, 'blk', axis=1, tiled=True)]
  transfers between devices with their start and end apart: 16 -> 22, of which waited for: 8 -> 9; matrix products, arithmetic and copies ran while one was open for 45% -> 16% of each run, Pallas kernels for 0% -> 38%
where the time goes in v3:
time: 290 us; the launch traced here: 288 us
  Pallas kernels  167 us (58%)
  waiting for transfers between devices  40.5 us (14%)
  other arithmetic  30.2 us (10%)
  starting transfers between devices  24.1 us (8%)
  local copies, waits for them, and re-layouts  24 us (8%)
    pallas_call x12, Pallas kernels, run(): pl.pallas_call(body, grid_spec=pltpu.PrefetchScalarGridSpec(num_scalar_pr...  167 us
    ppermute x8, waiting for transfers between devices, trade(): return lax.ppermute(x, 'blk', [(0, 1), (1, 0)])  33.5 us
    ppermute x14, starting transfers between devices, seq_swap(): return lax.ppermute(x, 'seq', [(i, i ^ bit) for i in range(16)])  13.8 us
    ppermute x8, starting transfers between devices, trade(): return lax.ppermute(x, 'blk', [(0, 1), (1, 0)])  10.2 us
    ppermute x14, waiting for transfers between devices, seq_swap(): return lax.ppermute(x, 'seq', [(i, i ^ bit) for i in range(16)])  7.03 us
    reduce_precision x6, other arithmetic, rounded(): return lax.reduce_precision(x, 8, 7)  6.45 us
    unnamed x62, local copies, waits for them, and re-layouts  6.34 us
  transfers between devices with their start and end apart: 22, of which 9 were waited for; matrix products, arithmetic and copies ran while one was open for 16% of the time, Pallas kernels for 38%

profile of v3, /device:TPU:0, one launch (start us, length us, event | category | flops | bytes accessed | tf_op | source)
XLA Modules:
  0.0 288.1 jit_solution(6395945281518763236)
XLA Ops:
  1.6 3.0 %collective-permute-start.1 = (s32[512]{0:T(512)S(1)}, s32[512]{0:T(512)S(1)}, u32[]{:S(2)}, u32[]{:S(2)}) collective-permute-start(s32[512]{0:T(512)S(1)} %bitcast.173), channel_id=1, source_target_pairs={{0,1},{1,0},{2,3},{3,2},{4,5},{5,4},{6,7},{7,6},{8,9},{9,8},{10,11... | collective-permute-start | bytes 6152 | tf_op jit(solution)/shard_map/ppermute | solution.py:1119
  4.6 1.2 dynamic-slice_bitcast_fusion.1
  8.4 2.0 collective-permute-start.2
  12.9 13.4 %collective-permute-done.refs_2_ = bf16[512,768]{1,0:T(8,128)(2,1)S(1)} collective-permute-done((bf16[512,768]{1,0:T(8,128)(2,1)S(1)}, bf16[512,768]{1,0:T(8,128)(2,1)S(1)}, u32[]{:S(2)}, u32[]{:S(2)}) %collective-permute-start) | collective-permute-done | bytes 786464 | tf_op jit(solution)/shard_map/ppermute | solution.py:1119
  27.2 26.3 %attention_forward.1 = (bf16[1024,768]{1,0:T(8,128)(2,1)}, bf16[1024,768]{1,0:T(8,128)(2,1)}, bf16[1024,768]{1,0:T(8,128)(2,1)}, bf16[2,1024,384]{2,1,0:T(8,128)...) custom-call(s32[1]{0:T(128)} %bitcast.refs_0_, bf16[2,512,768]{2,1,0:T(8,128)(2,1)} %refs_1_.1, ...), custom_call_target="tpu_custom_call" | custom-call | flops 160000000 | tf_op jit(solution)/shard_map/attention_forward/pallas_call | solution.py:379
  54.5 47.9 %token_pass.1 = (bf16[2,512,768]{2,1,0:T(8,128)(2,1)}, bf16[512,768]{1,0:T(8,128)(2,1)}, bf16[1024,768]{1,0:T(8,128)(2,1)}, bf16[1024,3072]{1,0:T(8,128)(2,1)}, ...) custom-call(s32[1]{0:T(128)} %bitcast.refs_0_, ...), custom_call_target="tpu_custom_call" | custom-call | flops 230000000 | tf_op jit(solution)/shard_map/token_pass/pallas_call | solution.py:379
  102.3 9.4 %outer_grad.1 = (bf16[2,2,4,224,384]{4,3,2,1,0:T(8,128)(2,1)}, bf16[2,2,4,224,384]{4,3,2,1,0:T(8,128)(2,1)}) custom-call(s32[1]{0:T(128)} %bitcast.8.refs_0_, bf16[1024,3072]{1,0:T(8,128)(2,1)} %get-tuple-element.81.refs_1_, bf16[1024,768]{1,0:T(8,128)(2,1)} %get-tuple-element.82.refs_2_, f32[8,768]{1,0:T(8,128)} %get-tuple-element.83.refs_3_, ...), custom_call_target="tpu_custom_call" | custom-call | flops 45000000 | tf_op jit(solution)/shard_map/outer_grad/pallas_call | solution.py:379
  111.8 11.7 %inner_grad.1 = (bf16[2,2,4,5,48,384]{5,4,3,2,1,0:T(8,128)(2,1)}, bf16[2,2,4,5,48,384]{5,4,3,2,1,0:T(8,128)(2,1)}, bf16[2,2,4,224,384]{4,3,2,1,0:T(8,128)(2,1)}) custom-call(s32[1]{0:T(128)} %bitcast.8.refs_0_, bf16[1024,768]{1,0:T(8,128)(2,1)} %get-tuple-element.78.refs_1_, ...), custom_call_target="tpu_custom_call", output_to_operand_aliasing={{2}: (6, {})} | custom-call | flops 60000000 | tf_op jit(solution)/shard_map/inner_grad/pallas_call | solution.py:379
  123.9 1.5 copy-done.7
  125.4 3.3 %fusion.3.refs_7_ = bf16[2,4,224,384]{3,2,1,0:T(8,128)(2,1)} fusion(bf16[2,2,4,224,384]{4,3,2,1,0:T(8,128)(2,1)} %copy-done.7, s32[]{:T(128)S(6)} %select_n.36, bf16[2,2,4,224,384]{4,3,2,1,0:T(8,128)(2,1)} %get-tuple-element.86.refs_9_), kind=kLoop, calls=%fused_computation.6 | loop fusion | flops 3440640 | bytes 4128772 | tf_op jit(solution)/shard_map/convert_element_type | solution.py:1182
  129.3 2.8 fusion.refs_8_
  132.1 1.5 collective-permute-start.6
  133.7 15.2 %attention_backward.3 = (bf16[3,1024,768]{2,1,0:T(8,128)(2,1)}, f32[8,768]{1,0:T(8,128)}) custom-call(bf16[1024,768]{1,0:T(8,128)(2,1)} %get-tuple-element.73.refs_0_, bf16[1024,768]{1,0:T(8,128)(2,1)} %get-tuple-element.74.refs_1_, bf16[1024,768]{1,0:T(8,128)(2,1)} %get-tuple-element.75.refs_2_, bf16[2,1024,384]{2,1,0:T(8,128)(2,1)} %get-tuple-element.76.refs_3_, ...), custom_call_target="tpu_custom_call" | custom-call | flops 80000000 | tf_op jit(solution)/shard_map/attention_backward/pallas_call | solution.py:379
  148.9 15.7 %attention_backward.4 = (bf16[3,1024,768]{2,1,0:T(8,128)(2,1)}, f32[8,768]{1,0:T(8,128)}, bf16[2,2,4,224,384]{4,3,2,1,0:T(8,128)(2,1)}, bf16[2,2,4,5,48,384]{5,4,3,2,1,0:T(8,128)(2,1)}) custom-call(bf16[1024,768]{1,0:T(8,128)(2,1)} %get-tuple-element.73.refs_0_, ...), custom_call_target="tpu_custom_call", output_to_operand_aliasing={{0}: (7, {}), {1}: (8, {}), {2}: (9, {}), {3}: (10, {})} | custom-call | flops 80000000 | tf_op jit(solution)/shard_map/attention_backward/pallas_call | solution.py:379
  164.6 2.7 fusion.5.refs_5_
  167.2 6.8 %projection_grad.2 = (bf16[2,2,4,160,256]{4,3,2,1,0:T(8,128)(2,1)}, bf16[2,2,4,160,256]{4,3,2,1,0:T(8,128)(2,1)}, bf16[2,2,4,5,48,384]{5,4,3,2,1,0:T(8,128)(2,1)}) custom-call(s32[1]{0:T(128)} %bitcast.8.refs_0_, bf16[1024,768]{1,0:T(8,128)(2,1)} %get-tuple-element.70.refs_1_, ...), custom_call_target="tpu_custom_call", output_to_operand_aliasing={{2}: (4, {})} | custom-call | flops 25000000 | tf_op jit(solution)/shard_map/projection_grad/pallas_call | solution.py:379
  174.2 1.1 copy-done.10
  175.3 1.9 fusion.2.refs_13_
  177.2 1.5 collective-permute-start.10
  179.8 1.9 constant_dynamic-slice_fusion.4
  181.8 15.2 %attention_backward.5 = (bf16[3,1024,768]{2,1,0:T(8,128)(2,1)}, f32[8,768]{1,0:T(8,128)}, bf16[2,2,4,224,384]{4,3,2,1,0:T(8,128)(2,1)}, bf16[2,2,4,5,48,384]{5,4...) custom-call(bf16[1024,768]{1,0:T(8,128)(2,1)} %get-tuple-element.73., ...), custom_call_target="tpu_custom_call", output_to_operand_aliasing={{0}: (7, {}), {1}: (8, {}), {2}: (9, {}), {3}: (10, {}), {4... | custom-call | flops 80000000 | tf_op jit(solution)/shard_map/attention_backward/pallas_call | solution.py:379
  197.0 2.1 constant_dynamic-slice_fusion.7
  199.1 1.2 fusion.7.refs_7_
  200.3 1.8 collective-permute-start.13
  202.1 10.8 %collective-permute-done.7.refs_6_ = bf16[512,768]{1,0:T(8,128)(2,1)S(1)} collective-permute-done((bf16[512,768]{1,0:T(8,128)(2,1)}, bf16[512,768]{1,0:T(8,128)(2,1)S(1)}, u32[]{:S(2)}, u32[]{:S(2)}) %collective-permute-start.7) | collective-permute-done | bytes 786464 | tf_op jit(solution)/shard_map/ppermute | solution.py:1119
  213.8 5.1 %projection_grad.3 = (bf16[2,2,4,160,128]{4,3,2,1,0:T(8,128)(2,1)}, bf16[2,2,4,160,128]{4,3,2,1,0:T(8,128)(2,1)}, bf16[2,2,4,224,384]{4,3,2,1,0:T(8,128)(2,1)}, ...) custom-call(s32[1]{0:T(128)} %bitcast.8.refs_0_, ...), custom_call_target="tpu_custom_call", output_to_operand_aliasing={{2}: (4, {}), {3}: (5, {}), {4}: (6, {})} | custom-call | flops 25000000 | tf_op jit(solution)/shard_map/projection_grad/pallas_call | solution.py:379
  219.0 1.5 add_reduce-precision_fusion.1
  220.6 2.6 fusion.25
  223.2 1.6 collective-permute-start.19
  224.9 5.7 %hidden_away.1 = (bf16[512,768]{1,0:T(8,128)(2,1)}, bf16[2,2,4,160,256]{4,3,2,1,0:T(8,128)(2,1)}, bf16[2,2,4,160,128]{4,3,2,1,0:T(8,128)(2,1)}) custom-call(f32[1024,768]{1,0:T(8,128)} %get-tuple-element.72.refs_0_.refs_1_, bf16[3,1024,768]{2,1,0:T(8,128)(2,1)} %get-tuple-element.99.refs_2_.refs_1_, ...), custom_call_target="tpu_custom_call", output_to_operand_aliasing={{1}: (5, {}), {2}: (6, {})} | custom-call | flops 30000000 | tf_op jit(solution)/shard_map/hidden_away/pallas_call | solution.py:379
  230.6 1.5 collective-permute-start.12
  233.0 2.6 collective-permute-start.20
  236.9 1.8 fusion.32.refs_12_
  238.7 6.0 %hidden_home.1 = (f32[2,512,768]{2,1,0:T(8,128)}, bf16[2,512,768]{2,1,0:T(8,128)(2,1)}, bf16[2,2,4,224,384]{4,3,2,1,0:T(8,128)(2,1)}, bf16[2,2,4,5,48,384]{5,4,3...) custom-call(s32[1]{0:T(128)} %bitcast.refs_0_, ...), custom_call_target="tpu_custom_call", output_to_operand_aliasing={{1}: (7, {}), {2}: (8, {}), {3}: (9, {}), {4}: (10, {}), {5... | custom-call | flops 30000000 | tf_op jit(solution)/shard_map/hidden_home/pallas_call | solution.py:379
  245.3 1.3 fusion.9
  246.6 1.4 fusion.46
  248.1 2.4 collective-permute-done.12.refs_1_
  251.4 2.2 place_far.1
  253.6 1.1 add_reduce-precision_fusion.2
  254.9 1.3 fusion.27
  256.2 1.1 fusion.34
  258.2 1.5 collective-permute-start.15
  260.1 1.4 fusion.6
  264.5 6.6 %collective-permute-done.15 = bf16[4,160,384]{2,1,0:T(8,128)(2,1)S(1)} collective-permute-done((bf16[4,160,384]{2,1,0:T(8,128)(2,1)}, bf16[4,160,384]{2,1,0:T(8,128)(2,1)S(1)}, u32[]{:S(2)}, u32[]{:S(2)}) %collective-permute-start.15) | collective-permute-done | bytes 491552 | tf_op jit(solution)/shard_map/ppermute | solution.py:1119
  271.1 1.2 collective-permute-start.16
  272.4 3.0 %collective-permute-start.18 = (bf16[160,384]{1,0:T(8,128)(2,1)S(1)}, bf16[160,384]{1,0:T(8,128)(2,1)S(1)}, u32[]{:S(2)}, u32[]{:S(2)}) collective-permute-start(bf16[160,384]{1,0:T(8,128)(2,1)S(1)} %get-tuple-element.154), channel_id=1, source_target_pairs={{0,24},{2,26},{4,28},{6,30},{8,16},{10,18},{12,20},{14,22},{16,8},... | collective-permute-start | bytes 368648 | tf_op jit(solution)/shard_map/ppermute | solution.py:1122
  279.7 2.3 collective-permute-done.18
  282.0 3.8 %collective-permute-done.17 = bf16[160,384]{1,0:T(8,128)(2,1)S(1)} collective-permute-done((bf16[160,384]{1,0:T(8,128)(2,1)S(1)}, bf16[160,384]{1,0:T(8,128)(2,1)S(1)}, u32[]{:S(2)}, u32[]{:S(2)}) %collective-permute-start.17) | collective-permute-done | bytes 122912 | tf_op jit(solution)/shard_map/ppermute | solution.py:1122
  (132 shorter events, 24.8 us)
Async XLA Ops:
  0.7 6.8 %copy-start.4 = (bf16[2,512,768]{2,1,0:T(8,128)(2,1)S(1)}, bf16[2,512,768]{2,1,0:T(8,128)(2,1)}, u32[]{:S(2)}) copy-start(bf16[2,512,768]{2,1,0:T(8,128)(2,1)} %refs_3_.5) | copy-start | bytes 4718596
  1.5 8.9 %copy-start.23 = (bf16[768]{0:T(1024)(128)(2,1)S(1)}, bf16[768]{0:T(1024)(128)(2,1)}, u32[]{:S(2)}) copy-start(bf16[768]{0:T(1024)(128)(2,1)} %param.21) | copy-start | bytes 4612
  1.5 9.5 %copy-start.24 = (bf16[768]{0:T(1024)(128)(2,1)S(1)}, bf16[768]{0:T(1024)(128)(2,1)}, u32[]{:S(2)}) copy-start(bf16[768]{0:T(1024)(128)(2,1)} %param.24) | copy-start | bytes 4612
  1.5 10.0 %copy-start.25 = (bf16[768]{0:T(1024)(128)(2,1)S(1)}, bf16[768]{0:T(1024)(128)(2,1)}, u32[]{:S(2)}) copy-start(bf16[768]{0:T(1024)(128)(2,1)} %param.26) | copy-start | bytes 4612
  1.5 10.0 %copy-start.26 = (bf16[768]{0:T(1024)(128)(2,1)S(1)}, bf16[768]{0:T(1024)(128)(2,1)}, u32[]{:S(2)}) copy-start(bf16[768]{0:T(1024)(128)(2,1)} %param.27) | copy-start | bytes 4612
  1.5 10.0 %copy-start.27 = (bf16[768]{0:T(1024)(128)(2,1)S(1)}, bf16[768]{0:T(1024)(128)(2,1)}, u32[]{:S(2)}) copy-start(bf16[768]{0:T(1024)(128)(2,1)} %param.28) | copy-start | bytes 4612
  1.6 10.1 %copy-start.28 = (bf16[768]{0:T(1024)(128)(2,1)S(1)}, bf16[768]{0:T(1024)(128)(2,1)}, u32[]{:S(2)}) copy-start(bf16[768]{0:T(1024)(128)(2,1)} %param.32) | copy-start | bytes 4612
  1.6 10.1 %copy-start.29 = (bf16[768]{0:T(1024)(128)(2,1)S(1)}, bf16[768]{0:T(1024)(128)(2,1)}, u32[]{:S(2)}) copy-start(bf16[768]{0:T(1024)(128)(2,1)} %param.33) | copy-start | bytes 4612
  1.6 10.1 %copy-start.30 = (bf16[768]{0:T(1024)(128)(2,1)S(1)}, bf16[768]{0:T(1024)(128)(2,1)}, u32[]{:S(2)}) copy-start(bf16[768]{0:T(1024)(128)(2,1)} %param.34) | copy-start | bytes 4612
  1.6 10.1 %copy-start.22 = (bf16[3072]{0:T(1024)(128)(2,1)S(1)}, bf16[3072]{0:T(1024)(128)(2,1)}, u32[]{:S(2)}) copy-start(bf16[3072]{0:T(1024)(128)(2,1)} %param.30) | copy-start | bytes 18436
  1.6 4.6 %collective-permute-start.1 = (s32[512]{0:T(512)S(1)}, s32[512]{0:T(512)S(1)}, u32[]{:S(2)}, u32[]{:S(2)}) collective-permute-start(s32[512]{0:T(512)S(1)} %bitcast.173), channel_id=1, source_target_pairs={{0,1},{1,0},{2,3},{3,2},{4,5},{5,4},{6,7},{7,6},{8,9},{9,8},{10,11... | collective-permute-start | bytes 6152 | tf_op jit(solution)/shard_map/ppermute | solution.py:1119
  5.8 20.5 %collective-permute-start = (bf16[512,768]{1,0:T(8,128)(2,1)S(1)}, bf16[512,768]{1,0:T(8,128)(2,1)S(1)}, u32[]{:S(2)}, u32[]{:S(2)}) collective-permute-start(bf16[512,768]{1,0:T(8,128)(2,1)S(1)} %dynamic-slice_bitcast_fusion.1), channel_id=1, source_target_pairs={{0,1},{1,0},{2,3},{3,2},{4,5},{5,4},{6,7},{7,6},{8,9},{9,8},{10,11... | collective-permute-start | bytes 2359304 | tf_op jit(solution)/shard_map/ppermute | solution.py:1119
  6.2 20.1 %copy-start.21 = (s32[1024]{0:T(1024)}, s32[1024]{0:T(1024)S(1)}, u32[]{:S(2)}) copy-start(s32[1024]{0:T(1024)S(1)} %pad_add_fusion) | copy-start | bytes 12292
  8.4 45.2 %collective-permute-start.2 = (bf16[512,768]{1,0:T(8,128)(2,1)}, bf16[512,768]{1,0:T(8,128)(2,1)S(1)}, u32[]{:S(2)}, u32[]{:S(2)}) collective-permute-start(bf16[512,768]{1,0:T(8,128)(2,1)} %dynamic-slice_bitcast_fusion), channel_id=1, source_target_pairs={{0,1},{1,0},{2,3},{3,2},{4,5},{5,4},{6,7},{7,6},{8,9},{9,8},{10,11... | collective-permute-start | bytes 2359304 | tf_op jit(solution)/shard_map/ppermute | solution.py:1119
  111.8 12.1 %collective-permute-start.3 = (bf16[2,2,4,224,384]{4,3,2,1,0:T(8,128)(2,1)}, bf16[2,2,4,224,384]{4,3,2,1,0:T(8,128)(2,1)S(1)}, u32[]{:S(2)}, u32[]{:S(2)}) collective-permute-start(bf16[2,2,4,224,384]{4,3,2,1,0:T(8,128)(2,1)} %get-tuple-element.87), channel_id=1, source_target_pairs={{0,2},{2,0},{4,6},{6,4},{8,10},{10,8},{12,14},{14,12},{16,18},{18,... | collective-permute-start | bytes 8257544 | tf_op jit(solution)/shard_map/ppermute | solution.py:1122
  123.4 5.8 %collective-permute-start.4 = (bf16[2,2,4,5,48,384]{5,4,3,2,1,0:T(8,128)(2,1)}, bf16[2,2,4,5,48,384]{5,4,3,2,1,0:T(8,128)(2,1)}, u32[]{:S(2)}, u32[]{:S(2)}) collective-permute-start(bf16[2,2,4,5,48,384]{5,4,3,2,1,0:T(8,128)(2,1)} %get-tuple-element.89), channel_id=1, source_target_pairs={{0,2},{2,0},{4,6},{6,4},{8,10},{10,8},{12,14},{14,12},{16,18},{18,... | collective-permute-start | bytes 8847368 | tf_op jit(solution)/shard_map/ppermute | solution.py:1122
  123.9 1.5 copy-start.7
  125.4 3.8 %copy-start = (bf16[2,2,4,5,48,384]{5,4,3,2,1,0:T(8,128)(2,1)S(1)}, bf16[2,2,4,5,48,384]{5,4,3,2,1,0:T(8,128)(2,1)}, u32[]{:S(2)}) copy-start(bf16[2,2,4,5,48,384]{5,4,3,2,1,0:T(8,128)(2,1)} %get-tuple-element.88.refs_10_) | copy-start | bytes 8847364
  128.8 35.8 %collective-permute-start.5 = (bf16[2,4,224,384]{3,2,1,0:T(8,128)(2,1)}, bf16[2,4,224,384]{3,2,1,0:T(8,128)(2,1)}, u32[]{:S(2)}, u32[]{:S(2)}) collective-permute-start(bf16[2,4,224,384]{3,2,1,0:T(8,128)(2,1)} %fusion.3.refs_7_), channel_id=1, source_target_pairs={{0,1},{1,0},{2,3},{3,2},{4,5},{5,4},{6,7},{7,6},{8,9},{9,8},{10,11... | collective-permute-start | bytes 4128776 | tf_op jit(solution)/shard_map/ppermute | solution.py:1119
  132.1 42.1 %collective-permute-start.6 = (bf16[2,4,5,48,384]{4,3,2,1,0:T(8,128)(2,1)}, bf16[2,4,5,48,384]{4,3,2,1,0:T(8,128)(2,1)S(1)}, u32[]{:S(2)}, u32[]{:S(2)}) collective-permute-start(bf16[2,4,5,48,384]{4,3,2,1,0:T(8,128)(2,1)} %fusion.refs_8_), channel_id=1, source_target_pairs={{0,4},{2,6},{4,0},{6,2},{8,12},{10,14},{12,8},{14,10},{16,20},{18,... | collective-permute-start | bytes 4423688 | tf_op jit(solution)/shard_map/ppermute | solution.py:1122
  174.1 5.2 %copy-start.8 = (bf16[4,224,384]{2,1,0:T(8,128)(2,1)S(1)}, bf16[4,224,384]{2,1,0:T(8,128)(2,1)}, u32[]{:S(2)}) copy-start(bf16[4,224,384]{2,1,0:T(8,128)(2,1)} %fusion.5.refs_5_) | copy-start | bytes 2064388
  174.1 25.0 %collective-permute-start.8 = (bf16[2,2,4,160,256]{4,3,2,1,0:T(8,128)(2,1)}, bf16[2,2,4,160,256]{4,3,2,1,0:T(8,128)(2,1)}, u32[]{:S(2)}, u32[]{:S(2)}) collective-permute-start(bf16[2,2,4,160,256]{4,3,2,1,0:T(8,128)(2,1)} %get-tuple-element.98.refs_12_), channel_id=1, source_target_pairs={{0,2},{2,0},{4,6},{6,4},{8,10},{10,8},{12,14},{14,12},{16,18},{18,... | collective-permute-start | bytes 3932168 | tf_op jit(solution)/shard_map/ppermute | solution.py:1122
  177.2 4.6 %copy-start.6 = (bf16[4,5,48,384]{3,2,1,0:T(8,128)(2,1)}, bf16[4,5,48,384]{3,2,1,0:T(8,128)(2,1)S(1)}, u32[]{:S(2)}) copy-start(bf16[4,5,48,384]{3,2,1,0:T(8,128)(2,1)S(1)} %fusion.2.refs_13_) | copy-start | bytes 2211844
  177.2 19.8 %collective-permute-start.10 = (bf16[4,5,48,384]{3,2,1,0:T(8,128)(2,1)S(1)}, bf16[4,5,48,384]{3,2,1,0:T(8,128)(2,1)}, u32[]{:S(2)}, u32[]{:S(2)}) collective-permute-start(bf16[4,5,48,384]{3,2,1,0:T(8,128)(2,1)S(1)} %fusion.2.refs_13_), channel_id=1, source_target_pairs={{0,1},{1,0},{2,3},{3,2},{4,5},{5,4},{6,7},{7,6},{8,9},{9,8},{10,11... | collective-permute-start | bytes 2211848 | tf_op jit(solution)/shard_map/ppermute | solution.py:1119
  178.7 34.2 %collective-permute-start.7 = (bf16[512,768]{1,0:T(8,128)(2,1)}, bf16[512,768]{1,0:T(8,128)(2,1)S(1)}, u32[]{:S(2)}, u32[]{:S(2)}) collective-permute-start(bf16[512,768]{1,0:T(8,128)(2,1)} %get-tuple-element.103), channel_id=1, source_target_pairs={{0,1},{1,0},{2,3},{3,2},{4,5},{5,4},{6,7},{7,6},{8,9},{9,8},{10,11... | collective-permute-start | bytes 2359304 | tf_op jit(solution)/shard_map/ppermute | solution.py:1119
  179.3 41.3 %collective-permute-start.9 = (bf16[4,224,384]{2,1,0:T(8,128)(2,1)S(1)}, bf16[4,224,384]{2,1,0:T(8,128)(2,1)}, u32[]{:S(2)}, u32[]{:S(2)}) collective-permute-start(bf16[4,224,384]{2,1,0:T(8,128)(2,1)S(1)} %copy-done.8), channel_id=1, source_target_pairs={{0,4},{2,6},{4,0},{6,2},{8,12},{10,14},{12,8},{14,10},{16,20},{18,... | collective-permute-start | bytes 2064392 | tf_op jit(solution)/shard_map/ppermute | solution.py:1122
  197.0 2.1 copy-start.1
  200.3 12.6 %copy-start.9 = (bf16[2,4,160,256]{3,2,1,0:T(8,128)(2,1)}, bf16[2,4,160,256]{3,2,1,0:T(8,128)(2,1)S(1)}, u32[]{:S(2)}) copy-start(bf16[2,4,160,256]{3,2,1,0:T(8,128)(2,1)S(1)} %fusion.7.refs_7_) | copy-start | bytes 1966084
  200.3 44.4 %collective-permute-start.13 = (bf16[2,4,160,256]{3,2,1,0:T(8,128)(2,1)S(1)}, bf16[2,4,160,256]{3,2,1,0:T(8,128)(2,1)}, u32[]{:S(2)}, u32[]{:S(2)}) collective-permute-start(bf16[2,4,160,256]{3,2,1,0:T(8,128)(2,1)S(1)} %fusion.7.refs_7_), channel_id=1, source_target_pairs={{0,4},{2,6},{4,0},{6,2},{8,12},{10,14},{12,8},{14,10},{16,20},{18,... | collective-permute-start | bytes 1966088 | tf_op jit(solution)/shard_map/ppermute | solution.py:1122
  219.0 17.6 %collective-permute-start.11 = (bf16[2,2,4,160,128]{4,3,2,1,0:T(8,128)(2,1)}, bf16[2,2,4,160,128]{4,3,2,1,0:T(8,128)(2,1)}, u32[]{:S(2)}, u32[]{:S(2)}) collective-permute-start(bf16[2,2,4,160,128]{4,3,2,1,0:T(8,128)(2,1)} %get-tuple-element.112), channel_id=1, source_target_pairs={{0,2},{2,0},{4,6},{6,4},{8,10},{10,8},{12,14},{14,12},{16,18},{18,... | collective-permute-start | bytes 1966088 | tf_op jit(solution)/shard_map/ppermute | solution.py:1122
  223.2 1.7 copy-start.11
  223.2 36.9 %collective-permute-start.19 = (bf16[464,384]{1,0:T(8,128)(2,1)S(1)}, bf16[464,384]{1,0:T(8,128)(2,1)}, u32[]{:S(2)}, u32[]{:S(2)}) collective-permute-start(bf16[464,384]{1,0:T(8,128)(2,1)S(1)} %pad_maximum_fusion.1.refs_7_), channel_id=1, source_target_pairs={{0,8},{2,10},{4,12},{6,14},{8,0},{10,2},{12,4},{14,6},{16,24},{18,... | collective-permute-start | bytes 1069064 | tf_op jit(solution)/shard_map/ppermute | solution.py:1122
  224.9 7.2 %copy-start.16 = (bf16[1,5,48,384]{3,2,1,0:T(8,128)(2,1)S(1)}, bf16[1,5,48,384]{3,2,1,0:T(8,128)(2,1)}, u32[]{:S(2)}) copy-start(bf16[1,5,48,384]{3,2,1,0:T(8,128)(2,1)} %get-tuple-element.141) | copy-start | bytes 552964
  230.6 5.1 %copy-start.19 = (bf16[224,384]{1,0:T(8,128)(2,1)S(1)}, bf16[224,384]{1,0:T(8,128)(2,1)}, u32[]{:S(2)}) copy-start(bf16[224,384]{1,0:T(8,128)(2,1)} %get-tuple-element.124) | copy-start | bytes 516100
  230.6 19.9 %collective-permute-start.12 = (bf16[512,768]{1,0:T(8,128)(2,1)}, bf16[512,768]{1,0:T(8,128)(2,1)S(1)}, u32[]{:S(2)}, u32[]{:S(2)}) collective-permute-start(bf16[512,768]{1,0:T(8,128)(2,1)} %get-tuple-element.114), channel_id=1, source_target_pairs={{0,1},{1,0},{2,3},{3,2},{4,5},{5,4},{6,7},{7,6},{8,9},{9,8},{10,11... | collective-permute-start | bytes 2359304 | tf_op jit(solution)/shard_map/ppermute | solution.py:1119
  232.1 4.8 %copy-start.2 = (bf16[2,2,4,160,128]{4,3,2,1,0:T(8,128)(2,1)S(1)}, bf16[2,2,4,160,128]{4,3,2,1,0:T(8,128)(2,1)}, u32[]{:S(2)}) copy-start(bf16[2,2,4,160,128]{4,3,2,1,0:T(8,128)(2,1)} %get-tuple-element.111.refs_11_) | copy-start | bytes 1966084
  233.0 27.1 %collective-permute-start.20 = (bf16[464,384]{1,0:T(8,128)(2,1)}, bf16[464,384]{1,0:T(8,128)(2,1)}, u32[]{:S(2)}, u32[]{:S(2)}) collective-permute-start(bf16[464,384]{1,0:T(8,128)(2,1)} %pad_maximum_fusion.2), channel_id=1, source_target_pairs={{0,16},{2,18},{4,20},{6,22},{8,24},{10,26},{12,28},{14,30},{16,0},... | collective-permute-start | bytes 1069064 | tf_op jit(solution)/shard_map/ppermute | solution.py:1122
  236.5 23.6 %collective-permute-start.21 = (bf16[464,384]{1,0:T(8,128)(2,1)}, bf16[464,384]{1,0:T(8,128)(2,1)}, u32[]{:S(2)}, u32[]{:S(2)}) collective-permute-start(bf16[464,384]{1,0:T(8,128)(2,1)} %pad_maximum_fusion.3), channel_id=1, source_target_pairs={{0,24},{2,26},{4,28},{6,30},{8,16},{10,18},{12,20},{14,22},{16,8},... | collective-permute-start | bytes 1069064 | tf_op jit(solution)/shard_map/ppermute | solution.py:1122
  238.7 6.0 %copy-start.12 = (bf16[2,4,160,128]{3,2,1,0:T(8,128)(2,1)S(1)}, bf16[2,4,160,128]{3,2,1,0:T(8,128)(2,1)}, u32[]{:S(2)}) copy-start(bf16[2,4,160,128]{3,2,1,0:T(8,128)(2,1)} %fusion.32.refs_12_) | copy-start | bytes 983044
  244.7 11.4 %collective-permute-start.14 = (bf16[2,4,160,128]{3,2,1,0:T(8,128)(2,1)S(1)}, bf16[2,4,160,128]{3,2,1,0:T(8,128)(2,1)S(1)}, u32[]{:S(2)}, u32[]{:S(2)}) collective-permute-start(bf16[2,4,160,128]{3,2,1,0:T(8,128)(2,1)S(1)} %copy-done.12), channel_id=1, source_target_pairs={{0,4},{2,6},{4,0},{6,2},{8,12},{10,14},{12,8},{14,10},{16,20},{18,... | collective-permute-start | bytes 983048 | tf_op jit(solution)/shard_map/ppermute | solution.py:1122
  251.4 3.4 %copy-start.17 = (bf16[1,1,5,48,384]{4,3,2,1,0:T(8,128)(2,1)S(1)}, bf16[1,1,5,48,384]{4,3,2,1,0:T(8,128)(2,1)}, u32[]{:S(2)}) copy-start(bf16[1,1,5,48,384]{4,3,2,1,0:T(8,128)(2,1)} %get-tuple-element.139) | copy-start | bytes 552964
  251.4 3.4 %copy-start.18 = (bf16[1,5,48,384]{3,2,1,0:T(8,128)(2,1)S(1)}, bf16[1,5,48,384]{3,2,1,0:T(8,128)(2,1)}, u32[]{:S(2)}) copy-start(bf16[1,5,48,384]{3,2,1,0:T(8,128)(2,1)} %get-tuple-element.143) | copy-start | bytes 552964
  253.6 2.6 copy-start.3
  256.2 1.1 copy-start.20
  258.2 12.8 %collective-permute-start.15 = (bf16[4,160,384]{2,1,0:T(8,128)(2,1)}, bf16[4,160,384]{2,1,0:T(8,128)(2,1)S(1)}, u32[]{:S(2)}, u32[]{:S(2)}) collective-permute-start(bf16[4,160,384]{2,1,0:T(8,128)(2,1)} %pad_maximum_fusion), channel_id=1, source_target_pairs={{0,1},{1,0},{2,3},{3,2},{4,5},{5,4},{6,7},{7,6},{8,9},{9,8},{10,11... | collective-permute-start | bytes 1474568 | tf_op jit(solution)/shard_map/ppermute | solution.py:1119
  271.1 8.5 %collective-permute-start.16 = (bf16[160,384]{1,0:T(8,128)(2,1)S(1)}, bf16[160,384]{1,0:T(8,128)(2,1)S(1)}, u32[]{:S(2)}, u32[]{:S(2)}) collective-permute-start(bf16[160,384]{1,0:T(8,128)(2,1)S(1)} %get-tuple-element.153), channel_id=1, source_target_pairs={{0,8},{2,10},{4,12},{6,14},{8,0},{10,2},{12,4},{14,6},{16,24},{18,... | collective-permute-start | bytes 368648 | tf_op jit(solution)/shard_map/ppermute | solution.py:1122
  272.4 9.6 %collective-permute-start.18 = (bf16[160,384]{1,0:T(8,128)(2,1)S(1)}, bf16[160,384]{1,0:T(8,128)(2,1)S(1)}, u32[]{:S(2)}, u32[]{:S(2)}) collective-permute-start(bf16[160,384]{1,0:T(8,128)(2,1)S(1)} %get-tuple-element.154), channel_id=1, source_target_pairs={{0,24},{2,26},{4,28},{6,30},{8,16},{10,18},{12,20},{14,22},{16,8},... | collective-permute-start | bytes 368648 | tf_op jit(solution)/shard_map/ppermute | solution.py:1122
  275.3 10.5 %collective-permute-start.17 = (bf16[160,384]{1,0:T(8,128)(2,1)S(1)}, bf16[160,384]{1,0:T(8,128)(2,1)S(1)}, u32[]{:S(2)}, u32[]{:S(2)}) collective-permute-start(bf16[160,384]{1,0:T(8,128)(2,1)S(1)} %get-tuple-element.155), channel_id=1, source_target_pairs={{0,16},{2,18},{4,20},{6,22},{8,24},{10,26},{12,28},{14,30},{16,0},... | collective-permute-start | bytes 368648 | tf_op jit(solution)/shard_map/ppermute | solution.py:1122
  (5 other events, 4.7 us)

commit v4 on v3

--- a/solution.py
+++ b/solution.py
@@ -561,7 +561,8 @@
     bi_ref,
     vec_ref,
     out_ref,
-    far_ref,
+    far0_ref,
+    far1_ref,
     first_ref,
     act_ref,
     og_ref,
@@ -613,7 +614,7 @@
 
         @pl.when(jnp.logical_not(near))
         def _():
-            far_ref[rows, :] = out
+            (far1_ref if rows.start else far0_ref)[...] = out
 
         e = jnp.where(near, cot_own_ref[0, rows, :], cot_far_ref[rows, :]).astype(F32)
         sums_ref[0:1, :] += row_sum(e * n2)
@@ -682,7 +683,8 @@
         ],
         (
             jax.ShapeDtypeStruct((2, half, width), BF16),
-            jax.ShapeDtypeStruct((half, width), BF16),
+            jax.ShapeDtypeStruct((half // 2, width), BF16),
+            jax.ShapeDtypeStruct((half // 2, width), BF16),
             low,
             low_ff,
             low,
@@ -695,7 +697,8 @@
         ),
         (
             own_rows,
-            far_rows,
+            pl.BlockSpec((half // 2, width), lambda i, b: (0, 0)),
+            pl.BlockSpec((half // 2, width), lambda i, b: (0, 0)),
             rows,
             wide_rows,
             rows,
@@ -720,8 +723,8 @@
             for x in range(2):
                 zero = lanes(*[res[base : base + rows, c] for c in columns[x]])
                 one = lanes(*[res[base + rows : base + 2 * rows, c] for c in columns[x]])
-                keep_ref[y, x, z, 0] = jnp.where(even, zero, one).astype(BF16)
-                send_ref[y, x, z, 0] = jnp.where(even, one, zero).astype(BF16)
+                keep_ref[x, y, z, 0] = jnp.where(even, zero, one).astype(BF16)
+                send_ref[x, y, z, 0] = jnp.where(even, one, zero).astype(BF16)
 
 
 HALVES = ((slice(0, 384),), (slice(384, 768),))
@@ -749,10 +752,10 @@
             columns = slice(x * middle, (x + 1) * middle)
             zero = res[2 * y * rows : (2 * y + 1) * rows, columns]
             one = res[(2 * y + 1) * rows : (2 * y + 2) * rows, columns]
-            keep_ref[x, y, 0, 0:rows, :] = jnp.where(even, zero, one).astype(BF16)
-            send_ref[x, y, 0, 0:rows, :] = jnp.where(even, one, zero).astype(BF16)
-            keep_ref[x, y, 0, rows:, :] = extra
-            send_ref[x, y, 0, rows:, :] = extra
+            keep_ref[y, x, 0, 0:rows, :] = jnp.where(even, zero, one).astype(BF16)
+            send_ref[y, x, 0, 0:rows, :] = jnp.where(even, one, zero).astype(BF16)
+            keep_ref[y, x, 0, rows:, :] = extra
+            send_ref[y, x, 0, rows:, :] = extra
 
 
 def pair_out(shape, block, index):
@@ -1003,10 +1006,10 @@
 
 
 def hidden_home_kernel(
-    here_ref, fp_ref, d_ref, wq_ref, wk_ref, wv_ref, came_ref, out_ref, layer_ref
+    here_ref, fp_ref, d_ref, wq_ref, wk_ref, wv_ref, came0_ref, came1_ref, out_ref, layer_ref
 ):
     out_ref[0] = hidden_total(fp_ref, d_ref, wq_ref, wk_ref, wv_ref)
-    layer_ref[0] = came_ref[...]
+    layer_ref[0] = jnp.where(pl.program_id(0) == 0, came0_ref[...], came1_ref[...])
 
 
 def hidden_away(fp, dqkv, wq, wk, wv, passes, after):
@@ -1031,7 +1034,7 @@
     )
 
 
-def hidden_home(here, fp, dqkv, wq, wk, wv, came, layer, passes, after):
+def hidden_home(here, fp, dqkv, wq, wk, wv, came0, came1, layer, passes, after):
     length, width = fp.shape
     half = length // 2
     steps = half // TILE
@@ -1039,13 +1042,13 @@
         hidden_home_kernel,
         "hidden_home",
         (steps,),
-        (here, fp, dqkv, wq, wk, wv, came),
+        (here, fp, dqkv, wq, wk, wv, came0, came1),
         [
             pl.BlockSpec((TILE, width), lambda i, b: (i, 0)),
             pl.BlockSpec((3, TILE, width), lambda i, b: (0, i, 0)),
         ]
         + [fixed((width, width))] * 3
-        + [pl.BlockSpec((TILE, width), lambda i, b: (i, 0))],
+        + [fixed((TILE, width))] * 2,
         (
             jax.ShapeDtypeStruct((2, half, width), F32),
             jax.ShapeDtypeStruct((2, half, width), BF16),
@@ -1169,82 +1172,87 @@
         ],
         axis=0,
     )
-    out, out_far, first, act, og, ig, fp, ag, dctx, sums, isum = token_pass(
+    out, out_far0, out_far1, first, act, og, ig, fp, ag, dctx, sums, isum = token_pass(
         here_id, h, ctx, cotangent, cot_far, output_matrix, inner_matrix, outer_matrix, row(inner_bias), vec
     )
-    out_came = trade(out_far)
+    out_came0, out_came1 = trade(out_far0), trade(out_far1)
     x_mine, x_away, y_mine, y_away = here, 1 - here, y_at, 1 - y_at
     a_keep, a_send = outer_grad_call(core_id, act, og, sums, isum)
     a0 = seq_swap(a_send, 1)
     b_keep, b_send, a_keep = inner_grad_call(core_id, first, ig, ctx, ag, (a_keep,))
     b0 = seq_swap(b_send, 1)
     a = (a_keep, a0)
-    a_away = sum_0(a, x_away).astype(BF16)
-    a1 = trade(a_away)
+    a_away = sum_0(a, y_away).astype(BF16)
+    a1 = seq_swap(a_away, 2)
     b = (b_keep, b0)
-    b_away = sum_0(b, y_away).astype(BF16)
-    b1 = seq_swap(b_away, 2)
+    b_away = sum_0(b, x_away).astype(BF16)
+    b1 = trade(b_away)
     bwd = (q, k, v, dctx, ctx, lse, seg)
     held = attention_backward(0, *bwd, (), (), (a_away, b_away))
     *held, a_keep, b_keep = attention_backward(1, *bwd, held, (a_keep, b_keep), ())
     a = (a_keep, a0, a1)
-    a_away = sum_1(a, x_mine, y_away).astype(BF16)
-    a2 = seq_swap(a_away, 2)
-    c_keep, c_send, b_keep = projection_grad_call(
-        core_id, h, held[0], sums, 0, 2 * GROUP, False, (b_keep,), (a_away,)
+    a_away = sum_1(a, y_mine, x_away).astype(BF16)
+    a2 = trade(a_away)
+    c_keep, c_send, b_keep, out_came0 = projection_grad_call(
+        core_id, h, held[0], sums, 0, 2 * GROUP, False, (b_keep, out_came0), (a_away,)
     )
     c0 = seq_swap(c_send, 1)
     b = (b_keep, b0, b1)
-    b_away = sum_1(b, y_mine, x_away).astype(BF16)
-    b2 = trade(b_away)
+    b_away = sum_1(b, x_mine, y_away).astype(BF16)
+    b2 = seq_swap(b_away, 2)
     dqkv, sums2, a_keep, b_keep, c_keep = attention_backward(
         2, *bwd, held, (a_keep, b_keep, c_keep), (c_send, b_away)
     )
     c = (c_keep, c0)
     c_away = sum_0(c, y_away).astype(BF16)
     c1 = seq_swap(c_away, 2)
-    d_keep, d_send, a_keep, b_keep, out_came = projection_grad_call(
-        core_id, h, dqkv, sums2, 2, GROUP, True, (a_keep, b_keep, out_came), (c_away,)
+    d_keep, d_send, a_keep, b_keep, out_came1 = projection_grad_call(
+        core_id, h, dqkv, sums2, 2, GROUP, True, (a_keep, b_keep, out_came1), (c_away,)
     )
     d0 = seq_swap(d_send, 1)
     a = (a_keep, a0, a1, a2)
     b = (b_keep, b0, b1, b2)
 
     def both(z):
-        a_part = sum_2(a, x_mine, y_mine, z)
-        b_part = sum_2(b, y_mine, x_mine, z)
+        a_part = sum_2(a, y_mine, x_mine, z)
+        b_part = sum_2(b, x_mine, y_mine, z)
         return jnp.concatenate([a_part, b_part.reshape(-1, width // 2)], axis=0)
 
     parts = [both(z_at ^ e).astype(BF16) for e in (1, 2, 3)]
     ab3 = send_z(parts)
     args = (fp, dqkv, query_matrix, key_matrix, value_matrix)
-    far_grad, c_keep, d_keep = hidden_away(*args, (c_keep, d_keep), (parts[0],))
-    came = trade(far_grad)
     d = (d_keep, d0)
     d_away = sum_0(d, y_away).astype(BF16)
     d1 = seq_swap(d_away, 2)
     hidden_grad, layer_out, a_keep, b_keep, c_keep, d_keep = hidden_home(
-        here_id, *args, out_came, out, (a_keep, b_keep, c_keep, d_keep), (d_away,)
+        here_id, *args, out_came0, out_came1, out, (a_keep, b_keep, c_keep, d_keep), (d_away, *parts)
     )
     c = (c_keep, c0, c1)
     d = (d_keep, d0, d1)
 
+    def lanes_of(*parts):
+        return jnp.concatenate(parts, axis=-1)
+
     def late_1(*at):
         return lanes_of(sum_1(c, y_mine, *at), sum_1(d, y_mine, *at))
 
-    def lanes_of(*parts):
-        return jnp.concatenate(parts, axis=-1)
-
-    e2 = trade(late_1(x_away).astype(BF16))
+    e_away = late_1(x_away).astype(BF16)
+    e2 = trade(e_away)
+    far_grad, a_keep, b_keep, c_keep, d_keep = hidden_away(
+        *args, (a_keep, b_keep, c_keep, d_keep), (e_away,)
+    )
+    came = trade(far_grad)
+    c = (c_keep, c0, c1)
+    d = (d_keep, d0, d1)
+    a = (a_keep, a0, a1, a2)
+    b = (b_keep, b0, b1, b2)
 
     def late_2(z):
         return rounded(late_1(x_mine, z) + pick(e2, z).astype(F32))
 
     e3 = send_z([late_2(z_at ^ e).astype(BF16) for e in (1, 2, 3)])
-    hidden_grad, a_keep, b_keep = place_far(here_id, came, hidden_grad, (a_keep, b_keep))
-    a = (a_keep, a0, a1, a2)
-    b = (b_keep, b0, b1, b2)
     early = add_z(both(z_at), ab3)
+    hidden_grad = place_far(here_id, came, hidden_grad, ())[0]
     late = add_z(late_2(z_at), e3)
     rows = width // 16
     outer_rows = 4 * rows
@@ -1279,7 +1287,7 @@
 
 def choose(sizes, *args):
     seq_count, row_count, width = args[0].shape
-    whole_here = sizes[1] == 2 and seq_count == 2 and row_count % TILE == 0 and width == 3 * GROUP
+    whole_here = sizes[1] == 2 and seq_count == 2 and row_count == 2 * TILE and width == 3 * GROUP
     return fast(*args) if whole_here and sizes[0] == 16 else general(*args)
 
 

time: 290 us -> 280 us (0.966)
  waiting for transfers between devices: 40.5 us -> 32.1 us
  other arithmetic: 30.2 us -> 24.9 us
  Pallas kernels: 167 us -> 170 us
    ppermute x8 -> x9, waiting for transfers between devices: 33.5 us -> 21 us  [trade(): return lax.ppermute(x, 'blk', [(0, 1), (1, 0)])]
    ppermute x14, waiting for transfers between devices: 7.03 us -> 11.1 us  [seq_swap(): return lax.ppermute(x, 'seq', [(i, i ^ bit) for i in range(16)])]
    ppermute x8 -> x9, starting transfers between devices: 10.2 us -> 11.1 us  [trade(): return lax.ppermute(x, 'blk', [(0, 1), (1, 0)])]
    unnamed x62 -> x74, local copies, waits for them, and re-layouts: 6.34 us -> 6.11 us
  transfers between devices with their start and end apart: 22 -> 23, of which waited for: 9 -> 6; matrix products, arithmetic and copies ran while one was open for 16% -> 15% of each run, Pallas kernels for 38% -> 39%
where the time goes in v4:
time: 280 us; the launch traced here: 278 us
  Pallas kernels  170 us (61%)
  waiting for transfers between devices  32.1 us (11%)
  starting transfers between devices  25.1 us (9%)
  other arithmetic  24.9 us (9%)
  local copies, waits for them, and re-layouts  23.9 us (9%)
    pallas_call x12, Pallas kernels, run(): pl.pallas_call(body, grid_spec=pltpu.PrefetchScalarGridSpec(num_scalar_pr...  170 us
    ppermute x9, waiting for transfers between devices, trade(): return lax.ppermute(x, 'blk', [(0, 1), (1, 0)])  21 us
    ppermute x14, starting transfers between devices, seq_swap(): return lax.ppermute(x, 'seq', [(i, i ^ bit) for i in range(16)])  14 us
    ppermute x9, starting transfers between devices, trade(): return lax.ppermute(x, 'blk', [(0, 1), (1, 0)])  11.1 us
    ppermute x14, waiting for transfers between devices, seq_swap(): return lax.ppermute(x, 'seq', [(i, i ^ bit) for i in range(16)])  11.1 us
    reduce_precision x6, other arithmetic, rounded(): return lax.reduce_precision(x, 8, 7)  7.1 us
    unnamed x74, local copies, waits for them, and re-layouts  6.11 us
  transfers between devices with their start and end apart: 23, of which 6 were waited for; matrix products, arithmetic and copies ran while one was open for 15% of the time, Pallas kernels for 39%

profile of v4, /device:TPU:0, one launch (start us, length us, event | category | flops | bytes accessed | tf_op | source)
XLA Modules:
  0.0 277.9 jit_solution(4819379495686055534)
XLA Ops:
  1.6 3.0 %collective-permute-start.1 = (s32[512]{0:T(512)S(1)}, s32[512]{0:T(512)S(1)}, u32[]{:S(2)}, u32[]{:S(2)}) collective-permute-start(s32[512]{0:T(512)S(1)} %bitcast.173), channel_id=1, source_target_pairs={{0,1},{1,0},{2,3},{3,2},{4,5},{5,4},{6,7},{7,6},{8,9},{9,8},{10,11... | collective-permute-start | bytes 6152 | tf_op jit(solution)/shard_map/ppermute | solution.py:1122
  4.6 1.2 dynamic-slice_bitcast_fusion.1
  7.4 0.9 dynamic-slice_bitcast_fusion
  8.4 2.0 collective-permute-start.2
  12.9 13.4 %collective-permute-done.refs_2_ = bf16[512,768]{1,0:T(8,128)(2,1)S(1)} collective-permute-done((bf16[512,768]{1,0:T(8,128)(2,1)S(1)}, bf16[512,768]{1,0:T(8,128)(2,1)S(1)}, u32[]{:S(2)}, u32[]{:S(2)}) %collective-permute-start) | collective-permute-done | bytes 786464 | tf_op jit(solution)/shard_map/ppermute | solution.py:1122
  27.2 26.3 %attention_forward.1 = (bf16[1024,768]{1,0:T(8,128)(2,1)}, bf16[1024,768]{1,0:T(8,128)(2,1)}, bf16[1024,768]{1,0:T(8,128)(2,1)}, bf16[2,1024,384]{2,1,0:T(8,128)...) custom-call(s32[1]{0:T(128)} %bitcast.refs_0_, bf16[2,512,768]{2,1,0:T(8,128)(2,1)} %refs_1_.1, ...), custom_call_target="tpu_custom_call" | custom-call | flops 160000000 | tf_op jit(solution)/shard_map/attention_forward/pallas_call | solution.py:379
  54.4 50.3 %token_pass.1 = (bf16[2,512,768]{2,1,0:T(8,128)(2,1)}, bf16[256,768]{1,0:T(8,128)(2,1)}, bf16[256,768]{1,0:T(8,128)(2,1)}, bf16[1024,768]{1,0:T(8,128)(2,1)}, bf...) custom-call(s32[1]{0:T(128)} %bitcast.refs_0_, ...), custom_call_target="tpu_custom_call" | custom-call | flops 230000000 | tf_op jit(solution)/shard_map/token_pass/pallas_call | solution.py:379
  104.8 9.4 %outer_grad.1 = (bf16[2,2,4,224,384]{4,3,2,1,0:T(8,128)(2,1)}, bf16[2,2,4,224,384]{4,3,2,1,0:T(8,128)(2,1)}) custom-call(s32[1]{0:T(128)} %bitcast.8.refs_0_, bf16[1024,3072]{1,0:T(8,128)(2,1)} %get-tuple-element.82.refs_1_, bf16[1024,768]{1,0:T(8,128)(2,1)} %get-tuple-element.83.refs_2_, f32[8,768]{1,0:T(8,128)} %get-tuple-element.84.refs_3_, ...), custom_call_target="tpu_custom_call" | custom-call | flops 45000000 | tf_op jit(solution)/shard_map/outer_grad/pallas_call | solution.py:379
  114.2 11.7 %inner_grad.1 = (bf16[2,2,4,5,48,384]{5,4,3,2,1,0:T(8,128)(2,1)}, bf16[2,2,4,5,48,384]{5,4,3,2,1,0:T(8,128)(2,1)}, bf16[2,2,4,224,384]{4,3,2,1,0:T(8,128)(2,1)}) custom-call(s32[1]{0:T(128)} %bitcast.8.refs_0_, bf16[1024,768]{1,0:T(8,128)(2,1)} %get-tuple-element.79.refs_1_, ...), custom_call_target="tpu_custom_call", output_to_operand_aliasing={{2}: (6, {})} | custom-call | flops 60000000 | tf_op jit(solution)/shard_map/inner_grad/pallas_call | solution.py:379
  126.3 1.5 copy-done.7
  127.9 2.2 fusion.3.refs_7_
  130.1 1.6 collective-permute-start.6
  131.7 1.8 fusion.refs_8_
  134.1 1.5 collective-permute-start.5
  135.6 15.2 %attention_backward.3 = (bf16[3,1024,768]{2,1,0:T(8,128)(2,1)}, f32[8,768]{1,0:T(8,128)}) custom-call(bf16[1024,768]{1,0:T(8,128)(2,1)} %get-tuple-element.74.refs_0_, bf16[1024,768]{1,0:T(8,128)(2,1)} %get-tuple-element.75.refs_1_, bf16[1024,768]{1,0:T(8,128)(2,1)} %get-tuple-element.76.refs_2_, bf16[2,1024,384]{2,1,0:T(8,128)(2,1)} %get-tuple-element.77.refs_3_, ...), custom_call_target="tpu_custom_call" | custom-call | flops 80000000 | tf_op jit(solution)/shard_map/attention_backward/pallas_call | solution.py:379
  150.8 15.7 %attention_backward.4 = (bf16[3,1024,768]{2,1,0:T(8,128)(2,1)}, f32[8,768]{1,0:T(8,128)}, bf16[2,2,4,224,384]{4,3,2,1,0:T(8,128)(2,1)}, bf16[2,2,4,5,48,384]{5,4,3,2,1,0:T(8,128)(2,1)}) custom-call(bf16[1024,768]{1,0:T(8,128)(2,1)} %get-tuple-element.74.refs_0_, ...), custom_call_target="tpu_custom_call", output_to_operand_aliasing={{0}: (7, {}), {1}: (8, {}), {2}: (9, {}), {3}: (10, {})} | custom-call | flops 80000000 | tf_op jit(solution)/shard_map/attention_backward/pallas_call | solution.py:379
  166.6 2.6 fusion.5.refs_6_
  169.2 7.3 %collective-permute-done.5.refs_5_ = bf16[256,768]{1,0:T(8,128)(2,1)S(1)} collective-permute-done((bf16[256,768]{1,0:T(8,128)(2,1)}, bf16[256,768]{1,0:T(8,128)(2,1)S(1)}, u32[]{:S(2)}, u32[]{:S(2)}) %collective-permute-start.5) | collective-permute-done | bytes 393248 | tf_op jit(solution)/shard_map/ppermute | solution.py:1122
  177.3 6.8 %projection_grad.2 = (bf16[2,2,4,160,256]{4,3,2,1,0:T(8,128)(2,1)}, bf16[2,2,4,160,256]{4,3,2,1,0:T(8,128)(2,1)}, bf16[2,2,4,5,48,384]{5,4,3,2,1,0:T(8,128)(2,1)}, bf16[256,768]{1,0:T(8,128)(2,1)}) custom-call(s32[1]{0:T(128)} %bitcast.8.refs_0_, bf16[1024,768]{1,0:T(8,128)(2,1)} %get-tuple-element.71.refs_1_, ...), custom_call_target="tpu_custom_call", output_to_operand_aliasing={{2}: (4, {}), {3}: (5, {})} | custom-call | flops 25000000 | tf_op jit(solution)/shard_map/projection_grad/pallas_call | solution.py:379
  184.3 2.0 fusion.2.refs_13_
  186.2 1.6 collective-permute-start.12
  188.4 1.5 collective-permute-start.11
  189.8 2.0 constant_dynamic-slice_fusion.7
  191.9 15.2 %attention_backward.5 = (bf16[3,1024,768]{2,1,0:T(8,128)(2,1)}, f32[8,768]{1,0:T(8,128)}, bf16[2,2,4,224,384]{4,3,2,1,0:T(8,128)(2,1)}, bf16[2,2,4,5,48,384]{5,4...) custom-call(bf16[1024,768]{1,0:T(8,128)(2,1)} %get-tuple-element.74., ...), custom_call_target="tpu_custom_call", output_to_operand_aliasing={{0}: (7, {}), {1}: (8, {}), {2}: (9, {}), {3}: (10, {}), {4... | custom-call | flops 80000000 | tf_op jit(solution)/shard_map/attention_backward/pallas_call | solution.py:379
  207.1 2.1 constant_dynamic-slice_fusion.6
  210.8 5.1 %projection_grad.3 = (bf16[2,2,4,160,128]{4,3,2,1,0:T(8,128)(2,1)}, bf16[2,2,4,160,128]{4,3,2,1,0:T(8,128)(2,1)}, bf16[2,2,4,224,384]{4,3,2,1,0:T(8,128)(2,1)}, ...) custom-call(s32[1]{0:T(128)} %bitcast.8.refs_0_, ...), custom_call_target="tpu_custom_call", output_to_operand_aliasing={{2}: (4, {}), {3}: (5, {}), {4}: (6, {})} | custom-call | flops 25000000 | tf_op jit(solution)/shard_map/projection_grad/pallas_call | solution.py:379
  215.8 1.5 add_reduce-precision_fusion.1
  217.5 2.0 fusion.24
  219.6 3.7 %collective-permute-start.22 = (bf16[464,384]{1,0:T(8,128)(2,1)S(1)}, bf16[464,384]{1,0:T(8,128)(2,1)}, u32[]{:S(2)}, u32[]{:S(2)}) collective-permute-start(bf16[464,384]{1,0:T(8,128)(2,1)S(1)} %pad_maximum_fusion.3.refs_16_), channel_id=1, source_target_pairs={{0,24},{2,26},{4,28},{6,30},{8,16},{10,18},{12,20},{14,22},{16,8},... | collective-permute-start | bytes 1069064 | tf_op jit(solution)/shard_map/ppermute | solution.py:1125
  223.7 1.6 collective-permute-start.14
  226.2 6.2 %hidden_home.1 = (f32[2,512,768]{2,1,0:T(8,128)}, bf16[2,512,768]{2,1,0:T(8,128)(2,1)}, bf16[2,2,4,224,384]{4,3,2,1,0:T(8,128)(2,1)}, bf16[2,2,4,5,48,384]{5,4,3...) custom-call(s32[1]{0:T(128)} %bitcast.refs_0_, ...), custom_call_target="tpu_custom_call", output_to_operand_aliasing={{1}: (8, {}), {2}: (9, {}), {3}: (10, {}), {4}: (11, {}), {... | custom-call | flops 30000000 | tf_op jit(solution)/shard_map/hidden_home/pallas_call | solution.py:379
  232.4 1.2 fusion.9
  233.6 1.2 fusion.34
  235.7 5.6 %hidden_away.1 = (bf16[512,768]{1,0:T(8,128)(2,1)}, bf16[2,2,4,224,384]{4,3,2,1,0:T(8,128)(2,1)}, bf16[2,2,4,5,48,384]{5,4,3,2,1,0:T(8,128)(2,1)}, bf16[2,2,4,16...) custom-call(f32[1024,768]{1,0:T(8,128)} %get-tuple-element.73.refs_1, ...), custom_call_target="tpu_custom_call", output_to_operand_aliasing={{1}: (5, {}), {2}: (6, {}), {3}: (7, {}), {4}: (8, {})} | custom-call | flops 30000000 | tf_op jit(solution)/shard_map/hidden_away/pallas_call | solution.py:379
  241.3 1.3 collective-permute-start.15
  242.6 1.1 add_reduce-precision_fusion
  243.7 1.3 fusion.21
  245.0 2.0 fusion.46
  247.0 1.1 fusion.50
  248.2 6.1 %collective-permute-done.21 = bf16[464,384]{1,0:T(8,128)(2,1)} collective-permute-done((bf16[464,384]{1,0:T(8,128)(2,1)S(1)}, bf16[464,384]{1,0:T(8,128)(2,1)}, u32[]{:S(2)}, u32[]{:S(2)}) %collective-permute-start.21) | collective-permute-done | bytes 356384 | tf_op jit(solution)/shard_map/ppermute | solution.py:1125
  254.3 1.4 fusion.6
  256.5 1.1 fusion.39
  257.6 2.5 collective-permute-start.19
  260.2 0.9 collective-permute-start.18
  267.0 4.7 %collective-permute-done.18 = bf16[160,384]{1,0:T(8,128)(2,1)S(1)} collective-permute-done((bf16[160,384]{1,0:T(8,128)(2,1)S(1)}, bf16[160,384]{1,0:T(8,128)(2,1)S(1)}, u32[]{:S(2)}, u32[]{:S(2)}) %collective-permute-start.18) | collective-permute-done | bytes 122912 | tf_op jit(solution)/shard_map/ppermute | solution.py:1125
  271.7 1.0 fusion.37
  274.6 0.9 copy-done.17
  275.5 2.2 place_far.1
  (146 shorter events, 21.2 us)
Async XLA Ops:
  0.7 6.8 %copy-start.5 = (bf16[2,512,768]{2,1,0:T(8,128)(2,1)S(1)}, bf16[2,512,768]{2,1,0:T(8,128)(2,1)}, u32[]{:S(2)}) copy-start(bf16[2,512,768]{2,1,0:T(8,128)(2,1)} %refs_3_.5) | copy-start | bytes 4718596
  1.5 8.9 %copy-start.29 = (bf16[768]{0:T(1024)(128)(2,1)S(1)}, bf16[768]{0:T(1024)(128)(2,1)}, u32[]{:S(2)}) copy-start(bf16[768]{0:T(1024)(128)(2,1)} %param.21) | copy-start | bytes 4612
  1.5 9.5 %copy-start.30 = (bf16[768]{0:T(1024)(128)(2,1)S(1)}, bf16[768]{0:T(1024)(128)(2,1)}, u32[]{:S(2)}) copy-start(bf16[768]{0:T(1024)(128)(2,1)} %param.24) | copy-start | bytes 4612
  1.5 10.0 %copy-start.31 = (bf16[768]{0:T(1024)(128)(2,1)S(1)}, bf16[768]{0:T(1024)(128)(2,1)}, u32[]{:S(2)}) copy-start(bf16[768]{0:T(1024)(128)(2,1)} %param.26) | copy-start | bytes 4612
  1.5 10.0 %copy-start.32 = (bf16[768]{0:T(1024)(128)(2,1)S(1)}, bf16[768]{0:T(1024)(128)(2,1)}, u32[]{:S(2)}) copy-start(bf16[768]{0:T(1024)(128)(2,1)} %param.27) | copy-start | bytes 4612
  1.5 10.0 %copy-start.33 = (bf16[768]{0:T(1024)(128)(2,1)S(1)}, bf16[768]{0:T(1024)(128)(2,1)}, u32[]{:S(2)}) copy-start(bf16[768]{0:T(1024)(128)(2,1)} %param.28) | copy-start | bytes 4612
  1.6 10.1 %copy-start.34 = (bf16[768]{0:T(1024)(128)(2,1)S(1)}, bf16[768]{0:T(1024)(128)(2,1)}, u32[]{:S(2)}) copy-start(bf16[768]{0:T(1024)(128)(2,1)} %param.32) | copy-start | bytes 4612
  1.6 10.1 %copy-start.35 = (bf16[768]{0:T(1024)(128)(2,1)S(1)}, bf16[768]{0:T(1024)(128)(2,1)}, u32[]{:S(2)}) copy-start(bf16[768]{0:T(1024)(128)(2,1)} %param.33) | copy-start | bytes 4612
  1.6 10.1 %copy-start.36 = (bf16[768]{0:T(1024)(128)(2,1)S(1)}, bf16[768]{0:T(1024)(128)(2,1)}, u32[]{:S(2)}) copy-start(bf16[768]{0:T(1024)(128)(2,1)} %param.34) | copy-start | bytes 4612
  1.6 10.1 %copy-start.28 = (bf16[3072]{0:T(1024)(128)(2,1)S(1)}, bf16[3072]{0:T(1024)(128)(2,1)}, u32[]{:S(2)}) copy-start(bf16[3072]{0:T(1024)(128)(2,1)} %param.30) | copy-start | bytes 18436
  1.6 4.6 %collective-permute-start.1 = (s32[512]{0:T(512)S(1)}, s32[512]{0:T(512)S(1)}, u32[]{:S(2)}, u32[]{:S(2)}) collective-permute-start(s32[512]{0:T(512)S(1)} %bitcast.173), channel_id=1, source_target_pairs={{0,1},{1,0},{2,3},{3,2},{4,5},{5,4},{6,7},{7,6},{8,9},{9,8},{10,11... | collective-permute-start | bytes 6152 | tf_op jit(solution)/shard_map/ppermute | solution.py:1122
  5.8 20.5 %collective-permute-start = (bf16[512,768]{1,0:T(8,128)(2,1)S(1)}, bf16[512,768]{1,0:T(8,128)(2,1)S(1)}, u32[]{:S(2)}, u32[]{:S(2)}) collective-permute-start(bf16[512,768]{1,0:T(8,128)(2,1)S(1)} %dynamic-slice_bitcast_fusion.1), channel_id=1, source_target_pairs={{0,1},{1,0},{2,3},{3,2},{4,5},{5,4},{6,7},{7,6},{8,9},{9,8},{10,11... | collective-permute-start | bytes 2359304 | tf_op jit(solution)/shard_map/ppermute | solution.py:1122
  6.2 20.1 %copy-start.27 = (s32[1024]{0:T(1024)}, s32[1024]{0:T(1024)S(1)}, u32[]{:S(2)}) copy-start(s32[1024]{0:T(1024)S(1)} %pad_add_fusion) | copy-start | bytes 12292
  8.4 45.1 %collective-permute-start.2 = (bf16[512,768]{1,0:T(8,128)(2,1)}, bf16[512,768]{1,0:T(8,128)(2,1)S(1)}, u32[]{:S(2)}, u32[]{:S(2)}) collective-permute-start(bf16[512,768]{1,0:T(8,128)(2,1)} %dynamic-slice_bitcast_fusion), channel_id=1, source_target_pairs={{0,1},{1,0},{2,3},{3,2},{4,5},{5,4},{6,7},{7,6},{8,9},{9,8},{10,11... | collective-permute-start | bytes 2359304 | tf_op jit(solution)/shard_map/ppermute | solution.py:1122
  114.2 12.1 %collective-permute-start.3 = (bf16[2,2,4,224,384]{4,3,2,1,0:T(8,128)(2,1)}, bf16[2,2,4,224,384]{4,3,2,1,0:T(8,128)(2,1)S(1)}, u32[]{:S(2)}, u32[]{:S(2)}) collective-permute-start(bf16[2,2,4,224,384]{4,3,2,1,0:T(8,128)(2,1)} %get-tuple-element.88), channel_id=1, source_target_pairs={{0,2},{2,0},{4,6},{6,4},{8,10},{10,8},{12,14},{14,12},{16,18},{18,... | collective-permute-start | bytes 8257544 | tf_op jit(solution)/shard_map/ppermute | solution.py:1125
  125.9 5.9 %collective-permute-start.4 = (bf16[2,2,4,5,48,384]{5,4,3,2,1,0:T(8,128)(2,1)}, bf16[2,2,4,5,48,384]{5,4,3,2,1,0:T(8,128)(2,1)}, u32[]{:S(2)}, u32[]{:S(2)}) collective-permute-start(bf16[2,2,4,5,48,384]{5,4,3,2,1,0:T(8,128)(2,1)} %get-tuple-element.90), channel_id=1, source_target_pairs={{0,2},{2,0},{4,6},{6,4},{8,10},{10,8},{12,14},{14,12},{16,18},{18,... | collective-permute-start | bytes 8847368 | tf_op jit(solution)/shard_map/ppermute | solution.py:1125
  127.9 3.8 %copy-start = (bf16[2,2,4,5,48,384]{5,4,3,2,1,0:T(8,128)(2,1)S(1)}, bf16[2,2,4,5,48,384]{5,4,3,2,1,0:T(8,128)(2,1)}, u32[]{:S(2)}) copy-start(bf16[2,2,4,5,48,384]{5,4,3,2,1,0:T(8,128)(2,1)} %get-tuple-element.89.refs_10_) | copy-start | bytes 8847364
  130.1 3.4 %copy-start.4 = (bf16[2,4,224,384]{3,2,1,0:T(8,128)(2,1)}, bf16[2,4,224,384]{3,2,1,0:T(8,128)(2,1)S(1)}, u32[]{:S(2)}) copy-start(bf16[2,4,224,384]{3,2,1,0:T(8,128)(2,1)S(1)} %fusion.3.refs_7_) | copy-start | bytes 4128772
  130.1 36.4 %collective-permute-start.6 = (bf16[2,4,224,384]{3,2,1,0:T(8,128)(2,1)S(1)}, bf16[2,4,224,384]{3,2,1,0:T(8,128)(2,1)}, u32[]{:S(2)}, u32[]{:S(2)}) collective-permute-start(bf16[2,4,224,384]{3,2,1,0:T(8,128)(2,1)S(1)} %fusion.3.refs_7_), channel_id=1, source_target_pairs={{0,4},{2,6},{4,0},{6,2},{8,12},{10,14},{12,8},{14,10},{16,20},{18,... | collective-permute-start | bytes 4128776 | tf_op jit(solution)/shard_map/ppermute | solution.py:1125
  133.5 2.1 copy-start.3
  133.5 50.7 %collective-permute-start.7 = (bf16[2,4,5,48,384]{4,3,2,1,0:T(8,128)(2,1)S(1)}, bf16[2,4,5,48,384]{4,3,2,1,0:T(8,128)(2,1)}, u32[]{:S(2)}, u32[]{:S(2)}) collective-permute-start(bf16[2,4,5,48,384]{4,3,2,1,0:T(8,128)(2,1)S(1)} %fusion.refs_8_), channel_id=1, source_target_pairs={{0,1},{1,0},{2,3},{3,2},{4,5},{5,4},{6,7},{7,6},{8,9},{9,8},{10,11... | collective-permute-start | bytes 4423688 | tf_op jit(solution)/shard_map/ppermute | solution.py:1122
  134.1 42.4 %collective-permute-start.5 = (bf16[256,768]{1,0:T(8,128)(2,1)}, bf16[256,768]{1,0:T(8,128)(2,1)S(1)}, u32[]{:S(2)}, u32[]{:S(2)}) collective-permute-start(bf16[256,768]{1,0:T(8,128)(2,1)} %get-tuple-element.97), channel_id=1, source_target_pairs={{0,1},{1,0},{2,3},{3,2},{4,5},{5,4},{6,7},{7,6},{8,9},{9,8},{10,11... | collective-permute-start | bytes 1179656 | tf_op jit(solution)/shard_map/ppermute | solution.py:1122
  184.2 4.2 %copy-start.8 = (bf16[4,224,384]{2,1,0:T(8,128)(2,1)S(1)}, bf16[4,224,384]{2,1,0:T(8,128)(2,1)}, u32[]{:S(2)}) copy-start(bf16[4,224,384]{2,1,0:T(8,128)(2,1)} %fusion.5.refs_6_) | copy-start | bytes 2064388
  184.2 25.0 %collective-permute-start.9 = (bf16[2,2,4,160,256]{4,3,2,1,0:T(8,128)(2,1)}, bf16[2,2,4,160,256]{4,3,2,1,0:T(8,128)(2,1)S(1)}, u32[]{:S(2)}, u32[]{:S(2)}) collective-permute-start(bf16[2,2,4,160,256]{4,3,2,1,0:T(8,128)(2,1)} %get-tuple-element.100.refs_12_), channel_id=1, source_target_pairs={{0,2},{2,0},{4,6},{6,4},{8,10},{10,8},{12,14},{14,12},{16,18},{18,... | collective-permute-start | bytes 3932168 | tf_op jit(solution)/shard_map/ppermute | solution.py:1125
  186.2 5.7 %copy-start.6 = (bf16[4,5,48,384]{3,2,1,0:T(8,128)(2,1)}, bf16[4,5,48,384]{3,2,1,0:T(8,128)(2,1)S(1)}, u32[]{:S(2)}) copy-start(bf16[4,5,48,384]{3,2,1,0:T(8,128)(2,1)S(1)} %fusion.2.refs_13_) | copy-start | bytes 2211844
  186.2 20.9 %collective-permute-start.12 = (bf16[4,5,48,384]{3,2,1,0:T(8,128)(2,1)S(1)}, bf16[4,5,48,384]{3,2,1,0:T(8,128)(2,1)}, u32[]{:S(2)}, u32[]{:S(2)}) collective-permute-start(bf16[4,5,48,384]{3,2,1,0:T(8,128)(2,1)S(1)} %fusion.2.refs_13_), channel_id=1, source_target_pairs={{0,4},{2,6},{4,0},{6,2},{8,12},{10,14},{12,8},{14,10},{16,20},{18,... | collective-permute-start | bytes 2211848 | tf_op jit(solution)/shard_map/ppermute | solution.py:1125
  187.8 22.2 %collective-permute-start.8 = (bf16[256,768]{1,0:T(8,128)(2,1)}, bf16[256,768]{1,0:T(8,128)(2,1)S(1)}, u32[]{:S(2)}, u32[]{:S(2)}) collective-permute-start(bf16[256,768]{1,0:T(8,128)(2,1)} %get-tuple-element.106), channel_id=1, source_target_pairs={{0,1},{1,0},{2,3},{3,2},{4,5},{5,4},{6,7},{7,6},{8,9},{9,8},{10,11... | collective-permute-start | bytes 1179656 | tf_op jit(solution)/shard_map/ppermute | solution.py:1122
  188.4 29.1 %collective-permute-start.11 = (bf16[4,224,384]{2,1,0:T(8,128)(2,1)S(1)}, bf16[4,224,384]{2,1,0:T(8,128)(2,1)}, u32[]{:S(2)}, u32[]{:S(2)}) collective-permute-start(bf16[4,224,384]{2,1,0:T(8,128)(2,1)S(1)} %copy-done.8), channel_id=1, source_target_pairs={{0,1},{1,0},{2,3},{3,2},{4,5},{5,4},{6,7},{7,6},{8,9},{9,8},{10,11... | collective-permute-start | bytes 2064392 | tf_op jit(solution)/shard_map/ppermute | solution.py:1122
  207.1 2.1 copy-start.1
  209.4 23.0 %collective-permute-start.13 = (bf16[2,4,160,256]{3,2,1,0:T(8,128)(2,1)S(1)}, bf16[2,4,160,256]{3,2,1,0:T(8,128)(2,1)}, u32[]{:S(2)}, u32[]{:S(2)}) collective-permute-start(bf16[2,4,160,256]{3,2,1,0:T(8,128)(2,1)S(1)} %fusion.7.refs_7_), channel_id=1, source_target_pairs={{0,4},{2,6},{4,0},{6,2},{8,12},{10,14},{12,8},{14,10},{16,20},{18,... | collective-permute-start | bytes 1966088 | tf_op jit(solution)/shard_map/ppermute | solution.py:1125
  215.8 7.7 %collective-permute-start.10 = (bf16[2,2,4,160,128]{4,3,2,1,0:T(8,128)(2,1)}, bf16[2,2,4,160,128]{4,3,2,1,0:T(8,128)(2,1)S(1)}, u32[]{:S(2)}, u32[]{:S(2)}) collective-permute-start(bf16[2,2,4,160,128]{4,3,2,1,0:T(8,128)(2,1)} %get-tuple-element.113), channel_id=1, source_target_pairs={{0,2},{2,0},{4,6},{6,4},{8,10},{10,8},{12,14},{14,12},{16,18},{18,... | collective-permute-start | bytes 1966088 | tf_op jit(solution)/shard_map/ppermute | solution.py:1125
  217.5 5.7 %copy-start.21 = (bf16[1,5,48,384]{3,2,1,0:T(8,128)(2,1)S(1)}, bf16[1,5,48,384]{3,2,1,0:T(8,128)(2,1)}, u32[]{:S(2)}) copy-start(bf16[1,5,48,384]{3,2,1,0:T(8,128)(2,1)} %get-tuple-element.145) | copy-start | bytes 552964
  219.5 4.0 %copy-start.2 = (bf16[2,2,4,160,128]{4,3,2,1,0:T(8,128)(2,1)S(1)}, bf16[2,2,4,160,128]{4,3,2,1,0:T(8,128)(2,1)}, u32[]{:S(2)}) copy-start(bf16[2,2,4,160,128]{4,3,2,1,0:T(8,128)(2,1)} %get-tuple-element.112.refs_12_) | copy-start | bytes 1966084
  219.6 5.8 %copy-start.13 = (bf16[464,384]{1,0:T(8,128)(2,1)}, bf16[464,384]{1,0:T(8,128)(2,1)S(1)}, u32[]{:S(2)}) copy-start(bf16[464,384]{1,0:T(8,128)(2,1)S(1)} %pad_maximum_fusion.3.refs_16_) | copy-start | bytes 1069060
  219.6 28.7 %collective-permute-start.22 = (bf16[464,384]{1,0:T(8,128)(2,1)S(1)}, bf16[464,384]{1,0:T(8,128)(2,1)}, u32[]{:S(2)}, u32[]{:S(2)}) collective-permute-start(bf16[464,384]{1,0:T(8,128)(2,1)S(1)} %pad_maximum_fusion.3.refs_16_), channel_id=1, source_target_pairs={{0,24},{2,26},{4,28},{6,30},{8,16},{10,18},{12,20},{14,22},{16,8},... | collective-permute-start | bytes 1069064 | tf_op jit(solution)/shard_map/ppermute | solution.py:1125
  223.4 2.8 %copy-start.14 = (bf16[464,384]{1,0:T(8,128)(2,1)}, bf16[464,384]{1,0:T(8,128)(2,1)S(1)}, u32[]{:S(2)}) copy-start(bf16[464,384]{1,0:T(8,128)(2,1)S(1)} %pad_maximum_fusion.2.refs_15_) | copy-start | bytes 1069060
  223.4 30.9 %collective-permute-start.21 = (bf16[464,384]{1,0:T(8,128)(2,1)S(1)}, bf16[464,384]{1,0:T(8,128)(2,1)}, u32[]{:S(2)}, u32[]{:S(2)}) collective-permute-start(bf16[464,384]{1,0:T(8,128)(2,1)S(1)} %pad_maximum_fusion.2.refs_15_), channel_id=1, source_target_pairs={{0,16},{2,18},{4,20},{6,22},{8,24},{10,26},{12,28},{14,30},{16,0},... | collective-permute-start | bytes 1069064 | tf_op jit(solution)/shard_map/ppermute | solution.py:1125
  223.6 2.6 copy-start.16
  223.7 10.0 %collective-permute-start.14 = (bf16[2,4,160,128]{3,2,1,0:T(8,128)(2,1)S(1)}, bf16[2,4,160,128]{3,2,1,0:T(8,128)(2,1)}, u32[]{:S(2)}, u32[]{:S(2)}) collective-permute-start(bf16[2,4,160,128]{3,2,1,0:T(8,128)(2,1)S(1)} %fusion.32.refs_13_), channel_id=1, source_target_pairs={{0,4},{2,6},{4,0},{6,2},{8,12},{10,14},{12,8},{14,10},{16,20},{18,... | collective-permute-start | bytes 983048 | tf_op jit(solution)/shard_map/ppermute | solution.py:1125
  225.4 28.9 %collective-permute-start.20 = (bf16[464,384]{1,0:T(8,128)(2,1)S(1)}, bf16[464,384]{1,0:T(8,128)(2,1)}, u32[]{:S(2)}, u32[]{:S(2)}) collective-permute-start(bf16[464,384]{1,0:T(8,128)(2,1)S(1)} %pad_maximum_fusion.1.refs_14_), channel_id=1, source_target_pairs={{0,8},{2,10},{4,12},{6,14},{8,0},{10,2},{12,4},{14,6},{16,24},{18,... | collective-permute-start | bytes 1069064 | tf_op jit(solution)/shard_map/ppermute | solution.py:1125
  234.9 21.6 %collective-permute-start.16 = (bf16[4,160,384]{2,1,0:T(8,128)(2,1)S(1)}, bf16[4,160,384]{2,1,0:T(8,128)(2,1)}, u32[]{:S(2)}, u32[]{:S(2)}) collective-permute-start(bf16[4,160,384]{2,1,0:T(8,128)(2,1)S(1)} %pad_maximum_fusion.refs_9_), channel_id=1, source_target_pairs={{0,1},{1,0},{2,3},{3,2},{4,5},{5,4},{6,7},{7,6},{8,9},{9,8},{10,11... | collective-permute-start | bytes 1474568 | tf_op jit(solution)/shard_map/ppermute | solution.py:1122
  241.3 33.3 %collective-permute-start.15 = (bf16[512,768]{1,0:T(8,128)(2,1)}, bf16[512,768]{1,0:T(8,128)(2,1)S(1)}, u32[]{:S(2)}, u32[]{:S(2)}) collective-permute-start(bf16[512,768]{1,0:T(8,128)(2,1)} %get-tuple-element.119), channel_id=1, source_target_pairs={{0,1},{1,0},{2,3},{3,2},{4,5},{5,4},{6,7},{7,6},{8,9},{9,8},{10,11... | collective-permute-start | bytes 2359304 | tf_op jit(solution)/shard_map/ppermute | solution.py:1122
  243.6 4.5 %copy-start.23 = (bf16[1,1,5,48,384]{4,3,2,1,0:T(8,128)(2,1)S(1)}, bf16[1,1,5,48,384]{4,3,2,1,0:T(8,128)(2,1)}, u32[]{:S(2)}) copy-start(bf16[1,1,5,48,384]{4,3,2,1,0:T(8,128)(2,1)} %get-tuple-element.139) | copy-start | bytes 552964
  243.7 4.5 %copy-start.24 = (bf16[1,5,48,384]{3,2,1,0:T(8,128)(2,1)S(1)}, bf16[1,5,48,384]{3,2,1,0:T(8,128)(2,1)}, u32[]{:S(2)}) copy-start(bf16[1,5,48,384]{3,2,1,0:T(8,128)(2,1)} %get-tuple-element.143) | copy-start | bytes 552964
  255.7 16.0 %copy-start.26 = (f32[160,256]{1,0:T(8,128)S(1)}, f32[160,256]{1,0:T(8,128)}, u32[]{:S(2)}) copy-start(f32[160,256]{1,0:T(8,128)} %get-tuple-element.134) | copy-start | bytes 491524
  257.6 9.1 %collective-permute-start.17 = (bf16[160,384]{1,0:T(8,128)(2,1)S(1)}, bf16[160,384]{1,0:T(8,128)(2,1)S(1)}, u32[]{:S(2)}, u32[]{:S(2)}) collective-permute-start(bf16[160,384]{1,0:T(8,128)(2,1)S(1)} %get-tuple-element.155), channel_id=1, source_target_pairs={{0,8},{2,10},{4,12},{6,14},{8,0},{10,2},{12,4},{14,6},{16,24},{18,... | collective-permute-start | bytes 368648 | tf_op jit(solution)/shard_map/ppermute | solution.py:1125
  257.6 9.4 %collective-permute-start.19 = (bf16[160,384]{1,0:T(8,128)(2,1)S(1)}, bf16[160,384]{1,0:T(8,128)(2,1)S(1)}, u32[]{:S(2)}, u32[]{:S(2)}) collective-permute-start(bf16[160,384]{1,0:T(8,128)(2,1)S(1)} %get-tuple-element.156), channel_id=1, source_target_pairs={{0,24},{2,26},{4,28},{6,30},{8,16},{10,18},{12,20},{14,22},{16,8},... | collective-permute-start | bytes 368648 | tf_op jit(solution)/shard_map/ppermute | solution.py:1125
  260.2 11.5 %collective-permute-start.18 = (bf16[160,384]{1,0:T(8,128)(2,1)S(1)}, bf16[160,384]{1,0:T(8,128)(2,1)S(1)}, u32[]{:S(2)}, u32[]{:S(2)}) collective-permute-start(bf16[160,384]{1,0:T(8,128)(2,1)S(1)} %get-tuple-element.157), channel_id=1, source_target_pairs={{0,16},{2,18},{4,20},{6,22},{8,24},{10,26},{12,28},{14,30},{16,0},... | collective-permute-start | bytes 368648 | tf_op jit(solution)/shard_map/ppermute | solution.py:1125
  (12 other events, 13.2 us)

commit v5 on v4

--- a/solution.py
+++ b/solution.py
@@ -391,7 +391,7 @@
             vmem_limit_bytes=VMEM_LIMIT, dimension_semantics=("arbitrary",) * len(grid)
         ),
         cost_estimate=pl.CostEstimate(
-            flops=int(micros * 1e7), bytes_accessed=0, transcendentals=0
+            flops=int(micros * 1e10), bytes_accessed=1, transcendentals=0
         ),
         name=name,
     )(*operands, *held.values(), *passes, *after)
@@ -829,68 +829,96 @@
     )
 
 
-def projection_grad_kernel(with_sums, core_ref, h_ref, d_ref, sums_ref, keep_ref, send_ref):
-    step = pl.program_id(0)
-    res = mm(h_ref[...], d_ref[0], TN)
-    rows = res.shape[0] // 16
-    units = res.shape[1] // UNIT
-    columns = [[slice(u * UNIT, (u + 1) * UNIT) for u in range(x, units, 2)] for x in range(2)]
+def rounded(x):
+    return x.astype(BF16).astype(F32)
+
+
+def sum_second(keep, came, came1):
+    total = rounded(keep.astype(F32) + came.astype(F32))
+    return rounded(total + came1.astype(F32))
+
+
+def quarter_kernel(plan, at_ref, *refs):
+    outs = refs[-4:]
+    here = at_ref[2]
+    for d in range(4):
+        z = lax.bitwise_xor(here, d)
+        for first, count, row, column, through in plan:
+            keep_ref, came_ref, came1_ref = refs[first : first + 3]
+            came2_ref = refs[through]
+            rows, part = keep_ref.shape[3:]
+            total = sum_second(keep_ref[0, 0, z], came_ref[0, 0, z], came1_ref[0, z])
+            came2 = came2_ref[z, :, column : column + part]
+            outs[d][row : row + rows, column : column + part] = rounded(
+                total + came2.astype(F32)
+            ).astype(BF16)
+
+
+def quarter(at, states, total_rows, total_width, passes, after):
+    specs, operands, plan, seen = [], [], [], {}
+    for keep, came, came1, came2, axis, row, column in states:
+        _, _, depth, rows, part = keep.shape
+        if axis == 0:
+            both = pl.BlockSpec((1, 1, depth, rows, part), lambda i, s: (s[0], s[1], 0, 0, 0))
+            one = pl.BlockSpec((1, depth, rows, part), lambda i, s: (s[1], 0, 0, 0))
+        else:
+            both = pl.BlockSpec((1, 1, depth, rows, part), lambda i, s: (s[1], s[0], 0, 0, 0))
+            one = pl.BlockSpec((1, depth, rows, part), lambda i, s: (s[0], 0, 0, 0))
+        first = len(operands)
+        specs += [both, both, one]
+        operands += [keep, came, came1]
+        if id(came2) not in seen:
+            seen[id(came2)] = len(operands)
+            specs.append(fixed(came2.shape))
+            operands.append(came2)
+        plan.append((first, 3, row, column, seen[id(came2)]))
+    part = jax.ShapeDtypeStruct((total_rows, total_width), BF16)
+    return run(
+        functools.partial(quarter_kernel, plan),
+        "quarter",
+        (1,),
+        (at, *operands),
+        specs,
+        (part,) * 4,
+        (pl.BlockSpec((total_rows, total_width), lambda i, s: (0, 0)),) * 4,
+        scalars=1,
+        passes=passes,
+        after=after,
+    )
+
+
+def projection_part(core_ref, h_ref, grads, sums, keep_ref, send_ref):
+    rows = h_ref.shape[1] // 16
     even = core_ref[0] == 0
     for s in range(3):
-
-        @pl.when(step == s)
-        def _(s=s):
-            place = slice(s * rows, (s + 1) * rows)
-            for z in range(4):
-                for y in range(2):
-                    base = (z * 2 + y) * 2 * rows
-                    for x in range(2):
-                        zero = lanes(*[res[base : base + rows, c] for c in columns[x]])
-                        one = lanes(*[res[base + rows : base + 2 * rows, c] for c in columns[x]])
-                        keep_ref[y, x, z, place, :] = jnp.where(even, zero, one).astype(BF16)
-                        send_ref[y, x, z, place, :] = jnp.where(even, one, zero).astype(BF16)
-
-    @pl.when(step == 0)
-    def _():
-        extra = jnp.zeros((BIAS_ROWS, keep_ref.shape[4]), F32)
-        if with_sums:
-            at = lax.broadcasted_iota(jnp.int32, extra.shape, 0)
-            count = sums_ref.shape[1] // UNIT
-            for r in range(2):
-                for u in range(count):
-                    part = sums_ref[r : r + 1, u * UNIT : (u + 1) * UNIT]
-                    extra = jnp.where(at == r * count + u, part, extra)
+        place = slice(s * rows, (s + 1) * rows)
+        parts = [mm(h_ref[...], ref[s], TN) for ref in grads]
         for z in range(4):
             for y in range(2):
+                base = (z * 2 + y) * 2 * rows
                 for x in range(2):
-                    keep_ref[y, x, z, 3 * rows :, :] = extra.astype(BF16)
-                    send_ref[y, x, z, 3 * rows :, :] = extra.astype(BF16)
-
-
-def projection_grad_call(core, h, dqkv, sums, at, span, with_sums, passes, after):
-    length, width = h.shape
-    shape = (2, 2, 4, 3 * width // 16 + BIAS_ROWS, span // 2)
-    kinds, specs = pair_out(shape, shape, lambda s: (0, 0, 0, 0, 0))
-    return run(
-        functools.partial(projection_grad_kernel, with_sums),
-        "projection_grad",
-        (3,),
-        (core, h, dqkv, sums),
-        [
-            SCALAR,
-            fixed((length, width)),
-            pl.BlockSpec((1, length, span), lambda s: (s, 0, at)),
-            fixed(sums.shape),
-        ],
-        kinds,
-        specs,
-        passes=passes,
-        after=after,
-        micros=2.5,
-    )
+                    unit = slice(x * UNIT, (x + 1) * UNIT)
+                    zero = lanes(*[p[base : base + rows, unit] for p in parts])
+                    one = lanes(*[p[base + rows : base + 2 * rows, unit] for p in parts])
+                    keep_ref[y, x, z, place, :] = jnp.where(even, zero, one).astype(BF16)
+                    send_ref[y, x, z, place, :] = jnp.where(even, one, zero).astype(BF16)
+    extra = jnp.zeros((BIAS_ROWS, keep_ref.shape[4]), F32)
+    at = lax.broadcasted_iota(jnp.int32, extra.shape, 0)
+    for r in range(2):
+        for g, ref in enumerate(sums):
+            for x in range(2):
+                part = ref[r : r + 1, x * UNIT : (x + 1) * UNIT]
+                extra = jnp.where(at == (r * len(sums) + g) * 2 + x, part, extra)
+    for z in range(4):
+        for y in range(2):
+            for x in range(2):
+                keep_ref[y, x, z, 3 * rows :, :] = extra.astype(BF16)
+                send_ref[y, x, z, 3 * rows :, :] = extra.astype(BF16)
 
 
 def attention_backward_kernel(
+    others,
+    before,
     q_ref,
     k_ref,
     v_ref,
@@ -898,14 +926,16 @@
     ctx_pair_ref,
     lse_ref,
     seg_ref,
-    grads_ref,
-    sums_ref,
-    delta_ref,
-    total_ref,
-    kt_ref,
-    dctx_ref,
-    segc_ref,
+    *refs,
 ):
+    delta_ref, total_ref, kt_ref, dctx_ref, segc_ref = refs[-5:]
+    if others is None:
+        grads_ref, sums_ref = refs[:2]
+    else:
+        core_ref, h_ref = refs[:2]
+        other_refs = refs[2 : 2 + others]
+        before_refs = refs[2 + others : 2 + others + before]
+        grads_ref, sums_ref, keep_ref, send_ref = refs[-9:-5]
     length = q_ref.shape[0]
     dctx_ref[...] = lanes(dctx_pair_ref[0], dctx_pair_ref[1])
     ctx = lanes(ctx_pair_ref[0], ctx_pair_ref[1])
@@ -952,31 +982,44 @@
     sums_ref[...] = jnp.zeros_like(sums_ref)
     sums_ref[0:1, :] = row_sum(dq.astype(F32))
     sums_ref[1:2, :] = dv_sum
-
-
-def attention_backward(g, q, k, v, dctx, ctx, lse, seg, held, passes, after):
+    if others is not None:
+        sums = (*before_refs, sums_ref) if before else ()
+        projection_part(core_ref, h_ref, (*other_refs, grads_ref), sums, keep_ref, send_ref)
+
+
+def attention_backward(g, q, k, v, dctx, ctx, lse, seg, weights, passes, after):
     length, width = q.shape
     rows = pl.BlockSpec((length, GROUP), lambda i: (0, g))
     pair_rows = pl.BlockSpec((2, length, UNIT), lambda i: (0, 0, g))
+    operands = [q, k, v, dctx, ctx, lse, seg]
+    specs = [
+        rows,
+        rows,
+        rows,
+        pair_rows,
+        pair_rows,
+        pl.BlockSpec((8, length), lambda i: (g, 0)),
+        fixed((1, length)),
+    ]
+    kinds = [jax.ShapeDtypeStruct((3, length, GROUP), BF16), jax.ShapeDtypeStruct((8, GROUP), F32)]
+    outs = [fixed((3, length, GROUP)), fixed((8, GROUP))]
+    others, before = None, 0
+    if weights:
+        core, h, grads, sums = weights
+        others, before = len(grads), len(sums)
+        operands += [core, h, *grads, *sums]
+        specs += [SCALAR] + [fixed(x.shape) for x in (h, *grads, *sums)]
+        shape = (2, 2, 4, 3 * width // 16 + BIAS_ROWS, (others + 1) * UNIT)
+        kinds += [jax.ShapeDtypeStruct(shape, BF16)] * 2
+        outs += [fixed(shape)] * 2
     return run(
-        attention_backward_kernel,
+        functools.partial(attention_backward_kernel, others, before),
         "attention_backward",
         (1,),
-        (q, k, v, dctx, ctx, lse, seg),
-        [
-            rows,
-            rows,
-            rows,
-            pair_rows,
-            pair_rows,
-            pl.BlockSpec((8, length), lambda i: (g, 0)),
-            fixed((1, length)),
-        ],
-        (jax.ShapeDtypeStruct((3, length, width), BF16), jax.ShapeDtypeStruct((8, width), F32)),
-        (
-            pl.BlockSpec((3, length, GROUP), lambda i: (0, 0, g)),
-            pl.BlockSpec((8, GROUP), lambda i: (0, g)),
-        ),
+        tuple(operands),
+        specs,
+        kinds,
+        outs,
         [
             pltpu.VMEM((8, length), F32),
             pltpu.VMEM((GROUP, length), F32),
@@ -984,35 +1027,31 @@
             pltpu.VMEM((length, GROUP), BF16),
             pltpu.VMEM((length, 1), F32),
         ],
-        held=dict(enumerate(held)),
         passes=passes,
         after=after,
         micros=8,
     )
 
 
-def hidden_total(fp_ref, d_ref, wq_ref, wk_ref, wv_ref):
+def hidden_total(fp_ref, d_refs, w_refs):
     total = fp_ref[...]
-    for at, w_ref in enumerate((wq_ref, wk_ref, wv_ref)):
-        units = d_ref.shape[2] // UNIT
-        order = list(range(0, units, 2)) + list(range(1, units, 2))
-        d = lanes(*[d_ref[at, :, u * UNIT : (u + 1) * UNIT] for u in order])
+    for at, w_ref in enumerate(w_refs):
+        d = lanes(*[ref[at, :, x * UNIT : (x + 1) * UNIT] for x in range(2) for ref in d_refs])
         total = total + mm(d, w_ref[...], NT)
     return total
 
 
-def hidden_away_kernel(fp_ref, d_ref, wq_ref, wk_ref, wv_ref, out_ref):
-    out_ref[...] = hidden_total(fp_ref, d_ref, wq_ref, wk_ref, wv_ref).astype(BF16)
-
-
-def hidden_home_kernel(
-    here_ref, fp_ref, d_ref, wq_ref, wk_ref, wv_ref, came0_ref, came1_ref, out_ref, layer_ref
-):
-    out_ref[0] = hidden_total(fp_ref, d_ref, wq_ref, wk_ref, wv_ref)
+def hidden_away_kernel(fp_ref, *refs):
+    refs[6][...] = hidden_total(fp_ref, refs[:3], refs[3:6]).astype(BF16)
+
+
+def hidden_home_kernel(here_ref, fp_ref, *refs):
+    came0_ref, came1_ref, out_ref, layer_ref = refs[6:]
+    out_ref[0] = hidden_total(fp_ref, refs[:3], refs[3:6])
     layer_ref[0] = jnp.where(pl.program_id(0) == 0, came0_ref[...], came1_ref[...])
 
 
-def hidden_away(fp, dqkv, wq, wk, wv, passes, after):
+def hidden_away(fp, d0, d1, d2, wq, wk, wv, passes, after):
     length, width = fp.shape
     half = length // 2
     steps = half // TILE
@@ -1020,11 +1059,11 @@
         hidden_away_kernel,
         "hidden_away",
         (steps,),
-        (fp, dqkv, wq, wk, wv),
+        (fp, d0, d1, d2, wq, wk, wv),
         [
             pl.BlockSpec((TILE, width), lambda i: (i + steps, 0)),
-            pl.BlockSpec((3, TILE, width), lambda i: (0, i + steps, 0)),
         ]
+        + [pl.BlockSpec((3, TILE, GROUP), lambda i: (0, i + steps, 0))] * 3
         + [fixed((width, width))] * 3,
         (jax.ShapeDtypeStruct((half, width), BF16),),
         (pl.BlockSpec((TILE, width), lambda i: (i, 0)),),
@@ -1034,7 +1073,7 @@
     )
 
 
-def hidden_home(here, fp, dqkv, wq, wk, wv, came0, came1, layer, passes, after):
+def hidden_home(here, fp, d0, d1, d2, wq, wk, wv, came0, came1, layer, passes, after):
     length, width = fp.shape
     half = length // 2
     steps = half // TILE
@@ -1042,11 +1081,11 @@
         hidden_home_kernel,
         "hidden_home",
         (steps,),
-        (here, fp, dqkv, wq, wk, wv, came0, came1),
+        (here, fp, d0, d1, d2, wq, wk, wv, came0, came1),
         [
             pl.BlockSpec((TILE, width), lambda i, b: (i, 0)),
-            pl.BlockSpec((3, TILE, width), lambda i, b: (0, i, 0)),
         ]
+        + [pl.BlockSpec((3, TILE, GROUP), lambda i, b: (0, i, 0))] * 3
         + [fixed((width, width))] * 3
         + [fixed((TILE, width))] * 2,
         (
@@ -1127,6 +1166,8 @@
     def row(x):
         return x.astype(F32)[None, :]
 
+    at = jnp.stack([here, y_at, z_at]).astype(jnp.int32)
+
     def rounded(x):
         return lax.reduce_precision(x, 8, 7)
 
@@ -1188,44 +1229,43 @@
     b_away = sum_0(b, x_away).astype(BF16)
     b1 = trade(b_away)
     bwd = (q, k, v, dctx, ctx, lse, seg)
-    held = attention_backward(0, *bwd, (), (), (a_away, b_away))
-    *held, a_keep, b_keep = attention_backward(1, *bwd, held, (a_keep, b_keep), ())
+    grads0, bias0 = attention_backward(0, *bwd, (), (), (a_away, b_away))
+    grads1, bias1, c_keep, c_send, a_keep, b_keep, out_came0 = attention_backward(
+        1, *bwd, (core_id, h, (grads0,), ()), (a_keep, b_keep, out_came0), ()
+    )
+    c0 = seq_swap(c_send, 1)
     a = (a_keep, a0, a1)
     a_away = sum_1(a, y_mine, x_away).astype(BF16)
     a2 = trade(a_away)
-    c_keep, c_send, b_keep, out_came0 = projection_grad_call(
-        core_id, h, held[0], sums, 0, 2 * GROUP, False, (b_keep, out_came0), (a_away,)
-    )
-    c0 = seq_swap(c_send, 1)
     b = (b_keep, b0, b1)
     b_away = sum_1(b, x_mine, y_away).astype(BF16)
     b2 = seq_swap(b_away, 2)
-    dqkv, sums2, a_keep, b_keep, c_keep = attention_backward(
-        2, *bwd, held, (a_keep, b_keep, c_keep), (c_send, b_away)
-    )
+    grads2, _, d_keep, d_send, a_keep, b_keep, c_keep = attention_backward(
+        2, *bwd, (core_id, h, (), (bias0, bias1)), (a_keep, b_keep, c_keep), (a_away, b_away)
+    )
+    d0 = seq_swap(d_send, 1)
     c = (c_keep, c0)
     c_away = sum_0(c, y_away).astype(BF16)
     c1 = seq_swap(c_away, 2)
-    d_keep, d_send, a_keep, b_keep, out_came1 = projection_grad_call(
-        core_id, h, dqkv, sums2, 2, GROUP, True, (a_keep, b_keep, out_came1), (c_away,)
-    )
-    d0 = seq_swap(d_send, 1)
-    a = (a_keep, a0, a1, a2)
-    b = (b_keep, b0, b1, b2)
-
-    def both(z):
-        a_part = sum_2(a, y_mine, x_mine, z)
-        b_part = sum_2(b, x_mine, y_mine, z)
-        return jnp.concatenate([a_part, b_part.reshape(-1, width // 2)], axis=0)
-
-    parts = [both(z_at ^ e).astype(BF16) for e in (1, 2, 3)]
+
+    def flat(x):
+        return x.reshape(*x.shape[:-3], -1, x.shape[-1])
+
+    a_rows, b_rows = a_keep.shape[3], 5 * width // 16
+    states = [
+        (a_keep, a0, a1, a2, 1, 0, 0),
+        (flat(b_keep), flat(b0), flat(b1), flat(b2), 0, a_rows, 0),
+    ]
+    ab_mine, *parts, out_came1, d_keep = quarter(
+        at, states, a_rows + b_rows, width // 2, (out_came1, d_keep), (c_away,)
+    )
     ab3 = send_z(parts)
-    args = (fp, dqkv, query_matrix, key_matrix, value_matrix)
+    args = (fp, grads0, grads1, grads2, query_matrix, key_matrix, value_matrix)
     d = (d_keep, d0)
     d_away = sum_0(d, y_away).astype(BF16)
     d1 = seq_swap(d_away, 2)
-    hidden_grad, layer_out, a_keep, b_keep, c_keep, d_keep = hidden_home(
-        here_id, *args, out_came0, out_came1, out, (a_keep, b_keep, c_keep, d_keep), (d_away, *parts)
+    hidden_grad, layer_out, c_keep, d_keep = hidden_home(
+        here_id, *args, out_came0, out_came1, out, (c_keep, d_keep), (d_away,)
     )
     c = (c_keep, c0, c1)
     d = (d_keep, d0, d1)
@@ -1238,20 +1278,16 @@
 
     e_away = late_1(x_away).astype(BF16)
     e2 = trade(e_away)
-    far_grad, a_keep, b_keep, c_keep, d_keep = hidden_away(
-        *args, (a_keep, b_keep, c_keep, d_keep), (e_away,)
-    )
+    far_grad, c_keep, d_keep, ab_mine = hidden_away(*args, (c_keep, d_keep, ab_mine), (e_away,))
     came = trade(far_grad)
     c = (c_keep, c0, c1)
     d = (d_keep, d0, d1)
-    a = (a_keep, a0, a1, a2)
-    b = (b_keep, b0, b1, b2)
 
     def late_2(z):
         return rounded(late_1(x_mine, z) + pick(e2, z).astype(F32))
 
     e3 = send_z([late_2(z_at ^ e).astype(BF16) for e in (1, 2, 3)])
-    early = add_z(both(z_at), ab3)
+    early = add_z(ab_mine.astype(F32), ab3)
     hidden_grad = place_far(here_id, came, hidden_grad, ())[0]
     late = add_z(late_2(z_at), e3)
     rows = width // 16

time: 280 us -> 267 us (0.954)
  local copies, waits for them, and re-layouts: 23.9 us -> 15.3 us
  other arithmetic: 24.9 us -> 18.6 us
  starting transfers between devices: 25.1 us -> 29.7 us
    ppermute x9, waiting for transfers between devices: 21 us -> 14.9 us  [trade(): return lax.ppermute(x, 'blk', [(0, 1), (1, 0)])]
    ppermute x14, waiting for transfers between devices: 11.1 us -> 16.1 us  [seq_swap(): return lax.ppermute(x, 'seq', [(i, i ^ bit) for i in range(16)])]
    dynamic_slice x3 -> x1, local copies, waits for them, and re-layouts: 4.98 us -> 0.01 us  [pick(): return lax.dynamic_slice(x, start, size).reshape(x.shape[len(at):])]
    ppermute x14, starting transfers between devices: 14 us -> 18.8 us  [seq_swap(): return lax.ppermute(x, 'seq', [(i, i ^ bit) for i in range(16)])]
    reduce_precision x6 -> x2, other arithmetic: 7.1 us -> 2.26 us  [rounded(): return lax.reduce_precision(x, 8, 7)]
    unnamed x74 -> x50, local copies, waits for them, and re-layouts: 6.11 us -> 2.41 us
    pallas_call x12 -> x11, Pallas kernels: 170 us -> 169 us  [run(): pl.pallas_call(body, grid_spec=pltpu.PrefetchScalarGridSpec(num_scalar_pr...]
  transfers between devices with their start and end apart: 23 -> 23, of which waited for: 6 -> 5; matrix products, arithmetic and copies ran while one was open for 15% -> 11% of each run, Pallas kernels for 39% -> 36%
where the time goes in v5:
time: 267 us; the launch traced here: 266 us
  Pallas kernels  169 us (63%)
  waiting for transfers between devices  31.1 us (12%)
  starting transfers between devices  29.7 us (11%)
  other arithmetic  18.6 us (7%)
  local copies, waits for them, and re-layouts  15.3 us (6%)
    pallas_call x11, Pallas kernels, run(): pl.pallas_call(body, grid_spec=pltpu.PrefetchScalarGridSpec(num_scalar_pr...  169 us
    ppermute x14, starting transfers between devices, seq_swap(): return lax.ppermute(x, 'seq', [(i, i ^ bit) for i in range(16)])  18.8 us
    ppermute x14, waiting for transfers between devices, seq_swap(): return lax.ppermute(x, 'seq', [(i, i ^ bit) for i in range(16)])  16.1 us
    ppermute x9, waiting for transfers between devices, trade(): return lax.ppermute(x, 'blk', [(0, 1), (1, 0)])  14.9 us
    ppermute x9, starting transfers between devices, trade(): return lax.ppermute(x, 'blk', [(0, 1), (1, 0)])  10.9 us
  transfers between devices with their start and end apart: 23, of which 5 were waited for; matrix products, arithmetic and copies ran while one was open for 11% of the time, Pallas kernels for 36%

profile of v5, /device:TPU:0, one launch (start us, length us, event | category | flops | bytes accessed | tf_op | source)
XLA Modules:
  0.0 265.5 jit_solution(4917621241218835222)
XLA Ops:
  0.8 1.3 dynamic-slice_bitcast_fusion.1
  2.1 3.0 %collective-permute-start = (bf16[512,768]{1,0:T(8,128)(2,1)S(1)}, bf16[512,768]{1,0:T(8,128)(2,1)S(1)}, u32[]{:S(2)}, u32[]{:S(2)}) collective-permute-start(bf16[512,768]{1,0:T(8,128)(2,1)S(1)} %dynamic-slice_bitcast_fusion.1), channel_id=1, source_target_pairs={{0,1},{1,0},{2,3},{3,2},{4,5},{5,4},{6,7},{7,6},{8,9},{9,8},{10,11... | collective-permute-start | bytes 2359304 | tf_op jit(solution)/shard_map/ppermute | solution.py:1161
  7.1 0.6 concatenate.23.refs_9_
  7.7 14.9 %collective-permute-done.1 = s32[512]{0:T(512)S(1)} collective-permute-done((s32[512]{0:T(512)S(1)}, s32[512]{0:T(512)S(1)}, u32[]{:S(2)}, u32[]{:S(2)}) %collective-permute-start.1) | collective-permute-done | bytes 2080 | tf_op jit(solution)/shard_map/ppermute | solution.py:1161
  23.9 0.9 dynamic-slice_bitcast_fusion
  24.9 1.7 collective-permute-start.2
  26.6 0.9 copy-done.22
  27.5 26.4 %attention_forward.1 = (bf16[1024,768]{1,0:T(8,128)(2,1)}, bf16[1024,768]{1,0:T(8,128)(2,1)}, bf16[1024,768]{1,0:T(8,128)(2,1)}, bf16[2,1024,384]{2,1,0:T(8,128)...) custom-call(s32[1]{0:T(128)} %bitcast.refs_0_, bf16[2,512,768]{2,1,0:T(8,128)(2,1)} %refs_1_.1, ...), custom_call_target="tpu_custom_call" | custom-call | flops 160000000000 | bytes 1 | tf_op jit(solution)/shard_map/attention_forward/pallas_call | solution.py:379
  53.9 50.2 %token_pass.1 = (bf16[2,512,768]{2,1,0:T(8,128)(2,1)}, bf16[256,768]{1,0:T(8,128)(2,1)}, bf16[256,768]{1,0:T(8,128)(2,1)}, bf16[1024,768]{1,0:T(8,128)(2,1)}, bf...) custom-call(s32[1]{0:T(128)} %bitcast.refs_0_, ...), custom_call_target="tpu_custom_call" | custom-call | flops 230000001024 | bytes 1 | tf_op jit(solution)/shard_map/token_pass/pallas_call | solution.py:379
  104.2 9.4 %outer_grad.1 = (bf16[2,2,4,224,384]{4,3,2,1,0:T(8,128)(2,1)}, bf16[2,2,4,224,384]{4,3,2,1,0:T(8,128)(2,1)}) custom-call(s32[1]{0:T(128)} %bitcast.8.refs_0_.refs_7_, bf16[1024,3072]{1,0:T(8,128)(2,1)} %get-tuple-element.80.refs_1_, bf16[1024,768]{1,0:T(8,128)(2,1)} %get-tuple-element.81.refs_2_, f32[8,768]{1,0:T(8,128)} %get-tuple-element.82.refs_3_, ...), custom_call_target="tpu_custom_call" | custom-call | flops 44999999488 | bytes 1 | tf_op jit(solution)/shard_map/outer_grad/pallas_call | solution.py:379
  113.6 11.8 %inner_grad.1 = (bf16[2,2,4,5,48,384]{5,4,3,2,1,0:T(8,128)(2,1)}, bf16[2,2,4,5,48,384]{5,4,3,2,1,0:T(8,128)(2,1)}, bf16[2,2,4,224,384]{4,3,2,1,0:T(8,128)(2,1)}) custom-call(s32[1]{0:T(128)} %bitcast.8.refs_0_.refs_7_, bf16[1024,768]{1,0:T(8,128)(2,1)} %get-tuple-element.77.refs_1_, ...), custom_call_target="tpu_custom_call", output_to_operand_aliasing={{2}: (6, {})} | custom-call | flops 60000002048 | bytes 1 | tf_op jit(solution)/shard_map/inner_grad/pallas_call | solution.py:379
  126.8 1.7 collective-permute-start.10
  128.5 6.5 %collective-permute-done.3.refs_2_ = bf16[2,2,4,224,384]{4,3,2,1,0:T(8,128)(2,1)} collective-permute-done((bf16[2,2,4,224,384]{4,3,2,1,0:T(8,128)(2,1)}, bf16[2,2,4,224,384]{4,3,2,1,0:T(8,128)(2,1)}, u32[]{:S(2)}, u32[]{:S(2)}) %collective-permute-start.3) | collective-permute-done | bytes 2752544 | tf_op jit(solution)/shard_map/ppermute | solution.py:1164
  135.1 3.3 %fusion.3.refs_7_ = bf16[2,4,224,384]{3,2,1,0:T(8,128)(2,1)} fusion(bf16[2,2,4,224,384]{4,3,2,1,0:T(8,128)(2,1)} %collective-permute-done.3.refs_2_, s32[]{:T(128)S(6)} %select_n.42, bf16[2,2,4,224,384]{4,3,2,1,0:T(8,128)(2,1)} %get-tuple-element.85.refs_10_), kind=kLoop, calls=%fused_computation.6 | loop fusion | flops 3440640 | bytes 4128772 | tf_op jit(solution)/shard_map/convert_element_type | solution.py:1226
  138.4 1.5 collective-permute-start.6
  139.9 1.9 fusion.refs_8_
  142.6 15.6 %attention_backward.3 = (bf16[3,1024,256]{2,1,0:T(8,128)(2,1)}, f32[8,256]{1,0:T(8,128)}) custom-call(bf16[1024,768]{1,0:T(8,128)(2,1)} %get-tuple-element.72.refs_0_, bf16[1024,768]{1,0:T(8,128)(2,1)} %get-tuple-element.73.refs_1_, bf16[1024,768]{1,0:T(8,128)(2,1)} %get-tuple-element.74.refs_2_, bf16[2,1024,384]{2,1,0:T(8,128)(2,1)} %get-tuple-element.75.refs_3_, ...), custom_call_target="tpu_custom_call" | custom-call | flops 80000000000 | bytes 1 | tf_op jit(solution)/shard_map/attention_backward/pallas_call | solution.py:379
  158.2 0.7 copy-done.24
  159.0 19.2 %attention_backward.4 = (bf16[3,1024,256]{2,1,0:T(8,128)(2,1)}, f32[8,256]{1,0:T(8,128)}, bf16[2,2,4,160,256]{4,3,2,1,0:T(8,128)(2,1)}, bf16[2,2,4,160,256]{4,3,...) custom-call(bf16[1024,768]{1,0:T(8,128)(2,1)} %get-tuple-element.72., ...), custom_call_target="tpu_custom_call", output_to_operand_aliasing={{4}: (10, {}), {5}: (11, {}), {6}: (12, {})} | custom-call | flops 80000000000 | bytes 1 | tf_op jit(solution)/shard_map/attention_backward/pallas_call | solution.py:379
  178.2 1.8 fusion.5.refs_14_
  180.0 1.5 collective-permute-start.8
  181.6 1.9 fusion.2.refs_15_
  184.3 17.2 %attention_backward.5 = (bf16[3,1024,256]{2,1,0:T(8,128)(2,1)}, f32[8,256]{1,0:T(8,128)}, bf16[2,2,4,160,128]{4,3,2,1,0:T(8,128)(2,1)}, bf16[2,2,4,160,128]{4,3,...) custom-call(bf16[1024,768]{1,0:T(8,128)(2,1)} %get-tuple-element.72., ...), custom_call_target="tpu_custom_call", output_to_operand_aliasing={{4}: (11, {}), {5}: (12, {}), {6}: (13, {})} | custom-call | flops 80000000000 | bytes 1 | tf_op jit(solution)/shard_map/attention_backward/pallas_call | solution.py:379
  201.7 1.2 fusion.6.refs_11_
  203.0 1.1 collective-permute-start.13
  204.1 5.0 %quarter.1 = (bf16[464,384]{1,0:T(8,128)(2,1)}, bf16[464,384]{1,0:T(8,128)(2,1)}, bf16[464,384]{1,0:T(8,128)(2,1)}, bf16[464,384]{1,0:T(8,128)(2,1)}, bf16[256,7...) custom-call(s32[3]{0:T(128)} %pad_add_fusion.1.refs_0_, ...), custom_call_target="tpu_custom_call", output_to_operand_aliasing={{4}: (9, {}), {5}: (10, {})} | custom-call | flops 10000000000 | bytes 1 | tf_op jit(solution)/shard_map/quarter/pallas_call | solution.py:379
  209.1 1.1 fusion.9.refs_13_
  210.2 1.1 collective-permute-start.14
  211.2 1.6 collective-permute-start.20
  212.8 2.6 collective-permute-start.21
  215.6 6.1 %hidden_home.1 = (f32[2,512,768]{2,1,0:T(8,128)}, bf16[2,512,768]{2,1,0:T(8,128)(2,1)}, bf16[2,2,4,160,256]{4,3,2,1,0:T(8,128)(2,1)}, bf16[2,2,4,160,128]{4,3,2,1,0:T(8,128)(2,1)}) custom-call(s32[1]{0:T(128)} %bitcast.refs_0_, f32[1024,768]{1,0:T(8,128)} %get-tuple-element.71.refs_1_.refs_0_, ...), custom_call_target="tpu_custom_call", output_to_operand_aliasing={{1}: (10, {}), {2}: (11, {}), {3}: (12, {})} | custom-call | flops 30000001024 | bytes 1 | tf_op jit(solution)/shard_map/hidden_home/pallas_call | solution.py:379
  221.7 1.2 fusion.8
  223.0 4.0 %collective-permute-done.14 = bf16[2,4,160,128]{3,2,1,0:T(8,128)(2,1)S(1)} collective-permute-done((bf16[2,4,160,128]{3,2,1,0:T(8,128)(2,1)S(1)}, bf16[2,4,160,128]{3,2,1,0:T(8,128)(2,1)S(1)}, u32[]{:S(2)}, u32[]{:S(2)}) %collective-permute-start.14) | collective-permute-done | bytes 327712 | tf_op jit(solution)/shard_map/ppermute | solution.py:1164
  227.0 1.1 fusion.11
  229.0 5.7 %hidden_away.1 = (bf16[512,768]{1,0:T(8,128)(2,1)}, bf16[2,2,4,160,256]{4,3,2,1,0:T(8,128)(2,1)}, bf16[2,2,4,160,128]{4,3,2,1,0:T(8,128)(2,1)}, bf16[464,384]{1,0:T(8,128)(2,1)}) custom-call(f32[1024,768]{1,0:T(8,128)} %get-tuple-element.71.refs_1_.refs_0_, ...), custom_call_target="tpu_custom_call", output_to_operand_aliasing={{1}: (7, {}), {2}: (8, {}), {3}: (9, {})} | custom-call | flops 30000001024 | bytes 1 | tf_op jit(solution)/shard_map/hidden_away/pallas_call | solution.py:379
  234.6 1.3 collective-permute-start.15
  236.0 0.9 fusion.27
  236.9 1.3 fusion.23
  238.2 2.3 collective-permute-done.21
  240.6 1.4 add_add_fusion
  242.0 0.8 fusion.30
  242.8 7.0 %collective-permute-start.17 = (bf16[160,384]{1,0:T(8,128)(2,1)S(1)}, bf16[160,384]{1,0:T(8,128)(2,1)S(1)}, u32[]{:S(2)}, u32[]{:S(2)}) collective-permute-start(bf16[160,384]{1,0:T(8,128)(2,1)S(1)} %get-tuple-element.137), channel_id=1, source_target_pairs={{0,8},{2,10},{4,12},{6,14},{8,0},{10,2},{12,4},{14,6},{16,24},{18,... | collective-permute-start | bytes 368648 | tf_op jit(solution)/shard_map/ppermute | solution.py:1164
  249.8 1.1 collective-permute-start.18
  250.9 1.4 collective-permute-start.19
  252.9 0.7 copy.54
  257.9 3.2 %collective-permute-done.18 = bf16[160,384]{1,0:T(8,128)(2,1)S(1)} collective-permute-done((bf16[160,384]{1,0:T(8,128)(2,1)S(1)}, bf16[160,384]{1,0:T(8,128)(2,1)S(1)}, u32[]{:S(2)}, u32[]{:S(2)}) %collective-permute-start.18) | collective-permute-done | bytes 122912 | tf_op jit(solution)/shard_map/ppermute | solution.py:1164
  262.4 0.7 fusion.31
  263.1 2.2 place_far.1
  (109 shorter events, 13.2 us)
Async XLA Ops:
  0.7 4.4 %copy-start.12 = (s32[2,512]{1,0:T(2,128)S(1)}, s32[2,512]{1,0:T(2,128)}, u32[]{:S(2)}) copy-start(s32[2,512]{1,0:T(2,128)} %param.19) | copy-start | bytes 12292
  0.7 4.5 %copy-start.14 = (bf16[768]{0:T(1024)(128)(2,1)S(1)}, bf16[768]{0:T(1024)(128)(2,1)}, u32[]{:S(2)}) copy-start(bf16[768]{0:T(1024)(128)(2,1)} %param.21) | copy-start | bytes 4612
  0.7 5.1 %copy-start.15 = (bf16[768]{0:T(1024)(128)(2,1)S(1)}, bf16[768]{0:T(1024)(128)(2,1)}, u32[]{:S(2)}) copy-start(bf16[768]{0:T(1024)(128)(2,1)} %param.24) | copy-start | bytes 4612
  0.7 5.7 %copy-start.16 = (bf16[768]{0:T(1024)(128)(2,1)S(1)}, bf16[768]{0:T(1024)(128)(2,1)}, u32[]{:S(2)}) copy-start(bf16[768]{0:T(1024)(128)(2,1)} %param.26) | copy-start | bytes 4612
  0.7 5.7 %copy-start.17 = (bf16[768]{0:T(1024)(128)(2,1)S(1)}, bf16[768]{0:T(1024)(128)(2,1)}, u32[]{:S(2)}) copy-start(bf16[768]{0:T(1024)(128)(2,1)} %param.27) | copy-start | bytes 4612
  0.7 5.7 %copy-start.18 = (bf16[768]{0:T(1024)(128)(2,1)S(1)}, bf16[768]{0:T(1024)(128)(2,1)}, u32[]{:S(2)}) copy-start(bf16[768]{0:T(1024)(128)(2,1)} %param.28) | copy-start | bytes 4612
  0.7 5.7 %copy-start.19 = (bf16[768]{0:T(1024)(128)(2,1)S(1)}, bf16[768]{0:T(1024)(128)(2,1)}, u32[]{:S(2)}) copy-start(bf16[768]{0:T(1024)(128)(2,1)} %param.32) | copy-start | bytes 4612
  0.7 5.7 %copy-start.20 = (bf16[768]{0:T(1024)(128)(2,1)S(1)}, bf16[768]{0:T(1024)(128)(2,1)}, u32[]{:S(2)}) copy-start(bf16[768]{0:T(1024)(128)(2,1)} %param.33) | copy-start | bytes 4612
  0.7 5.7 %copy-start.21 = (bf16[768]{0:T(1024)(128)(2,1)S(1)}, bf16[768]{0:T(1024)(128)(2,1)}, u32[]{:S(2)}) copy-start(bf16[768]{0:T(1024)(128)(2,1)} %param.34) | copy-start | bytes 4612
  0.7 5.7 %copy-start.11 = (bf16[3072]{0:T(1024)(128)(2,1)S(1)}, bf16[3072]{0:T(1024)(128)(2,1)}, u32[]{:S(2)}) copy-start(bf16[3072]{0:T(1024)(128)(2,1)} %param.30) | copy-start | bytes 18436
  0.8 23.2 %copy-start.6 = (bf16[2,512,768]{2,1,0:T(8,128)(2,1)S(1)}, bf16[2,512,768]{2,1,0:T(8,128)(2,1)}, u32[]{:S(2)}) copy-start(bf16[2,512,768]{2,1,0:T(8,128)(2,1)} %refs_3_.3) | copy-start | bytes 4718596
  2.1 24.5 %collective-permute-start = (bf16[512,768]{1,0:T(8,128)(2,1)S(1)}, bf16[512,768]{1,0:T(8,128)(2,1)S(1)}, u32[]{:S(2)}, u32[]{:S(2)}) collective-permute-start(bf16[512,768]{1,0:T(8,128)(2,1)S(1)} %dynamic-slice_bitcast_fusion.1), channel_id=1, source_target_pairs={{0,1},{1,0},{2,3},{3,2},{4,5},{5,4},{6,7},{7,6},{8,9},{9,8},{10,11... | collective-permute-start | bytes 2359304 | tf_op jit(solution)/shard_map/ppermute | solution.py:1161
  5.1 17.6 %collective-permute-start.1 = (s32[512]{0:T(512)S(1)}, s32[512]{0:T(512)S(1)}, u32[]{:S(2)}, u32[]{:S(2)}) collective-permute-start(s32[512]{0:T(512)S(1)} %bitcast.117), channel_id=1, source_target_pairs={{0,1},{1,0},{2,3},{3,2},{4,5},{5,4},{6,7},{7,6},{8,9},{9,8},{10,11... | collective-permute-start | bytes 6152 | tf_op jit(solution)/shard_map/ppermute | solution.py:1161
  22.7 3.9 %copy-start.13 = (s32[1024]{0:T(1024)}, s32[1024]{0:T(1024)S(1)}, u32[]{:S(2)}) copy-start(s32[1024]{0:T(1024)S(1)} %pad_add_fusion) | copy-start | bytes 12292
  24.9 29.0 %collective-permute-start.2 = (bf16[512,768]{1,0:T(8,128)(2,1)}, bf16[512,768]{1,0:T(8,128)(2,1)}, u32[]{:S(2)}, u32[]{:S(2)}) collective-permute-start(bf16[512,768]{1,0:T(8,128)(2,1)} %dynamic-slice_bitcast_fusion), channel_id=1, source_target_pairs={{0,1},{1,0},{2,3},{3,2},{4,5},{5,4},{6,7},{7,6},{8,9},{9,8},{10,11... | collective-permute-start | bytes 2359304 | tf_op jit(solution)/shard_map/ppermute | solution.py:1161
  26.6 0.9 copy-start.22
  113.6 12.9 %copy-start.23 = (bf16[256,768]{1,0:T(8,128)(2,1)S(1)}, bf16[256,768]{1,0:T(8,128)(2,1)}, u32[]{:S(2)}) copy-start(bf16[256,768]{1,0:T(8,128)(2,1)} %get-tuple-element.90) | copy-start | bytes 1179652
  125.4 14.5 %collective-permute-start.4 = (bf16[2,2,4,5,48,384]{5,4,3,2,1,0:T(8,128)(2,1)}, bf16[2,2,4,5,48,384]{5,4,3,2,1,0:T(8,128)(2,1)S(1)}, u32[]{:S(2)}, u32[]{:S(2)}) collective-permute-start(bf16[2,2,4,5,48,384]{5,4,3,2,1,0:T(8,128)(2,1)} %get-tuple-element.88), channel_id=1, source_target_pairs={{0,2},{2,0},{4,6},{6,4},{8,10},{10,8},{12,14},{14,12},{16,18},{18,... | collective-permute-start | bytes 8847368 | tf_op jit(solution)/shard_map/ppermute | solution.py:1164
  125.4 9.7 %collective-permute-start.3 = (bf16[2,2,4,224,384]{4,3,2,1,0:T(8,128)(2,1)}, bf16[2,2,4,224,384]{4,3,2,1,0:T(8,128)(2,1)}, u32[]{:S(2)}, u32[]{:S(2)}) collective-permute-start(bf16[2,2,4,224,384]{4,3,2,1,0:T(8,128)(2,1)} %get-tuple-element.86), channel_id=1, source_target_pairs={{0,2},{2,0},{4,6},{6,4},{8,10},{10,8},{12,14},{14,12},{16,18},{18,... | collective-permute-start | bytes 8257544 | tf_op jit(solution)/shard_map/ppermute | solution.py:1164
  126.5 31.7 %collective-permute-start.5 = (bf16[256,768]{1,0:T(8,128)(2,1)S(1)}, bf16[256,768]{1,0:T(8,128)(2,1)S(1)}, u32[]{:S(2)}, u32[]{:S(2)}) collective-permute-start(bf16[256,768]{1,0:T(8,128)(2,1)S(1)} %copy-done.23), channel_id=1, source_target_pairs={{0,1},{1,0},{2,3},{3,2},{4,5},{5,4},{6,7},{7,6},{8,9},{9,8},{10,11... | collective-permute-start | bytes 1179656 | tf_op jit(solution)/shard_map/ppermute | solution.py:1161
  126.8 77.3 %collective-permute-start.10 = (bf16[256,768]{1,0:T(8,128)(2,1)}, bf16[256,768]{1,0:T(8,128)(2,1)}, u32[]{:S(2)}, u32[]{:S(2)}) collective-permute-start(bf16[256,768]{1,0:T(8,128)(2,1)} %get-tuple-element.101), channel_id=1, source_target_pairs={{0,1},{1,0},{2,3},{3,2},{4,5},{5,4},{6,7},{7,6},{8,9},{9,8},{10,11... | collective-permute-start | bytes 1179656 | tf_op jit(solution)/shard_map/ppermute | solution.py:1161
  135.1 4.9 %copy-start.1 = (bf16[2,2,4,5,48,384]{5,4,3,2,1,0:T(8,128)(2,1)S(1)}, bf16[2,2,4,5,48,384]{5,4,3,2,1,0:T(8,128)(2,1)}, u32[]{:S(2)}) copy-start(bf16[2,2,4,5,48,384]{5,4,3,2,1,0:T(8,128)(2,1)} %get-tuple-element.87.refs_11_) | copy-start | bytes 8847364
  138.4 39.8 %collective-permute-start.6 = (bf16[2,4,224,384]{3,2,1,0:T(8,128)(2,1)}, bf16[2,4,224,384]{3,2,1,0:T(8,128)(2,1)}, u32[]{:S(2)}, u32[]{:S(2)}) collective-permute-start(bf16[2,4,224,384]{3,2,1,0:T(8,128)(2,1)} %fusion.3.refs_7_), channel_id=1, source_target_pairs={{0,4},{2,6},{4,0},{6,2},{8,12},{10,14},{12,8},{14,10},{16,20},{18,... | collective-permute-start | bytes 4128776 | tf_op jit(solution)/shard_map/ppermute | solution.py:1164
  139.9 2.2 copy-start
  142.1 39.5 %collective-permute-start.7 = (bf16[2,4,5,48,384]{4,3,2,1,0:T(8,128)(2,1)}, bf16[2,4,5,48,384]{4,3,2,1,0:T(8,128)(2,1)}, u32[]{:S(2)}, u32[]{:S(2)}) collective-permute-start(bf16[2,4,5,48,384]{4,3,2,1,0:T(8,128)(2,1)} %fusion.refs_8_), channel_id=1, source_target_pairs={{0,1},{1,0},{2,3},{3,2},{4,5},{5,4},{6,7},{7,6},{8,9},{9,8},{10,11... | collective-permute-start | bytes 4423688 | tf_op jit(solution)/shard_map/ppermute | solution.py:1161
  158.2 0.8 copy-start.24
  178.2 23.5 %collective-permute-start.11 = (bf16[2,2,4,160,256]{4,3,2,1,0:T(8,128)(2,1)}, bf16[2,2,4,160,256]{4,3,2,1,0:T(8,128)(2,1)S(1)}, u32[]{:S(2)}, u32[]{:S(2)}) collective-permute-start(bf16[2,2,4,160,256]{4,3,2,1,0:T(8,128)(2,1)} %get-tuple-element.104), channel_id=1, source_target_pairs={{0,2},{2,0},{4,6},{6,4},{8,10},{10,8},{12,14},{14,12},{16,18},{18,... | collective-permute-start | bytes 3932168 | tf_op jit(solution)/shard_map/ppermute | solution.py:1164
  180.0 4.0 %copy-start.3 = (bf16[4,224,384]{2,1,0:T(8,128)(2,1)}, bf16[4,224,384]{2,1,0:T(8,128)(2,1)S(1)}, u32[]{:S(2)}) copy-start(bf16[4,224,384]{2,1,0:T(8,128)(2,1)S(1)} %fusion.5.refs_14_) | copy-start | bytes 2064388
  180.0 24.1 %collective-permute-start.8 = (bf16[4,224,384]{2,1,0:T(8,128)(2,1)S(1)}, bf16[4,224,384]{2,1,0:T(8,128)(2,1)}, u32[]{:S(2)}, u32[]{:S(2)}) collective-permute-start(bf16[4,224,384]{2,1,0:T(8,128)(2,1)S(1)} %fusion.5.refs_14_), channel_id=1, source_target_pairs={{0,1},{1,0},{2,3},{3,2},{4,5},{5,4},{6,7},{7,6},{8,9},{9,8},{10,11... | collective-permute-start | bytes 2064392 | tf_op jit(solution)/shard_map/ppermute | solution.py:1161
  183.5 0.9 copy-start.2
  183.5 20.6 %collective-permute-start.9 = (bf16[4,5,48,384]{3,2,1,0:T(8,128)(2,1)S(1)}, bf16[4,5,48,384]{3,2,1,0:T(8,128)(2,1)}, u32[]{:S(2)}, u32[]{:S(2)}) collective-permute-start(bf16[4,5,48,384]{3,2,1,0:T(8,128)(2,1)S(1)} %fusion.2.refs_15_), channel_id=1, source_target_pairs={{0,4},{2,6},{4,0},{6,2},{8,12},{10,14},{12,8},{14,10},{16,20},{18,... | collective-permute-start | bytes 2211848 | tf_op jit(solution)/shard_map/ppermute | solution.py:1164
  201.5 7.6 %collective-permute-start.12 = (bf16[2,2,4,160,128]{4,3,2,1,0:T(8,128)(2,1)}, bf16[2,2,4,160,128]{4,3,2,1,0:T(8,128)(2,1)S(1)}, u32[]{:S(2)}, u32[]{:S(2)}) collective-permute-start(bf16[2,2,4,160,128]{4,3,2,1,0:T(8,128)(2,1)} %get-tuple-element.108), channel_id=1, source_target_pairs={{0,2},{2,0},{4,6},{6,4},{8,10},{10,8},{12,14},{14,12},{16,18},{18,... | collective-permute-start | bytes 1966088 | tf_op jit(solution)/shard_map/ppermute | solution.py:1164
  203.0 1.1 copy-start.4
  203.0 18.8 %collective-permute-start.13 = (bf16[2,4,160,256]{3,2,1,0:T(8,128)(2,1)S(1)}, bf16[2,4,160,256]{3,2,1,0:T(8,128)(2,1)}, u32[]{:S(2)}, u32[]{:S(2)}) collective-permute-start(bf16[2,4,160,256]{3,2,1,0:T(8,128)(2,1)S(1)} %fusion.6.refs_11_), channel_id=1, source_target_pairs={{0,4},{2,6},{4,0},{6,2},{8,12},{10,14},{12,8},{14,10},{16,20},{18,... | collective-permute-start | bytes 1966088 | tf_op jit(solution)/shard_map/ppermute | solution.py:1164
  210.2 5.5 %copy-start.8 = (bf16[2,4,160,128]{3,2,1,0:T(8,128)(2,1)}, bf16[2,4,160,128]{3,2,1,0:T(8,128)(2,1)S(1)}, u32[]{:S(2)}) copy-start(bf16[2,4,160,128]{3,2,1,0:T(8,128)(2,1)S(1)} %fusion.9.refs_13_) | copy-start | bytes 983044
  210.2 16.8 %collective-permute-start.14 = (bf16[2,4,160,128]{3,2,1,0:T(8,128)(2,1)S(1)}, bf16[2,4,160,128]{3,2,1,0:T(8,128)(2,1)S(1)}, u32[]{:S(2)}, u32[]{:S(2)}) collective-permute-start(bf16[2,4,160,128]{3,2,1,0:T(8,128)(2,1)S(1)} %fusion.9.refs_13_), channel_id=1, source_target_pairs={{0,4},{2,6},{4,0},{6,2},{8,12},{10,14},{12,8},{14,10},{16,20},{18,... | collective-permute-start | bytes 983048 | tf_op jit(solution)/shard_map/ppermute | solution.py:1164
  211.2 27.0 %collective-permute-start.20 = (bf16[464,384]{1,0:T(8,128)(2,1)}, bf16[464,384]{1,0:T(8,128)(2,1)}, u32[]{:S(2)}, u32[]{:S(2)}) collective-permute-start(bf16[464,384]{1,0:T(8,128)(2,1)} %get-tuple-element.118), channel_id=1, source_target_pairs={{0,8},{2,10},{4,12},{6,14},{8,0},{10,2},{12,4},{14,6},{16,24},{18,... | collective-permute-start | bytes 1069064 | tf_op jit(solution)/shard_map/ppermute | solution.py:1164
  212.8 27.7 %collective-permute-start.21 = (bf16[464,384]{1,0:T(8,128)(2,1)}, bf16[464,384]{1,0:T(8,128)(2,1)}, u32[]{:S(2)}, u32[]{:S(2)}) collective-permute-start(bf16[464,384]{1,0:T(8,128)(2,1)} %get-tuple-element.119), channel_id=1, source_target_pairs={{0,16},{2,18},{4,20},{6,22},{8,24},{10,26},{12,28},{14,30},{16,0},... | collective-permute-start | bytes 1069064 | tf_op jit(solution)/shard_map/ppermute | solution.py:1164
  215.4 25.1 %collective-permute-start.22 = (bf16[464,384]{1,0:T(8,128)(2,1)}, bf16[464,384]{1,0:T(8,128)(2,1)}, u32[]{:S(2)}, u32[]{:S(2)}) collective-permute-start(bf16[464,384]{1,0:T(8,128)(2,1)} %get-tuple-element.120), channel_id=1, source_target_pairs={{0,24},{2,26},{4,28},{6,30},{8,16},{10,18},{12,20},{14,22},{16,8},... | collective-permute-start | bytes 1069064 | tf_op jit(solution)/shard_map/ppermute | solution.py:1164
  227.0 1.1 copy-start.9
  228.2 0.8 copy-start.5
  228.2 14.5 %collective-permute-start.16 = (bf16[4,160,384]{2,1,0:T(8,128)(2,1)S(1)}, bf16[4,160,384]{2,1,0:T(8,128)(2,1)S(1)}, u32[]{:S(2)}, u32[]{:S(2)}) collective-permute-start(bf16[4,160,384]{2,1,0:T(8,128)(2,1)S(1)} %pad_maximum_fusion.refs_10_), channel_id=1, source_target_pairs={{0,1},{1,0},{2,3},{3,2},{4,5},{5,4},{6,7},{7,6},{8,9},{9,8},{10,11... | collective-permute-start | bytes 1474568 | tf_op jit(solution)/shard_map/ppermute | solution.py:1161
  229.0 7.0 %copy-start.10 = (bf16[2,4,160,128]{3,2,1,0:T(8,128)(2,1)S(1)}, bf16[2,4,160,128]{3,2,1,0:T(8,128)(2,1)}, u32[]{:S(2)}) copy-start(bf16[2,4,160,128]{3,2,1,0:T(8,128)(2,1)} %copy-done.9) | copy-start | bytes 983044
  234.6 5.9 %copy-start.7 = (bf16[464,384]{1,0:T(8,128)(2,1)S(1)}, bf16[464,384]{1,0:T(8,128)(2,1)}, u32[]{:S(2)}) copy-start(bf16[464,384]{1,0:T(8,128)(2,1)} %get-tuple-element.117) | copy-start | bytes 1069060
  234.6 28.5 %collective-permute-start.15 = (bf16[512,768]{1,0:T(8,128)(2,1)}, bf16[512,768]{1,0:T(8,128)(2,1)}, u32[]{:S(2)}, u32[]{:S(2)}) collective-permute-start(bf16[512,768]{1,0:T(8,128)(2,1)} %get-tuple-element.113), channel_id=1, source_target_pairs={{0,1},{1,0},{2,3},{3,2},{4,5},{5,4},{6,7},{7,6},{8,9},{9,8},{10,11... | collective-permute-start | bytes 2359304 | tf_op jit(solution)/shard_map/ppermute | solution.py:1161
  242.8 15.1 %collective-permute-start.17 = (bf16[160,384]{1,0:T(8,128)(2,1)S(1)}, bf16[160,384]{1,0:T(8,128)(2,1)S(1)}, u32[]{:S(2)}, u32[]{:S(2)}) collective-permute-start(bf16[160,384]{1,0:T(8,128)(2,1)S(1)} %get-tuple-element.137), channel_id=1, source_target_pairs={{0,8},{2,10},{4,12},{6,14},{8,0},{10,2},{12,4},{14,6},{16,24},{18,... | collective-permute-start | bytes 368648 | tf_op jit(solution)/shard_map/ppermute | solution.py:1164
  249.8 11.3 %collective-permute-start.18 = (bf16[160,384]{1,0:T(8,128)(2,1)S(1)}, bf16[160,384]{1,0:T(8,128)(2,1)S(1)}, u32[]{:S(2)}, u32[]{:S(2)}) collective-permute-start(bf16[160,384]{1,0:T(8,128)(2,1)S(1)} %get-tuple-element.139), channel_id=1, source_target_pairs={{0,16},{2,18},{4,20},{6,22},{8,24},{10,26},{12,28},{14,30},{16,0},... | collective-permute-start | bytes 368648 | tf_op jit(solution)/shard_map/ppermute | solution.py:1164
  250.9 10.2 %collective-permute-start.19 = (bf16[160,384]{1,0:T(8,128)(2,1)S(1)}, bf16[160,384]{1,0:T(8,128)(2,1)S(1)}, u32[]{:S(2)}, u32[]{:S(2)}) collective-permute-start(bf16[160,384]{1,0:T(8,128)(2,1)S(1)} %get-tuple-element.138), channel_id=1, source_target_pairs={{0,24},{2,26},{4,28},{6,30},{8,16},{10,18},{12,20},{14,22},{16,8},... | collective-permute-start | bytes 368648 | tf_op jit(solution)/shard_map/ppermute | solution.py:1164

commit v6 on v5

--- a/solution.py
+++ b/solution.py
@@ -608,14 +608,8 @@
         n2, r2 = normed(x)
         out = (n2 * gain2 + shift2).astype(BF16)
 
-        @pl.when(near)
-        def _():
-            out_ref[0, rows, :] = out
-
-        @pl.when(jnp.logical_not(near))
-        def _():
-            (far1_ref if rows.start else far0_ref)[...] = out
-
+        out_ref[0, rows, :] = jnp.where(near, out, out_ref[0, rows, :])
+        (far1_ref if rows.start else far0_ref)[...] = out
         e = jnp.where(near, cot_own_ref[0, rows, :], cot_far_ref[rows, :]).astype(F32)
         sums_ref[0:1, :] += row_sum(e * n2)
         sums_ref[1:2, :] += row_sum(e)
@@ -715,11 +709,13 @@
     )
 
 
-def put_pairs(res, core_ref, keep_ref, send_ref, columns, rows, count):
+def put_pairs(a, b, core_ref, keep_ref, send_ref, columns, rows, count):
     even = core_ref[0] == 0
     for z in range(count):
+        if z % 2 == 0:
+            res = mm(a[:, 4 * z * rows : 4 * (z + 2) * rows], b, TN)
         for y in range(2):
-            base = (z * 2 + y) * 2 * rows
+            base = (z % 2 * 2 + y) * 2 * rows
             for x in range(2):
                 zero = lanes(*[res[base : base + rows, c] for c in columns[x]])
                 one = lanes(*[res[base + rows : base + 2 * rows, c] for c in columns[x]])
@@ -733,9 +729,8 @@
 
 
 def outer_grad_kernel(core_ref, act_ref, og_ref, sums_ref, isum_ref, keep_ref, send_ref, rows_ref):
-    res = mm(act_ref[...], og_ref[...], TN)
-    middle = res.shape[1] // 2
-    rows = res.shape[0] // 4
+    middle = og_ref.shape[1] // 2
+    rows = act_ref.shape[1] // 4
     even = core_ref[0] == 0
     rows_ref[...] = jnp.zeros_like(rows_ref)
     at = 0
@@ -748,10 +743,11 @@
         at += 1
     extra = rows_ref[...].astype(BF16)
     for y in range(2):
+        res = mm(act_ref[:, 2 * y * rows : 2 * (y + 1) * rows], og_ref[...], TN)
         for x in range(2):
             columns = slice(x * middle, (x + 1) * middle)
-            zero = res[2 * y * rows : (2 * y + 1) * rows, columns]
-            one = res[(2 * y + 1) * rows : (2 * y + 2) * rows, columns]
+            zero = res[0:rows, columns]
+            one = res[rows:, columns]
             keep_ref[y, x, 0, 0:rows, :] = jnp.where(even, zero, one).astype(BF16)
             send_ref[y, x, 0, 0:rows, :] = jnp.where(even, one, zero).astype(BF16)
             keep_ref[y, x, 0, rows:, :] = extra
@@ -796,13 +792,13 @@
 
     @pl.when(step < 4)
     def _():
-        res = mm(first_ref[...], lanes(low_ref[...], high_ref[...]), TN)
-        put_pairs(res, core_ref, keep_ref, send_ref, HALVES, rows, 4)
+        both = lanes(low_ref[...], high_ref[...])
+        put_pairs(first_ref[...], both, core_ref, keep_ref, send_ref, HALVES, rows, 4)
 
     @pl.when(step == 4)
     def _():
-        res = mm(lanes(ctx_ref[0], ctx_ref[1]), ag_ref[...], TN)
-        put_pairs(res, core_ref, keep_ref, send_ref, HALVES, rows, 4)
+        ctx = lanes(ctx_ref[0], ctx_ref[1])
+        put_pairs(ctx, ag_ref[...], core_ref, keep_ref, send_ref, HALVES, rows, 4)
 
 
 def inner_grad_call(core, first, ig, ctx, ag, passes):
@@ -831,6 +827,26 @@
 
 def rounded(x):
     return x.astype(BF16).astype(F32)
+
+
+def halve_first_kernel(at_ref, keep_ref, came_ref, out_ref):
+    out_ref[...] = (keep_ref[0].astype(F32) + came_ref[0].astype(F32)).astype(BF16)
+
+
+def halve_first(at, axis, keep, came, passes):
+    _, _, depth, rows, width = keep.shape
+    half = pl.BlockSpec((1, 2, depth, rows, width), lambda i, s: (1 - s[axis], 0, 0, 0, 0))
+    return run(
+        halve_first_kernel,
+        "halve_first",
+        (1,),
+        (at, keep, came),
+        [half, half],
+        (jax.ShapeDtypeStruct((2, depth, rows, width), BF16),),
+        (fixed((2, depth, rows, width)),),
+        scalars=1,
+        passes=passes,
+    )
 
 
 def sum_second(keep, came, came1):
@@ -1216,23 +1232,24 @@
     out, out_far0, out_far1, first, act, og, ig, fp, ag, dctx, sums, isum = token_pass(
         here_id, h, ctx, cotangent, cot_far, output_matrix, inner_matrix, outer_matrix, row(inner_bias), vec
     )
-    out_came0, out_came1 = trade(out_far0), trade(out_far1)
     x_mine, x_away, y_mine, y_away = here, 1 - here, y_at, 1 - y_at
     a_keep, a_send = outer_grad_call(core_id, act, og, sums, isum)
     a0 = seq_swap(a_send, 1)
     b_keep, b_send, a_keep = inner_grad_call(core_id, first, ig, ctx, ag, (a_keep,))
     b0 = seq_swap(b_send, 1)
     a = (a_keep, a0)
-    a_away = sum_0(a, y_away).astype(BF16)
+    a_away, out_far0 = halve_first(at, 1, a_keep, a0, (out_far0,))
     a1 = seq_swap(a_away, 2)
+    out_came0 = trade(out_far0)
     b = (b_keep, b0)
     b_away = sum_0(b, x_away).astype(BF16)
     b1 = trade(b_away)
     bwd = (q, k, v, dctx, ctx, lse, seg)
     grads0, bias0 = attention_backward(0, *bwd, (), (), (a_away, b_away))
-    grads1, bias1, c_keep, c_send, a_keep, b_keep, out_came0 = attention_backward(
-        1, *bwd, (core_id, h, (grads0,), ()), (a_keep, b_keep, out_came0), ()
-    )
+    grads1, bias1, c_keep, c_send, a_keep, b_keep, out_came0, out_far1 = attention_backward(
+        1, *bwd, (core_id, h, (grads0,), ()), (a_keep, b_keep, out_came0, out_far1), ()
+    )
+    out_came1 = trade(out_far1)
     c0 = seq_swap(c_send, 1)
     a = (a_keep, a0, a1)
     a_away = sum_1(a, y_mine, x_away).astype(BF16)

time: 267 us -> 261 us (0.978)
  waiting for transfers between devices: 31.1 us -> 24.8 us
    ppermute x14, waiting for transfers between devices: 16.1 us -> 9.72 us  [seq_swap(): return lax.ppermute(x, 'seq', [(i, i ^ bit) for i in range(16)])]
    convert_element_type x1 -> x0, other arithmetic: 3.34 us -> none  [fast(): a_away = sum_0(a, y_away).astype(BF16)]
    pallas_call x11 -> x12, Pallas kernels: 169 us -> 170 us  [run(): pl.pallas_call(body, grid_spec=pltpu.PrefetchScalarGridSpec(num_scalar_pr...]
  transfers between devices with their start and end apart: 23 -> 23, of which waited for: 5 -> 5; matrix products, arithmetic and copies ran while one was open for 11% -> 11% of each run, Pallas kernels for 36% -> 43%
where the time goes in v6:
time: 261 us; the launch traced here: 259 us
  Pallas kernels  170 us (65%)
  starting transfers between devices  29.5 us (11%)
  waiting for transfers between devices  24.8 us (10%)
  other arithmetic  17.4 us (7%)
  local copies, waits for them, and re-layouts  15.2 us (6%)
    pallas_call x12, Pallas kernels, run(): pl.pallas_call(body, grid_spec=pltpu.PrefetchScalarGridSpec(num_scalar_pr...  170 us
    ppermute x14, starting transfers between devices, seq_swap(): return lax.ppermute(x, 'seq', [(i, i ^ bit) for i in range(16)])  18.8 us
    ppermute x9, waiting for transfers between devices, trade(): return lax.ppermute(x, 'blk', [(0, 1), (1, 0)])  15.1 us
    ppermute x9, starting transfers between devices, trade(): return lax.ppermute(x, 'blk', [(0, 1), (1, 0)])  10.6 us
    ppermute x14, waiting for transfers between devices, seq_swap(): return lax.ppermute(x, 'seq', [(i, i ^ bit) for i in range(16)])  9.72 us
  transfers between devices with their start and end apart: 23, of which 5 were waited for; matrix products, arithmetic and copies ran while one was open for 11% of the time, Pallas kernels for 43%

profile of v6, /device:TPU:0, one launch (start us, length us, event | category | flops | bytes accessed | tf_op | source)
XLA Modules:
  0.0 258.6 jit_solution(5098314068625165729)
XLA Ops:
  0.8 1.3 dynamic-slice_bitcast_fusion.1
  2.1 3.0 %collective-permute-start = (bf16[512,768]{1,0:T(8,128)(2,1)S(1)}, bf16[512,768]{1,0:T(8,128)(2,1)S(1)}, u32[]{:S(2)}, u32[]{:S(2)}) collective-permute-start(bf16[512,768]{1,0:T(8,128)(2,1)S(1)} %dynamic-slice_bitcast_fusion.1), channel_id=1, source_target_pairs={{0,1},{1,0},{2,3},{3,2},{4,5},{5,4},{6,7},{7,6},{8,9},{9,8},{10,11... | collective-permute-start | bytes 2359304 | tf_op jit(solution)/shard_map/ppermute | solution.py:1177
  7.1 0.6 concatenate.23.refs_9_
  7.7 14.9 %collective-permute-done.1 = s32[512]{0:T(512)S(1)} collective-permute-done((s32[512]{0:T(512)S(1)}, s32[512]{0:T(512)S(1)}, u32[]{:S(2)}, u32[]{:S(2)}) %collective-permute-start.1) | collective-permute-done | bytes 2080 | tf_op jit(solution)/shard_map/ppermute | solution.py:1177
  23.9 0.9 dynamic-slice_bitcast_fusion
  24.9 1.7 collective-permute-start.2
  26.6 0.9 copy-done.21
  27.5 26.3 %attention_forward.1 = (bf16[1024,768]{1,0:T(8,128)(2,1)}, bf16[1024,768]{1,0:T(8,128)(2,1)}, bf16[1024,768]{1,0:T(8,128)(2,1)}, bf16[2,1024,384]{2,1,0:T(8,128)...) custom-call(s32[1]{0:T(128)} %bitcast.refs_0_, bf16[2,512,768]{2,1,0:T(8,128)(2,1)} %refs_1_.1, ...), custom_call_target="tpu_custom_call" | custom-call | flops 160000000000 | bytes 1 | tf_op jit(solution)/shard_map/attention_forward/pallas_call | solution.py:379
  53.9 48.1 %token_pass.1 = (bf16[2,512,768]{2,1,0:T(8,128)(2,1)}, bf16[256,768]{1,0:T(8,128)(2,1)}, bf16[256,768]{1,0:T(8,128)(2,1)}, bf16[1024,768]{1,0:T(8,128)(2,1)}, bf...) custom-call(s32[1]{0:T(128)} %bitcast.refs_0_, ...), custom_call_target="tpu_custom_call" | custom-call | flops 230000001024 | bytes 1 | tf_op jit(solution)/shard_map/token_pass/pallas_call | solution.py:379
  101.9 9.4 %outer_grad.1 = (bf16[2,2,4,224,384]{4,3,2,1,0:T(8,128)(2,1)}, bf16[2,2,4,224,384]{4,3,2,1,0:T(8,128)(2,1)}) custom-call(s32[1]{0:T(128)} %bitcast.10.refs_0_.refs_7_, bf16[1024,3072]{1,0:T(8,128)(2,1)} %get-tuple-element.83.refs_1_, bf16[1024,768]{1,0:T(8,128)(2,1)} %get-tuple-element.84.refs_2_, f32[8,768]{1,0:T(8,128)} %get-tuple-element.85.refs_3_, ...), custom_call_target="tpu_custom_call" | custom-call | flops 44999999488 | bytes 1 | tf_op jit(solution)/shard_map/outer_grad/pallas_call | solution.py:379
  111.4 11.6 %inner_grad.1 = (bf16[2,2,4,5,48,384]{5,4,3,2,1,0:T(8,128)(2,1)}, bf16[2,2,4,5,48,384]{5,4,3,2,1,0:T(8,128)(2,1)}, bf16[2,2,4,224,384]{4,3,2,1,0:T(8,128)(2,1)}) custom-call(s32[1]{0:T(128)} %bitcast.10.refs_0_.refs_7_, bf16[1024,768]{1,0:T(8,128)(2,1)} %get-tuple-element.80.refs_1_, ...), custom_call_target="tpu_custom_call", output_to_operand_aliasing={{2}: (6, {})} | custom-call | flops 60000002048 | bytes 1 | tf_op jit(solution)/shard_map/inner_grad/pallas_call | solution.py:379
  124.0 3.8 %halve_first.1 = (bf16[2,4,224,384]{3,2,1,0:T(8,128)(2,1)}, bf16[256,768]{1,0:T(8,128)(2,1)}) custom-call(s32[3]{0:T(128)} %pad_add_fusion.1.refs_0_, bf16[2,2,4,224,384]{4,3,2,1,0:T(8,128)(2,1)} %get-tuple-element.88.refs_1_.refs_10_, bf16[2,2,4,224,384]{4,3,2,1,0:T(8,128)(2,1)} %collective-permute-done.3.refs_2_, ...), custom_call_target="tpu_custom_call", output_to_operand_aliasing={{1}: (3, {})} | custom-call | flops 10000000000 | bytes 1 | tf_op jit(solution)/shard_map/halve_first/pallas_call | solution.py:379
  128.2 1.8 collective-permute-start.6
  129.9 4.0 %fusion.refs_8_ = bf16[2,4,5,48,384]{4,3,2,1,0:T(8,128)(2,1)} fusion(bf16[2,2,4,5,48,384]{5,4,3,2,1,0:T(8,128)(2,1)S(1)} %collective-permute-done.4, s32[]{:T(128)S(6)} %select_n.36, bf16[2,2,4,5,48,384]{5,4,3,2,1,0:T(8,128)(2,1)} %get-tuple-element.92.refs_11_), kind=kLoop, calls=%fused_computation.1 | loop fusion | flops 3686400 | bytes 4423684 | tf_op jit(solution)/shard_map/convert_element_type | solution.py:1245
  133.9 1.5 collective-permute-start.7
  135.4 15.2 %attention_backward.3 = (bf16[3,1024,256]{2,1,0:T(8,128)(2,1)}, f32[8,256]{1,0:T(8,128)}) custom-call(bf16[1024,768]{1,0:T(8,128)(2,1)} %get-tuple-element.75.refs_0_, bf16[1024,768]{1,0:T(8,128)(2,1)} %get-tuple-element.76.refs_1_, bf16[1024,768]{1,0:T(8,128)(2,1)} %get-tuple-element.77.refs_2_, bf16[2,1024,384]{2,1,0:T(8,128)(2,1)} %get-tuple-element.78.refs_3_, ...), custom_call_target="tpu_custom_call" | custom-call | flops 80000000000 | bytes 1 | tf_op jit(solution)/shard_map/attention_backward/pallas_call | solution.py:379
  150.6 0.8 copy-done.22
  151.4 19.2 %attention_backward.4 = (bf16[3,1024,256]{2,1,0:T(8,128)(2,1)}, f32[8,256]{1,0:T(8,128)}, bf16[2,2,4,160,256]{4,3,2,1,0:T(8,128)(2,1)}, bf16[2,2,4,160,256]{4,3,...) custom-call(bf16[1024,768]{1,0:T(8,128)(2,1)} %get-tuple-element.75., ...), custom_call_target="tpu_custom_call", output_to_operand_aliasing={{4}: (10, {}), {5}: (11, {}), {6}: (12, {}), {7}: (13, {})} | custom-call | flops 80000000000 | bytes 1 | tf_op jit(solution)/shard_map/attention_backward/pallas_call | solution.py:379
  171.1 1.8 fusion.4.refs_14_
  172.9 1.6 collective-permute-start.8
  174.5 1.9 fusion.2.refs_15_
  177.3 17.2 %attention_backward.5 = (bf16[3,1024,256]{2,1,0:T(8,128)(2,1)}, f32[8,256]{1,0:T(8,128)}, bf16[2,2,4,160,128]{4,3,2,1,0:T(8,128)(2,1)}, bf16[2,2,4,160,128]{4,3,...) custom-call(bf16[1024,768]{1,0:T(8,128)(2,1)} %get-tuple-element.75., ...), custom_call_target="tpu_custom_call", output_to_operand_aliasing={{4}: (11, {}), {5}: (12, {}), {6}: (13, {})} | custom-call | flops 80000000000 | bytes 1 | tf_op jit(solution)/shard_map/attention_backward/pallas_call | solution.py:379
  194.5 1.3 fusion.5.refs_11_
  195.8 1.2 collective-permute-start.13
  197.2 5.0 %quarter.1 = (bf16[464,384]{1,0:T(8,128)(2,1)}, bf16[464,384]{1,0:T(8,128)(2,1)}, bf16[464,384]{1,0:T(8,128)(2,1)}, bf16[464,384]{1,0:T(8,128)(2,1)}, bf16[256,7...) custom-call(s32[3]{0:T(128)} %pad_add_fusion.1.refs_0_, ...), custom_call_target="tpu_custom_call", output_to_operand_aliasing={{4}: (9, {}), {5}: (10, {})} | custom-call | flops 10000000000 | bytes 1 | tf_op jit(solution)/shard_map/quarter/pallas_call | solution.py:379
  202.2 1.1 fusion.8.refs_13_
  203.3 0.8 collective-permute-start.14
  204.1 1.6 collective-permute-start.20
  205.7 2.6 %collective-permute-start.21 = (bf16[464,384]{1,0:T(8,128)(2,1)}, bf16[464,384]{1,0:T(8,128)(2,1)}, u32[]{:S(2)}, u32[]{:S(2)}) collective-permute-start(bf16[464,384]{1,0:T(8,128)(2,1)} %get-tuple-element.125), channel_id=1, source_target_pairs={{0,16},{2,18},{4,20},{6,22},{8,24},{10,26},{12,28},{14,30},{16,0},... | collective-permute-start | bytes 1069064 | tf_op jit(solution)/shard_map/ppermute | solution.py:1180
  208.5 6.1 %hidden_home.1 = (f32[2,512,768]{2,1,0:T(8,128)}, bf16[2,512,768]{2,1,0:T(8,128)(2,1)}, bf16[2,2,4,160,256]{4,3,2,1,0:T(8,128)(2,1)}, bf16[2,2,4,160,128]{4,3,2,1,0:T(8,128)(2,1)}) custom-call(s32[1]{0:T(128)} %bitcast.refs_0_, f32[1024,768]{1,0:T(8,128)} %get-tuple-element.74.refs_1_.refs_0_, ...), custom_call_target="tpu_custom_call", output_to_operand_aliasing={{1}: (10, {}), {2}: (11, {}), {3}: (12, {})} | custom-call | flops 30000001024 | bytes 1 | tf_op jit(solution)/shard_map/hidden_home/pallas_call | solution.py:379
  214.6 1.2 fusion.7
  215.8 4.2 %collective-permute-done.14 = bf16[2,4,160,128]{3,2,1,0:T(8,128)(2,1)S(1)} collective-permute-done((bf16[2,4,160,128]{3,2,1,0:T(8,128)(2,1)S(1)}, bf16[2,4,160,128]{3,2,1,0:T(8,128)(2,1)S(1)}, u32[]{:S(2)}, u32[]{:S(2)}) %collective-permute-start.14) | collective-permute-done | bytes 327712 | tf_op jit(solution)/shard_map/ppermute | solution.py:1180
  220.0 1.1 fusion.10
  222.0 5.7 %hidden_away.1 = (bf16[512,768]{1,0:T(8,128)(2,1)}, bf16[2,2,4,160,256]{4,3,2,1,0:T(8,128)(2,1)}, bf16[2,2,4,160,128]{4,3,2,1,0:T(8,128)(2,1)}, bf16[464,384]{1,0:T(8,128)(2,1)}) custom-call(f32[1024,768]{1,0:T(8,128)} %get-tuple-element.74.refs_1_.refs_0_, ...), custom_call_target="tpu_custom_call", output_to_operand_aliasing={{1}: (7, {}), {2}: (8, {}), {3}: (9, {})} | custom-call | flops 30000001024 | bytes 1 | tf_op jit(solution)/shard_map/hidden_away/pallas_call | solution.py:379
  227.6 1.3 collective-permute-start.15
  229.0 0.9 fusion.26
  229.9 1.3 fusion.22
  231.2 2.1 collective-permute-done.21
  233.4 1.4 add_add_fusion
  234.8 0.8 fusion.29
  235.6 7.1 %collective-permute-start.17 = (bf16[160,384]{1,0:T(8,128)(2,1)S(1)}, bf16[160,384]{1,0:T(8,128)(2,1)S(1)}, u32[]{:S(2)}, u32[]{:S(2)}) collective-permute-start(bf16[160,384]{1,0:T(8,128)(2,1)S(1)} %get-tuple-element.143), channel_id=1, source_target_pairs={{0,8},{2,10},{4,12},{6,14},{8,0},{10,2},{12,4},{14,6},{16,24},{18,... | collective-permute-start | bytes 368648 | tf_op jit(solution)/shard_map/ppermute | solution.py:1180
  242.7 1.1 collective-permute-start.18
  243.8 1.4 collective-permute-start.19
  245.2 0.6 slice.102
  245.8 0.7 copy.56
  250.8 3.4 %collective-permute-done.18 = bf16[160,384]{1,0:T(8,128)(2,1)S(1)} collective-permute-done((bf16[160,384]{1,0:T(8,128)(2,1)S(1)}, bf16[160,384]{1,0:T(8,128)(2,1)S(1)}, u32[]{:S(2)}, u32[]{:S(2)}) %collective-permute-start.18) | collective-permute-done | bytes 122912 | tf_op jit(solution)/shard_map/ppermute | solution.py:1180
  255.5 0.7 fusion.30
  256.2 2.2 place_far.1
  (105 shorter events, 12.3 us)
Async XLA Ops:
  0.7 4.4 %copy-start.11 = (s32[2,512]{1,0:T(2,128)S(1)}, s32[2,512]{1,0:T(2,128)}, u32[]{:S(2)}) copy-start(s32[2,512]{1,0:T(2,128)} %param.19) | copy-start | bytes 12292
  0.7 4.5 %copy-start.13 = (bf16[768]{0:T(1024)(128)(2,1)S(1)}, bf16[768]{0:T(1024)(128)(2,1)}, u32[]{:S(2)}) copy-start(bf16[768]{0:T(1024)(128)(2,1)} %param.21) | copy-start | bytes 4612
  0.7 5.1 %copy-start.14 = (bf16[768]{0:T(1024)(128)(2,1)S(1)}, bf16[768]{0:T(1024)(128)(2,1)}, u32[]{:S(2)}) copy-start(bf16[768]{0:T(1024)(128)(2,1)} %param.24) | copy-start | bytes 4612
  0.7 5.7 %copy-start.15 = (bf16[768]{0:T(1024)(128)(2,1)S(1)}, bf16[768]{0:T(1024)(128)(2,1)}, u32[]{:S(2)}) copy-start(bf16[768]{0:T(1024)(128)(2,1)} %param.26) | copy-start | bytes 4612
  0.7 5.7 %copy-start.16 = (bf16[768]{0:T(1024)(128)(2,1)S(1)}, bf16[768]{0:T(1024)(128)(2,1)}, u32[]{:S(2)}) copy-start(bf16[768]{0:T(1024)(128)(2,1)} %param.27) | copy-start | bytes 4612
  0.7 5.7 %copy-start.17 = (bf16[768]{0:T(1024)(128)(2,1)S(1)}, bf16[768]{0:T(1024)(128)(2,1)}, u32[]{:S(2)}) copy-start(bf16[768]{0:T(1024)(128)(2,1)} %param.28) | copy-start | bytes 4612
  0.7 5.7 %copy-start.18 = (bf16[768]{0:T(1024)(128)(2,1)S(1)}, bf16[768]{0:T(1024)(128)(2,1)}, u32[]{:S(2)}) copy-start(bf16[768]{0:T(1024)(128)(2,1)} %param.32) | copy-start | bytes 4612
  0.7 5.7 %copy-start.19 = (bf16[768]{0:T(1024)(128)(2,1)S(1)}, bf16[768]{0:T(1024)(128)(2,1)}, u32[]{:S(2)}) copy-start(bf16[768]{0:T(1024)(128)(2,1)} %param.33) | copy-start | bytes 4612
  0.7 5.7 %copy-start.20 = (bf16[768]{0:T(1024)(128)(2,1)S(1)}, bf16[768]{0:T(1024)(128)(2,1)}, u32[]{:S(2)}) copy-start(bf16[768]{0:T(1024)(128)(2,1)} %param.34) | copy-start | bytes 4612
  0.7 5.7 %copy-start.10 = (bf16[3072]{0:T(1024)(128)(2,1)S(1)}, bf16[3072]{0:T(1024)(128)(2,1)}, u32[]{:S(2)}) copy-start(bf16[3072]{0:T(1024)(128)(2,1)} %param.30) | copy-start | bytes 18436
  0.8 23.2 %copy-start.5 = (bf16[2,512,768]{2,1,0:T(8,128)(2,1)S(1)}, bf16[2,512,768]{2,1,0:T(8,128)(2,1)}, u32[]{:S(2)}) copy-start(bf16[2,512,768]{2,1,0:T(8,128)(2,1)} %refs_3_.3) | copy-start | bytes 4718596
  2.1 24.5 %collective-permute-start = (bf16[512,768]{1,0:T(8,128)(2,1)S(1)}, bf16[512,768]{1,0:T(8,128)(2,1)S(1)}, u32[]{:S(2)}, u32[]{:S(2)}) collective-permute-start(bf16[512,768]{1,0:T(8,128)(2,1)S(1)} %dynamic-slice_bitcast_fusion.1), channel_id=1, source_target_pairs={{0,1},{1,0},{2,3},{3,2},{4,5},{5,4},{6,7},{7,6},{8,9},{9,8},{10,11... | collective-permute-start | bytes 2359304 | tf_op jit(solution)/shard_map/ppermute | solution.py:1177
  5.1 17.6 %collective-permute-start.1 = (s32[512]{0:T(512)S(1)}, s32[512]{0:T(512)S(1)}, u32[]{:S(2)}, u32[]{:S(2)}) collective-permute-start(s32[512]{0:T(512)S(1)} %bitcast.115), channel_id=1, source_target_pairs={{0,1},{1,0},{2,3},{3,2},{4,5},{5,4},{6,7},{7,6},{8,9},{9,8},{10,11... | collective-permute-start | bytes 6152 | tf_op jit(solution)/shard_map/ppermute | solution.py:1177
  22.7 3.9 %copy-start.12 = (s32[1024]{0:T(1024)}, s32[1024]{0:T(1024)S(1)}, u32[]{:S(2)}) copy-start(s32[1024]{0:T(1024)S(1)} %pad_add_fusion) | copy-start | bytes 12292
  24.9 29.0 %collective-permute-start.2 = (bf16[512,768]{1,0:T(8,128)(2,1)}, bf16[512,768]{1,0:T(8,128)(2,1)}, u32[]{:S(2)}, u32[]{:S(2)}) collective-permute-start(bf16[512,768]{1,0:T(8,128)(2,1)} %dynamic-slice_bitcast_fusion), channel_id=1, source_target_pairs={{0,1},{1,0},{2,3},{3,2},{4,5},{5,4},{6,7},{7,6},{8,9},{9,8},{10,11... | collective-permute-start | bytes 2359304 | tf_op jit(solution)/shard_map/ppermute | solution.py:1177
  26.6 0.9 copy-start.21
  111.4 12.7 %collective-permute-start.3 = (bf16[2,2,4,224,384]{4,3,2,1,0:T(8,128)(2,1)}, bf16[2,2,4,224,384]{4,3,2,1,0:T(8,128)(2,1)}, u32[]{:S(2)}, u32[]{:S(2)}) collective-permute-start(bf16[2,2,4,224,384]{4,3,2,1,0:T(8,128)(2,1)} %get-tuple-element.89), channel_id=1, source_target_pairs={{0,2},{2,0},{4,6},{6,4},{8,10},{10,8},{12,14},{14,12},{16,18},{18,... | collective-permute-start | bytes 8257544 | tf_op jit(solution)/shard_map/ppermute | solution.py:1180
  123.0 6.9 %collective-permute-start.4 = (bf16[2,2,4,5,48,384]{5,4,3,2,1,0:T(8,128)(2,1)}, bf16[2,2,4,5,48,384]{5,4,3,2,1,0:T(8,128)(2,1)S(1)}, u32[]{:S(2)}, u32[]{:S(2)}) collective-permute-start(bf16[2,2,4,5,48,384]{5,4,3,2,1,0:T(8,128)(2,1)} %get-tuple-element.93), channel_id=1, source_target_pairs={{0,2},{2,0},{4,6},{6,4},{8,10},{10,8},{12,14},{14,12},{16,18},{18,... | collective-permute-start | bytes 8847368 | tf_op jit(solution)/shard_map/ppermute | solution.py:1180
  127.9 22.7 %collective-permute-start.5 = (bf16[256,768]{1,0:T(8,128)(2,1)}, bf16[256,768]{1,0:T(8,128)(2,1)S(1)}, u32[]{:S(2)}, u32[]{:S(2)}) collective-permute-start(bf16[256,768]{1,0:T(8,128)(2,1)} %get-tuple-element.95), channel_id=1, source_target_pairs={{0,1},{1,0},{2,3},{3,2},{4,5},{5,4},{6,7},{7,6},{8,9},{9,8},{10,11... | collective-permute-start | bytes 1179656 | tf_op jit(solution)/shard_map/ppermute | solution.py:1177
  128.2 43.0 %collective-permute-start.6 = (bf16[2,4,224,384]{3,2,1,0:T(8,128)(2,1)}, bf16[2,4,224,384]{3,2,1,0:T(8,128)(2,1)}, u32[]{:S(2)}, u32[]{:S(2)}) collective-permute-start(bf16[2,4,224,384]{3,2,1,0:T(8,128)(2,1)} %get-tuple-element.91.refs_7_), channel_id=1, source_target_pairs={{0,4},{2,6},{4,0},{6,2},{8,12},{10,14},{12,8},{14,10},{16,20},{18,... | collective-permute-start | bytes 4128776 | tf_op jit(solution)/shard_map/ppermute | solution.py:1180
  129.9 4.0 %copy-start = (bf16[2,2,4,5,48,384]{5,4,3,2,1,0:T(8,128)(2,1)}, bf16[2,2,4,5,48,384]{5,4,3,2,1,0:T(8,128)(2,1)S(1)}, u32[]{:S(2)}) copy-start(bf16[2,2,4,5,48,384]{5,4,3,2,1,0:T(8,128)(2,1)S(1)} %collective-permute-done.4) | copy-start | bytes 8847364
  133.9 40.6 %collective-permute-start.7 = (bf16[2,4,5,48,384]{4,3,2,1,0:T(8,128)(2,1)}, bf16[2,4,5,48,384]{4,3,2,1,0:T(8,128)(2,1)}, u32[]{:S(2)}, u32[]{:S(2)}) collective-permute-start(bf16[2,4,5,48,384]{4,3,2,1,0:T(8,128)(2,1)} %fusion.refs_8_), channel_id=1, source_target_pairs={{0,1},{1,0},{2,3},{3,2},{4,5},{5,4},{6,7},{7,6},{8,9},{9,8},{10,11... | collective-permute-start | bytes 4423688 | tf_op jit(solution)/shard_map/ppermute | solution.py:1177
  150.6 0.8 copy-start.22
  170.6 23.9 %collective-permute-start.11 = (bf16[2,2,4,160,256]{4,3,2,1,0:T(8,128)(2,1)}, bf16[2,2,4,160,256]{4,3,2,1,0:T(8,128)(2,1)S(1)}, u32[]{:S(2)}, u32[]{:S(2)}) collective-permute-start(bf16[2,2,4,160,256]{4,3,2,1,0:T(8,128)(2,1)} %get-tuple-element.110), channel_id=1, source_target_pairs={{0,2},{2,0},{4,6},{6,4},{8,10},{10,8},{12,14},{14,12},{16,18},{18,... | collective-permute-start | bytes 3932168 | tf_op jit(solution)/shard_map/ppermute | solution.py:1180
  170.6 26.4 %collective-permute-start.10 = (bf16[256,768]{1,0:T(8,128)(2,1)}, bf16[256,768]{1,0:T(8,128)(2,1)}, u32[]{:S(2)}, u32[]{:S(2)}) collective-permute-start(bf16[256,768]{1,0:T(8,128)(2,1)} %get-tuple-element.107), channel_id=1, source_target_pairs={{0,1},{1,0},{2,3},{3,2},{4,5},{5,4},{6,7},{7,6},{8,9},{9,8},{10,11... | collective-permute-start | bytes 1179656 | tf_op jit(solution)/shard_map/ppermute | solution.py:1177
  172.9 4.0 %copy-start.2 = (bf16[4,224,384]{2,1,0:T(8,128)(2,1)}, bf16[4,224,384]{2,1,0:T(8,128)(2,1)S(1)}, u32[]{:S(2)}) copy-start(bf16[4,224,384]{2,1,0:T(8,128)(2,1)S(1)} %fusion.4.refs_14_) | copy-start | bytes 2064388
  172.9 24.2 %collective-permute-start.8 = (bf16[4,224,384]{2,1,0:T(8,128)(2,1)S(1)}, bf16[4,224,384]{2,1,0:T(8,128)(2,1)}, u32[]{:S(2)}, u32[]{:S(2)}) collective-permute-start(bf16[4,224,384]{2,1,0:T(8,128)(2,1)S(1)} %fusion.4.refs_14_), channel_id=1, source_target_pairs={{0,1},{1,0},{2,3},{3,2},{4,5},{5,4},{6,7},{7,6},{8,9},{9,8},{10,11... | collective-permute-start | bytes 2064392 | tf_op jit(solution)/shard_map/ppermute | solution.py:1177
  176.4 0.9 copy-start.1
  176.4 20.8 %collective-permute-start.9 = (bf16[4,5,48,384]{3,2,1,0:T(8,128)(2,1)S(1)}, bf16[4,5,48,384]{3,2,1,0:T(8,128)(2,1)}, u32[]{:S(2)}, u32[]{:S(2)}) collective-permute-start(bf16[4,5,48,384]{3,2,1,0:T(8,128)(2,1)S(1)} %fusion.2.refs_15_), channel_id=1, source_target_pairs={{0,4},{2,6},{4,0},{6,2},{8,12},{10,14},{12,8},{14,10},{16,20},{18,... | collective-permute-start | bytes 2211848 | tf_op jit(solution)/shard_map/ppermute | solution.py:1180
  194.5 7.7 %collective-permute-start.12 = (bf16[2,2,4,160,128]{4,3,2,1,0:T(8,128)(2,1)}, bf16[2,2,4,160,128]{4,3,2,1,0:T(8,128)(2,1)S(1)}, u32[]{:S(2)}, u32[]{:S(2)}) collective-permute-start(bf16[2,2,4,160,128]{4,3,2,1,0:T(8,128)(2,1)} %get-tuple-element.114), channel_id=1, source_target_pairs={{0,2},{2,0},{4,6},{6,4},{8,10},{10,8},{12,14},{14,12},{16,18},{18,... | collective-permute-start | bytes 1966088 | tf_op jit(solution)/shard_map/ppermute | solution.py:1180
  195.8 1.4 copy-start.3
  195.8 18.8 %collective-permute-start.13 = (bf16[2,4,160,256]{3,2,1,0:T(8,128)(2,1)S(1)}, bf16[2,4,160,256]{3,2,1,0:T(8,128)(2,1)}, u32[]{:S(2)}, u32[]{:S(2)}) collective-permute-start(bf16[2,4,160,256]{3,2,1,0:T(8,128)(2,1)S(1)} %fusion.5.refs_11_), channel_id=1, source_target_pairs={{0,4},{2,6},{4,0},{6,2},{8,12},{10,14},{12,8},{14,10},{16,20},{18,... | collective-permute-start | bytes 1966088 | tf_op jit(solution)/shard_map/ppermute | solution.py:1180
  203.3 5.2 %copy-start.7 = (bf16[2,4,160,128]{3,2,1,0:T(8,128)(2,1)}, bf16[2,4,160,128]{3,2,1,0:T(8,128)(2,1)S(1)}, u32[]{:S(2)}) copy-start(bf16[2,4,160,128]{3,2,1,0:T(8,128)(2,1)S(1)} %fusion.8.refs_13_) | copy-start | bytes 983044
  203.3 16.7 %collective-permute-start.14 = (bf16[2,4,160,128]{3,2,1,0:T(8,128)(2,1)S(1)}, bf16[2,4,160,128]{3,2,1,0:T(8,128)(2,1)S(1)}, u32[]{:S(2)}, u32[]{:S(2)}) collective-permute-start(bf16[2,4,160,128]{3,2,1,0:T(8,128)(2,1)S(1)} %fusion.8.refs_13_), channel_id=1, source_target_pairs={{0,4},{2,6},{4,0},{6,2},{8,12},{10,14},{12,8},{14,10},{16,20},{18,... | collective-permute-start | bytes 983048 | tf_op jit(solution)/shard_map/ppermute | solution.py:1180
  204.1 27.2 %collective-permute-start.20 = (bf16[464,384]{1,0:T(8,128)(2,1)}, bf16[464,384]{1,0:T(8,128)(2,1)}, u32[]{:S(2)}, u32[]{:S(2)}) collective-permute-start(bf16[464,384]{1,0:T(8,128)(2,1)} %get-tuple-element.124), channel_id=1, source_target_pairs={{0,8},{2,10},{4,12},{6,14},{8,0},{10,2},{12,4},{14,6},{16,24},{18,... | collective-permute-start | bytes 1069064 | tf_op jit(solution)/shard_map/ppermute | solution.py:1180
  205.7 27.7 %collective-permute-start.21 = (bf16[464,384]{1,0:T(8,128)(2,1)}, bf16[464,384]{1,0:T(8,128)(2,1)}, u32[]{:S(2)}, u32[]{:S(2)}) collective-permute-start(bf16[464,384]{1,0:T(8,128)(2,1)} %get-tuple-element.125), channel_id=1, source_target_pairs={{0,16},{2,18},{4,20},{6,22},{8,24},{10,26},{12,28},{14,30},{16,0},... | collective-permute-start | bytes 1069064 | tf_op jit(solution)/shard_map/ppermute | solution.py:1180
  208.2 25.1 %collective-permute-start.22 = (bf16[464,384]{1,0:T(8,128)(2,1)}, bf16[464,384]{1,0:T(8,128)(2,1)}, u32[]{:S(2)}, u32[]{:S(2)}) collective-permute-start(bf16[464,384]{1,0:T(8,128)(2,1)} %get-tuple-element.126), channel_id=1, source_target_pairs={{0,24},{2,26},{4,28},{6,30},{8,16},{10,18},{12,20},{14,22},{16,8},... | collective-permute-start | bytes 1069064 | tf_op jit(solution)/shard_map/ppermute | solution.py:1180
  220.0 1.1 copy-start.8
  221.2 0.8 copy-start.4
  221.2 14.3 %collective-permute-start.16 = (bf16[4,160,384]{2,1,0:T(8,128)(2,1)S(1)}, bf16[4,160,384]{2,1,0:T(8,128)(2,1)S(1)}, u32[]{:S(2)}, u32[]{:S(2)}) collective-permute-start(bf16[4,160,384]{2,1,0:T(8,128)(2,1)S(1)} %pad_maximum_fusion.refs_10_), channel_id=1, source_target_pairs={{0,1},{1,0},{2,3},{3,2},{4,5},{5,4},{6,7},{7,6},{8,9},{9,8},{10,11... | collective-permute-start | bytes 1474568 | tf_op jit(solution)/shard_map/ppermute | solution.py:1177
  222.0 7.0 %copy-start.9 = (bf16[2,4,160,128]{3,2,1,0:T(8,128)(2,1)S(1)}, bf16[2,4,160,128]{3,2,1,0:T(8,128)(2,1)}, u32[]{:S(2)}) copy-start(bf16[2,4,160,128]{3,2,1,0:T(8,128)(2,1)} %copy-done.8) | copy-start | bytes 983044
  227.6 5.7 %copy-start.6 = (bf16[464,384]{1,0:T(8,128)(2,1)S(1)}, bf16[464,384]{1,0:T(8,128)(2,1)}, u32[]{:S(2)}) copy-start(bf16[464,384]{1,0:T(8,128)(2,1)} %get-tuple-element.123) | copy-start | bytes 1069060
  227.6 28.5 %collective-permute-start.15 = (bf16[512,768]{1,0:T(8,128)(2,1)}, bf16[512,768]{1,0:T(8,128)(2,1)}, u32[]{:S(2)}, u32[]{:S(2)}) collective-permute-start(bf16[512,768]{1,0:T(8,128)(2,1)} %get-tuple-element.119), channel_id=1, source_target_pairs={{0,1},{1,0},{2,3},{3,2},{4,5},{5,4},{6,7},{7,6},{8,9},{9,8},{10,11... | collective-permute-start | bytes 2359304 | tf_op jit(solution)/shard_map/ppermute | solution.py:1177
  235.6 15.2 %collective-permute-start.17 = (bf16[160,384]{1,0:T(8,128)(2,1)S(1)}, bf16[160,384]{1,0:T(8,128)(2,1)S(1)}, u32[]{:S(2)}, u32[]{:S(2)}) collective-permute-start(bf16[160,384]{1,0:T(8,128)(2,1)S(1)} %get-tuple-element.143), channel_id=1, source_target_pairs={{0,8},{2,10},{4,12},{6,14},{8,0},{10,2},{12,4},{14,6},{16,24},{18,... | collective-permute-start | bytes 368648 | tf_op jit(solution)/shard_map/ppermute | solution.py:1180
  242.7 11.4 %collective-permute-start.18 = (bf16[160,384]{1,0:T(8,128)(2,1)S(1)}, bf16[160,384]{1,0:T(8,128)(2,1)S(1)}, u32[]{:S(2)}, u32[]{:S(2)}) collective-permute-start(bf16[160,384]{1,0:T(8,128)(2,1)S(1)} %get-tuple-element.145), channel_id=1, source_target_pairs={{0,16},{2,18},{4,20},{6,22},{8,24},{10,26},{12,28},{14,30},{16,0},... | collective-permute-start | bytes 368648 | tf_op jit(solution)/shard_map/ppermute | solution.py:1180
  243.8 10.3 %collective-permute-start.19 = (bf16[160,384]{1,0:T(8,128)(2,1)S(1)}, bf16[160,384]{1,0:T(8,128)(2,1)S(1)}, u32[]{:S(2)}, u32[]{:S(2)}) collective-permute-start(bf16[160,384]{1,0:T(8,128)(2,1)S(1)} %get-tuple-element.144), channel_id=1, source_target_pairs={{0,24},{2,26},{4,28},{6,30},{8,16},{10,18},{12,20},{14,22},{16,8},... | collective-permute-start | bytes 368648 | tf_op jit(solution)/shard_map/ppermute | solution.py:1180

commit v7 on v6

--- a/solution.py
+++ b/solution.py
@@ -924,7 +924,7 @@
         for g, ref in enumerate(sums):
             for x in range(2):
                 part = ref[r : r + 1, x * UNIT : (x + 1) * UNIT]
-                extra = jnp.where(at == (r * len(sums) + g) * 2 + x, part, extra)
+                extra = jnp.where(at == (2 * r + x) * len(sums) + g, part, extra)
     for z in range(4):
         for y in range(2):
             for x in range(2):
@@ -1315,8 +1315,7 @@
     output_grad = inner_all[4]
     inner_grad = jnp.transpose(inner_all[:4], (1, 0, 2)).reshape(rows, -1)
     units = width // UNIT
-    biases = late[3 * rows :, 2 * UNIT :][: 2 * units].reshape(2, units // 2, 2, UNIT)
-    biases = jnp.transpose(biases, (0, 2, 1, 3)).reshape(2, width)
+    biases = late[3 * rows :, 2 * UNIT :][: 2 * units].reshape(2, width)
     return (
         layer_out,
         hidden_grad,

time: 261 us -> 260 us (level)
  no operation moved by 1% of the time
where the time goes in v7:
time: 260 us; the launch traced here: 258 us
  Pallas kernels  170 us (65%)
  starting transfers between devices  29.5 us (11%)
  waiting for transfers between devices  24.8 us (10%)
  other arithmetic  17.4 us (7%)
  local copies, waits for them, and re-layouts  14.6 us (6%)
    pallas_call x12, Pallas kernels, run(): pl.pallas_call(body, grid_spec=pltpu.PrefetchScalarGridSpec(num_scalar_pr...  170 us
    ppermute x14, starting transfers between devices, seq_swap(): return lax.ppermute(x, 'seq', [(i, i ^ bit) for i in range(16)])  18.8 us
    ppermute x9, waiting for transfers between devices, trade(): return lax.ppermute(x, 'blk', [(0, 1), (1, 0)])  15.1 us
    ppermute x9, starting transfers between devices, trade(): return lax.ppermute(x, 'blk', [(0, 1), (1, 0)])  10.6 us
    ppermute x14, waiting for transfers between devices, seq_swap(): return lax.ppermute(x, 'seq', [(i, i ^ bit) for i in range(16)])  9.72 us
  transfers between devices with their start and end apart: 23, of which 5 were waited for; matrix products, arithmetic and copies ran while one was open for 11% of the time, Pallas kernels for 43%

profile of v7, /device:TPU:0, one launch (start us, length us, event | category | flops | bytes accessed | tf_op | source)
XLA Modules:
  0.0 257.9 jit_solution(6136068161541787866)
XLA Ops:
  0.8 1.3 dynamic-slice_bitcast_fusion.1
  2.1 3.0 %collective-permute-start = (bf16[512,768]{1,0:T(8,128)(2,1)S(1)}, bf16[512,768]{1,0:T(8,128)(2,1)S(1)}, u32[]{:S(2)}, u32[]{:S(2)}) collective-permute-start(bf16[512,768]{1,0:T(8,128)(2,1)S(1)} %dynamic-slice_bitcast_fusion.1), channel_id=1, source_target_pairs={{0,1},{1,0},{2,3},{3,2},{4,5},{5,4},{6,7},{7,6},{8,9},{9,8},{10,11... | collective-permute-start | bytes 2359304 | tf_op jit(solution)/shard_map/ppermute | solution.py:1177
  7.1 0.6 concatenate.23.refs_9_
  7.7 14.9 %collective-permute-done.1 = s32[512]{0:T(512)S(1)} collective-permute-done((s32[512]{0:T(512)S(1)}, s32[512]{0:T(512)S(1)}, u32[]{:S(2)}, u32[]{:S(2)}) %collective-permute-start.1) | collective-permute-done | bytes 2080 | tf_op jit(solution)/shard_map/ppermute | solution.py:1177
  23.9 0.9 dynamic-slice_bitcast_fusion
  24.9 1.7 collective-permute-start.2
  26.6 0.9 copy-done.21
  27.5 26.3 %attention_forward.1 = (bf16[1024,768]{1,0:T(8,128)(2,1)}, bf16[1024,768]{1,0:T(8,128)(2,1)}, bf16[1024,768]{1,0:T(8,128)(2,1)}, bf16[2,1024,384]{2,1,0:T(8,128)...) custom-call(s32[1]{0:T(128)} %bitcast.refs_0_, bf16[2,512,768]{2,1,0:T(8,128)(2,1)} %refs_1_.1, ...), custom_call_target="tpu_custom_call" | custom-call | flops 160000000000 | bytes 1 | tf_op jit(solution)/shard_map/attention_forward/pallas_call | solution.py:379
  53.9 48.1 %token_pass.1 = (bf16[2,512,768]{2,1,0:T(8,128)(2,1)}, bf16[256,768]{1,0:T(8,128)(2,1)}, bf16[256,768]{1,0:T(8,128)(2,1)}, bf16[1024,768]{1,0:T(8,128)(2,1)}, bf...) custom-call(s32[1]{0:T(128)} %bitcast.refs_0_, ...), custom_call_target="tpu_custom_call" | custom-call | flops 230000001024 | bytes 1 | tf_op jit(solution)/shard_map/token_pass/pallas_call | solution.py:379
  101.9 9.4 %outer_grad.1 = (bf16[2,2,4,224,384]{4,3,2,1,0:T(8,128)(2,1)}, bf16[2,2,4,224,384]{4,3,2,1,0:T(8,128)(2,1)}) custom-call(s32[1]{0:T(128)} %bitcast.10.refs_0_.refs_7_, bf16[1024,3072]{1,0:T(8,128)(2,1)} %get-tuple-element.83.refs_1_, bf16[1024,768]{1,0:T(8,128)(2,1)} %get-tuple-element.84.refs_2_, f32[8,768]{1,0:T(8,128)} %get-tuple-element.85.refs_3_, ...), custom_call_target="tpu_custom_call" | custom-call | flops 44999999488 | bytes 1 | tf_op jit(solution)/shard_map/outer_grad/pallas_call | solution.py:379
  111.4 11.6 %inner_grad.1 = (bf16[2,2,4,5,48,384]{5,4,3,2,1,0:T(8,128)(2,1)}, bf16[2,2,4,5,48,384]{5,4,3,2,1,0:T(8,128)(2,1)}, bf16[2,2,4,224,384]{4,3,2,1,0:T(8,128)(2,1)}) custom-call(s32[1]{0:T(128)} %bitcast.10.refs_0_.refs_7_, bf16[1024,768]{1,0:T(8,128)(2,1)} %get-tuple-element.80.refs_1_, ...), custom_call_target="tpu_custom_call", output_to_operand_aliasing={{2}: (6, {})} | custom-call | flops 60000002048 | bytes 1 | tf_op jit(solution)/shard_map/inner_grad/pallas_call | solution.py:379
  124.0 3.8 %halve_first.1 = (bf16[2,4,224,384]{3,2,1,0:T(8,128)(2,1)}, bf16[256,768]{1,0:T(8,128)(2,1)}) custom-call(s32[3]{0:T(128)} %pad_add_fusion.1.refs_0_, bf16[2,2,4,224,384]{4,3,2,1,0:T(8,128)(2,1)} %get-tuple-element.88.refs_1_.refs_10_, bf16[2,2,4,224,384]{4,3,2,1,0:T(8,128)(2,1)} %collective-permute-done.3.refs_2_, ...), custom_call_target="tpu_custom_call", output_to_operand_aliasing={{1}: (3, {})} | custom-call | flops 10000000000 | bytes 1 | tf_op jit(solution)/shard_map/halve_first/pallas_call | solution.py:379
  128.2 1.8 collective-permute-start.6
  129.9 4.0 %fusion.refs_8_ = bf16[2,4,5,48,384]{4,3,2,1,0:T(8,128)(2,1)} fusion(bf16[2,2,4,5,48,384]{5,4,3,2,1,0:T(8,128)(2,1)S(1)} %collective-permute-done.4, s32[]{:T(128)S(6)} %select_n.36, bf16[2,2,4,5,48,384]{5,4,3,2,1,0:T(8,128)(2,1)} %get-tuple-element.92.refs_11_), kind=kLoop, calls=%fused_computation.1 | loop fusion | flops 3686400 | bytes 4423684 | tf_op jit(solution)/shard_map/convert_element_type | solution.py:1245
  133.9 1.5 collective-permute-start.7
  135.4 15.2 %attention_backward.3 = (bf16[3,1024,256]{2,1,0:T(8,128)(2,1)}, f32[8,256]{1,0:T(8,128)}) custom-call(bf16[1024,768]{1,0:T(8,128)(2,1)} %get-tuple-element.75.refs_0_, bf16[1024,768]{1,0:T(8,128)(2,1)} %get-tuple-element.76.refs_1_, bf16[1024,768]{1,0:T(8,128)(2,1)} %get-tuple-element.77.refs_2_, bf16[2,1024,384]{2,1,0:T(8,128)(2,1)} %get-tuple-element.78.refs_3_, ...), custom_call_target="tpu_custom_call" | custom-call | flops 80000000000 | bytes 1 | tf_op jit(solution)/shard_map/attention_backward/pallas_call | solution.py:379
  150.6 0.8 copy-done.22
  151.4 19.2 %attention_backward.4 = (bf16[3,1024,256]{2,1,0:T(8,128)(2,1)}, f32[8,256]{1,0:T(8,128)}, bf16[2,2,4,160,256]{4,3,2,1,0:T(8,128)(2,1)}, bf16[2,2,4,160,256]{4,3,...) custom-call(bf16[1024,768]{1,0:T(8,128)(2,1)} %get-tuple-element.75., ...), custom_call_target="tpu_custom_call", output_to_operand_aliasing={{4}: (10, {}), {5}: (11, {}), {6}: (12, {}), {7}: (13, {})} | custom-call | flops 80000000000 | bytes 1 | tf_op jit(solution)/shard_map/attention_backward/pallas_call | solution.py:379
  171.1 1.8 fusion.4.refs_14_
  172.9 1.6 collective-permute-start.8
  174.5 1.9 fusion.2.refs_15_
  177.3 17.2 %attention_backward.5 = (bf16[3,1024,256]{2,1,0:T(8,128)(2,1)}, f32[8,256]{1,0:T(8,128)}, bf16[2,2,4,160,128]{4,3,2,1,0:T(8,128)(2,1)}, bf16[2,2,4,160,128]{4,3,...) custom-call(bf16[1024,768]{1,0:T(8,128)(2,1)} %get-tuple-element.75., ...), custom_call_target="tpu_custom_call", output_to_operand_aliasing={{4}: (11, {}), {5}: (12, {}), {6}: (13, {})} | custom-call | flops 80000000000 | bytes 1 | tf_op jit(solution)/shard_map/attention_backward/pallas_call | solution.py:379
  194.5 1.3 fusion.5.refs_11_
  195.8 1.2 collective-permute-start.13
  197.2 5.0 %quarter.1 = (bf16[464,384]{1,0:T(8,128)(2,1)}, bf16[464,384]{1,0:T(8,128)(2,1)}, bf16[464,384]{1,0:T(8,128)(2,1)}, bf16[464,384]{1,0:T(8,128)(2,1)}, bf16[256,7...) custom-call(s32[3]{0:T(128)} %pad_add_fusion.1.refs_0_, ...), custom_call_target="tpu_custom_call", output_to_operand_aliasing={{4}: (9, {}), {5}: (10, {})} | custom-call | flops 10000000000 | bytes 1 | tf_op jit(solution)/shard_map/quarter/pallas_call | solution.py:379
  202.2 1.1 fusion.8.refs_13_
  203.3 0.8 collective-permute-start.14
  204.1 1.6 collective-permute-start.20
  205.7 2.6 %collective-permute-start.21 = (bf16[464,384]{1,0:T(8,128)(2,1)}, bf16[464,384]{1,0:T(8,128)(2,1)}, u32[]{:S(2)}, u32[]{:S(2)}) collective-permute-start(bf16[464,384]{1,0:T(8,128)(2,1)} %get-tuple-element.125), channel_id=1, source_target_pairs={{0,16},{2,18},{4,20},{6,22},{8,24},{10,26},{12,28},{14,30},{16,0},... | collective-permute-start | bytes 1069064 | tf_op jit(solution)/shard_map/ppermute | solution.py:1180
  208.5 6.1 %hidden_home.1 = (f32[2,512,768]{2,1,0:T(8,128)}, bf16[2,512,768]{2,1,0:T(8,128)(2,1)}, bf16[2,2,4,160,256]{4,3,2,1,0:T(8,128)(2,1)}, bf16[2,2,4,160,128]{4,3,2,1,0:T(8,128)(2,1)}) custom-call(s32[1]{0:T(128)} %bitcast.refs_0_, f32[1024,768]{1,0:T(8,128)} %get-tuple-element.74.refs_1_.refs_0_, ...), custom_call_target="tpu_custom_call", output_to_operand_aliasing={{1}: (10, {}), {2}: (11, {}), {3}: (12, {})} | custom-call | flops 30000001024 | bytes 1 | tf_op jit(solution)/shard_map/hidden_home/pallas_call | solution.py:379
  214.6 1.2 fusion.7
  215.8 4.2 %collective-permute-done.14 = bf16[2,4,160,128]{3,2,1,0:T(8,128)(2,1)S(1)} collective-permute-done((bf16[2,4,160,128]{3,2,1,0:T(8,128)(2,1)S(1)}, bf16[2,4,160,128]{3,2,1,0:T(8,128)(2,1)S(1)}, u32[]{:S(2)}, u32[]{:S(2)}) %collective-permute-start.14) | collective-permute-done | bytes 327712 | tf_op jit(solution)/shard_map/ppermute | solution.py:1180
  220.0 1.1 fusion.10
  222.0 5.7 %hidden_away.1 = (bf16[512,768]{1,0:T(8,128)(2,1)}, bf16[2,2,4,160,256]{4,3,2,1,0:T(8,128)(2,1)}, bf16[2,2,4,160,128]{4,3,2,1,0:T(8,128)(2,1)}, bf16[464,384]{1,0:T(8,128)(2,1)}) custom-call(f32[1024,768]{1,0:T(8,128)} %get-tuple-element.74.refs_1_.refs_0_, ...), custom_call_target="tpu_custom_call", output_to_operand_aliasing={{1}: (7, {}), {2}: (8, {}), {3}: (9, {})} | custom-call | flops 30000001024 | bytes 1 | tf_op jit(solution)/shard_map/hidden_away/pallas_call | solution.py:379
  227.6 1.3 collective-permute-start.15
  229.0 0.9 fusion.26
  229.9 1.3 fusion.22
  231.2 2.1 collective-permute-done.21
  233.4 1.4 add_add_fusion
  234.8 0.8 fusion.29
  235.6 7.1 %collective-permute-start.17 = (bf16[160,384]{1,0:T(8,128)(2,1)S(1)}, bf16[160,384]{1,0:T(8,128)(2,1)S(1)}, u32[]{:S(2)}, u32[]{:S(2)}) collective-permute-start(bf16[160,384]{1,0:T(8,128)(2,1)S(1)} %get-tuple-element.143), channel_id=1, source_target_pairs={{0,8},{2,10},{4,12},{6,14},{8,0},{10,2},{12,4},{14,6},{16,24},{18,... | collective-permute-start | bytes 368648 | tf_op jit(solution)/shard_map/ppermute | solution.py:1180
  242.7 1.1 collective-permute-start.18
  243.8 1.4 collective-permute-start.19
  245.2 0.6 slice.100
  245.8 0.7 copy.54
  250.8 3.4 %collective-permute-done.18 = bf16[160,384]{1,0:T(8,128)(2,1)S(1)} collective-permute-done((bf16[160,384]{1,0:T(8,128)(2,1)S(1)}, bf16[160,384]{1,0:T(8,128)(2,1)S(1)}, u32[]{:S(2)}, u32[]{:S(2)}) %collective-permute-start.18) | collective-permute-done | bytes 122912 | tf_op jit(solution)/shard_map/ppermute | solution.py:1180
  254.8 0.7 fusion.30
  255.5 2.2 place_far.1
  (100 shorter events, 11.6 us)
Async XLA Ops:
  0.7 4.4 %copy-start.11 = (s32[2,512]{1,0:T(2,128)S(1)}, s32[2,512]{1,0:T(2,128)}, u32[]{:S(2)}) copy-start(s32[2,512]{1,0:T(2,128)} %param.19) | copy-start | bytes 12292
  0.7 4.5 %copy-start.13 = (bf16[768]{0:T(1024)(128)(2,1)S(1)}, bf16[768]{0:T(1024)(128)(2,1)}, u32[]{:S(2)}) copy-start(bf16[768]{0:T(1024)(128)(2,1)} %param.21) | copy-start | bytes 4612
  0.7 5.1 %copy-start.14 = (bf16[768]{0:T(1024)(128)(2,1)S(1)}, bf16[768]{0:T(1024)(128)(2,1)}, u32[]{:S(2)}) copy-start(bf16[768]{0:T(1024)(128)(2,1)} %param.24) | copy-start | bytes 4612
  0.7 5.7 %copy-start.15 = (bf16[768]{0:T(1024)(128)(2,1)S(1)}, bf16[768]{0:T(1024)(128)(2,1)}, u32[]{:S(2)}) copy-start(bf16[768]{0:T(1024)(128)(2,1)} %param.26) | copy-start | bytes 4612
  0.7 5.7 %copy-start.16 = (bf16[768]{0:T(1024)(128)(2,1)S(1)}, bf16[768]{0:T(1024)(128)(2,1)}, u32[]{:S(2)}) copy-start(bf16[768]{0:T(1024)(128)(2,1)} %param.27) | copy-start | bytes 4612
  0.7 5.7 %copy-start.17 = (bf16[768]{0:T(1024)(128)(2,1)S(1)}, bf16[768]{0:T(1024)(128)(2,1)}, u32[]{:S(2)}) copy-start(bf16[768]{0:T(1024)(128)(2,1)} %param.28) | copy-start | bytes 4612
  0.7 5.7 %copy-start.18 = (bf16[768]{0:T(1024)(128)(2,1)S(1)}, bf16[768]{0:T(1024)(128)(2,1)}, u32[]{:S(2)}) copy-start(bf16[768]{0:T(1024)(128)(2,1)} %param.32) | copy-start | bytes 4612
  0.7 5.7 %copy-start.19 = (bf16[768]{0:T(1024)(128)(2,1)S(1)}, bf16[768]{0:T(1024)(128)(2,1)}, u32[]{:S(2)}) copy-start(bf16[768]{0:T(1024)(128)(2,1)} %param.33) | copy-start | bytes 4612
  0.7 5.7 %copy-start.20 = (bf16[768]{0:T(1024)(128)(2,1)S(1)}, bf16[768]{0:T(1024)(128)(2,1)}, u32[]{:S(2)}) copy-start(bf16[768]{0:T(1024)(128)(2,1)} %param.34) | copy-start | bytes 4612
  0.7 5.7 %copy-start.10 = (bf16[3072]{0:T(1024)(128)(2,1)S(1)}, bf16[3072]{0:T(1024)(128)(2,1)}, u32[]{:S(2)}) copy-start(bf16[3072]{0:T(1024)(128)(2,1)} %param.30) | copy-start | bytes 18436
  0.8 23.2 %copy-start.5 = (bf16[2,512,768]{2,1,0:T(8,128)(2,1)S(1)}, bf16[2,512,768]{2,1,0:T(8,128)(2,1)}, u32[]{:S(2)}) copy-start(bf16[2,512,768]{2,1,0:T(8,128)(2,1)} %refs_3_.3) | copy-start | bytes 4718596
  2.1 24.5 %collective-permute-start = (bf16[512,768]{1,0:T(8,128)(2,1)S(1)}, bf16[512,768]{1,0:T(8,128)(2,1)S(1)}, u32[]{:S(2)}, u32[]{:S(2)}) collective-permute-start(bf16[512,768]{1,0:T(8,128)(2,1)S(1)} %dynamic-slice_bitcast_fusion.1), channel_id=1, source_target_pairs={{0,1},{1,0},{2,3},{3,2},{4,5},{5,4},{6,7},{7,6},{8,9},{9,8},{10,11... | collective-permute-start | bytes 2359304 | tf_op jit(solution)/shard_map/ppermute | solution.py:1177
  5.1 17.6 %collective-permute-start.1 = (s32[512]{0:T(512)S(1)}, s32[512]{0:T(512)S(1)}, u32[]{:S(2)}, u32[]{:S(2)}) collective-permute-start(s32[512]{0:T(512)S(1)} %bitcast.115), channel_id=1, source_target_pairs={{0,1},{1,0},{2,3},{3,2},{4,5},{5,4},{6,7},{7,6},{8,9},{9,8},{10,11... | collective-permute-start | bytes 6152 | tf_op jit(solution)/shard_map/ppermute | solution.py:1177
  22.7 3.9 %copy-start.12 = (s32[1024]{0:T(1024)}, s32[1024]{0:T(1024)S(1)}, u32[]{:S(2)}) copy-start(s32[1024]{0:T(1024)S(1)} %pad_add_fusion) | copy-start | bytes 12292
  24.9 29.0 %collective-permute-start.2 = (bf16[512,768]{1,0:T(8,128)(2,1)}, bf16[512,768]{1,0:T(8,128)(2,1)}, u32[]{:S(2)}, u32[]{:S(2)}) collective-permute-start(bf16[512,768]{1,0:T(8,128)(2,1)} %dynamic-slice_bitcast_fusion), channel_id=1, source_target_pairs={{0,1},{1,0},{2,3},{3,2},{4,5},{5,4},{6,7},{7,6},{8,9},{9,8},{10,11... | collective-permute-start | bytes 2359304 | tf_op jit(solution)/shard_map/ppermute | solution.py:1177
  26.6 0.9 copy-start.21
  111.4 12.7 %collective-permute-start.3 = (bf16[2,2,4,224,384]{4,3,2,1,0:T(8,128)(2,1)}, bf16[2,2,4,224,384]{4,3,2,1,0:T(8,128)(2,1)}, u32[]{:S(2)}, u32[]{:S(2)}) collective-permute-start(bf16[2,2,4,224,384]{4,3,2,1,0:T(8,128)(2,1)} %get-tuple-element.89), channel_id=1, source_target_pairs={{0,2},{2,0},{4,6},{6,4},{8,10},{10,8},{12,14},{14,12},{16,18},{18,... | collective-permute-start | bytes 8257544 | tf_op jit(solution)/shard_map/ppermute | solution.py:1180
  123.0 6.9 %collective-permute-start.4 = (bf16[2,2,4,5,48,384]{5,4,3,2,1,0:T(8,128)(2,1)}, bf16[2,2,4,5,48,384]{5,4,3,2,1,0:T(8,128)(2,1)S(1)}, u32[]{:S(2)}, u32[]{:S(2)}) collective-permute-start(bf16[2,2,4,5,48,384]{5,4,3,2,1,0:T(8,128)(2,1)} %get-tuple-element.93), channel_id=1, source_target_pairs={{0,2},{2,0},{4,6},{6,4},{8,10},{10,8},{12,14},{14,12},{16,18},{18,... | collective-permute-start | bytes 8847368 | tf_op jit(solution)/shard_map/ppermute | solution.py:1180
  127.9 22.7 %collective-permute-start.5 = (bf16[256,768]{1,0:T(8,128)(2,1)}, bf16[256,768]{1,0:T(8,128)(2,1)S(1)}, u32[]{:S(2)}, u32[]{:S(2)}) collective-permute-start(bf16[256,768]{1,0:T(8,128)(2,1)} %get-tuple-element.95), channel_id=1, source_target_pairs={{0,1},{1,0},{2,3},{3,2},{4,5},{5,4},{6,7},{7,6},{8,9},{9,8},{10,11... | collective-permute-start | bytes 1179656 | tf_op jit(solution)/shard_map/ppermute | solution.py:1177
  128.2 43.0 %collective-permute-start.6 = (bf16[2,4,224,384]{3,2,1,0:T(8,128)(2,1)}, bf16[2,4,224,384]{3,2,1,0:T(8,128)(2,1)}, u32[]{:S(2)}, u32[]{:S(2)}) collective-permute-start(bf16[2,4,224,384]{3,2,1,0:T(8,128)(2,1)} %get-tuple-element.91.refs_7_), channel_id=1, source_target_pairs={{0,4},{2,6},{4,0},{6,2},{8,12},{10,14},{12,8},{14,10},{16,20},{18,... | collective-permute-start | bytes 4128776 | tf_op jit(solution)/shard_map/ppermute | solution.py:1180
  129.9 4.0 %copy-start = (bf16[2,2,4,5,48,384]{5,4,3,2,1,0:T(8,128)(2,1)}, bf16[2,2,4,5,48,384]{5,4,3,2,1,0:T(8,128)(2,1)S(1)}, u32[]{:S(2)}) copy-start(bf16[2,2,4,5,48,384]{5,4,3,2,1,0:T(8,128)(2,1)S(1)} %collective-permute-done.4) | copy-start | bytes 8847364
  133.9 40.6 %collective-permute-start.7 = (bf16[2,4,5,48,384]{4,3,2,1,0:T(8,128)(2,1)}, bf16[2,4,5,48,384]{4,3,2,1,0:T(8,128)(2,1)}, u32[]{:S(2)}, u32[]{:S(2)}) collective-permute-start(bf16[2,4,5,48,384]{4,3,2,1,0:T(8,128)(2,1)} %fusion.refs_8_), channel_id=1, source_target_pairs={{0,1},{1,0},{2,3},{3,2},{4,5},{5,4},{6,7},{7,6},{8,9},{9,8},{10,11... | collective-permute-start | bytes 4423688 | tf_op jit(solution)/shard_map/ppermute | solution.py:1177
  150.6 0.8 copy-start.22
  170.6 23.9 %collective-permute-start.11 = (bf16[2,2,4,160,256]{4,3,2,1,0:T(8,128)(2,1)}, bf16[2,2,4,160,256]{4,3,2,1,0:T(8,128)(2,1)S(1)}, u32[]{:S(2)}, u32[]{:S(2)}) collective-permute-start(bf16[2,2,4,160,256]{4,3,2,1,0:T(8,128)(2,1)} %get-tuple-element.110), channel_id=1, source_target_pairs={{0,2},{2,0},{4,6},{6,4},{8,10},{10,8},{12,14},{14,12},{16,18},{18,... | collective-permute-start | bytes 3932168 | tf_op jit(solution)/shard_map/ppermute | solution.py:1180
  170.6 26.4 %collective-permute-start.10 = (bf16[256,768]{1,0:T(8,128)(2,1)}, bf16[256,768]{1,0:T(8,128)(2,1)}, u32[]{:S(2)}, u32[]{:S(2)}) collective-permute-start(bf16[256,768]{1,0:T(8,128)(2,1)} %get-tuple-element.107), channel_id=1, source_target_pairs={{0,1},{1,0},{2,3},{3,2},{4,5},{5,4},{6,7},{7,6},{8,9},{9,8},{10,11... | collective-permute-start | bytes 1179656 | tf_op jit(solution)/shard_map/ppermute | solution.py:1177
  172.9 4.0 %copy-start.2 = (bf16[4,224,384]{2,1,0:T(8,128)(2,1)}, bf16[4,224,384]{2,1,0:T(8,128)(2,1)S(1)}, u32[]{:S(2)}) copy-start(bf16[4,224,384]{2,1,0:T(8,128)(2,1)S(1)} %fusion.4.refs_14_) | copy-start | bytes 2064388
  172.9 24.2 %collective-permute-start.8 = (bf16[4,224,384]{2,1,0:T(8,128)(2,1)S(1)}, bf16[4,224,384]{2,1,0:T(8,128)(2,1)}, u32[]{:S(2)}, u32[]{:S(2)}) collective-permute-start(bf16[4,224,384]{2,1,0:T(8,128)(2,1)S(1)} %fusion.4.refs_14_), channel_id=1, source_target_pairs={{0,1},{1,0},{2,3},{3,2},{4,5},{5,4},{6,7},{7,6},{8,9},{9,8},{10,11... | collective-permute-start | bytes 2064392 | tf_op jit(solution)/shard_map/ppermute | solution.py:1177
  176.4 0.9 copy-start.1
  176.4 20.8 %collective-permute-start.9 = (bf16[4,5,48,384]{3,2,1,0:T(8,128)(2,1)S(1)}, bf16[4,5,48,384]{3,2,1,0:T(8,128)(2,1)}, u32[]{:S(2)}, u32[]{:S(2)}) collective-permute-start(bf16[4,5,48,384]{3,2,1,0:T(8,128)(2,1)S(1)} %fusion.2.refs_15_), channel_id=1, source_target_pairs={{0,4},{2,6},{4,0},{6,2},{8,12},{10,14},{12,8},{14,10},{16,20},{18,... | collective-permute-start | bytes 2211848 | tf_op jit(solution)/shard_map/ppermute | solution.py:1180
  194.5 7.7 %collective-permute-start.12 = (bf16[2,2,4,160,128]{4,3,2,1,0:T(8,128)(2,1)}, bf16[2,2,4,160,128]{4,3,2,1,0:T(8,128)(2,1)S(1)}, u32[]{:S(2)}, u32[]{:S(2)}) collective-permute-start(bf16[2,2,4,160,128]{4,3,2,1,0:T(8,128)(2,1)} %get-tuple-element.114), channel_id=1, source_target_pairs={{0,2},{2,0},{4,6},{6,4},{8,10},{10,8},{12,14},{14,12},{16,18},{18,... | collective-permute-start | bytes 1966088 | tf_op jit(solution)/shard_map/ppermute | solution.py:1180
  195.8 1.4 copy-start.3
  195.8 18.8 %collective-permute-start.13 = (bf16[2,4,160,256]{3,2,1,0:T(8,128)(2,1)S(1)}, bf16[2,4,160,256]{3,2,1,0:T(8,128)(2,1)}, u32[]{:S(2)}, u32[]{:S(2)}) collective-permute-start(bf16[2,4,160,256]{3,2,1,0:T(8,128)(2,1)S(1)} %fusion.5.refs_11_), channel_id=1, source_target_pairs={{0,4},{2,6},{4,0},{6,2},{8,12},{10,14},{12,8},{14,10},{16,20},{18,... | collective-permute-start | bytes 1966088 | tf_op jit(solution)/shard_map/ppermute | solution.py:1180
  203.3 5.2 %copy-start.7 = (bf16[2,4,160,128]{3,2,1,0:T(8,128)(2,1)}, bf16[2,4,160,128]{3,2,1,0:T(8,128)(2,1)S(1)}, u32[]{:S(2)}) copy-start(bf16[2,4,160,128]{3,2,1,0:T(8,128)(2,1)S(1)} %fusion.8.refs_13_) | copy-start | bytes 983044
  203.3 16.7 %collective-permute-start.14 = (bf16[2,4,160,128]{3,2,1,0:T(8,128)(2,1)S(1)}, bf16[2,4,160,128]{3,2,1,0:T(8,128)(2,1)S(1)}, u32[]{:S(2)}, u32[]{:S(2)}) collective-permute-start(bf16[2,4,160,128]{3,2,1,0:T(8,128)(2,1)S(1)} %fusion.8.refs_13_), channel_id=1, source_target_pairs={{0,4},{2,6},{4,0},{6,2},{8,12},{10,14},{12,8},{14,10},{16,20},{18,... | collective-permute-start | bytes 983048 | tf_op jit(solution)/shard_map/ppermute | solution.py:1180
  204.1 27.2 %collective-permute-start.20 = (bf16[464,384]{1,0:T(8,128)(2,1)}, bf16[464,384]{1,0:T(8,128)(2,1)}, u32[]{:S(2)}, u32[]{:S(2)}) collective-permute-start(bf16[464,384]{1,0:T(8,128)(2,1)} %get-tuple-element.124), channel_id=1, source_target_pairs={{0,8},{2,10},{4,12},{6,14},{8,0},{10,2},{12,4},{14,6},{16,24},{18,... | collective-permute-start | bytes 1069064 | tf_op jit(solution)/shard_map/ppermute | solution.py:1180
  205.7 27.7 %collective-permute-start.21 = (bf16[464,384]{1,0:T(8,128)(2,1)}, bf16[464,384]{1,0:T(8,128)(2,1)}, u32[]{:S(2)}, u32[]{:S(2)}) collective-permute-start(bf16[464,384]{1,0:T(8,128)(2,1)} %get-tuple-element.125), channel_id=1, source_target_pairs={{0,16},{2,18},{4,20},{6,22},{8,24},{10,26},{12,28},{14,30},{16,0},... | collective-permute-start | bytes 1069064 | tf_op jit(solution)/shard_map/ppermute | solution.py:1180
  208.2 25.1 %collective-permute-start.22 = (bf16[464,384]{1,0:T(8,128)(2,1)}, bf16[464,384]{1,0:T(8,128)(2,1)}, u32[]{:S(2)}, u32[]{:S(2)}) collective-permute-start(bf16[464,384]{1,0:T(8,128)(2,1)} %get-tuple-element.126), channel_id=1, source_target_pairs={{0,24},{2,26},{4,28},{6,30},{8,16},{10,18},{12,20},{14,22},{16,8},... | collective-permute-start | bytes 1069064 | tf_op jit(solution)/shard_map/ppermute | solution.py:1180
  220.0 1.1 copy-start.8
  221.2 0.8 copy-start.4
  221.2 14.3 %collective-permute-start.16 = (bf16[4,160,384]{2,1,0:T(8,128)(2,1)S(1)}, bf16[4,160,384]{2,1,0:T(8,128)(2,1)S(1)}, u32[]{:S(2)}, u32[]{:S(2)}) collective-permute-start(bf16[4,160,384]{2,1,0:T(8,128)(2,1)S(1)} %pad_maximum_fusion.refs_10_), channel_id=1, source_target_pairs={{0,1},{1,0},{2,3},{3,2},{4,5},{5,4},{6,7},{7,6},{8,9},{9,8},{10,11... | collective-permute-start | bytes 1474568 | tf_op jit(solution)/shard_map/ppermute | solution.py:1177
  222.0 7.0 %copy-start.9 = (bf16[2,4,160,128]{3,2,1,0:T(8,128)(2,1)S(1)}, bf16[2,4,160,128]{3,2,1,0:T(8,128)(2,1)}, u32[]{:S(2)}) copy-start(bf16[2,4,160,128]{3,2,1,0:T(8,128)(2,1)} %copy-done.8) | copy-start | bytes 983044
  227.6 5.7 %copy-start.6 = (bf16[464,384]{1,0:T(8,128)(2,1)S(1)}, bf16[464,384]{1,0:T(8,128)(2,1)}, u32[]{:S(2)}) copy-start(bf16[464,384]{1,0:T(8,128)(2,1)} %get-tuple-element.123) | copy-start | bytes 1069060
  227.6 27.9 %collective-permute-start.15 = (bf16[512,768]{1,0:T(8,128)(2,1)}, bf16[512,768]{1,0:T(8,128)(2,1)}, u32[]{:S(2)}, u32[]{:S(2)}) collective-permute-start(bf16[512,768]{1,0:T(8,128)(2,1)} %get-tuple-element.119), channel_id=1, source_target_pairs={{0,1},{1,0},{2,3},{3,2},{4,5},{5,4},{6,7},{7,6},{8,9},{9,8},{10,11... | collective-permute-start | bytes 2359304 | tf_op jit(solution)/shard_map/ppermute | solution.py:1177
  235.6 15.2 %collective-permute-start.17 = (bf16[160,384]{1,0:T(8,128)(2,1)S(1)}, bf16[160,384]{1,0:T(8,128)(2,1)S(1)}, u32[]{:S(2)}, u32[]{:S(2)}) collective-permute-start(bf16[160,384]{1,0:T(8,128)(2,1)S(1)} %get-tuple-element.143), channel_id=1, source_target_pairs={{0,8},{2,10},{4,12},{6,14},{8,0},{10,2},{12,4},{14,6},{16,24},{18,... | collective-permute-start | bytes 368648 | tf_op jit(solution)/shard_map/ppermute | solution.py:1180
  242.7 11.4 %collective-permute-start.18 = (bf16[160,384]{1,0:T(8,128)(2,1)S(1)}, bf16[160,384]{1,0:T(8,128)(2,1)S(1)}, u32[]{:S(2)}, u32[]{:S(2)}) collective-permute-start(bf16[160,384]{1,0:T(8,128)(2,1)S(1)} %get-tuple-element.145), channel_id=1, source_target_pairs={{0,16},{2,18},{4,20},{6,22},{8,24},{10,26},{12,28},{14,30},{16,0},... | collective-permute-start | bytes 368648 | tf_op jit(solution)/shard_map/ppermute | solution.py:1180
  243.8 10.3 %collective-permute-start.19 = (bf16[160,384]{1,0:T(8,128)(2,1)S(1)}, bf16[160,384]{1,0:T(8,128)(2,1)S(1)}, u32[]{:S(2)}, u32[]{:S(2)}) collective-permute-start(bf16[160,384]{1,0:T(8,128)(2,1)S(1)} %get-tuple-element.144), channel_id=1, source_target_pairs={{0,24},{2,26},{4,28},{6,30},{8,16},{10,18},{12,20},{14,22},{16,8},... | collective-permute-start | bytes 368648 | tf_op jit(solution)/shard_map/ppermute | solution.py:1180

commit v8 on v7

--- a/solution.py
+++ b/solution.py
@@ -337,6 +337,7 @@
 GROUP = 256
 PER_GROUP = GROUP // HEAD
 TILE = 256
+KEYS = 512
 TOKENS = 512
 VMEM_LIMIT = 60 * 2**20
 SCALAR = pl.BlockSpec(memory_space=pltpu.SMEM)
@@ -968,14 +969,14 @@
     kt_ref[...] = jnp.transpose(k_ref[...])
 
     def block(j, carry):
-        rows = pl.ds(pl.multiple_of(j * TILE, TILE), TILE)
+        rows = pl.ds(pl.multiple_of(j * KEYS, KEYS), KEYS)
         kb = k_ref[rows, :]
         vb = v_ref[rows, :]
         mask = jnp.where(segc_ref[rows, :] == segr, 0.0, NEGATIVE)
-        dk = jnp.zeros((TILE, GROUP), F32)
-        dv = jnp.zeros((TILE, GROUP), F32)
+        dk = jnp.zeros((KEYS, GROUP), F32)
+        dv = jnp.zeros((KEYS, GROUP), F32)
         for head in range(PER_GROUP):
-            mine = head_lanes((TILE, GROUP), head)
+            mine = head_lanes((KEYS, GROUP), head)
             km = jnp.where(mine, kb, BF16(0)) * BF16(HEAD**-0.5)
             vm = jnp.where(mine, vb, BF16(0))
             s = mm(km, q_ref[...], NT) + mask
@@ -992,7 +993,7 @@
         grads_ref[2, rows, :] = dvb
         return carry + row_sum(dvb.astype(F32))
 
-    dv_sum = lax.fori_loop(0, length // TILE, block, jnp.zeros((1, GROUP), F32), unroll=True)
+    dv_sum = lax.fori_loop(0, length // KEYS, block, jnp.zeros((1, GROUP), F32), unroll=True)
     dq = jnp.transpose(total_ref[...] * HEAD**-0.5).astype(BF16)
     grads_ref[0] = dq
     sums_ref[...] = jnp.zeros_like(sums_ref)

time: 260 us -> 259 us (level)
  no operation moved by 1% of the time
where the time goes in v8:
time: 259 us; the launch traced here: 257 us
  Pallas kernels  169 us (65%)
  starting transfers between devices  29.2 us (11%)
  waiting for transfers between devices  25 us (10%)
  other arithmetic  17.4 us (7%)
  local copies, waits for them, and re-layouts  14.6 us (6%)
    pallas_call x12, Pallas kernels, run(): pl.pallas_call(body, grid_spec=pltpu.PrefetchScalarGridSpec(num_scalar_pr...  169 us
    ppermute x14, starting transfers between devices, seq_swap(): return lax.ppermute(x, 'seq', [(i, i ^ bit) for i in range(16)])  18.6 us
    ppermute x9, waiting for transfers between devices, trade(): return lax.ppermute(x, 'blk', [(0, 1), (1, 0)])  15.3 us
    ppermute x9, starting transfers between devices, trade(): return lax.ppermute(x, 'blk', [(0, 1), (1, 0)])  10.6 us
    ppermute x14, waiting for transfers between devices, seq_swap(): return lax.ppermute(x, 'seq', [(i, i ^ bit) for i in range(16)])  9.69 us
  transfers between devices with their start and end apart: 23, of which 5 were waited for; matrix products, arithmetic and copies ran while one was open for 11% of the time, Pallas kernels for 43%

profile of v8, /device:TPU:0, one launch (start us, length us, event | category | flops | bytes accessed | tf_op | source)
XLA Modules:
  0.0 257.4 jit_solution(10275407586343997281)
XLA Ops:
  0.8 1.3 dynamic-slice_bitcast_fusion.1
  2.1 3.0 %collective-permute-start = (bf16[512,768]{1,0:T(8,128)(2,1)S(1)}, bf16[512,768]{1,0:T(8,128)(2,1)S(1)}, u32[]{:S(2)}, u32[]{:S(2)}) collective-permute-start(bf16[512,768]{1,0:T(8,128)(2,1)S(1)} %dynamic-slice_bitcast_fusion.1), channel_id=1, source_target_pairs={{0,1},{1,0},{2,3},{3,2},{4,5},{5,4},{6,7},{7,6},{8,9},{9,8},{10,11... | collective-permute-start | bytes 2359304 | tf_op jit(solution)/shard_map/ppermute | solution.py:1178
  7.1 0.6 concatenate.23.refs_9_
  7.7 14.9 %collective-permute-done.1 = s32[512]{0:T(512)S(1)} collective-permute-done((s32[512]{0:T(512)S(1)}, s32[512]{0:T(512)S(1)}, u32[]{:S(2)}, u32[]{:S(2)}) %collective-permute-start.1) | collective-permute-done | bytes 2080 | tf_op jit(solution)/shard_map/ppermute | solution.py:1178
  23.9 0.9 dynamic-slice_bitcast_fusion
  24.9 1.7 collective-permute-start.2
  26.6 0.9 copy-done.21
  27.5 26.3 %attention_forward.1 = (bf16[1024,768]{1,0:T(8,128)(2,1)}, bf16[1024,768]{1,0:T(8,128)(2,1)}, bf16[1024,768]{1,0:T(8,128)(2,1)}, bf16[2,1024,384]{2,1,0:T(8,128)...) custom-call(s32[1]{0:T(128)} %bitcast.refs_0_, bf16[2,512,768]{2,1,0:T(8,128)(2,1)} %refs_1_.1, ...), custom_call_target="tpu_custom_call" | custom-call | flops 160000000000 | bytes 1 | tf_op jit(solution)/shard_map/attention_forward/pallas_call | solution.py:380
  53.9 48.1 %token_pass.1 = (bf16[2,512,768]{2,1,0:T(8,128)(2,1)}, bf16[256,768]{1,0:T(8,128)(2,1)}, bf16[256,768]{1,0:T(8,128)(2,1)}, bf16[1024,768]{1,0:T(8,128)(2,1)}, bf...) custom-call(s32[1]{0:T(128)} %bitcast.refs_0_, ...), custom_call_target="tpu_custom_call" | custom-call | flops 230000001024 | bytes 1 | tf_op jit(solution)/shard_map/token_pass/pallas_call | solution.py:380
  101.9 9.4 %outer_grad.1 = (bf16[2,2,4,224,384]{4,3,2,1,0:T(8,128)(2,1)}, bf16[2,2,4,224,384]{4,3,2,1,0:T(8,128)(2,1)}) custom-call(s32[1]{0:T(128)} %bitcast.10.refs_0_.refs_7_, bf16[1024,3072]{1,0:T(8,128)(2,1)} %get-tuple-element.83.refs_1_, bf16[1024,768]{1,0:T(8,128)(2,1)} %get-tuple-element.84.refs_2_, f32[8,768]{1,0:T(8,128)} %get-tuple-element.85.refs_3_, ...), custom_call_target="tpu_custom_call" | custom-call | flops 44999999488 | bytes 1 | tf_op jit(solution)/shard_map/outer_grad/pallas_call | solution.py:380
  111.4 11.6 %inner_grad.1 = (bf16[2,2,4,5,48,384]{5,4,3,2,1,0:T(8,128)(2,1)}, bf16[2,2,4,5,48,384]{5,4,3,2,1,0:T(8,128)(2,1)}, bf16[2,2,4,224,384]{4,3,2,1,0:T(8,128)(2,1)}) custom-call(s32[1]{0:T(128)} %bitcast.10.refs_0_.refs_7_, bf16[1024,768]{1,0:T(8,128)(2,1)} %get-tuple-element.80.refs_1_, ...), custom_call_target="tpu_custom_call", output_to_operand_aliasing={{2}: (6, {})} | custom-call | flops 60000002048 | bytes 1 | tf_op jit(solution)/shard_map/inner_grad/pallas_call | solution.py:380
  124.0 3.8 %halve_first.1 = (bf16[2,4,224,384]{3,2,1,0:T(8,128)(2,1)}, bf16[256,768]{1,0:T(8,128)(2,1)}) custom-call(s32[3]{0:T(128)} %pad_add_fusion.1.refs_0_, bf16[2,2,4,224,384]{4,3,2,1,0:T(8,128)(2,1)} %get-tuple-element.88.refs_1_.refs_10_, bf16[2,2,4,224,384]{4,3,2,1,0:T(8,128)(2,1)} %collective-permute-done.3.refs_2_, ...), custom_call_target="tpu_custom_call", output_to_operand_aliasing={{1}: (3, {})} | custom-call | flops 10000000000 | bytes 1 | tf_op jit(solution)/shard_map/halve_first/pallas_call | solution.py:380
  128.2 1.8 collective-permute-start.6
  129.9 4.0 %fusion.refs_8_ = bf16[2,4,5,48,384]{4,3,2,1,0:T(8,128)(2,1)} fusion(bf16[2,2,4,5,48,384]{5,4,3,2,1,0:T(8,128)(2,1)S(1)} %collective-permute-done.4, s32[]{:T(128)S(6)} %select_n.36, bf16[2,2,4,5,48,384]{5,4,3,2,1,0:T(8,128)(2,1)} %get-tuple-element.92.refs_11_), kind=kLoop, calls=%fused_computation.1 | loop fusion | flops 3686400 | bytes 4423684 | tf_op jit(solution)/shard_map/convert_element_type | solution.py:1246
  133.9 1.5 collective-permute-start.7
  135.4 14.8 %attention_backward.3 = (bf16[3,1024,256]{2,1,0:T(8,128)(2,1)}, f32[8,256]{1,0:T(8,128)}) custom-call(bf16[1024,768]{1,0:T(8,128)(2,1)} %get-tuple-element.75.refs_0_, bf16[1024,768]{1,0:T(8,128)(2,1)} %get-tuple-element.76.refs_1_, bf16[1024,768]{1,0:T(8,128)(2,1)} %get-tuple-element.77.refs_2_, bf16[2,1024,384]{2,1,0:T(8,128)(2,1)} %get-tuple-element.78.refs_3_, ...), custom_call_target="tpu_custom_call" | custom-call | flops 80000000000 | bytes 1 | tf_op jit(solution)/shard_map/attention_backward/pallas_call | solution.py:380
  150.2 0.8 copy-done.22
  151.0 19.3 %attention_backward.4 = (bf16[3,1024,256]{2,1,0:T(8,128)(2,1)}, f32[8,256]{1,0:T(8,128)}, bf16[2,2,4,160,256]{4,3,2,1,0:T(8,128)(2,1)}, bf16[2,2,4,160,256]{4,3,...) custom-call(bf16[1024,768]{1,0:T(8,128)(2,1)} %get-tuple-element.75., ...), custom_call_target="tpu_custom_call", output_to_operand_aliasing={{4}: (10, {}), {5}: (11, {}), {6}: (12, {}), {7}: (13, {})} | custom-call | flops 80000000000 | bytes 1 | tf_op jit(solution)/shard_map/attention_backward/pallas_call | solution.py:380
  170.9 1.8 fusion.4.refs_14_
  172.7 1.6 collective-permute-start.8
  174.2 1.9 fusion.2.refs_15_
  177.1 16.9 %attention_backward.5 = (bf16[3,1024,256]{2,1,0:T(8,128)(2,1)}, f32[8,256]{1,0:T(8,128)}, bf16[2,2,4,160,128]{4,3,2,1,0:T(8,128)(2,1)}, bf16[2,2,4,160,128]{4,3,...) custom-call(bf16[1024,768]{1,0:T(8,128)(2,1)} %get-tuple-element.75., ...), custom_call_target="tpu_custom_call", output_to_operand_aliasing={{4}: (11, {}), {5}: (12, {}), {6}: (13, {})} | custom-call | flops 80000000000 | bytes 1 | tf_op jit(solution)/shard_map/attention_backward/pallas_call | solution.py:380
  194.0 1.3 fusion.5.refs_11_
  195.3 1.2 collective-permute-start.13
  196.9 5.0 %quarter.1 = (bf16[464,384]{1,0:T(8,128)(2,1)}, bf16[464,384]{1,0:T(8,128)(2,1)}, bf16[464,384]{1,0:T(8,128)(2,1)}, bf16[464,384]{1,0:T(8,128)(2,1)}, bf16[256,7...) custom-call(s32[3]{0:T(128)} %pad_add_fusion.1.refs_0_, ...), custom_call_target="tpu_custom_call", output_to_operand_aliasing={{4}: (9, {}), {5}: (10, {})} | custom-call | flops 10000000000 | bytes 1 | tf_op jit(solution)/shard_map/quarter/pallas_call | solution.py:380
  201.9 1.1 fusion.8.refs_13_
  203.6 1.6 collective-permute-start.20
  205.2 2.6 %collective-permute-start.21 = (bf16[464,384]{1,0:T(8,128)(2,1)}, bf16[464,384]{1,0:T(8,128)(2,1)}, u32[]{:S(2)}, u32[]{:S(2)}) collective-permute-start(bf16[464,384]{1,0:T(8,128)(2,1)} %get-tuple-element.125), channel_id=1, source_target_pairs={{0,16},{2,18},{4,20},{6,22},{8,24},{10,26},{12,28},{14,30},{16,0},... | collective-permute-start | bytes 1069064 | tf_op jit(solution)/shard_map/ppermute | solution.py:1181
  208.0 6.1 %hidden_home.1 = (f32[2,512,768]{2,1,0:T(8,128)}, bf16[2,512,768]{2,1,0:T(8,128)(2,1)}, bf16[2,2,4,160,256]{4,3,2,1,0:T(8,128)(2,1)}, bf16[2,2,4,160,128]{4,3,2,1,0:T(8,128)(2,1)}) custom-call(s32[1]{0:T(128)} %bitcast.refs_0_, f32[1024,768]{1,0:T(8,128)} %get-tuple-element.74.refs_1_.refs_0_, ...), custom_call_target="tpu_custom_call", output_to_operand_aliasing={{1}: (10, {}), {2}: (11, {}), {3}: (12, {})} | custom-call | flops 30000001024 | bytes 1 | tf_op jit(solution)/shard_map/hidden_home/pallas_call | solution.py:380
  214.1 1.2 fusion.7
  215.3 4.2 %collective-permute-done.14 = bf16[2,4,160,128]{3,2,1,0:T(8,128)(2,1)S(1)} collective-permute-done((bf16[2,4,160,128]{3,2,1,0:T(8,128)(2,1)S(1)}, bf16[2,4,160,128]{3,2,1,0:T(8,128)(2,1)S(1)}, u32[]{:S(2)}, u32[]{:S(2)}) %collective-permute-start.14) | collective-permute-done | bytes 327712 | tf_op jit(solution)/shard_map/ppermute | solution.py:1181
  219.5 1.1 fusion.10
  220.7 0.6 collective-permute-start.16
  221.5 5.7 %hidden_away.1 = (bf16[512,768]{1,0:T(8,128)(2,1)}, bf16[2,2,4,160,256]{4,3,2,1,0:T(8,128)(2,1)}, bf16[2,2,4,160,128]{4,3,2,1,0:T(8,128)(2,1)}, bf16[464,384]{1,0:T(8,128)(2,1)}) custom-call(f32[1024,768]{1,0:T(8,128)} %get-tuple-element.74.refs_1_.refs_0_, ...), custom_call_target="tpu_custom_call", output_to_operand_aliasing={{1}: (7, {}), {2}: (8, {}), {3}: (9, {})} | custom-call | flops 30000001024 | bytes 1 | tf_op jit(solution)/shard_map/hidden_away/pallas_call | solution.py:380
  227.1 1.3 collective-permute-start.15
  228.5 0.9 fusion.26
  229.4 1.3 fusion.22
  230.7 2.2 collective-permute-done.21
  232.9 1.4 add_add_fusion
  234.3 0.8 fusion.29
  235.1 7.1 %collective-permute-start.17 = (bf16[160,384]{1,0:T(8,128)(2,1)S(1)}, bf16[160,384]{1,0:T(8,128)(2,1)S(1)}, u32[]{:S(2)}, u32[]{:S(2)}) collective-permute-start(bf16[160,384]{1,0:T(8,128)(2,1)S(1)} %get-tuple-element.143), channel_id=1, source_target_pairs={{0,8},{2,10},{4,12},{6,14},{8,0},{10,2},{12,4},{14,6},{16,24},{18,... | collective-permute-start | bytes 368648 | tf_op jit(solution)/shard_map/ppermute | solution.py:1181
  242.2 1.1 collective-permute-start.18
  243.3 1.4 collective-permute-start.19
  244.7 0.6 slice.100
  245.3 0.7 copy.54
  250.3 3.3 %collective-permute-done.18 = bf16[160,384]{1,0:T(8,128)(2,1)S(1)} collective-permute-done((bf16[160,384]{1,0:T(8,128)(2,1)S(1)}, bf16[160,384]{1,0:T(8,128)(2,1)S(1)}, u32[]{:S(2)}, u32[]{:S(2)}) %collective-permute-start.18) | collective-permute-done | bytes 122912 | tf_op jit(solution)/shard_map/ppermute | solution.py:1181
  254.3 0.7 fusion.30
  255.0 2.2 place_far.1
  (100 shorter events, 11.9 us)
Async XLA Ops:
  0.7 4.4 %copy-start.11 = (s32[2,512]{1,0:T(2,128)S(1)}, s32[2,512]{1,0:T(2,128)}, u32[]{:S(2)}) copy-start(s32[2,512]{1,0:T(2,128)} %param.19) | copy-start | bytes 12292
  0.7 4.5 %copy-start.13 = (bf16[768]{0:T(1024)(128)(2,1)S(1)}, bf16[768]{0:T(1024)(128)(2,1)}, u32[]{:S(2)}) copy-start(bf16[768]{0:T(1024)(128)(2,1)} %param.21) | copy-start | bytes 4612
  0.7 5.1 %copy-start.14 = (bf16[768]{0:T(1024)(128)(2,1)S(1)}, bf16[768]{0:T(1024)(128)(2,1)}, u32[]{:S(2)}) copy-start(bf16[768]{0:T(1024)(128)(2,1)} %param.24) | copy-start | bytes 4612
  0.7 5.7 %copy-start.15 = (bf16[768]{0:T(1024)(128)(2,1)S(1)}, bf16[768]{0:T(1024)(128)(2,1)}, u32[]{:S(2)}) copy-start(bf16[768]{0:T(1024)(128)(2,1)} %param.26) | copy-start | bytes 4612
  0.7 5.7 %copy-start.16 = (bf16[768]{0:T(1024)(128)(2,1)S(1)}, bf16[768]{0:T(1024)(128)(2,1)}, u32[]{:S(2)}) copy-start(bf16[768]{0:T(1024)(128)(2,1)} %param.27) | copy-start | bytes 4612
  0.7 5.7 %copy-start.17 = (bf16[768]{0:T(1024)(128)(2,1)S(1)}, bf16[768]{0:T(1024)(128)(2,1)}, u32[]{:S(2)}) copy-start(bf16[768]{0:T(1024)(128)(2,1)} %param.28) | copy-start | bytes 4612
  0.7 5.7 %copy-start.18 = (bf16[768]{0:T(1024)(128)(2,1)S(1)}, bf16[768]{0:T(1024)(128)(2,1)}, u32[]{:S(2)}) copy-start(bf16[768]{0:T(1024)(128)(2,1)} %param.32) | copy-start | bytes 4612
  0.7 5.7 %copy-start.19 = (bf16[768]{0:T(1024)(128)(2,1)S(1)}, bf16[768]{0:T(1024)(128)(2,1)}, u32[]{:S(2)}) copy-start(bf16[768]{0:T(1024)(128)(2,1)} %param.33) | copy-start | bytes 4612
  0.7 5.7 %copy-start.20 = (bf16[768]{0:T(1024)(128)(2,1)S(1)}, bf16[768]{0:T(1024)(128)(2,1)}, u32[]{:S(2)}) copy-start(bf16[768]{0:T(1024)(128)(2,1)} %param.34) | copy-start | bytes 4612
  0.7 5.7 %copy-start.10 = (bf16[3072]{0:T(1024)(128)(2,1)S(1)}, bf16[3072]{0:T(1024)(128)(2,1)}, u32[]{:S(2)}) copy-start(bf16[3072]{0:T(1024)(128)(2,1)} %param.30) | copy-start | bytes 18436
  0.8 23.2 %copy-start.5 = (bf16[2,512,768]{2,1,0:T(8,128)(2,1)S(1)}, bf16[2,512,768]{2,1,0:T(8,128)(2,1)}, u32[]{:S(2)}) copy-start(bf16[2,512,768]{2,1,0:T(8,128)(2,1)} %refs_3_.3) | copy-start | bytes 4718596
  2.1 24.5 %collective-permute-start = (bf16[512,768]{1,0:T(8,128)(2,1)S(1)}, bf16[512,768]{1,0:T(8,128)(2,1)S(1)}, u32[]{:S(2)}, u32[]{:S(2)}) collective-permute-start(bf16[512,768]{1,0:T(8,128)(2,1)S(1)} %dynamic-slice_bitcast_fusion.1), channel_id=1, source_target_pairs={{0,1},{1,0},{2,3},{3,2},{4,5},{5,4},{6,7},{7,6},{8,9},{9,8},{10,11... | collective-permute-start | bytes 2359304 | tf_op jit(solution)/shard_map/ppermute | solution.py:1178
  5.1 17.6 %collective-permute-start.1 = (s32[512]{0:T(512)S(1)}, s32[512]{0:T(512)S(1)}, u32[]{:S(2)}, u32[]{:S(2)}) collective-permute-start(s32[512]{0:T(512)S(1)} %bitcast.115), channel_id=1, source_target_pairs={{0,1},{1,0},{2,3},{3,2},{4,5},{5,4},{6,7},{7,6},{8,9},{9,8},{10,11... | collective-permute-start | bytes 6152 | tf_op jit(solution)/shard_map/ppermute | solution.py:1178
  22.7 3.9 %copy-start.12 = (s32[1024]{0:T(1024)}, s32[1024]{0:T(1024)S(1)}, u32[]{:S(2)}) copy-start(s32[1024]{0:T(1024)S(1)} %pad_add_fusion) | copy-start | bytes 12292
  24.9 29.0 %collective-permute-start.2 = (bf16[512,768]{1,0:T(8,128)(2,1)}, bf16[512,768]{1,0:T(8,128)(2,1)}, u32[]{:S(2)}, u32[]{:S(2)}) collective-permute-start(bf16[512,768]{1,0:T(8,128)(2,1)} %dynamic-slice_bitcast_fusion), channel_id=1, source_target_pairs={{0,1},{1,0},{2,3},{3,2},{4,5},{5,4},{6,7},{7,6},{8,9},{9,8},{10,11... | collective-permute-start | bytes 2359304 | tf_op jit(solution)/shard_map/ppermute | solution.py:1178
  26.6 0.9 copy-start.21
  111.4 12.7 %collective-permute-start.3 = (bf16[2,2,4,224,384]{4,3,2,1,0:T(8,128)(2,1)}, bf16[2,2,4,224,384]{4,3,2,1,0:T(8,128)(2,1)}, u32[]{:S(2)}, u32[]{:S(2)}) collective-permute-start(bf16[2,2,4,224,384]{4,3,2,1,0:T(8,128)(2,1)} %get-tuple-element.89), channel_id=1, source_target_pairs={{0,2},{2,0},{4,6},{6,4},{8,10},{10,8},{12,14},{14,12},{16,18},{18,... | collective-permute-start | bytes 8257544 | tf_op jit(solution)/shard_map/ppermute | solution.py:1181
  123.0 6.9 %collective-permute-start.4 = (bf16[2,2,4,5,48,384]{5,4,3,2,1,0:T(8,128)(2,1)}, bf16[2,2,4,5,48,384]{5,4,3,2,1,0:T(8,128)(2,1)S(1)}, u32[]{:S(2)}, u32[]{:S(2)}) collective-permute-start(bf16[2,2,4,5,48,384]{5,4,3,2,1,0:T(8,128)(2,1)} %get-tuple-element.93), channel_id=1, source_target_pairs={{0,2},{2,0},{4,6},{6,4},{8,10},{10,8},{12,14},{14,12},{16,18},{18,... | collective-permute-start | bytes 8847368 | tf_op jit(solution)/shard_map/ppermute | solution.py:1181
  127.9 22.4 %collective-permute-start.5 = (bf16[256,768]{1,0:T(8,128)(2,1)}, bf16[256,768]{1,0:T(8,128)(2,1)S(1)}, u32[]{:S(2)}, u32[]{:S(2)}) collective-permute-start(bf16[256,768]{1,0:T(8,128)(2,1)} %get-tuple-element.95), channel_id=1, source_target_pairs={{0,1},{1,0},{2,3},{3,2},{4,5},{5,4},{6,7},{7,6},{8,9},{9,8},{10,11... | collective-permute-start | bytes 1179656 | tf_op jit(solution)/shard_map/ppermute | solution.py:1178
  128.2 42.7 %collective-permute-start.6 = (bf16[2,4,224,384]{3,2,1,0:T(8,128)(2,1)}, bf16[2,4,224,384]{3,2,1,0:T(8,128)(2,1)}, u32[]{:S(2)}, u32[]{:S(2)}) collective-permute-start(bf16[2,4,224,384]{3,2,1,0:T(8,128)(2,1)} %get-tuple-element.91.refs_7_), channel_id=1, source_target_pairs={{0,4},{2,6},{4,0},{6,2},{8,12},{10,14},{12,8},{14,10},{16,20},{18,... | collective-permute-start | bytes 4128776 | tf_op jit(solution)/shard_map/ppermute | solution.py:1181
  129.9 4.0 %copy-start = (bf16[2,2,4,5,48,384]{5,4,3,2,1,0:T(8,128)(2,1)}, bf16[2,2,4,5,48,384]{5,4,3,2,1,0:T(8,128)(2,1)S(1)}, u32[]{:S(2)}) copy-start(bf16[2,2,4,5,48,384]{5,4,3,2,1,0:T(8,128)(2,1)S(1)} %collective-permute-done.4) | copy-start | bytes 8847364
  133.9 40.3 %collective-permute-start.7 = (bf16[2,4,5,48,384]{4,3,2,1,0:T(8,128)(2,1)}, bf16[2,4,5,48,384]{4,3,2,1,0:T(8,128)(2,1)}, u32[]{:S(2)}, u32[]{:S(2)}) collective-permute-start(bf16[2,4,5,48,384]{4,3,2,1,0:T(8,128)(2,1)} %fusion.refs_8_), channel_id=1, source_target_pairs={{0,1},{1,0},{2,3},{3,2},{4,5},{5,4},{6,7},{7,6},{8,9},{9,8},{10,11... | collective-permute-start | bytes 4423688 | tf_op jit(solution)/shard_map/ppermute | solution.py:1178
  150.2 0.8 copy-start.22
  170.3 23.7 %collective-permute-start.11 = (bf16[2,2,4,160,256]{4,3,2,1,0:T(8,128)(2,1)}, bf16[2,2,4,160,256]{4,3,2,1,0:T(8,128)(2,1)S(1)}, u32[]{:S(2)}, u32[]{:S(2)}) collective-permute-start(bf16[2,2,4,160,256]{4,3,2,1,0:T(8,128)(2,1)} %get-tuple-element.110), channel_id=1, source_target_pairs={{0,2},{2,0},{4,6},{6,4},{8,10},{10,8},{12,14},{14,12},{16,18},{18,... | collective-permute-start | bytes 3932168 | tf_op jit(solution)/shard_map/ppermute | solution.py:1181
  170.3 26.2 %collective-permute-start.10 = (bf16[256,768]{1,0:T(8,128)(2,1)}, bf16[256,768]{1,0:T(8,128)(2,1)}, u32[]{:S(2)}, u32[]{:S(2)}) collective-permute-start(bf16[256,768]{1,0:T(8,128)(2,1)} %get-tuple-element.107), channel_id=1, source_target_pairs={{0,1},{1,0},{2,3},{3,2},{4,5},{5,4},{6,7},{7,6},{8,9},{9,8},{10,11... | collective-permute-start | bytes 1179656 | tf_op jit(solution)/shard_map/ppermute | solution.py:1178
  172.7 4.0 %copy-start.2 = (bf16[4,224,384]{2,1,0:T(8,128)(2,1)}, bf16[4,224,384]{2,1,0:T(8,128)(2,1)S(1)}, u32[]{:S(2)}) copy-start(bf16[4,224,384]{2,1,0:T(8,128)(2,1)S(1)} %fusion.4.refs_14_) | copy-start | bytes 2064388
  172.7 24.2 %collective-permute-start.8 = (bf16[4,224,384]{2,1,0:T(8,128)(2,1)S(1)}, bf16[4,224,384]{2,1,0:T(8,128)(2,1)}, u32[]{:S(2)}, u32[]{:S(2)}) collective-permute-start(bf16[4,224,384]{2,1,0:T(8,128)(2,1)S(1)} %fusion.4.refs_14_), channel_id=1, source_target_pairs={{0,1},{1,0},{2,3},{3,2},{4,5},{5,4},{6,7},{7,6},{8,9},{9,8},{10,11... | collective-permute-start | bytes 2064392 | tf_op jit(solution)/shard_map/ppermute | solution.py:1178
  176.1 0.9 copy-start.1
  176.1 20.8 %collective-permute-start.9 = (bf16[4,5,48,384]{3,2,1,0:T(8,128)(2,1)S(1)}, bf16[4,5,48,384]{3,2,1,0:T(8,128)(2,1)}, u32[]{:S(2)}, u32[]{:S(2)}) collective-permute-start(bf16[4,5,48,384]{3,2,1,0:T(8,128)(2,1)S(1)} %fusion.2.refs_15_), channel_id=1, source_target_pairs={{0,4},{2,6},{4,0},{6,2},{8,12},{10,14},{12,8},{14,10},{16,20},{18,... | collective-permute-start | bytes 2211848 | tf_op jit(solution)/shard_map/ppermute | solution.py:1181
  194.0 8.0 %collective-permute-start.12 = (bf16[2,2,4,160,128]{4,3,2,1,0:T(8,128)(2,1)}, bf16[2,2,4,160,128]{4,3,2,1,0:T(8,128)(2,1)S(1)}, u32[]{:S(2)}, u32[]{:S(2)}) collective-permute-start(bf16[2,2,4,160,128]{4,3,2,1,0:T(8,128)(2,1)} %get-tuple-element.114), channel_id=1, source_target_pairs={{0,2},{2,0},{4,6},{6,4},{8,10},{10,8},{12,14},{14,12},{16,18},{18,... | collective-permute-start | bytes 1966088 | tf_op jit(solution)/shard_map/ppermute | solution.py:1181
  195.2 1.7 copy-start.3
  195.3 18.8 %collective-permute-start.13 = (bf16[2,4,160,256]{3,2,1,0:T(8,128)(2,1)S(1)}, bf16[2,4,160,256]{3,2,1,0:T(8,128)(2,1)}, u32[]{:S(2)}, u32[]{:S(2)}) collective-permute-start(bf16[2,4,160,256]{3,2,1,0:T(8,128)(2,1)S(1)} %fusion.5.refs_11_), channel_id=1, source_target_pairs={{0,4},{2,6},{4,0},{6,2},{8,12},{10,14},{12,8},{14,10},{16,20},{18,... | collective-permute-start | bytes 1966088 | tf_op jit(solution)/shard_map/ppermute | solution.py:1181
  203.0 5.0 %copy-start.7 = (bf16[2,4,160,128]{3,2,1,0:T(8,128)(2,1)}, bf16[2,4,160,128]{3,2,1,0:T(8,128)(2,1)S(1)}, u32[]{:S(2)}) copy-start(bf16[2,4,160,128]{3,2,1,0:T(8,128)(2,1)S(1)} %fusion.8.refs_13_) | copy-start | bytes 983044
  203.0 16.5 %collective-permute-start.14 = (bf16[2,4,160,128]{3,2,1,0:T(8,128)(2,1)S(1)}, bf16[2,4,160,128]{3,2,1,0:T(8,128)(2,1)S(1)}, u32[]{:S(2)}, u32[]{:S(2)}) collective-permute-start(bf16[2,4,160,128]{3,2,1,0:T(8,128)(2,1)S(1)} %fusion.8.refs_13_), channel_id=1, source_target_pairs={{0,4},{2,6},{4,0},{6,2},{8,12},{10,14},{12,8},{14,10},{16,20},{18,... | collective-permute-start | bytes 983048 | tf_op jit(solution)/shard_map/ppermute | solution.py:1181
  203.6 27.1 %collective-permute-start.20 = (bf16[464,384]{1,0:T(8,128)(2,1)}, bf16[464,384]{1,0:T(8,128)(2,1)}, u32[]{:S(2)}, u32[]{:S(2)}) collective-permute-start(bf16[464,384]{1,0:T(8,128)(2,1)} %get-tuple-element.124), channel_id=1, source_target_pairs={{0,8},{2,10},{4,12},{6,14},{8,0},{10,2},{12,4},{14,6},{16,24},{18,... | collective-permute-start | bytes 1069064 | tf_op jit(solution)/shard_map/ppermute | solution.py:1181
  205.2 27.7 %collective-permute-start.21 = (bf16[464,384]{1,0:T(8,128)(2,1)}, bf16[464,384]{1,0:T(8,128)(2,1)}, u32[]{:S(2)}, u32[]{:S(2)}) collective-permute-start(bf16[464,384]{1,0:T(8,128)(2,1)} %get-tuple-element.125), channel_id=1, source_target_pairs={{0,16},{2,18},{4,20},{6,22},{8,24},{10,26},{12,28},{14,30},{16,0},... | collective-permute-start | bytes 1069064 | tf_op jit(solution)/shard_map/ppermute | solution.py:1181
  207.8 25.1 %collective-permute-start.22 = (bf16[464,384]{1,0:T(8,128)(2,1)}, bf16[464,384]{1,0:T(8,128)(2,1)}, u32[]{:S(2)}, u32[]{:S(2)}) collective-permute-start(bf16[464,384]{1,0:T(8,128)(2,1)} %get-tuple-element.126), channel_id=1, source_target_pairs={{0,24},{2,26},{4,28},{6,30},{8,16},{10,18},{12,20},{14,22},{16,8},... | collective-permute-start | bytes 1069064 | tf_op jit(solution)/shard_map/ppermute | solution.py:1181
  219.5 1.1 copy-start.8
  220.7 0.8 copy-start.4
  220.7 14.4 %collective-permute-start.16 = (bf16[4,160,384]{2,1,0:T(8,128)(2,1)S(1)}, bf16[4,160,384]{2,1,0:T(8,128)(2,1)S(1)}, u32[]{:S(2)}, u32[]{:S(2)}) collective-permute-start(bf16[4,160,384]{2,1,0:T(8,128)(2,1)S(1)} %pad_maximum_fusion.refs_10_), channel_id=1, source_target_pairs={{0,1},{1,0},{2,3},{3,2},{4,5},{5,4},{6,7},{7,6},{8,9},{9,8},{10,11... | collective-permute-start | bytes 1474568 | tf_op jit(solution)/shard_map/ppermute | solution.py:1178
  221.5 7.0 %copy-start.9 = (bf16[2,4,160,128]{3,2,1,0:T(8,128)(2,1)S(1)}, bf16[2,4,160,128]{3,2,1,0:T(8,128)(2,1)}, u32[]{:S(2)}) copy-start(bf16[2,4,160,128]{3,2,1,0:T(8,128)(2,1)} %copy-done.8) | copy-start | bytes 983044
  227.1 5.8 %copy-start.6 = (bf16[464,384]{1,0:T(8,128)(2,1)S(1)}, bf16[464,384]{1,0:T(8,128)(2,1)}, u32[]{:S(2)}) copy-start(bf16[464,384]{1,0:T(8,128)(2,1)} %get-tuple-element.123) | copy-start | bytes 1069060
  227.1 27.9 %collective-permute-start.15 = (bf16[512,768]{1,0:T(8,128)(2,1)}, bf16[512,768]{1,0:T(8,128)(2,1)}, u32[]{:S(2)}, u32[]{:S(2)}) collective-permute-start(bf16[512,768]{1,0:T(8,128)(2,1)} %get-tuple-element.119), channel_id=1, source_target_pairs={{0,1},{1,0},{2,3},{3,2},{4,5},{5,4},{6,7},{7,6},{8,9},{9,8},{10,11... | collective-permute-start | bytes 2359304 | tf_op jit(solution)/shard_map/ppermute | solution.py:1178
  235.1 15.2 %collective-permute-start.17 = (bf16[160,384]{1,0:T(8,128)(2,1)S(1)}, bf16[160,384]{1,0:T(8,128)(2,1)S(1)}, u32[]{:S(2)}, u32[]{:S(2)}) collective-permute-start(bf16[160,384]{1,0:T(8,128)(2,1)S(1)} %get-tuple-element.143), channel_id=1, source_target_pairs={{0,8},{2,10},{4,12},{6,14},{8,0},{10,2},{12,4},{14,6},{16,24},{18,... | collective-permute-start | bytes 368648 | tf_op jit(solution)/shard_map/ppermute | solution.py:1181
  242.2 11.4 %collective-permute-start.18 = (bf16[160,384]{1,0:T(8,128)(2,1)S(1)}, bf16[160,384]{1,0:T(8,128)(2,1)S(1)}, u32[]{:S(2)}, u32[]{:S(2)}) collective-permute-start(bf16[160,384]{1,0:T(8,128)(2,1)S(1)} %get-tuple-element.145), channel_id=1, source_target_pairs={{0,16},{2,18},{4,20},{6,22},{8,24},{10,26},{12,28},{14,30},{16,0},... | collective-permute-start | bytes 368648 | tf_op jit(solution)/shard_map/ppermute | solution.py:1181
  243.3 10.3 %collective-permute-start.19 = (bf16[160,384]{1,0:T(8,128)(2,1)S(1)}, bf16[160,384]{1,0:T(8,128)(2,1)S(1)}, u32[]{:S(2)}, u32[]{:S(2)}) collective-permute-start(bf16[160,384]{1,0:T(8,128)(2,1)S(1)} %get-tuple-element.144), channel_id=1, source_target_pairs={{0,24},{2,26},{4,28},{6,30},{8,16},{10,18},{12,20},{14,22},{16,8},... | collective-permute-start | bytes 368648 | tf_op jit(solution)/shard_map/ppermute | solution.py:1181
